TPU v7x, 32 devices: a whole 2x2x4 slice. The times are simulated.
32 devices in a mesh: batch: 4 (over y, x), neuron: 8 (over z, core).
Axes of the slice: x: 2, y: 2, z: 4, core: 2. Of those that a mesh axis runs over, the one named last changes fastest.
Arguments:
- inputs: float32 [2048, 5120], P('neuron', 'batch'), may hold values from -19 to 19
- weights: float32 [2, 2048, 2048], P(None, 'neuron'), may hold values from -0.1875 to 0.1875
- gains: float32 [2, 2048], P(None, 'neuron'), may hold values from 0.5 to 1.5
- shifts: float32 [2, 2048], P(None, 'neuron'), may hold values from -3 to 3
- decays: float32 [2, 2048], P(None, 'neuron'), may hold values from 0.1 to 0.95
- biases: float32 [2, 2048], P(None, 'neuron'), may hold values from -3 to 3
- lengths: int32 [16], P('batch'), may hold values from 21 to 320, as said below
- frame_mask: int32 [16, 320], P('batch'), may hold values 0 or 1
- grad_out: float32 [2048, 5120], P('neuron', 'batch'), may hold values from -6 to 6
Outputs:
- output: float32 [2048, 5120], P('neuron', 'batch')
- grad_in: float32 [2048, 5120], P('neuron', 'batch')
- grad_weights: float32 [2, 2048, 2048], P(None, 'neuron')
- grad_gains: float32 [2, 2048], P(None, 'neuron')
- grad_shifts: float32 [2, 2048], P(None, 'neuron')
- grad_decays: float32 [2, 2048], P(None, 'neuron')
- grad_biases: float32 [2, 2048], P(None, 'neuron')
Inputs may be any that keep to these rules, and one draw needn't show every extreme that they name: `lengths`: some clip has exactly 320 frames.
All inputs are finite; a program needn't handle non-finite values. No bound on the sum of `frame_mask` on one device may be relied on, other than what follows from the above.
Results may differ from a plain program's by a relative error of at most 0.0003.
Values sent between devices are 32-bit elements; how exact they have to be, the bound alone decides.
No kernel may reach another device: no remote copies, remote signals or barrier semaphores. Data moves between devices by JAX's collectives and lax.ppermute only.
A program may use at most 128 MiB of HBM per device.

v0:
```python
from functools import partial
import math

import jax
import jax.numpy as jnp
from jax import lax
from jax.experimental import pallas as pl
from jax.experimental.pallas import tpu as pltpu
from jax.sharding import Mesh, PartitionSpec as P

LAYERS = 2
EPS = 1e-05
HIGH = lax.Precision.HIGHEST
ROOT_TWO = math.sqrt(2.0)
ROOT_TWO_PI = math.sqrt(2.0 * math.pi)
F32 = jnp.float32
BF16 = jnp.bfloat16
LANES = 128
VMEM_LIMIT = 24 * 1024 * 1024
SMEM_SPEC = pl.BlockSpec(memory_space=pltpu.SMEM)
VMEM_SPEC = pl.BlockSpec(memory_space=pltpu.VMEM)


FLIP2 = [(0, 1), (1, 0)]
DIAGONAL = [(0, 3), (1, 2), (2, 1), (3, 0)]


def swap_half(array):
    return lax.ppermute(array, "l", FLIP2)


def after(value, *others):
    return lax.optimization_barrier((value, others))[0]


def split(value):
    high = value.astype(BF16)
    return high, (value - high.astype(F32)).astype(BF16)


def dot(a, b, dims):
    return lax.dot_general(a, b, (dims, ((), ())), preferred_element_type=F32)


NT = ((1,), (1,))
NN = ((1,), (0,))


def in_hbm(array):
    return pltpu.with_memory_space_constraint(array, pltpu.HBM)


def call(body, out_shape, hbm_outs=(), **kwargs):
    if hbm_outs:
        out_shape = [
            pltpu.HBM(a.shape, a.dtype) if i in hbm_outs else a for i, a in enumerate(out_shape)
        ]
    return pl.pallas_call(
        body,
        out_shape=out_shape,
        compiler_params=pltpu.CompilerParams(vmem_limit_bytes=VMEM_LIMIT),
        **kwargs,
    )


def cost(flops, byte_count):
    return pl.CostEstimate(flops=int(flops) // 64, bytes_accessed=int(byte_count) // 64, transcendentals=0)


def pack_body(frames, place_ref, in_ref, near_ref, far_ref, turned):
    slots = in_ref.shape[1]
    for start in range(0, slots, LANES):
        turned[start : start + LANES, :] = in_ref[:, start : start + LANES].T
    for rel in range(4):
        first = pl.multiple_of(place_ref[rel] * frames, 8)
        out = (near_ref, far_ref)[rel // 2]
        out[(rel % 2) * frames : (rel % 2 + 1) * frames, :] = turned[pl.ds(first, frames), :]


def pack(place, array, frames, waits=False):
    width, slots = array.shape
    out = jax.ShapeDtypeStruct((2 * frames, width), F32)
    return call(
        partial(pack_body, frames),
        grid=(1,),
        out_shape=[out, out],
        in_specs=[SMEM_SPEC, pl.BlockSpec((width, slots), lambda i: (0, 0))],
        out_specs=[pl.BlockSpec(out.shape, lambda i: (0, 0))] * 2,
        scratch_shapes=[pltpu.VMEM((slots, width), F32)],
        hbm_outs=(0, 1) if waits else (),
        cost_estimate=cost(0, 8 * width * slots),
        name="pack",
    )(place, in_hbm(array))


def part_spec(part, frames):
    array, i = part
    if i is None:
        return pl.BlockSpec(array.shape, lambda *_: (0,) * array.ndim)
    return pl.BlockSpec((frames, array.shape[1]), lambda *_: (i, 0))


def arrays_of(parts):
    return [array for array, _ in parts]


def unpack_body(frames, place_ref, *refs):
    ins, out_ref, turned = refs[:4], refs[4], refs[5]
    slots = out_ref.shape[1]
    for rel in range(4):
        first = pl.multiple_of(place_ref[rel] * frames, 8)
        turned[pl.ds(first, frames), :] = ins[rel][...]
    for start in range(0, slots, LANES):
        out_ref[:, start : start + LANES] = turned[start : start + LANES, :].T


def unpack(place, parts, frames, waited=False):
    width = parts[0][0].shape[1]
    slots = 4 * frames
    return call(
        partial(unpack_body, frames),
        grid=(1,),
        out_shape=jax.ShapeDtypeStruct((width, slots), F32),
        in_specs=[SMEM_SPEC] + [part_spec(part, frames) for part in parts],
        out_specs=pl.BlockSpec((width, slots), lambda i: (0, 0)),
        scratch_shapes=[pltpu.VMEM((slots, width), F32)],
        cost_estimate=cost(0, 8 * width * slots),
        name="unpack",
    )(place, *[in_hbm(a) if waited else a for a in arrays_of(parts)])


def merge_body(kept_ref, come_ref, *outs):
    frames, columns = kept_ref.shape
    width = columns // 2
    for i in range(2):
        some = slice(i * width, (i + 1) * width)
        if len(outs) > 1:
            outs[i][...] = kept_ref[:, some] + come_ref[:, some]
            continue
        (out_ref,) = outs
        out_ref[i * frames : (i + 1) * frames, :] = kept_ref[:, some] + come_ref[:, some]


def merge(kept, half, come, apart=False):
    frames, columns = come.shape
    rows, n = (frames, 2) if apart else (2 * frames, 1)
    outs = call(
        merge_body,
        grid=(1,),
        out_shape=[jax.ShapeDtypeStruct((rows, columns // 2), F32)] * n,
        in_specs=[
            pl.BlockSpec((frames, columns), lambda i: (0, half)),
            pl.BlockSpec((frames, columns), lambda i: (0, 0)),
        ],
        out_specs=[pl.BlockSpec((rows, columns // 2), lambda i: (0, 0))] * n,
        cost_estimate=cost(0, 12 * frames * columns),
        name="merge",
    )(kept, come)
    return outs if apart else outs[0]


def project_body(n_parts, n_flat, spots, n_weights, first, with_acc, with_stats, with_params, cols_ref, place_ref, *refs):
    del cols_ref

    def take(n):
        nonlocal refs
        some, refs = refs[:n], refs[n:]
        return some

    parts, flat_parts, weights = take(n_parts), take(n_flat), take(n_weights)
    acc, valid, stats_in, params = take(with_acc), take(with_stats > 0), take(with_stats > 1), take(with_params)
    (out_ref,) = take(1)
    stats, flat = take(with_stats > 0), take(n_flat > 0)
    x_high, x_low, far_ref = refs
    step = pl.program_id(0)
    width = x_high.shape[2]

    @pl.when(step == 0)
    def _():
        for block, part in zip(spots, parts):
            for start in range(0, part.shape[1], width):
                high, low = split(part[:, start : start + width])
                x_high[block + start // width] = high
                x_low[block + start // width] = low
        column = 0
        for part in flat_parts:
            flat[0][:, column : column + part.shape[1]] = part[...]
            column += part.shape[1]
        if with_acc:
            out_ref[...] = acc[0][...]
        else:
            out_ref[...] = jnp.zeros_like(out_ref)

    stacked = jnp.concatenate([x_high[step], x_low[step], x_high[step]], axis=1)
    for block, weight in enumerate(weight_blocks(place_ref, weights, far_ref)):
        w_high, w_low = split(weight)
        columns = slice(block * width, (block + 1) * width)
        out_ref[:, columns] += dot(stacked, jnp.concatenate([w_high, w_high, w_low], axis=1), NT)

    if with_stats:
        (stats_ref,) = stats

        @pl.when(step == pl.num_programs(0) - 1)
        def _():
            if stats_in:
                stats_ref[...] = stats_in[0][...]
            own = jnp.sum(valid[0][...], axis=0, keepdims=True)
            per = width // LANES
            for row in range(out_ref.shape[1] // LANES):
                z = out_ref[:, row * LANES : (row + 1) * LANES]
                total = jnp.sum(valid[0][...] * z, axis=0, keepdims=True)
                centred = valid[0][...] * (z - total / own)
                squares = jnp.sum(centred * centred, axis=0, keepdims=True)
                at = place_ref[first + row // per] * per + row % per
                stats_ref[0, pl.ds(at, 1), :] = total
                stats_ref[1, pl.ds(at, 1), :] = squares
                stats_ref[2, pl.ds(at, 1), :] = own
            if with_params:
                rest = params[0].shape[0] - 8
                stats_ref[3] = params[0][:8, :]
                stats_ref[4] = jnp.zeros_like(stats_ref[4])
                stats_ref[4, :rest, :] = params[0][8:, :]


def weight_specs(weights, layer, pairs=2):
    specs = []
    for weight in weights:
        if weight.ndim == 3:
            shape = (1, weight.shape[1], pairs * weight.shape[1])
            specs.append(pl.BlockSpec(shape, lambda s, cols, *_: (layer, 0, cols[s])))
        else:
            shape = (weight.shape[0], pairs * 4 * weight.shape[0])
            specs.append(pl.BlockSpec(shape, lambda s, cols, *_: (0, cols[s])))
    return specs


def far_scratch(width, pairs=2):
    return pltpu.VMEM((2, width, pairs * width), F32)


def weight_blocks(place_ref, refs, far_ref):
    near = [ref[0] for ref in refs if len(ref.shape) == 3]
    pieces = [ref for ref in refs if len(ref.shape) == 2]
    far = []
    for i in range(len(pieces) // 4):
        for rel, piece in enumerate(pieces[4 * i : 4 * i + 4]):
            rows = piece.shape[0]
            row = 2 * (place_ref[4] ^ (rel // 2)) + (place_ref[5] ^ (rel % 2))
            far_ref[i, pl.ds(pl.multiple_of(row * rows, rows), rows), :] = piece[...]
        far.append(far_ref[i])
    return near + far


def project(
    place, frames, parts, blocks, weights, layer, acc=None, valid=None, stats=None, params=None, flat=()
):
    near = weights[0].ndim == 3
    units = sum(1 if w.ndim == 3 else 0.25 for w in weights)
    width = weights[0].shape[1] if near else 4 * weights[0].shape[0]
    n = blocks.shape[0]
    spots, block = [], 0
    for array, _ in parts:
        spots.append(block)
        block += array.shape[1] // width
    full = pl.BlockSpec(memory_space=pltpu.VMEM)
    in_specs = [part_spec(part, frames) for part in (*parts, *flat)]
    in_specs += weight_specs(weights, layer, 1)
    operands = arrays_of(parts) + arrays_of(flat) + [in_hbm(w) for w in weights]
    array = jax.ShapeDtypeStruct((frames, int(units) * width), F32)
    array_spec = pl.BlockSpec(array.shape, lambda s, cols, place: (0, 0))
    out_shape, out_specs = [array], [array_spec]
    if acc is not None:
        in_specs.append(array_spec)
        operands.append(in_hbm(acc))
    if valid is not None:
        in_specs.append(full)
        operands.append(valid)
        shape = (3 if params is None else 5, 4 * width // LANES, LANES)
        out_shape.append(jax.ShapeDtypeStruct(shape, F32))
        out_specs.append(pl.BlockSpec(shape, lambda s, cols, place: (0, 0, 0)))
    for extra in (stats, params):
        if extra is not None:
            in_specs.append(full)
            operands.append(extra)
    if flat:
        out_shape.append(jax.ShapeDtypeStruct((frames, 4 * width), F32))
        out_specs.append(pl.BlockSpec((frames, 4 * width), lambda s, cols, place: (0, 0)))
    return call(
        partial(
            project_body,
            len(parts),
            len(flat),
            spots,
            len(weights),
            0 if near else 2,
            acc is not None,
            (valid is not None) + (stats is not None),
            params is not None,
        ),
        grid_spec=pltpu.PrefetchScalarGridSpec(
            num_scalar_prefetch=2,
            grid=(n,),
            in_specs=in_specs,
            out_specs=out_specs,
            scratch_shapes=[pltpu.VMEM((n, frames, width), BF16)] * 2 + [far_scratch(width, 1)],
        ),
        out_shape=out_shape,
        hbm_outs=(0, len(out_shape) - 1) if flat else (0,),
        cost_estimate=cost(6 * frames * n * width * units * width, 4 * n * width * units * width),
        name="project",
    )(blocks, place, *operands)


def to_relative(place_ref, spread, rows_ref, value, slot):
    per = value.shape[0] // 4
    spread[...] = value
    for rel in range(4):
        first = place_ref[rel] * per
        for row in range(per):
            rows_ref[slot, rel * per + row : rel * per + row + 1, :] = spread[
                pl.ds(first + row, 1), :
            ]


def tree(values):
    while len(values) > 1:
        values = [a + b for a, b in zip(values[::2], values[1::2])]
    return values[0]


def gathered(ref, slot):
    return [ref[i] for i in range(slot, ref.shape[0], ref.shape[0] // 16)]


def norm_terms(stats_ref):
    each = [gathered(stats_ref, slot) for slot in range(3)]
    totals, squares, owns = each
    count = tree(owns)
    mean = tree(totals) / count
    away = [total / own - mean for total, own in zip(totals, owns)]
    spread = tree([s + n * a * a for s, n, a in zip(squares, owns, away)])
    return count, mean, lax.rsqrt(spread / count + EPS)


CHUNKS = 4


def columns_of(refs, row):
    for ref in refs:
        if row * LANES < ref.shape[1]:
            return ref[:, row * LANES : (row + 1) * LANES]
        row -= ref.shape[1] // LANES


def recur_body(n_z, last, layer, spread_params, place_ref, gate_ref, *refs):
    z_refs, refs = refs[:n_z], refs[n_z:]
    (stats_ref, params_ref, valid_ref, x_ref), refs = refs[:4], refs[4:]
    outs, refs = refs[: 1 + 3 * last], refs[1 + 3 * last :]
    if spread_params:
        state_ref, slope_ref, params_out, rows, spread, held, drive_s, state_s, slope_s = refs
    else:
        state_ref, slope_ref, rows, spread, held, drive_s, state_s, slope_s = refs
    frames, features = x_ref.shape
    blocks = features // LANES
    per = blocks // 4
    chunk = pl.program_id(0)

    @pl.when(chunk == 0)
    def _():
        if spread_params:
            for rel in range(4):
                first = place_ref[rel] * (stats_ref.shape[0] // 16) + 3
                for row in range(LAYERS * 3 * per):
                    at = rel * per + row % per
                    params_out[row // per, at : at + 1, :] = stats_ref[
                        first + row // 8, row % 8 : row % 8 + 1, :
                    ]
            params = [params_out[3 * layer + i] for i in range(3)]
        else:
            params = [params_ref[3 * layer + i] for i in range(3)]
        _, mean, inv_std = norm_terms(stats_ref)
        to_relative(place_ref, spread, rows, mean, 0)
        to_relative(place_ref, spread, rows, inv_std, 1)
        rows[1] = rows[1] * params[0]
        rows[2] = params[1]
        rows[3] = params[2]
        held[...] = jnp.zeros_like(held)

    for row in range(blocks):
        drive_s[row * frames : (row + 1) * frames, :] = (
            columns_of(z_refs, row) - rows[0, row : row + 1, :]
        ) * rows[1, row : row + 1, :] + rows[2, row : row + 1, :]
    decay = rows[3]

    def step(t, state):
        at = pl.ds(t, blocks, stride=frames)
        pre = drive_s[at, :] + decay * state
        half = 0.5 + 0.5 * lax.erf(pre * (1.0 / ROOT_TWO))
        gate = gate_ref[chunk * frames + t] > 0.0
        slope = half + pre * jnp.exp(-0.5 * pre * pre) * (1.0 / ROOT_TWO_PI)
        state = jnp.where(gate, pre * half, state)
        state_s[at, :] = state
        slope_s[at, :] = jnp.where(gate, slope, 0.0)
        return state

    held[...] = lax.fori_loop(0, frames, step, held[...], unroll=8)
    valid = valid_ref[...]
    for row in range(blocks):
        lanes = slice(row * LANES, (row + 1) * LANES)
        state = state_s[row * frames : (row + 1) * frames, :]
        state_ref[:, lanes] = state
        slope_ref[:, lanes] = slope_s[row * frames : (row + 1) * frames, :]
        value = x_ref[:, lanes] + valid * state
        out, at = (outs[row // per], row % per) if last else (outs[0], row)
        out[:, at * LANES : (at + 1) * LANES] = value


def recur(layer, place, gate, z, stats, params, valid, x, last):
    frames, features = x.shape
    blocks = features // LANES
    some = frames // CHUNKS
    whole = lambda array: pl.BlockSpec(array.shape, lambda i: (0,) * array.ndim)
    by_chunk = lambda array: pl.BlockSpec((some, array.shape[1]), lambda i: (i, 0))
    full = jax.ShapeDtypeStruct((frames, features), F32)
    piece = jax.ShapeDtypeStruct((frames, features // 4), F32)
    out_shape = [piece] * 4 if last else [full]
    out_shape += [full, full]
    out_specs = [by_chunk(a) for a in out_shape]
    spread_params = params is None
    if spread_params:
        out_shape.append(jax.ShapeDtypeStruct((3 * LAYERS, blocks, LANES), F32))
        out_specs.append(whole(out_shape[-1]))
        params = valid
    return call(
        partial(recur_body, len(z), last, layer, spread_params),
        grid=(CHUNKS,),
        in_specs=[SMEM_SPEC, SMEM_SPEC]
        + [by_chunk(a) for a in z]
        + [whole(a) for a in (stats, params)]
        + [by_chunk(a) for a in (valid, x)],
        out_specs=out_specs,
        out_shape=out_shape,
        hbm_outs=tuple(range(len(out_shape) - spread_params)) if last else (1, 2),
        scratch_shapes=[
            pltpu.VMEM((4, blocks, LANES), F32),
            pltpu.VMEM((blocks, LANES), F32),
            pltpu.VMEM((blocks, LANES), F32),
        ]
        + [pltpu.VMEM((blocks * some, LANES), F32)] * 3,
        cost_estimate=cost(100 * frames * features, 20 * frames * features),
        name="recur",
    )(place, gate, *[in_hbm(a) for a in z], stats, params, valid, in_hbm(x))


def back_body(n_z, n_ups, spots, layer, place_ref, gate_ref, *refs):
    z_refs, refs = refs[:n_z], refs[n_z:]
    (stats_ref, params_ref), refs = refs[:2], refs[2:]
    ups, (state_ref, slope_ref), refs = refs[:n_ups], refs[n_ups : n_ups + 2], refs[n_ups + 2 :]
    grad_ref, sums_ref, rows, spread, held, up_s, state_s, slope_s = refs
    frames, features = state_ref.shape
    blocks = features // LANES
    per = blocks // 4
    tall = frames + 8
    step_no = pl.program_id(0)
    chunk = pl.num_programs(0) - 1 - step_no

    @pl.when(step_no == 0)
    def _():
        _, mean, inv_std = norm_terms(stats_ref)
        to_relative(place_ref, spread, rows, mean, 0)
        to_relative(place_ref, spread, rows, inv_std, 1)
        held[...] = jnp.zeros_like(held)

    for row in range(blocks):
        lanes = slice(row * LANES, (row + 1) * LANES)
        base = row * frames
        up = None
        for (_, column), part in zip(spots, ups):
            if column <= row * LANES < column + part.shape[1]:
                value = part[:, row * LANES - column : (row + 1) * LANES - column]
                up = value if up is None else up + value
        up_s[base : base + frames, :] = up
        state_s[row * tall : row * tall + 8, :] = jnp.zeros((8, LANES), F32)
        state_s[row * tall + 8 : (row + 1) * tall, :] = state_ref[:, lanes]
        slope_s[base : base + frames, :] = slope_ref[:, lanes]
    decay = params_ref[3 * layer + 2]

    def step(i, carry):
        t = frames - 1 - i
        at = pl.ds(t, blocks, stride=frames)
        slope = slope_s[at, :]
        gate = gate_ref[chunk * frames + t]
        total = gate * up_s[at, :] + carry
        up_s[at, :] = total * slope
        return total * (slope * decay + (1.0 - gate))

    held[0] = lax.fori_loop(0, frames, step, held[0], unroll=8)
    held[4] += held[1] * state_s[pl.ds(tall - 1, blocks, stride=tall), :]
    held[1] = up_s[pl.ds(0, blocks, stride=frames), :]
    for row in range(blocks):
        lanes = slice(row * LANES, (row + 1) * LANES)
        grad = up_s[row * frames : (row + 1) * frames, :]
        grad_ref[:, lanes] = grad
        zhat = (columns_of(z_refs, row) - rows[0, row : row + 1, :]) * rows[1, row : row + 1, :]
        before = state_s[row * tall + 7 : row * tall + 7 + frames, :]
        for slot, value in enumerate((grad * zhat, grad, grad * before)):
            held[2 + slot, row : row + 1, :] += jnp.sum(value, axis=0, keepdims=True)

    @pl.when(chunk == 0)
    def _():
        for row in range(blocks):
            at = place_ref[row // per] * per + row % per
            for slot in range(3):
                sums_ref[slot, pl.ds(at, 1), :] = held[2 + slot, row : row + 1, :]


def spots_of_sum(parts, width):
    spots, column = [], 0
    for array, _ in parts:
        spots.append((0, column % (4 * width)))
        column += array.shape[1]
    return spots


def back(layer, place, gate, z, stats, params, ups, states, slopes):
    frames, features = states.shape
    width = features // 4
    blocks = features // LANES
    some = frames // CHUNKS
    whole = lambda array: pl.BlockSpec(array.shape, lambda i: (0,) * array.ndim)

    def by_chunk(array, first=0):
        return pl.BlockSpec(
            (some, array.shape[1]), lambda i: ((first or 0) * CHUNKS + CHUNKS - 1 - i, 0)
        )

    out_shape = [
        jax.ShapeDtypeStruct((frames, features), F32),
        jax.ShapeDtypeStruct((3, blocks, LANES), F32),
    ]
    return call(
        partial(back_body, len(z), len(ups), spots_of_sum(ups, width), layer),
        grid=(CHUNKS,),
        in_specs=[SMEM_SPEC] * 2
        + [by_chunk(a) for a in z]
        + [whole(a) for a in (stats, params)]
        + [by_chunk(*up) for up in ups]
        + [by_chunk(a) for a in (states, slopes)],
        out_specs=[by_chunk(out_shape[0]), whole(out_shape[1])],
        out_shape=out_shape,
        scratch_shapes=[
            pltpu.VMEM((2, blocks, LANES), F32),
            pltpu.VMEM((blocks, LANES), F32),
            pltpu.VMEM((5, blocks, LANES), F32),
            pltpu.VMEM((blocks * some, LANES), F32),
            pltpu.VMEM((blocks * (some + 8), LANES), F32),
            pltpu.VMEM((blocks * some, LANES), F32),
        ],
        cost_estimate=cost(30 * frames * features, 20 * frames * features),
        name="back",
    )(
        place,
        gate,
        *[in_hbm(a) for a in z],
        stats,
        params,
        *arrays_of(ups),
        in_hbm(states),
        in_hbm(slopes),
    )


def input_terms(high_s, low_s, weights):
    left, right = [], []
    for block, weight in enumerate(weights):
        w_high, w_low = split(weight)
        left += [high_s[block], low_s[block], high_s[block]]
        right += [w_high, w_high, w_low]
    return dot(jnp.concatenate(left, axis=1), jnp.concatenate(right, axis=0), NN)


def norm_back_body(n_z, split_terms, layer, cols_ref, place_ref, grad_ref, *refs):
    del cols_ref
    z_refs, refs = refs[:n_z], refs[n_z:]
    params_ref, valid_ref, stats_ref, sums_ref, *refs = refs
    weights, refs = refs[:10], refs[10:]
    if split_terms:
        out_ref, leave_ref, near_term_ref, far_term_ref, sums_out_ref, *refs = refs
        term_refs, starts = (far_term_ref, near_term_ref), (0, 0)
    else:
        out_ref, leave_ref, term_ref, sums_out_ref, *refs = refs
        term_refs, starts = (term_ref, term_ref), (2 * grad_ref.shape[1] // 4, 0)
    rows, spread, high_s, low_s, far_ref = refs
    blocks = grad_ref.shape[1] // LANES
    width = high_s.shape[2]
    per = width // LANES

    @pl.when(pl.program_id(0) == 0)
    def _():
        count, mean, inv_std = norm_terms(stats_ref)
        to_relative(place_ref, spread, rows, mean, 0)
        to_relative(place_ref, spread, rows, inv_std, 1)
        rows[2] = rows[1] * params_ref[3 * layer]
        sums = [tree(gathered(sums_ref, slot)) for slot in range(3)]
        for slot in range(3):
            sums_out_ref[slot] = sums[slot]
        to_relative(place_ref, spread, rows, sums[0] / count, 3)
        to_relative(place_ref, spread, rows, sums[1] / count, 4)
        valid = valid_ref[...]
        for row in range(blocks):
            lanes = slice(row * LANES, (row + 1) * LANES)
            one = lambda slot: rows[slot, row : row + 1, :]
            zhat = (columns_of(z_refs, row) - one(0)) * one(1)
            value = one(2) * (grad_ref[:, lanes] - valid * (one(4) + zhat * one(3)))
            out_ref[:, lanes] = value
            if (row // per) % 2:
                at = (row // per // 2) * width + (row % per) * LANES
                leave_ref[:, at : at + LANES] = value
            high, low = split(value)
            inner = slice((row % per) * LANES, (row % per + 1) * LANES)
            high_s[row // per, :, inner] = high
            low_s[row // per, :, inner] = low

    value = input_terms(high_s, low_s, weight_blocks(place_ref, weights, far_ref))
    for step, (term_ref, first) in enumerate(zip(term_refs, starts)):

        @pl.when(pl.program_id(0) == step)
        def _():
            for pair in range(2):
                at = pl.multiple_of(((place_ref[0] & 1) ^ pair) * width, width)
                term_ref[:, pl.ds(first + at, width)] = value[
                    :, pair * width : (pair + 1) * width
                ]


def norm_back(columns, place, grad, z, params, valid, stats, sums, weights, layer, split_terms):
    frames, features = grad.shape
    width = features // 4
    blocks = features // LANES
    whole = lambda array: pl.BlockSpec(array.shape, lambda s, cols, place: (0,) * array.ndim)
    operands = [grad, *[in_hbm(a) for a in z], params, valid, stats, sums]
    full = jax.ShapeDtypeStruct((frames, features), F32)
    half = jax.ShapeDtypeStruct((frames, 2 * width), F32)
    terms = [half, half] if split_terms else [full]
    out_shape = [full, half, *terms, jax.ShapeDtypeStruct((3, blocks, LANES), F32)]
    return call(
        partial(norm_back_body, len(z), split_terms, layer),
        grid_spec=pltpu.PrefetchScalarGridSpec(
            num_scalar_prefetch=2,
            grid=(2,),
            in_specs=[whole(a) for a in operands] + weight_specs(weights, layer),
            out_specs=[whole(a) for a in out_shape],
            scratch_shapes=[
                pltpu.VMEM((5, blocks, LANES), F32),
                pltpu.VMEM((blocks, LANES), F32),
                pltpu.VMEM((4, frames, width), BF16),
                pltpu.VMEM((4, frames, width), BF16),
                far_scratch(width),
            ],
        ),
        out_shape=out_shape,
        hbm_outs=(0,),
        cost_estimate=cost(6 * frames * features * features, 4 * features * features),
        name="norm_back",
    )(columns, place, *operands, *[in_hbm(w) for w in weights])


def own_terms_body(n_ups, spots, cols_ref, place_ref, grad_ref, *refs):
    del cols_ref
    ups, refs = refs[:n_ups], refs[n_ups:]
    weights, refs = refs[:10], refs[10:]
    out_ref, high_s, low_s, far_ref = refs
    width = high_s.shape[2]
    step = pl.program_id(0)

    @pl.when(step == 0)
    def _():
        for block in range(4):
            high, low = split(grad_ref[:, block * width : (block + 1) * width])
            high_s[block] = high
            low_s[block] = low

    value = input_terms(high_s, low_s, weight_blocks(place_ref, weights, far_ref))
    for pair in range(2):
        at = pl.multiple_of(((place_ref[0] & 1) ^ pair) * width, width)
        out_ref[:, pl.ds(at, width)] = value[:, pair * width : (pair + 1) * width]
    for half in range(2):

        @pl.when(step == half)
        def _():
            first = 2 * half * width
            for (_, column), up in zip(spots, ups):
                low = max(column, first)
                high = min(column + up.shape[1], first + 2 * width)
                if low < high:
                    out_ref[:, low - first : high - first] += up[:, low - column : high - column]


def own_terms(columns, place, grad, ups, weights, layer):
    frames, features = grad.shape
    width = features // 4
    whole = lambda array: pl.BlockSpec(array.shape, lambda s, cols, place: (0,) * array.ndim)
    step_block = pl.BlockSpec((frames, 2 * width), lambda s, cols, place: (0, s))
    return call(
        partial(own_terms_body, len(ups), spots_of_sum(ups, width)),
        grid_spec=pltpu.PrefetchScalarGridSpec(
            num_scalar_prefetch=2,
            grid=(2,),
            in_specs=[whole(grad)]
            + [part_spec(up, frames) for up in ups]
            + weight_specs(weights, layer),
            out_specs=step_block,
            scratch_shapes=[pltpu.VMEM((4, frames, width), BF16)] * 2 + [far_scratch(width)],
        ),
        out_shape=jax.ShapeDtypeStruct((frames, features), F32),
        cost_estimate=cost(6 * frames * features * features, 4 * features * features),
        name="own_terms",
    )(columns, place, in_hbm(grad), *arrays_of(ups), *[in_hbm(w) for w in weights])


def prepare_body(lists_ref, place_ref, own_ref, near_ref, high_ref, low_ref):
    del lists_ref
    padded = high_ref.shape[0] // 2
    width = high_ref.shape[1] // 2
    for clip, part in enumerate((own_ref, near_ref)):
        rows = part.shape[0]
        for dc in range(2):
            at = pl.multiple_of((place_ref[6] ^ clip ^ dc) * width, width)
            high, low = split(part[:, dc * width : (dc + 1) * width])
            high_ref[clip * padded : clip * padded + rows, pl.ds(at, width)] = high
            low_ref[clip * padded : clip * padded + rows, pl.ds(at, width)] = low
        zeros = jnp.zeros((padded - rows, 2 * width), BF16)
        high_ref[clip * padded + rows : (clip + 1) * padded, :] = zeros
        low_ref[clip * padded + rows : (clip + 1) * padded, :] = zeros


def prepare(place, own, near):
    frames, features = own.shape
    width = features // 4
    padded = -(-frames // LANES) * LANES
    in_spec = pl.BlockSpec((frames, 2 * width), lambda s, *_: (0, s))
    out = jax.ShapeDtypeStruct((2 * padded, features), BF16)
    out_spec = pl.BlockSpec((2 * padded, 2 * width), lambda s, order, place: (0, order[s]))
    order = jnp.stack([place[0] >> 1, 1 - (place[0] >> 1)])
    return call(
        prepare_body,
        grid_spec=pltpu.PrefetchScalarGridSpec(
            num_scalar_prefetch=2,
            grid=(2,),
            in_specs=[in_spec, in_spec],
            out_specs=[out_spec, out_spec],
        ),
        out_shape=[out, out],
        hbm_outs=(0, 1),
        cost_estimate=cost(0, 16 * frames * features),
        name="prepare",
    )(order, place, in_hbm(own), in_hbm(near))


def product(g_high, g_low, x_high, x_low):
    return dot(g_high, x_high, NN) + (dot(g_high, x_low, NN) + dot(g_low, x_high, NN))


def weight_body(turn, place_ref, *refs):
    if turn:
        grad_ref, near_ref, x_high, x_low, kept, sent, g_high, g_low, t_high, t_low = refs

        @pl.when(pl.program_id(0) == 0)
        def _():
            frames, features = grad_ref.shape
            width = features // 4
            rows = width // 4
            padded = t_high.shape[1] // 2
            t_high[...] = jnp.zeros_like(t_high)
            t_low[...] = jnp.zeros_like(t_low)
            for clip in range(2):
                for dh in range(2):
                    if clip == 0:
                        part = grad_ref[:, 2 * dh * width : (2 * dh + 1) * width]
                    else:
                        part = near_ref[:, dh * width : (dh + 1) * width]
                    high, low = split(part.T)
                    at = (
                        slice(dh * width, (dh + 1) * width),
                        slice(clip * padded, clip * padded + frames),
                    )
                    t_high[at] = high
                    t_low[at] = low
            for group in range(8):
                first, second, dh = group // 4, group // 2 % 2, group % 2
                core = place_ref[6]
                y = place_ref[4] ^ (first * core + second * (1 - core))
                x = place_ref[5] ^ (first * (1 - core) + second * core)
                at = pl.multiple_of(dh * width + (2 * y + x) * rows, rows)
                g_high[group * rows : (group + 1) * rows, :] = t_high[pl.ds(at, rows), :]
                g_low[group * rows : (group + 1) * rows, :] = t_low[pl.ds(at, rows), :]

    else:
        g_high, g_low, x_high, x_low, kept, sent = refs
    half = g_high.shape[0] // 2
    value = product(g_high[...], g_low[...], x_high[...], x_low[...])
    kept[...] = value[:half].reshape(kept.shape)
    sent[...] = value[half:].reshape(sent.shape)


def weight_rows(side, place, grads, x_split, width):
    turn = side == 0
    whole = lambda array: pl.BlockSpec(array.shape, lambda s, place: (0,) * array.ndim)
    x_spec = pl.BlockSpec((x_split[0].shape[0], width), lambda s, place: (0, s))
    shape = (2, 2, width // 4, 4 * width)
    out_shape = [jax.ShapeDtypeStruct(shape, F32)] * 2
    out_specs = [pl.BlockSpec(shape[:3] + (width,), lambda s, place: (0, 0, 0, s))] * 2
    scratch = []
    if turn:
        turned = (2 * width, x_split[0].shape[0])
        out_shape += [jax.ShapeDtypeStruct(turned, BF16)] * 2
        out_specs += [whole(out_shape[-1])] * 2
        scratch = [pltpu.VMEM(turned, BF16)] * 2
    return call(
        partial(weight_body, turn),
        grid_spec=pltpu.PrefetchScalarGridSpec(
            num_scalar_prefetch=1,
            grid=(4,),
            in_specs=[whole(a) for a in grads] + [x_spec] * 2,
            out_specs=out_specs,
            scratch_shapes=scratch,
        ),
        out_shape=out_shape,
        hbm_outs=(0,),
        cost_estimate=cost(12 * x_split[0].shape[0] * width * 4 * width, 4 * 8 * width * width),
        name="weight_rows",
    )(place, *([in_hbm(grads[0]), grads[1]] if turn else grads), *[in_hbm(x) for x in x_split])


def step_body(n, widths, cut, *refs):
    ins, outs = refs[: 2 * n], refs[2 * n :]
    starts = [sum(widths[:i]) for i in range(len(widths))]
    column = 0
    for i in range(n):
        total = ins[2 * i][...] + ins[2 * i + 1][...]
        end = column + total.shape[-1]
        for j, (start, columns) in enumerate(zip(starts, widths)):
            low, high = max(start, column), min(start + columns, end)
            if low < high:
                to = (Ellipsis, slice(low - start, high - start))
                piece = total[..., low - column : high - column]
                pieces = [piece]
                for _ in range(cut):
                    pieces = [half[k] for half in pieces for k in range(2)]
                for k, some in enumerate(pieces):
                    outs[len(pieces) * j + k][to] = some
        column = end


def step_of(*pairs, cut=1, widths=None):
    shape = list(pairs[0][0].shape)
    widths = widths or [sum(pair[0].shape[-1] for pair in pairs)]
    outs = []
    for columns in widths:
        shape[-1] = columns
        outs += [jax.ShapeDtypeStruct(tuple(shape[cut:]), F32)] * 2**cut
    whole = lambda array: pl.BlockSpec(array.shape, lambda i: (0,) * array.ndim)
    operands = [array for pair in pairs for array in pair]
    return call(
        partial(step_body, len(pairs), widths, cut),
        grid=(1,),
        in_specs=[whole(a) for a in operands],
        out_specs=[whole(a) for a in outs],
        out_shape=outs,
        cost_estimate=cost(0, 4 * sum(a.size for a in operands)),
        name="reduction_step",
    )(*operands)


def plane_swap(array, step):
    pairs = []
    for i in range(8):
        over_x = (i % 2 == 0) == (step == 0)
        pairs.append((i, i ^ 2 if over_x else i ^ 4))
    return lax.ppermute(array, ("y", "x", "c"), pairs)


def plane_gather(share, *before):
    first = plane_swap(share, 0)
    second = plane_swap(share, 1)
    return [share, second, first, plane_swap(after(first, second, *before), 1)]


def assemble_body(place_ref, *refs):
    out_ref = refs[-1]
    core = place_ref[6]
    rows, columns = refs[0].shape
    quarter = columns // 4
    for i in range(4):
        first, second = i // 2, i % 2
        y = place_ref[4] ^ (first * core + second * (1 - core))
        x = place_ref[5] ^ (first * (1 - core) + second * core)
        at = pl.multiple_of((2 * y + x) * rows, rows)
        for side in range(2):
            for h in range(2):
                to = pl.multiple_of((2 * h + (place_ref[7] ^ side)) * quarter, quarter)
                some = slice((2 * side + h) * quarter, (2 * side + h + 1) * quarter)
                out_ref[0, pl.ds(at, rows), pl.ds(to, quarter)] = refs[i][:, some]


def assemble(place, pieces, layer, onto=None):
    rows, columns = 4 * pieces[0].shape[0], pieces[0].shape[1]
    aliases, extra, extra_specs = {}, [], []
    if onto is not None:
        aliases, extra = {1 + len(pieces): 0}, [onto]
        extra_specs = [pl.BlockSpec(memory_space=pl.ANY)]
    (out,) = call(
        assemble_body,
        grid=(1,),
        out_shape=[jax.ShapeDtypeStruct((LAYERS, rows, columns), F32)],
        hbm_outs=(0,),
        in_specs=[SMEM_SPEC]
        + [pl.BlockSpec(p.shape, lambda i: (0, 0)) for p in pieces]
        + extra_specs,
        out_specs=[pl.BlockSpec((1, rows, columns), lambda i: (layer, 0, 0))],
        input_output_aliases=aliases,
        cost_estimate=cost(0, 8 * rows * columns),
        name="assemble",
    )(place, *[p if extra else in_hbm(p) for p in pieces], *extra)
    return out


def half_features(inputs, weights, gains, shifts, decays, biases, lengths, frame_mask, grad_out):
    width, slots = inputs.shape
    clips, frames = frame_mask.shape
    depth = weights.shape[2]
    blocks = 4 * width // LANES
    y, x, h, l, c = (lax.axis_index(name) for name in ("y", "x", "h", "l", "c"))
    b = 2 * y + x
    numbers = [2 * (h ^ (rel // 2)) + (c ^ (rel % 2)) for rel in range(4)] + [y, x, c, l]
    place = jnp.stack(numbers).astype(jnp.int32)
    own_blocks, other_blocks = (
        jnp.stack(
            [2 * (2 * (h ^ (rel // 2)) + half) + (c ^ (rel % 2)) for rel in range(4)]
        ).astype(jnp.int32)
        for half in (l, 1 - l)
    )
    own_columns = jnp.stack([2 * h + l, 2 * (1 - h) + l]).astype(jnp.int32)
    other_columns = jnp.stack([2 * (1 - h) + 1 - l, 2 * h + 1 - l]).astype(jnp.int32)
    rows = width // 4

    clip = 2 * h + c
    seen = lax.dynamic_index_in_dim(frame_mask, clip, 0, keepdims=False)
    length = lax.dynamic_index_in_dim(lengths, clip, 0, keepdims=False)
    moments = jnp.arange(frames, dtype=jnp.int32)
    gate = ((moments < length) & ((seen == 1) | (moments == 0))).astype(F32)
    valid = jnp.broadcast_to(gate[:, None], (frames, LANES))

    def far_share(layer):
        return lax.dynamic_slice(weights, (layer, b * rows, 0), (1, rows, depth))[0]

    def over_h(array):
        return lax.ppermute(array, "h", FLIP2)

    def over_c(array):
        return lax.ppermute(array, "c", FLIP2)

    def over_second(array):
        return plane_swap(array, 1)

    def four_of(near_rows, far_rows):
        return [
            (near_rows, 0),
            (over_c(near_rows), 1),
            (far_rows, 0),
            (over_c(far_rows), 1),
        ]

    def four_of_plane(share):
        both = lax.ppermute(share, ("y", "x"), DIAGONAL)
        return [share, lax.ppermute(share, "x", FLIP2), lax.ppermute(share, "y", FLIP2), both]

    near = over_c(weights)
    share = far_share(0)
    close, away = pack(place, after(inputs, share), frames)
    share = over_h(share)
    away = over_h(away)
    other_close = swap_half(close)
    up_close, up_away = pack(place, after(grad_out, close), frames, waits=True)
    share = after(share, up_close, valid, near, other_close)
    pieces = four_of_plane(share)
    away = after(away, pieces[1:])
    half_weights = [[weights, near, *pieces, *map(over_c, after(pieces, away))]]
    own = four_of(after(close, away), away)
    other_away = swap_half(away)
    others = [(other_close, 0), (over_c(other_close), 1)]
    params = jnp.stack([gains, shifts + biases, decays], axis=1)
    own_params = params.reshape(LAYERS * 3 * width // LANES, LANES)
    params = None

    def gather(array, axes):
        return lax.all_gather(array, axes, tiled=True)

    weight = half_weights[0]
    early = jnp.concatenate([own_blocks, other_blocks[:2]])
    z, own_flat = project(place, frames, own + others, early, weight, 0, flat=own)
    others += [(other_away, 0), (over_c(after(other_away, z)), 1)]
    z, stats, other_flat = project(
        place,
        frames,
        others[2:],
        other_blocks[2:],
        weight,
        0,
        z,
        valid,
        params=own_params,
        flat=others,
    )
    z = [z]
    stats = gather(stats, ("h", "c"))
    share = over_c(lax.ppermute(after(far_share(1), stats), ("h", "c"), DIAGONAL))
    stats = gather(stats, ("y", "x"))
    x, states, slopes, params = recur(0, place, gate, z, stats, None, valid, own_flat, False)
    own_near, other_near = over_c(after(own_flat, z[0])), over_c(after(other_flat, z[0]))
    x_near = over_c(x)
    own_split = prepare(place, after(own_flat, x_near), own_near)
    other_split = prepare(place, after(other_flat, x_near), other_near)
    saved = [(own_split, other_split, z, stats, states, slopes)]

    pieces = four_of_plane(after(share, slopes, own_near, other_near))
    near = [weights, near]
    other = swap_half(x)
    x_own = after(x, own_split[0], other_split[0])
    z, *_ = project(place, frames, [(x_own, None)], own_blocks, near, 1)
    own_split = prepare(place, after(x, z), x_near)
    far = [*pieces, *map(over_c, after(pieces, own_split[0]))]
    up_away = over_h(after(up_away, other, own_split[0]))
    half_weights.append(near + far)
    z, stats = project(place, frames, [(other, None)], other_blocks, near, 1, z, valid)
    both = jnp.concatenate([own_blocks, other_blocks])
    z_far, stats = project(
        place,
        frames,
        [(x, None), (other, None)],
        both,
        far,
        1,
        None,
        valid,
        stats,
    )
    z = [z, z_far]
    stats = gather(gather(stats, ("y", "x")), ("h", "c"))
    upstream = four_of(up_close, after(up_away, stats))
    *output, states, slopes = recur(1, place, gate, z, stats, params, valid, x, True)
    other_near = over_c(after(other, slopes))
    saved.append((own_split, (other, other_near), z, stats, states, slopes))
    diagonal = over_c(over_h(output[3]))

    ups = upstream
    results = [None] * LAYERS
    for layer in range(LAYERS - 1, -1, -1):
        own_split, other_split, z, stats, states, slopes = saved[layer]
        weight = half_weights[layer]
        grad_pre, sums = back(layer, place, gate, z, stats, params, ups, states, slopes)
        sums = gather(sums, ("y", "x"))
        if layer == 0:
            come[0] = after(come[0], sums, away, output[1][0])
            later, go = step_of((in_hbm(stay[0]), come[0]), (in_hbm(stay[1]), come[1]))
            sums = after(sums, later)
            go = over_second(go)
        sums = gather(sums, ("h", "c"))
        grad_z, leaving, *terms, sums = norm_back(
            other_columns, place, grad_pre, z, params, valid, stats, sums, weight, layer,
            layer == 0,
        )
        leaving = over_c(leaving)
        if layer > 0:
            received = [swap_half(terms[0])]
            other_split = prepare(place, *after(other_split, grad_z))
            leaving = after(leaving, diagonal, other_split[0])
        else:
            received = [None, swap_half(terms[1])]
            later, go = step_of((later, after(go, grad_z)))
            leaving = after(leaving, later)
            go = lax.ppermute(go, ("h", "c"), DIAGONAL)
            later = (later, go)
        *first, g_high, g_low = weight_rows(0, place, (grad_z, leaving), own_split, width)
        turned = (g_high, g_low)
        come = [plane_swap(first[1], 0)]
        if layer == 0:
            received[0] = swap_half(after(terms[0], received[1]))
        second = weight_rows(1, place, turned, other_split, width)
        come.append(plane_swap(second[1], 0))
        stay = (first[0], second[0])
        kept = own_terms(own_columns, place, after(grad_z, second[0]), ups, weight, layer)
        if layer > 0:
            away = over_h(after(output[2], kept))
            output = [(a, 0) for a in (output[0], over_c(output[1]), away, diagonal)]
        ups = [(kept, None)] + [(r, None) for r in received]
        results[layer] = lax.dynamic_index_in_dim(
            sums.reshape(3, 4, width), clip, axis=1, keepdims=False
        )

    sums = jnp.stack(results)
    sums = [sums[:, 0], sums[:, 1], sums[:, 2]]
    aways = merge(kept, 1, received[1], apart=True)
    later = (later[0], over_c(after(later[1], aways[0])))
    come[0] = after(come[0], sums, later[1])
    far_near = over_c(lax.ppermute(aways[0], ("h", "c"), DIAGONAL))
    near_sum, far_sum, near_go, far_go = step_of(
        (in_hbm(stay[0]), come[0]), (in_hbm(stay[1]), come[1]), cut=2
    )
    near_go, far_go = over_second(near_go), over_second(far_go)
    (go,) = step_of((far_sum, after(far_go, far_near)), cut=0)
    (later,) = step_of(later, cut=0)
    later = after(later, go)
    go = over_h(go)
    later = plane_gather(later)
    (total,) = step_of((near_sum, near_go), cut=0)
    output = unpack(place, [(after(array, total), i) for array, i in output], frames, waited=True)
    close = merge(kept, 0, after(received[0], output))
    far = over_c(over_h(after(aways[1], go)))
    (share,) = step_of((total, after(go, close, *later[1:])), cut=0)
    gathered = plane_gather(share, far)
    grad_in = [(close, 0), (over_c(close[frames:]), 0), (far_near, 0), (far, 0)]
    grad_in = unpack(place, grad_in, frames)
    grad_weights = assemble(place, after(later, share), 1)
    grad_weights = assemble(place, after(gathered, grad_in), 0, grad_weights)
    return (output, grad_in, grad_weights, *sums, sums[1])


def gelu_slope(value):
    return (
        0.5 * (1.0 + jax.scipy.special.erf(value / ROOT_TWO))
        + value * jnp.exp(-0.5 * value * value) / ROOT_TWO_PI
    )


def recur_step(decay, state, inputs):
    drive_t, valid_t = inputs
    pre = drive_t + decay * state
    state = state + valid_t * (jax.nn.gelu(pre, approximate=False) - state)
    return (state, state)


def back_step(decay, carry, inputs):
    upstream_t, valid_t, pre_t = inputs
    total = upstream_t + carry
    grad_pre = total * valid_t * gelu_slope(pre_t)
    carry = total * (1.0 - valid_t) + grad_pre * decay
    return (carry, grad_pre)


def add_piece(weight, piece):
    return jnp.dot(weight, piece, precision=HIGH, preferred_element_type=jnp.float32)


def weight_columns(grad_pre_norm, piece):
    return jnp.einsum("jf,kf->jk", grad_pre_norm, piece, precision=HIGH)


def split_features(inputs, weights, gains, shifts, decays, biases, lengths, frame_mask, grad_out):
    width, slots = inputs.shape
    clips, frames_len = frame_mask.shape
    frames = jnp.arange(frames_len, dtype=jnp.int32)
    valid_grid = (
        (frames[None, :] < lengths[:, None]) & ((frame_mask == 1) | (frames[None, :] == 0))
    ).astype(jnp.float32)
    valid = valid_grid.reshape(-1)
    valid_row = valid[None, :]
    valid_time = jnp.broadcast_to(valid_grid.T[:, :, None], (frames_len, clips, width)).reshape(
        frames_len, clips * width
    )
    count_local = jnp.sum(valid)

    def to_time(array):
        return jnp.transpose(array.reshape(width, clips, frames_len), (2, 1, 0)).reshape(
            frames_len, clips * width
        )

    def from_time(array):
        return jnp.transpose(array.reshape(frames_len, clips, width), (2, 1, 0)).reshape(
            width, slots
        )

    layer_in = inputs
    saved = []
    for layer_no in range(LAYERS):
        weight = weights[layer_no]
        gathered = lax.all_gather(layer_in, "neuron", axis=0, tiled=True)
        pre_norm = add_piece(weight, gathered)
        first_sum, count = lax.psum((jnp.sum(valid_row * pre_norm, axis=1), count_local), "batch")
        mean = first_sum / count
        centered = pre_norm - mean[:, None]
        var = lax.psum(jnp.sum(valid_row * centered * centered, axis=1), "batch") / count
        inv_std = lax.rsqrt(var + EPS)
        zhat = (pre_norm - mean[:, None]) * inv_std[:, None]
        drive = gains[layer_no][:, None] * zhat + (shifts[layer_no] + biases[layer_no])[:, None]
        drive_time = to_time(drive)
        decay_wide = jnp.tile(decays[layer_no], clips)
        start_state = jnp.zeros((clips * width,), jnp.float32)
        _, states = lax.scan(
            partial(recur_step, decay_wide), start_state, (drive_time, valid_time), unroll=8
        )
        saved.append((gathered, zhat, inv_std, drive_time, states, count))
        layer_in = layer_in + valid_row * from_time(states)
    upstream = grad_out
    grad_parts = [None] * LAYERS
    for layer_no in range(LAYERS - 1, -1, -1):
        gathered, zhat, inv_std, drive_time, states, count = saved[layer_no]
        decay_wide = jnp.tile(decays[layer_no], clips)
        gain = gains[layer_no]
        previous = jnp.concatenate([jnp.zeros_like(states[:1]), states[:-1]], axis=0)
        pre_time = drive_time + decay_wide[None, :] * previous
        grad_state = to_time(valid_row * upstream)
        start_carry = jnp.zeros((clips * width,), jnp.float32)
        _, grad_pre_time = lax.scan(
            partial(back_step, decay_wide),
            start_carry,
            (grad_state, valid_time, pre_time),
            reverse=True,
            unroll=8,
        )
        decay_local = jnp.sum(
            jnp.sum(grad_pre_time * previous, axis=0).reshape(clips, width), axis=0
        )
        grad_pre = from_time(grad_pre_time)
        gain_local = jnp.sum(grad_pre * zhat, axis=1)
        shift_local = jnp.sum(grad_pre, axis=1)
        grad_gain, grad_shift, grad_decay = lax.psum(
            (gain_local, shift_local, decay_local), "batch"
        )
        grad_pre_norm = (gain * inv_std)[:, None] * (
            grad_pre - valid_row * (grad_shift[:, None] + zhat * grad_gain[:, None]) / count
        )
        weight_local = weight_columns(grad_pre_norm, gathered)
        input_terms = jnp.einsum("jk,jf->kf", weights[layer_no], grad_pre_norm, precision=HIGH)
        input_grad = lax.psum_scatter(input_terms, "neuron", scatter_dimension=0, tiled=True)
        grad_weight = lax.psum(weight_local, "batch")
        upstream = upstream + input_grad
        grad_parts[layer_no] = (grad_weight, grad_gain, grad_shift, grad_decay)
    grad_weights = jnp.stack([grad_parts[layer_no][0] for layer_no in range(LAYERS)])
    grad_gains = jnp.stack([grad_parts[layer_no][1] for layer_no in range(LAYERS)])
    grad_shifts = jnp.stack([grad_parts[layer_no][2] for layer_no in range(LAYERS)])
    grad_decays = jnp.stack([grad_parts[layer_no][3] for layer_no in range(LAYERS)])
    return (layer_in, upstream, grad_weights, grad_gains, grad_shifts, grad_decays, grad_shifts)


def solution(mesh):
    if (mesh.shape["batch"], mesh.shape["neuron"]) == (4, 8):
        cut = Mesh(mesh.devices.reshape(2, 2, 2, 2, 2), ("y", "x", "h", "l", "c"))
        batch, neuron, body = ("y", "x"), ("h", "l", "c"), half_features
    else:
        cut, batch, neuron, body = mesh, "batch", "neuron", split_features
    in_specs = (
        P(neuron, batch),
        P(None, neuron, None),
        P(None, neuron),
        P(None, neuron),
        P(None, neuron),
        P(None, neuron),
        P(batch),
        P(batch, None),
        P(neuron, batch),
    )
    out_specs = (
        P(neuron, batch),
        P(neuron, batch),
        P(None, neuron, None),
        P(None, neuron),
        P(None, neuron),
        P(None, neuron),
        P(None, neuron),
    )
    return jax.shard_map(
        body, mesh=cut, in_specs=in_specs, out_specs=out_specs, check_vma=False
    )
```

profile of v0, /device:TPU:0, one launch (start us, length us, event | category | flops | bytes accessed | tf_op | source)
XLA Modules:
  0.0 395.6 jit_solution(12883577991081292258)
XLA Ops:
  5.2 2.7 collective-permute-start.3
  7.8 2.6 collective-permute-start.1
  10.8 2.9 pack.3
  15.6 18.6 %collective-permute-done.1.refs_12_.refs_8_.refs_7_.refs_4_ = f32[64,2048]{1,0:T(8,128)} collective-permute-done((f32[64,2048]{1,0:T(8,128)S(1)}, f32[64,2048]{1,0:T(8,128)}, u32[]{:S(2)}, u32[]{:S(2)}) %collective-permute-start.1) | collective-permute-done | bytes 524320 | tf_op jit(solution)/shard_map/ppermute | solution.py:958
  34.2 3.0 collective-permute-done.3.refs_4_.refs_2_
  37.2 2.7 collective-permute-start.6
  40.8 21.3 %collective-permute-done.refs_2_.refs_8_ = f32[640,256]{1,0:T(8,128)S(1)} collective-permute-done((f32[640,256]{1,0:T(8,128)S(1)}, f32[640,256]{1,0:T(8,128)S(1)}, u32[]{:S(2)}, u32[]{:S(2)}) %collective-permute-start) | collective-permute-done | bytes 655392 | tf_op jit(solution)/shard_map/ppermute | solution.py:958
  69.9 9.9 %project.5 = (f32[320,1024]{1,0:T(8,128)}, f32[320,1024]{1,0:T(8,128)}) custom-call(s32[6]{0:T(128)S(1)} %concatenate.11.cols_ref, s32[8]{0:T(128)S(1)} %stack.124.place_ref, f32[640,256]{1,0:T(8,128)S(1)} %get-tuple-element.137.refs_0_.refs_6_, f32[640,256]{1,0:T(8,128)} %collective-permute-done.8.refs_1_.refs_7_, ...), custom_call_target="tpu_custom_call" | custom-call | flops 47185920 | bytes 98304 | tf_op jit(solution)/shard_map/project/pallas_call | solution.py:288
  83.3 6.0 %project.6 = (f32[320,1024]{1,0:T(8,128)}, f32[5,8,128]{2,1,0:T(8,128)S(1)}, f32[320,1024]{1,0:T(8,128)}) custom-call(s32[2]{0:T(128)S(1)} %pad_add_fusion.1.cols_ref, s32[8]{0:T(128)S(1)} %stack.124.place_ref, f32[640,256]{1,0:T(8,128)S(1)} %collective-permute-done.7.refs_0_.refs_4_, f32[640,256]{1,0:T(8,128)S(1)} %collective-permute-done.15.refs_1_.refs_5_, ...), custom_call_target="tpu_custom_call" | custom-call | flops 15728640 | bytes 32768 | tf_op jit(solution)/shard_map/project/pallas_call | solution.py:288
  89.9 6.2 %all_gather.24 = f32[20,8,128]{2,1,0:T(8,128)S(1)} all-gather(f32[5,8,128]{2,1,0:T(8,128)S(1)} %get-tuple-element.145), channel_id=1, replica_groups=mesh['y'=2,'x'=2,'h'=2,'l'=2,'c'=2] {'h','c'}, dimensions={0}, use_global_device_ids=true | all-gather | bytes 102400 | tf_op jit(solution)/shard_map/all_gather | solution.py:997
  97.3 9.2 %all_gather.25.refs_1_.refs_3_ = f32[80,8,128]{2,1,0:T(8,128)S(1)} all-gather(f32[20,8,128]{2,1,0:T(8,128)S(1)} %all_gather.24), channel_id=1, replica_groups=mesh['y'=2,'x'=2,'h'=2,'l'=2,'c'=2] {'y','x'}, dimensions={0}, use_global_device_ids=true | all-gather | bytes 409600 | tf_op jit(solution)/shard_map/all_gather | solution.py:997
  106.6 7.3 %recur.2 = (f32[320,1024]{1,0:T(8,128)S(1)}, f32[320,1024]{1,0:T(8,128)}, f32[320,1024]{1,0:T(8,128)}, f32[6,8,128]{2,1,0:T(8,128)S(1)}) custom-call(s32[8]{0:T(128)S(1)} %stack.124.place_ref, f32[320]{0:T(512)S(1)} %fusion.6.gate_ref, f32[320,1024]{1,0:T(8,128)} %get-tuple-element.144.refs_0_, f32[80,8,128]{2,1,0:T(8,128)S(1)} %all_gather.25.refs_1_.refs_3_, ...), custom_call_target="tpu_custom_call" | custom-call | flops 512000 | bytes 102400 | tf_op jit(solution)/shard_map/recur/pallas_call | solution.py:434
  115.7 6.6 %collective-permute-done.20 = f32[64,2048]{1,0:T(8,128)S(1)} collective-permute-done((f32[64,2048]{1,0:T(8,128)S(1)}, f32[64,2048]{1,0:T(8,128)S(1)}, u32[]{:S(2)}, u32[]{:S(2)}) %collective-permute-start.20) | collective-permute-done | bytes 524320 | tf_op jit(solution)/shard_map/ppermute | solution.py:1017
  129.1 3.8 prepare.4
  132.9 3.8 prepare.5
  136.6 5.2 %project.7.refs_3_ = f32[320,512]{1,0:T(8,128)} custom-call(s32[4]{0:T(128)S(1)} %pad_add_fusion.2.cols_ref, s32[8]{0:T(128)S(1)} %stack.124.place_ref, f32[320,1024]{1,0:T(8,128)S(1)} %get-tuple-element.160.refs_0_.own_ref.refs_5_, f32[2,256,2048]{2,1,0:T(8,128)} %refs_2_.1, ...), custom_call_target="tpu_custom_call" | custom-call | flops 15728640 | bytes 32768 | tf_op jit(solution)/shard_map/project/pallas_call | solution.py:288
  141.8 3.8 prepare.6
  145.6 4.7 %collective-permute-done.16.refs_0_.refs_1_.own_ref = f32[320,1024]{1,0:T(8,128)S(1)} collective-permute-done((f32[320,1024]{1,0:T(8,128)S(1)}, f32[320,1024]{1,0:T(8,128)S(1)}, u32[]{:S(2)}, u32[]{:S(2)}) %collective-permute-start.16) | collective-permute-done | bytes 1310752 | tf_op jit(solution)/shard_map/ppermute | solution.py:29
  153.1 5.7 %project.8 = (f32[320,512]{1,0:T(8,128)}, f32[3,8,128]{2,1,0:T(8,128)S(1)}) custom-call(s32[4]{0:T(128)S(1)} %pad_add_fusion.cols_ref, s32[8]{0:T(128)S(1)} %stack.124.place_ref, f32[320,1024]{1,0:T(8,128)S(1)} %collective-permute-done.16.refs_0_.refs_1_.own_ref, f32[2,256,2048]{2,1,0:T(8,128)} %refs_2_.1, ...), custom_call_target="tpu_custom_call" | custom-call | flops 15728640 | bytes 32768 | tf_op jit(solution)/shard_map/project/pallas_call | solution.py:288
  158.9 9.2 %project.9 = (f32[320,512]{1,0:T(8,128)}, f32[3,8,128]{2,1,0:T(8,128)S(1)}) custom-call(s32[8]{0:T(128)S(1)} %concatenate.12.cols_ref, s32[8]{0:T(128)S(1)} %stack.124.place_ref, f32[320,1024]{1,0:T(8,128)S(1)} %copy-done.1, f32[320,1024]{1,0:T(8,128)S(1)} %collective-permute-done.16.refs_0_.refs_1_.own_ref, ...), custom_call_target="tpu_custom_call" | custom-call | flops 31457280 | bytes 65536 | tf_op jit(solution)/shard_map/project/pallas_call | solution.py:288
  168.1 8.1 %all_gather.26 = f32[12,8,128]{2,1,0:T(8,128)S(1)} all-gather(f32[3,8,128]{2,1,0:T(8,128)S(1)} %get-tuple-element.168), channel_id=1, replica_groups=mesh['y'=2,'x'=2,'h'=2,'l'=2,'c'=2] {'y','x'}, dimensions={0}, use_global_device_ids=true | all-gather | bytes 61440 | tf_op jit(solution)/shard_map/all_gather | solution.py:997
  176.2 8.8 %all_gather.27.refs_2_.refs_4_ = f32[48,8,128]{2,1,0:T(8,128)S(1)} all-gather(f32[12,8,128]{2,1,0:T(8,128)S(1)} %all_gather.26), channel_id=1, replica_groups=mesh['y'=2,'x'=2,'h'=2,'l'=2,'c'=2] {'h','c'}, dimensions={0}, use_global_device_ids=true | all-gather | bytes 245760 | tf_op jit(solution)/shard_map/all_gather | solution.py:997
  185.3 7.4 %recur.3 = (f32[320,256]{1,0:T(8,128)}, f32[320,256]{1,0:T(8,128)}, f32[320,256]{1,0:T(8,128)}, f32[320,256]{1,0:T(8,128)}, f32[320,1024]{1,0:T(8,128)}, /*index=5*/f32[320,1024]{1,0:T(8,128)}) custom-call(s32[8]{0:T(128)S(1)} %stack.124.place_ref, f32[320]{0:T(512)S(1)} %fusion.6.gate_ref, f32[320,512]{1,0:T(8,128)} %get-tuple-element.156.refs_0_, ...), custom_call_target="tpu_custom_call" | custom-call | flops 512000 | bytes 102400 | tf_op jit(solution)/shard_map/recur/pallas_call | solution.py:434
  193.1 5.6 %back.2 = (f32[320,1024]{1,0:T(8,128)S(1)}, f32[3,8,128]{2,1,0:T(8,128)S(1)}) custom-call(s32[8]{0:T(128)S(1)} %stack.124.place_ref, f32[320]{0:T(512)S(1)} %fusion.6.gate_ref, f32[320,512]{1,0:T(8,128)} %get-tuple-element.156.refs_0_, f32[320,512]{1,0:T(8,128)} %get-tuple-element.167.refs_1_, f32[48,8,128]{2,1,0:T(8,128)S(1)} %all_gather.27.refs_2_.refs_4_, ...), custom_call_target="tpu_custom_call" | custom-call | flops 153600 | bytes 102400 | tf_op jit(solution)/shard_map/back/pallas_call | solution.py:541
  198.7 8.2 %all_gather.28 = f32[12,8,128]{2,1,0:T(8,128)S(1)} all-gather(f32[3,8,128]{2,1,0:T(8,128)S(1)} %get-tuple-element.177), channel_id=1, replica_groups=mesh['y'=2,'x'=2,'h'=2,'l'=2,'c'=2] {'y','x'}, dimensions={0}, use_global_device_ids=true | all-gather | bytes 61440 | tf_op jit(solution)/shard_map/all_gather | solution.py:997
  206.9 6.8 %all_gather.29.refs_5_ = f32[48,8,128]{2,1,0:T(8,128)S(1)} all-gather(f32[12,8,128]{2,1,0:T(8,128)S(1)} %all_gather.28), channel_id=1, replica_groups=mesh['y'=2,'x'=2,'h'=2,'l'=2,'c'=2] {'h','c'}, dimensions={0}, use_global_device_ids=true | all-gather | bytes 245760 | tf_op jit(solution)/shard_map/all_gather | solution.py:997
  213.7 7.7 %norm_back.2 = (f32[320,1024]{1,0:T(8,128)}, f32[320,512]{1,0:T(8,128)S(1)}, f32[320,1024]{1,0:T(8,128)}, f32[3,8,128]{2,1,0:T(8,128)S(1)}) custom-call(s32[2]{0:T(128)S(1)} %pad_add_fusion.4.cols_ref, s32[8]{0:T(128)S(1)} %stack.124.place_ref, f32[320,1024]{1,0:T(8,128)S(1)} %get-tuple-element.176.grad_ref, f32[320,512]{1,0:T(8,128)} %get-tuple-element.156.refs_0_, ...), custom_call_target="tpu_custom_call" | custom-call | flops 31457280 | bytes 65536 | tf_op jit(solution)/shard_map/norm_back/pallas_call | solution.py:646
  223.7 3.8 prepare.7
  228.2 7.2 %weight_rows.4 = (f32[2,2,64,1024]{3,2,1,0:T(8,128)}, f32[2,2,64,1024]{3,2,1,0:T(8,128)}, bf16[512,768]{1,0:T(8,128)(2,1)S(1)}, bf16[512,768]{1,0:T(8,128)(2,1)S(1)}) custom-call(s32[8]{0:T(128)S(1)} %stack.124.place_ref, f32[320,1024]{1,0:T(8,128)} %get-tuple-element.191.refs_0_.grad_ref, f32[320,512]{1,0:T(8,128)S(1)} %collective-permute-done.32.refs_1_, ...), custom_call_target="tpu_custom_call" | custom-call | flops 37748736 | bytes 32768 | tf_op jit(solution)/shard_map/weight_rows/pallas_call | solution.py:819
  236.2 6.1 %weight_rows.5 = (f32[2,2,64,1024]{3,2,1,0:T(8,128)}, f32[2,2,64,1024]{3,2,1,0:T(8,128)}) custom-call(s32[8]{0:T(128)S(1)} %stack.124.place_ref, bf16[512,768]{1,0:T(8,128)(2,1)S(1)} %get-tuple-element.187.refs_0_, bf16[512,768]{1,0:T(8,128)(2,1)S(1)} %get-tuple-element.188.refs_1_, bf16[768,1024]{1,0:T(8,128)(2,1)} %get-tuple-element.184.refs_2_, ...), custom_call_target="tpu_custom_call" | custom-call | flops 37748736 | bytes 32768 | tf_op jit(solution)/shard_map/weight_rows/pallas_call | solution.py:819
  243.7 6.1 %own_terms.2.refs_3_.refs_0_ = f32[320,1024]{1,0:T(8,128)S(1)} custom-call(s32[2]{0:T(128)S(1)} %pad_add_fusion.5.cols_ref, s32[8]{0:T(128)S(1)} %stack.124.place_ref, f32[320,1024]{1,0:T(8,128)} %get-tuple-element.191.refs_0_.grad_ref, f32[640,256]{1,0:T(8,128)S(1)} %copy-done.6, f32[640,256]{1,0:T(8,128)} %collective-permute-done.29.refs_5_.refs_1_, ...), custom_call_target="tpu_custom_call" | custom-call | flops 31457280 | bytes 65536 | tf_op jit(solution)/shard_map/own_terms/pallas_call | solution.py:704
  253.2 5.9 %back.3 = (f32[320,1024]{1,0:T(8,128)S(1)}, f32[3,8,128]{2,1,0:T(8,128)S(1)}) custom-call(s32[8]{0:T(128)S(1)} %stack.124.place_ref, f32[320]{0:T(512)S(1)} %fusion.6.gate_ref, f32[320,1024]{1,0:T(8,128)} %get-tuple-element.144.refs_0_, f32[80,8,128]{2,1,0:T(8,128)S(1)} %all_gather.25.refs_1_.refs_3_, ...), custom_call_target="tpu_custom_call" | custom-call | flops 153600 | bytes 102400 | tf_op jit(solution)/shard_map/back/pallas_call | solution.py:541
  259.1 7.5 %all_gather.30 = f32[12,8,128]{2,1,0:T(8,128)S(1)} all-gather(f32[3,8,128]{2,1,0:T(8,128)S(1)} %get-tuple-element.195), channel_id=1, replica_groups=mesh['y'=2,'x'=2,'h'=2,'l'=2,'c'=2] {'y','x'}, dimensions={0}, use_global_device_ids=true | all-gather | bytes 61440 | tf_op jit(solution)/shard_map/all_gather | solution.py:997
  271.9 6.9 %all_gather.31.refs_4_ = f32[48,8,128]{2,1,0:T(8,128)S(1)} all-gather(f32[12,8,128]{2,1,0:T(8,128)S(1)} %all_gather.30), channel_id=1, replica_groups=mesh['y'=2,'x'=2,'h'=2,'l'=2,'c'=2] {'h','c'}, dimensions={0}, use_global_device_ids=true | all-gather | bytes 245760 | tf_op jit(solution)/shard_map/all_gather | solution.py:997
  278.7 7.3 %norm_back.3 = (f32[320,1024]{1,0:T(8,128)}, f32[320,512]{1,0:T(8,128)S(1)}, f32[320,512]{1,0:T(8,128)S(1)}, f32[320,512]{1,0:T(8,128)S(1)}, f32[3,8,128]{2,1,0:T(8,128)S(1)}) custom-call(s32[2]{0:T(128)S(1)} %pad_add_fusion.4.cols_ref, s32[8]{0:T(128)S(1)} %stack.124.place_ref, f32[320,1024]{1,0:T(8,128)S(1)} %get-tuple-element.194.grad_ref, ...), custom_call_target="tpu_custom_call" | custom-call | flops 31457280 | bytes 65536 | tf_op jit(solution)/shard_map/norm_back/pallas_call | solution.py:646
  291.3 7.2 %weight_rows.6 = (f32[2,2,64,1024]{3,2,1,0:T(8,128)}, f32[2,2,64,1024]{3,2,1,0:T(8,128)}, bf16[512,768]{1,0:T(8,128)(2,1)S(1)}, bf16[512,768]{1,0:T(8,128)(2,1)S(1)}) custom-call(s32[8]{0:T(128)S(1)} %stack.124.place_ref, f32[320,1024]{1,0:T(8,128)} %get-tuple-element.221.refs_0_.grad_ref, f32[320,512]{1,0:T(8,128)S(1)} %collective-permute-done.41.refs_1_, ...), custom_call_target="tpu_custom_call" | custom-call | flops 37748736 | bytes 32768 | tf_op jit(solution)/shard_map/weight_rows/pallas_call | solution.py:819
  299.3 6.1 %weight_rows.7 = (f32[2,2,64,1024]{3,2,1,0:T(8,128)}, f32[2,2,64,1024]{3,2,1,0:T(8,128)}) custom-call(s32[8]{0:T(128)S(1)} %stack.124.place_ref, bf16[512,768]{1,0:T(8,128)(2,1)S(1)} %get-tuple-element.217.refs_0_, bf16[512,768]{1,0:T(8,128)(2,1)S(1)} %get-tuple-element.218.refs_1_, bf16[768,1024]{1,0:T(8,128)(2,1)} %get-tuple-element.154.refs_2_, ...), custom_call_target="tpu_custom_call" | custom-call | flops 37748736 | bytes 32768 | tf_op jit(solution)/shard_map/weight_rows/pallas_call | solution.py:819
  306.6 6.0 %own_terms.3.kept_ref = f32[320,1024]{1,0:T(8,128)S(1)} custom-call(s32[2]{0:T(128)S(1)} %pad_add_fusion.5.cols_ref, s32[8]{0:T(128)S(1)} %stack.124.place_ref, f32[320,1024]{1,0:T(8,128)} %get-tuple-element.221.refs_0_.grad_ref, f32[320,1024]{1,0:T(8,128)S(1)} %own_terms.2.refs_3_.refs_0_, f32[320,1024]{1,0:T(8,128)S(1)} %copy-done.4, ...), custom_call_target="tpu_custom_call" | custom-call | flops 31457280 | bytes 65536 | tf_op jit(solution)/shard_map/own_terms/pallas_call | solution.py:704
  312.7 2.6 collective-permute-done.45.come_ref
  319.1 5.6 %collective-permute-done.47.refs_3_ = f32[2,2,64,1024]{3,2,1,0:T(8,128)S(1)} collective-permute-done((f32[2,2,64,1024]{3,2,1,0:T(8,128)}, f32[2,2,64,1024]{3,2,1,0:T(8,128)S(1)}, u32[]{:S(2)}, u32[]{:S(2)}) %collective-permute-start.47) | collective-permute-done | bytes 1048608 | tf_op jit(solution)/shard_map/ppermute | solution.py:880
  327.4 7.4 %collective-permute-done.51 = f32[320,256]{1,0:T(8,128)S(1)} collective-permute-done((f32[320,256]{1,0:T(8,128)}, f32[320,256]{1,0:T(8,128)S(1)}, u32[]{:S(2)}, u32[]{:S(2)}) %collective-permute-start.51) | collective-permute-done | bytes 327712 | tf_op jit(solution)/shard_map/ppermute | solution.py:1106
  341.9 9.5 %collective-permute-done.58.refs_2_ = f32[64,2048]{1,0:T(8,128)S(1)} collective-permute-done((f32[64,2048]{1,0:T(8,128)S(1)}, f32[64,2048]{1,0:T(8,128)S(1)}, u32[]{:S(2)}, u32[]{:S(2)}) %collective-permute-start.58) | collective-permute-done | bytes 524320 | tf_op jit(solution)/shard_map/ppermute | solution.py:880
  352.6 11.3 %collective-permute-done.54.refs_1_ = f32[64,2048]{1,0:T(8,128)S(1)} collective-permute-done((f32[64,2048]{1,0:T(8,128)S(1)}, f32[64,2048]{1,0:T(8,128)S(1)}, u32[]{:S(2)}, u32[]{:S(2)}) %collective-permute-start.54) | collective-permute-done | bytes 524320 | tf_op jit(solution)/shard_map/ppermute | solution.py:958
  363.9 3.4 collective-permute-start.55
  367.3 2.8 unpack.2
  372.4 8.6 %collective-permute-done.55 = f32[320,256]{1,0:T(8,128)S(1)} collective-permute-done((f32[320,256]{1,0:T(8,128)S(1)}, f32[320,256]{1,0:T(8,128)S(1)}, u32[]{:S(2)}, u32[]{:S(2)}) %collective-permute-start.55) | collective-permute-done | bytes 327712 | tf_op jit(solution)/shard_map/ppermute | solution.py:958
  384.8 3.0 assemble.2.refs_4_
  389.8 3.2 collective-permute-done.62.refs_3_
  (214 shorter events, 79.4 us)
Async XLA Ops:
  0.6 36.5 %collective-permute-start.2 = (f32[2,256,2048]{2,1,0:T(8,128)}, f32[2,256,2048]{2,1,0:T(8,128)}, u32[]{:S(2)}, u32[]{:S(2)}) collective-permute-start(f32[2,256,2048]{2,1,0:T(8,128)} %refs_2_.1), channel_id=1, source_target_pairs={{0,1},{1,0},{2,3},{3,2},{4,5},{5,4},{6,7},{7,6},{8,9},{9,8},{10,11... | collective-permute-start | bytes 12582920 | tf_op jit(solution)/shard_map/ppermute | solution.py:961
  5.2 32.0 %collective-permute-start.3 = (f32[640,256]{1,0:T(8,128)S(1)}, f32[640,256]{1,0:T(8,128)S(1)}, u32[]{:S(2)}, u32[]{:S(2)}) collective-permute-start(f32[640,256]{1,0:T(8,128)S(1)} %get-tuple-element.137.refs_0_.refs_6_), channel_id=1, source_target_pairs={{0,2},{2,0},{1,3},{3,1},{4,6},{6,4},{5,7},{7,5},{8,10},{10,8},{9,1... | collective-permute-start | bytes 1966088 | tf_op jit(solution)/shard_map/ppermute | solution.py:29
  7.8 26.3 %collective-permute-start.1 = (f32[64,2048]{1,0:T(8,128)S(1)}, f32[64,2048]{1,0:T(8,128)}, u32[]{:S(2)}, u32[]{:S(2)}) collective-permute-start(f32[64,2048]{1,0:T(8,128)S(1)} %get-tuple-element.254), channel_id=1, source_target_pairs={{0,4},{4,0},{1,5},{5,1},{2,6},{6,2},{3,7},{7,3},{8,12},{12,8},{9,1... | collective-permute-start | bytes 1572872 | tf_op jit(solution)/shard_map/ppermute | solution.py:958
  10.4 51.7 %collective-permute-start = (f32[640,256]{1,0:T(8,128)S(1)}, f32[640,256]{1,0:T(8,128)S(1)}, u32[]{:S(2)}, u32[]{:S(2)}) collective-permute-start(f32[640,256]{1,0:T(8,128)S(1)} %get-tuple-element.131), channel_id=1, source_target_pairs={{0,4},{4,0},{1,5},{5,1},{2,6},{6,2},{3,7},{7,3},{8,12},{12,8},{9,1... | collective-permute-start | bytes 1966088 | tf_op jit(solution)/shard_map/ppermute | solution.py:958
  37.2 24.9 %collective-permute-start.6 = (f32[64,2048]{1,0:T(8,128)}, f32[64,2048]{1,0:T(8,128)}, u32[]{:S(2)}, u32[]{:S(2)}) collective-permute-start(f32[64,2048]{1,0:T(8,128)} %collective-permute-done.1.refs_12_.refs_8_.refs_7_.refs_4_), channel_id=1, source_target_pairs={{0,24},{8,16},{16,8},{24,0},{1,25},{9,17},{17,9},{25,1},{2,26},{10... | collective-permute-start | bytes 1572872 | tf_op jit(solution)/shard_map/ppermute | solution.py:975
  39.9 23.6 %collective-permute-start.5 = (f32[64,2048]{1,0:T(8,128)}, f32[64,2048]{1,0:T(8,128)}, u32[]{:S(2)}, u32[]{:S(2)}) collective-permute-start(f32[64,2048]{1,0:T(8,128)} %collective-permute-done.1.refs_12_.refs_8_.refs_7_.refs_4_), channel_id=1, source_target_pairs={{0,16},{16,0},{1,17},{17,1},{2,18},{18,2},{3,19},{19,3},{4,20},{20... | collective-permute-start | bytes 1572872 | tf_op jit(solution)/shard_map/ppermute | solution.py:976
  40.4 23.1 %collective-permute-start.4 = (f32[64,2048]{1,0:T(8,128)}, f32[64,2048]{1,0:T(8,128)S(1)}, u32[]{:S(2)}, u32[]{:S(2)}) collective-permute-start(f32[64,2048]{1,0:T(8,128)} %collective-permute-done.1.refs_12_.refs_8_.refs_7_.refs_4_), channel_id=1, source_target_pairs={{0,8},{8,0},{1,9},{9,1},{2,10},{10,2},{3,11},{11,3},{4,12},{12,4},... | collective-permute-start | bytes 1572872 | tf_op jit(solution)/shard_map/ppermute | solution.py:976
  40.8 23.7 %collective-permute-start.10 = (f32[640,256]{1,0:T(8,128)S(1)}, f32[640,256]{1,0:T(8,128)S(1)}, u32[]{:S(2)}, u32[]{:S(2)}) collective-permute-start(f32[640,256]{1,0:T(8,128)S(1)} %collective-permute-done.3.refs_4_.refs_2_), channel_id=1, source_target_pairs={{0,1},{1,0},{2,3},{3,2},{4,5},{5,4},{6,7},{7,6},{8,9},{9,8},{10,11... | collective-permute-start | bytes 1966088 | tf_op jit(solution)/shard_map/ppermute | solution.py:961
  64.5 16.7 %collective-permute-start.7 = (f32[640,256]{1,0:T(8,128)S(1)}, f32[640,256]{1,0:T(8,128)S(1)}, u32[]{:S(2)}, u32[]{:S(2)}) collective-permute-start(f32[640,256]{1,0:T(8,128)S(1)} %collective-permute-done.refs_2_.refs_8_), channel_id=1, source_target_pairs={{0,2},{2,0},{1,3},{3,1},{4,6},{6,4},{5,7},{7,5},{8,10},{10,8},{9,1... | collective-permute-start | bytes 1966088 | tf_op jit(solution)/shard_map/ppermute | solution.py:29
  89.4 34.9 %collective-permute-start.18 = (f32[320,1024]{1,0:T(8,128)S(1)}, f32[320,1024]{1,0:T(8,128)S(1)}, u32[]{:S(2)}, u32[]{:S(2)}) collective-permute-start(f32[320,1024]{1,0:T(8,128)S(1)} %copy-done.18), channel_id=1, source_target_pairs={{0,1},{1,0},{2,3},{3,2},{4,5},{5,4},{6,7},{7,6},{8,9},{9,8},{10,11... | collective-permute-start | bytes 3932168 | tf_op jit(solution)/shard_map/ppermute | solution.py:961
  89.6 35.9 %collective-permute-start.19 = (f32[320,1024]{1,0:T(8,128)}, f32[320,1024]{1,0:T(8,128)}, u32[]{:S(2)}, u32[]{:S(2)}) collective-permute-start(f32[320,1024]{1,0:T(8,128)} %get-tuple-element.153.own_ref), channel_id=1, source_target_pairs={{0,1},{1,0},{2,3},{3,2},{4,5},{5,4},{6,7},{7,6},{8,9},{9,8},{10,11... | collective-permute-start | bytes 3932168 | tf_op jit(solution)/shard_map/ppermute | solution.py:961
  96.1 26.1 %collective-permute-start.20 = (f32[64,2048]{1,0:T(8,128)S(1)}, f32[64,2048]{1,0:T(8,128)S(1)}, u32[]{:S(2)}, u32[]{:S(2)}) collective-permute-start(f32[64,2048]{1,0:T(8,128)S(1)} %copy-done.20), channel_id=1, source_target_pairs={{0,5},{1,4},{4,1},{5,0},{2,7},{3,6},{6,3},{7,2},{8,13},{9,12},{12,... | collective-permute-start | bytes 1572872 | tf_op jit(solution)/shard_map/ppermute | solution.py:1017
  113.8 15.3 %collective-permute-start.17 = (f32[320,1024]{1,0:T(8,128)S(1)}, f32[320,1024]{1,0:T(8,128)}, u32[]{:S(2)}, u32[]{:S(2)}) collective-permute-start(f32[320,1024]{1,0:T(8,128)S(1)} %get-tuple-element.160.refs_0_.own_ref.refs_5_), channel_id=1, source_target_pairs={{0,1},{1,0},{2,3},{3,2},{4,5},{5,4},{6,7},{7,6},{8,9},{9,8},{10,11... | collective-permute-start | bytes 3932168 | tf_op jit(solution)/shard_map/ppermute | solution.py:961
  113.8 36.5 %collective-permute-start.16 = (f32[320,1024]{1,0:T(8,128)S(1)}, f32[320,1024]{1,0:T(8,128)S(1)}, u32[]{:S(2)}, u32[]{:S(2)}) collective-permute-start(f32[320,1024]{1,0:T(8,128)S(1)} %get-tuple-element.160.refs_0_.own_ref.refs_5_), channel_id=1, source_target_pairs={{0,2},{2,0},{1,3},{3,1},{4,6},{6,4},{5,7},{7,5},{8,10},{10,8},{9,1... | collective-permute-start | bytes 3932168 | tf_op jit(solution)/shard_map/ppermute | solution.py:29
  125.4 25.4 %collective-permute-start.24 = (f32[64,2048]{1,0:T(8,128)}, f32[64,2048]{1,0:T(8,128)}, u32[]{:S(2)}, u32[]{:S(2)}) collective-permute-start(f32[64,2048]{1,0:T(8,128)} %collective-permute-done.21.refs_2_.refs_8_.refs_6_), channel_id=1, source_target_pairs={{0,24},{8,16},{16,8},{24,0},{1,25},{9,17},{17,9},{25,1},{2,26},{10... | collective-permute-start | bytes 1572872 | tf_op jit(solution)/shard_map/ppermute | solution.py:975
  127.2 24.7 %collective-permute-start.23 = (f32[64,2048]{1,0:T(8,128)}, f32[64,2048]{1,0:T(8,128)}, u32[]{:S(2)}, u32[]{:S(2)}) collective-permute-start(f32[64,2048]{1,0:T(8,128)} %collective-permute-done.21.refs_2_.refs_8_.refs_6_), channel_id=1, source_target_pairs={{0,16},{16,0},{1,17},{17,1},{2,18},{18,2},{3,19},{19,3},{4,20},{20... | collective-permute-start | bytes 1572872 | tf_op jit(solution)/shard_map/ppermute | solution.py:976
  128.4 23.6 %collective-permute-start.22 = (f32[64,2048]{1,0:T(8,128)}, f32[64,2048]{1,0:T(8,128)}, u32[]{:S(2)}, u32[]{:S(2)}) collective-permute-start(f32[64,2048]{1,0:T(8,128)} %collective-permute-done.21.refs_2_.refs_8_.refs_6_), channel_id=1, source_target_pairs={{0,8},{8,0},{1,9},{9,1},{2,10},{10,2},{3,11},{11,3},{4,12},{12,4},... | collective-permute-start | bytes 1572872 | tf_op jit(solution)/shard_map/ppermute | solution.py:976
  150.3 34.7 %collective-permute-start.30 = (f32[640,256]{1,0:T(8,128)}, f32[640,256]{1,0:T(8,128)}, u32[]{:S(2)}, u32[]{:S(2)}) collective-permute-start(f32[640,256]{1,0:T(8,128)} %get-tuple-element.172), channel_id=1, source_target_pairs={{0,4},{4,0},{1,5},{5,1},{2,6},{6,2},{3,7},{7,3},{8,12},{12,8},{9,1... | collective-permute-start | bytes 1966088 | tf_op jit(solution)/shard_map/ppermute | solution.py:958
  152.0 6.9 %collective-permute-start.25 = (f32[64,2048]{1,0:T(8,128)}, f32[64,2048]{1,0:T(8,128)}, u32[]{:S(2)}, u32[]{:S(2)}) collective-permute-start(f32[64,2048]{1,0:T(8,128)} %collective-permute-done.21.refs_2_.refs_8_.refs_6_), channel_id=1, source_target_pairs={{0,1},{1,0},{2,3},{3,2},{4,5},{5,4},{6,7},{7,6},{8,9},{9,8},{10,11... | collective-permute-start | bytes 1572872 | tf_op jit(solution)/shard_map/ppermute | solution.py:961
  152.0 6.9 %collective-permute-start.26 = (f32[64,2048]{1,0:T(8,128)}, f32[64,2048]{1,0:T(8,128)}, u32[]{:S(2)}, u32[]{:S(2)}) collective-permute-start(f32[64,2048]{1,0:T(8,128)} %collective-permute-done.22.refs_3_.refs_9_.refs_7_), channel_id=1, source_target_pairs={{0,1},{1,0},{2,3},{3,2},{4,5},{5,4},{6,7},{7,6},{8,9},{9,8},{10,11... | collective-permute-start | bytes 1572872 | tf_op jit(solution)/shard_map/ppermute | solution.py:961
  152.5 6.4 %collective-permute-start.27 = (f32[64,2048]{1,0:T(8,128)}, f32[64,2048]{1,0:T(8,128)}, u32[]{:S(2)}, u32[]{:S(2)}) collective-permute-start(f32[64,2048]{1,0:T(8,128)} %collective-permute-done.23.refs_4_.refs_10_.refs_8_), channel_id=1, source_target_pairs={{0,1},{1,0},{2,3},{3,2},{4,5},{5,4},{6,7},{7,6},{8,9},{9,8},{10,11... | collective-permute-start | bytes 1572872 | tf_op jit(solution)/shard_map/ppermute | solution.py:961
  152.5 6.4 %collective-permute-start.28 = (f32[64,2048]{1,0:T(8,128)}, f32[64,2048]{1,0:T(8,128)}, u32[]{:S(2)}, u32[]{:S(2)}) collective-permute-start(f32[64,2048]{1,0:T(8,128)} %collective-permute-done.24.refs_5_.refs_11_.refs_9_), channel_id=1, source_target_pairs={{0,1},{1,0},{2,3},{3,2},{4,5},{5,4},{6,7},{7,6},{8,9},{9,8},{10,11... | collective-permute-start | bytes 1572872 | tf_op jit(solution)/shard_map/ppermute | solution.py:961
  158.8 34.2 %collective-permute-start.29 = (f32[640,256]{1,0:T(8,128)S(1)}, f32[640,256]{1,0:T(8,128)}, u32[]{:S(2)}, u32[]{:S(2)}) collective-permute-start(f32[640,256]{1,0:T(8,128)S(1)} %copy-done.5), channel_id=1, source_target_pairs={{0,1},{1,0},{2,3},{3,2},{4,5},{5,4},{6,7},{7,6},{8,9},{9,8},{10,11... | collective-permute-start | bytes 1966088 | tf_op jit(solution)/shard_map/ppermute | solution.py:961
  185.0 8.1 %collective-permute-start.31 = (f32[640,256]{1,0:T(8,128)}, f32[640,256]{1,0:T(8,128)}, u32[]{:S(2)}, u32[]{:S(2)}) collective-permute-start(f32[640,256]{1,0:T(8,128)} %collective-permute-done.30.refs_6_.refs_2_), channel_id=1, source_target_pairs={{0,1},{1,0},{2,3},{3,2},{4,5},{5,4},{6,7},{7,6},{8,9},{9,8},{10,11... | collective-permute-start | bytes 1966088 | tf_op jit(solution)/shard_map/ppermute | solution.py:961
  192.7 31.0 %collective-permute-start.35 = (f32[320,1024]{1,0:T(8,128)S(1)}, f32[320,1024]{1,0:T(8,128)}, u32[]{:S(2)}, u32[]{:S(2)}) collective-permute-start(f32[320,1024]{1,0:T(8,128)S(1)} %collective-permute-done.16.refs_0_.refs_1_.own_ref), channel_id=1, source_target_pairs={{0,1},{1,0},{2,3},{3,2},{4,5},{5,4},{6,7},{7,6},{8,9},{9,8},{10,11... | collective-permute-start | bytes 3932168 | tf_op jit(solution)/shard_map/ppermute | solution.py:961
  193.0 28.8 %collective-permute-start.33 = (f32[320,256]{1,0:T(8,128)}, f32[320,256]{1,0:T(8,128)S(1)}, u32[]{:S(2)}, u32[]{:S(2)}) collective-permute-start(f32[320,256]{1,0:T(8,128)} %get-tuple-element.180), channel_id=1, source_target_pairs={{0,4},{4,0},{1,5},{5,1},{2,6},{6,2},{3,7},{7,3},{8,12},{12,8},{9,1... | collective-permute-start | bytes 983048 | tf_op jit(solution)/shard_map/ppermute | solution.py:958
  222.0 31.3 %collective-permute-start.36 = (f32[320,1024]{1,0:T(8,128)}, f32[320,1024]{1,0:T(8,128)S(1)}, u32[]{:S(2)}, u32[]{:S(2)}) collective-permute-start(f32[320,1024]{1,0:T(8,128)} %get-tuple-element.192), channel_id=1, source_target_pairs={{0,2},{2,0},{1,3},{3,1},{4,6},{6,4},{5,7},{7,5},{8,10},{10,8},{9,1... | collective-permute-start | bytes 3932168 | tf_op jit(solution)/shard_map/ppermute | solution.py:29
  235.4 32.4 %collective-permute-start.37 = (f32[2,2,64,1024]{3,2,1,0:T(8,128)}, f32[2,2,64,1024]{3,2,1,0:T(8,128)}, u32[]{:S(2)}, u32[]{:S(2)}) collective-permute-start(f32[2,2,64,1024]{3,2,1,0:T(8,128)} %get-tuple-element.197), channel_id=1, source_target_pairs={{0,8},{1,17},{8,0},{9,25},{16,24},{17,1},{24,16},{25,9},{2,10},{3,... | collective-permute-start | bytes 3145736 | tf_op jit(solution)/shard_map/ppermute | solution.py:880
  242.4 25.5 %collective-permute-start.40 = (f32[2,2,64,1024]{3,2,1,0:T(8,128)}, f32[2,2,64,1024]{3,2,1,0:T(8,128)}, u32[]{:S(2)}, u32[]{:S(2)}) collective-permute-start(f32[2,2,64,1024]{3,2,1,0:T(8,128)} %get-tuple-element.202), channel_id=1, source_target_pairs={{0,8},{1,17},{8,0},{9,25},{16,24},{17,1},{24,16},{25,9},{2,10},{3,... | collective-permute-start | bytes 3145736 | tf_op jit(solution)/shard_map/ppermute | solution.py:880
  243.7 23.0 %collective-permute-start.39 = (f32[320,256]{1,0:T(8,128)}, f32[320,256]{1,0:T(8,128)S(1)}, u32[]{:S(2)}, u32[]{:S(2)}) collective-permute-start(f32[320,256]{1,0:T(8,128)} %get-tuple-element.200), channel_id=1, source_target_pairs={{0,1},{1,0},{2,3},{3,2},{4,5},{5,4},{6,7},{7,6},{8,9},{9,8},{10,11... | collective-permute-start | bytes 983048 | tf_op jit(solution)/shard_map/ppermute | solution.py:961
  249.8 18.1 %collective-permute-start.38 = (f32[320,256]{1,0:T(8,128)S(1)}, f32[320,256]{1,0:T(8,128)S(1)}, u32[]{:S(2)}, u32[]{:S(2)}) collective-permute-start(f32[320,256]{1,0:T(8,128)S(1)} %copy-done.32), channel_id=1, source_target_pairs={{0,4},{4,0},{1,5},{5,1},{2,6},{6,2},{3,7},{7,3},{8,12},{12,8},{9,1... | collective-permute-start | bytes 983048 | tf_op jit(solution)/shard_map/ppermute | solution.py:958
  271.0 17.8 %collective-permute-start.42 = (f32[2,64,2048]{2,1,0:T(8,128)S(1)}, f32[2,64,2048]{2,1,0:T(8,128)S(1)}, u32[]{:S(2)}, u32[]{:S(2)}) collective-permute-start(f32[2,64,2048]{2,1,0:T(8,128)S(1)} %get-tuple-element.207), channel_id=1, source_target_pairs={{0,16},{1,9},{8,24},{9,1},{16,0},{17,25},{24,8},{25,17},{2,18},{3,... | collective-permute-start | bytes 3145736 | tf_op jit(solution)/shard_map/ppermute | solution.py:880
  287.3 28.0 %collective-permute-start.45 = (f32[320,512]{1,0:T(8,128)S(1)}, f32[320,512]{1,0:T(8,128)S(1)}, u32[]{:S(2)}, u32[]{:S(2)}) collective-permute-start(f32[320,512]{1,0:T(8,128)S(1)} %get-tuple-element.222), channel_id=1, source_target_pairs={{0,2},{2,0},{1,3},{3,1},{4,6},{6,4},{5,7},{7,5},{8,10},{10,8},{9,1... | collective-permute-start | bytes 1966088 | tf_op jit(solution)/shard_map/ppermute | solution.py:29
  289.7 26.5 %collective-permute-start.44 = (f32[64,2048]{1,0:T(8,128)S(1)}, f32[64,2048]{1,0:T(8,128)}, u32[]{:S(2)}, u32[]{:S(2)}) collective-permute-start(f32[64,2048]{1,0:T(8,128)S(1)} %get-tuple-element.216), channel_id=1, source_target_pairs={{0,5},{1,4},{4,1},{5,0},{2,7},{3,6},{6,3},{7,2},{8,13},{9,12},{12,... | collective-permute-start | bytes 1572872 | tf_op jit(solution)/shard_map/ppermute | solution.py:1082
  298.5 19.5 %collective-permute-start.43 = (f32[2,2,64,1024]{3,2,1,0:T(8,128)}, f32[2,2,64,1024]{3,2,1,0:T(8,128)S(1)}, u32[]{:S(2)}, u32[]{:S(2)}) collective-permute-start(f32[2,2,64,1024]{3,2,1,0:T(8,128)} %get-tuple-element.213), channel_id=1, source_target_pairs={{0,8},{1,17},{8,0},{9,25},{16,24},{17,1},{24,16},{25,9},{2,10},{3,... | collective-permute-start | bytes 3145736 | tf_op jit(solution)/shard_map/ppermute | solution.py:880
  305.4 19.3 %collective-permute-start.47 = (f32[2,2,64,1024]{3,2,1,0:T(8,128)}, f32[2,2,64,1024]{3,2,1,0:T(8,128)S(1)}, u32[]{:S(2)}, u32[]{:S(2)}) collective-permute-start(f32[2,2,64,1024]{3,2,1,0:T(8,128)} %get-tuple-element.226), channel_id=1, source_target_pairs={{0,8},{1,17},{8,0},{9,25},{16,24},{17,1},{24,16},{25,9},{2,10},{3,... | collective-permute-start | bytes 3145736 | tf_op jit(solution)/shard_map/ppermute | solution.py:880
  316.9 17.9 %collective-permute-start.51 = (f32[320,256]{1,0:T(8,128)}, f32[320,256]{1,0:T(8,128)S(1)}, u32[]{:S(2)}, u32[]{:S(2)}) collective-permute-start(f32[320,256]{1,0:T(8,128)} %copy-done.14), channel_id=1, source_target_pairs={{0,5},{1,4},{4,1},{5,0},{2,7},{3,6},{6,3},{7,2},{8,13},{9,12},{12,... | collective-permute-start | bytes 983048 | tf_op jit(solution)/shard_map/ppermute | solution.py:1106
  326.6 9.9 %collective-permute-start.53 = (f32[64,2048]{1,0:T(8,128)S(1)}, f32[64,2048]{1,0:T(8,128)S(1)}, u32[]{:S(2)}, u32[]{:S(2)}) collective-permute-start(f32[64,2048]{1,0:T(8,128)S(1)} %get-tuple-element.238), channel_id=1, source_target_pairs={{0,16},{1,9},{8,24},{9,1},{16,0},{17,25},{24,8},{25,17},{2,18},{3,... | collective-permute-start | bytes 1572872 | tf_op jit(solution)/shard_map/ppermute | solution.py:880
  336.5 14.8 %collective-permute-start.58 = (f32[64,2048]{1,0:T(8,128)S(1)}, f32[64,2048]{1,0:T(8,128)S(1)}, u32[]{:S(2)}, u32[]{:S(2)}) collective-permute-start(f32[64,2048]{1,0:T(8,128)S(1)} %reduction_step.12.refs_0_), channel_id=1, source_target_pairs={{0,8},{1,17},{8,0},{9,25},{16,24},{17,1},{24,16},{25,9},{2,10},{3,... | collective-permute-start | bytes 1572872 | tf_op jit(solution)/shard_map/ppermute | solution.py:880
  337.7 13.6 %collective-permute-start.57 = (f32[64,2048]{1,0:T(8,128)S(1)}, f32[64,2048]{1,0:T(8,128)S(1)}, u32[]{:S(2)}, u32[]{:S(2)}) collective-permute-start(f32[64,2048]{1,0:T(8,128)S(1)} %reduction_step.12.refs_0_), channel_id=1, source_target_pairs={{0,16},{1,9},{8,24},{9,1},{16,0},{17,25},{24,8},{25,17},{2,18},{3,... | collective-permute-start | bytes 1572872 | tf_op jit(solution)/shard_map/ppermute | solution.py:880
  338.6 31.5 %collective-permute-start.49 = (f32[320,512]{1,0:T(8,128)S(1)}, f32[320,512]{1,0:T(8,128)S(1)}, u32[]{:S(2)}, u32[]{:S(2)}) collective-permute-start(f32[320,512]{1,0:T(8,128)S(1)} %copy-done.11), channel_id=1, source_target_pairs={{0,2},{2,0},{1,3},{3,1},{4,6},{6,4},{5,7},{7,5},{8,10},{10,8},{9,1... | collective-permute-start | bytes 1966088 | tf_op jit(solution)/shard_map/ppermute | solution.py:29
  338.7 25.2 %collective-permute-start.54 = (f32[64,2048]{1,0:T(8,128)S(1)}, f32[64,2048]{1,0:T(8,128)S(1)}, u32[]{:S(2)}, u32[]{:S(2)}) collective-permute-start(f32[64,2048]{1,0:T(8,128)S(1)} %reduction_step.11), channel_id=1, source_target_pairs={{0,4},{4,0},{1,5},{5,1},{2,6},{6,2},{3,7},{7,3},{8,12},{12,8},{9,1... | collective-permute-start | bytes 1572872 | tf_op jit(solution)/shard_map/ppermute | solution.py:958
  341.0 26.2 %collective-permute-start.48 = (f32[64,2048]{1,0:T(8,128)S(1)}, f32[64,2048]{1,0:T(8,128)S(1)}, u32[]{:S(2)}, u32[]{:S(2)}) collective-permute-start(f32[64,2048]{1,0:T(8,128)S(1)} %get-tuple-element.228), channel_id=1, source_target_pairs={{0,16},{1,9},{8,24},{9,1},{16,0},{17,25},{24,8},{25,17},{2,18},{3,... | collective-permute-start | bytes 1572872 | tf_op jit(solution)/shard_map/ppermute | solution.py:880
  351.4 18.9 %collective-permute-start.59 = (f32[64,2048]{1,0:T(8,128)S(1)}, f32[64,2048]{1,0:T(8,128)S(1)}, u32[]{:S(2)}, u32[]{:S(2)}) collective-permute-start(f32[64,2048]{1,0:T(8,128)S(1)} %collective-permute-done.58.refs_2_), channel_id=1, source_target_pairs={{0,16},{1,9},{8,24},{9,1},{16,0},{17,25},{24,8},{25,17},{2,18},{3,... | collective-permute-start | bytes 1572872 | tf_op jit(solution)/shard_map/ppermute | solution.py:880
  363.9 17.2 %collective-permute-start.55 = (f32[320,256]{1,0:T(8,128)S(1)}, f32[320,256]{1,0:T(8,128)S(1)}, u32[]{:S(2)}, u32[]{:S(2)}) collective-permute-start(f32[320,256]{1,0:T(8,128)S(1)} %copy-done.13), channel_id=1, source_target_pairs={{0,4},{4,0},{1,5},{5,1},{2,6},{6,2},{3,7},{7,3},{8,12},{12,8},{9,1... | collective-permute-start | bytes 983048 | tf_op jit(solution)/shard_map/ppermute | solution.py:958
  370.4 13.5 %collective-permute-start.61 = (f32[64,2048]{1,0:T(8,128)S(1)}, f32[64,2048]{1,0:T(8,128)S(1)}, u32[]{:S(2)}, u32[]{:S(2)}) collective-permute-start(f32[64,2048]{1,0:T(8,128)S(1)} %reduction_step.13.refs_0_), channel_id=1, source_target_pairs={{0,8},{1,17},{8,0},{9,25},{16,24},{17,1},{24,16},{25,9},{2,10},{3,... | collective-permute-start | bytes 1572872 | tf_op jit(solution)/shard_map/ppermute | solution.py:880
  371.6 12.3 %collective-permute-start.60 = (f32[64,2048]{1,0:T(8,128)S(1)}, f32[64,2048]{1,0:T(8,128)S(1)}, u32[]{:S(2)}, u32[]{:S(2)}) collective-permute-start(f32[64,2048]{1,0:T(8,128)S(1)} %reduction_step.13.refs_0_), channel_id=1, source_target_pairs={{0,16},{1,9},{8,24},{9,1},{16,0},{17,25},{24,8},{25,17},{2,18},{3,... | collective-permute-start | bytes 1572872 | tf_op jit(solution)/shard_map/ppermute | solution.py:880
  383.8 9.2 %collective-permute-start.62 = (f32[64,2048]{1,0:T(8,128)S(1)}, f32[64,2048]{1,0:T(8,128)S(1)}, u32[]{:S(2)}, u32[]{:S(2)}) collective-permute-start(f32[64,2048]{1,0:T(8,128)S(1)} %collective-permute-done.61.refs_2_), channel_id=1, source_target_pairs={{0,16},{1,9},{8,24},{9,1},{16,0},{17,25},{24,8},{25,17},{2,18},{3,... | collective-permute-start | bytes 1572872 | tf_op jit(solution)/shard_map/ppermute | solution.py:880
  (49 other events, 469.8 us)
where the time goes:
time: 397 us; the launch traced here: 396 us
  Pallas kernels  151 us (38%)
  waiting for transfers between devices  123 us (31%)
  blocking collectives  61.7 us (16%)
  starting transfers between devices  46.3 us (12%)
  local copies, waits for them, and re-layouts  10.2 us (3%)
    all_gather x8, blocking collectives, gather(): return lax.all_gather(array, axes, tiled=True)  61.7 us
    ppermute x7, waiting for transfers between devices, over_h(): return lax.ppermute(array, 'h', FLIP2)  61 us
    pallas_call x5, Pallas kernels, project(): call(partial(project_body, len(parts), len(flat), spots, len(weights), 0...  35.9 us
    pallas_call x4, Pallas kernels, weight_rows(): call(partial(weight_body, turn), grid_spec=pltpu.PrefetchScalarGridSpec(n...  26.6 us
    ppermute x13, waiting for transfers between devices, plane_swap(): return lax.ppermute(array, ('y', 'x', 'c'), pairs)  19.4 us
    pallas_call x4, Pallas kernels, prepare(): call(prepare_body, grid_spec=pltpu.PrefetchScalarGridSpec(num_scalar_pref...  15.1 us
    pallas_call x2, Pallas kernels, norm_back(): call(partial(norm_back_body, len(z), split_terms, layer), grid_spec=pltpu...  15 us
    pallas_call x2, Pallas kernels, recur(): call(partial(recur_body, len(z), last, layer, spread_params), grid=(CHUNK...  14.7 us
  transfers between devices with their start and end apart: 63, of which 28 were waited for; matrix products, arithmetic and copies ran while one was open for 1% of the time, Pallas kernels for 36%

commit v1 on v0

--- a/solution.py
+++ b/solution.py
@@ -880,10 +880,10 @@
     return lax.ppermute(array, ("y", "x", "c"), pairs)
 
 
-def plane_gather(share, *before):
+def plane_gather(share):
     first = plane_swap(share, 0)
     second = plane_swap(share, 1)
-    return [share, second, first, plane_swap(after(first, second, *before), 1)]
+    return [share, second, first, plane_swap(after(first, second), 1)]
 
 
 def assemble_body(place_ref, *refs):
@@ -1118,7 +1118,7 @@
     close = merge(kept, 0, after(received[0], output))
     far = over_c(over_h(after(aways[1], go)))
     (share,) = step_of((total, after(go, close, *later[1:])), cut=0)
-    gathered = plane_gather(share, far)
+    gathered = plane_gather(share)
     grad_in = [(close, 0), (over_c(close[frames:]), 0), (far_near, 0), (far, 0)]
     grad_in = unpack(place, grad_in, frames)
     grad_weights = assemble(place, after(later, share), 1)

time: 397 us -> 394 us (level)
    ppermute x7, waiting for transfers between devices: 61 us -> 44.4 us  [over_h(): return lax.ppermute(array, 'h', FLIP2)]
    ppermute x13, waiting for transfers between devices: 19.4 us -> 29.1 us  [plane_swap(): return lax.ppermute(array, ('y', 'x', 'c'), pairs)]
    ppermute x6, waiting for transfers between devices: 14.3 us -> 21.3 us  [swap_half(): return lax.ppermute(array, 'l', FLIP2)]
  transfers between devices with their start and end apart: 63 -> 63, of which waited for: 28 -> 27; matrix products, arithmetic and copies ran while one was open for 1% -> 1% of each run, Pallas kernels for 36% -> 36%
where the time goes in v1:
time: 394 us; the launch traced here: 392 us
  Pallas kernels  151 us (38%)
  waiting for transfers between devices  121 us (31%)
  blocking collectives  61.7 us (16%)
  starting transfers between devices  43.9 us (11%)
  local copies, waits for them, and re-layouts  10.2 us (3%)
    all_gather x8, blocking collectives, gather(): return lax.all_gather(array, axes, tiled=True)  61.7 us
    ppermute x7, waiting for transfers between devices, over_h(): return lax.ppermute(array, 'h', FLIP2)  44.4 us
    pallas_call x5, Pallas kernels, project(): call(partial(project_body, len(parts), len(flat), spots, len(weights), 0...  35.9 us
    ppermute x13, waiting for transfers between devices, plane_swap(): return lax.ppermute(array, ('y', 'x', 'c'), pairs)  29.1 us
    pallas_call x4, Pallas kernels, weight_rows(): call(partial(weight_body, turn), grid_spec=pltpu.PrefetchScalarGridSpec(n...  26.6 us
    ppermute x6, waiting for transfers between devices, swap_half(): return lax.ppermute(array, 'l', FLIP2)  21.3 us
    pallas_call x4, Pallas kernels, prepare(): call(prepare_body, grid_spec=pltpu.PrefetchScalarGridSpec(num_scalar_pref...  15.1 us
    pallas_call x2, Pallas kernels, norm_back(): call(partial(norm_back_body, len(z), split_terms, layer), grid_spec=pltpu...  15 us
  transfers between devices with their start and end apart: 63, of which 27 were waited for; matrix products, arithmetic and copies ran while one was open for 1% of the time, Pallas kernels for 36%

profile of v1, /device:TPU:0, one launch (start us, length us, event | category | flops | bytes accessed | tf_op | source)
XLA Modules:
  0.0 391.7 jit_solution(5470130926620244180)
XLA Ops:
  5.2 2.7 collective-permute-start.3
  7.8 2.6 collective-permute-start.1
  10.8 2.9 pack.3
  15.6 18.6 %collective-permute-done.1.refs_12_.refs_8_.refs_7_.refs_4_ = f32[64,2048]{1,0:T(8,128)} collective-permute-done((f32[64,2048]{1,0:T(8,128)S(1)}, f32[64,2048]{1,0:T(8,128)}, u32[]{:S(2)}, u32[]{:S(2)}) %collective-permute-start.1) | collective-permute-done | bytes 524320 | tf_op jit(solution)/shard_map/ppermute | solution.py:958
  34.2 3.0 collective-permute-done.3.refs_4_.refs_2_
  37.2 2.7 collective-permute-start.6
  40.8 21.3 %collective-permute-done.refs_2_.refs_8_ = f32[640,256]{1,0:T(8,128)S(1)} collective-permute-done((f32[640,256]{1,0:T(8,128)S(1)}, f32[640,256]{1,0:T(8,128)S(1)}, u32[]{:S(2)}, u32[]{:S(2)}) %collective-permute-start) | collective-permute-done | bytes 655392 | tf_op jit(solution)/shard_map/ppermute | solution.py:958
  69.9 9.9 %project.5 = (f32[320,1024]{1,0:T(8,128)}, f32[320,1024]{1,0:T(8,128)}) custom-call(s32[6]{0:T(128)S(1)} %concatenate.11.cols_ref, s32[8]{0:T(128)S(1)} %stack.124.place_ref, f32[640,256]{1,0:T(8,128)S(1)} %get-tuple-element.137.refs_0_.refs_6_, f32[640,256]{1,0:T(8,128)} %collective-permute-done.8.refs_1_.refs_7_, ...), custom_call_target="tpu_custom_call" | custom-call | flops 47185920 | bytes 98304 | tf_op jit(solution)/shard_map/project/pallas_call | solution.py:288
  83.3 6.0 %project.6 = (f32[320,1024]{1,0:T(8,128)}, f32[5,8,128]{2,1,0:T(8,128)S(1)}, f32[320,1024]{1,0:T(8,128)}) custom-call(s32[2]{0:T(128)S(1)} %pad_add_fusion.1.cols_ref, s32[8]{0:T(128)S(1)} %stack.124.place_ref, f32[640,256]{1,0:T(8,128)S(1)} %collective-permute-done.7.refs_0_.refs_4_, f32[640,256]{1,0:T(8,128)S(1)} %collective-permute-done.15.refs_1_.refs_5_, ...), custom_call_target="tpu_custom_call" | custom-call | flops 15728640 | bytes 32768 | tf_op jit(solution)/shard_map/project/pallas_call | solution.py:288
  89.9 6.2 %all_gather.24 = f32[20,8,128]{2,1,0:T(8,128)S(1)} all-gather(f32[5,8,128]{2,1,0:T(8,128)S(1)} %get-tuple-element.145), channel_id=1, replica_groups=mesh['y'=2,'x'=2,'h'=2,'l'=2,'c'=2] {'h','c'}, dimensions={0}, use_global_device_ids=true | all-gather | bytes 102400 | tf_op jit(solution)/shard_map/all_gather | solution.py:997
  97.3 9.2 %all_gather.25.refs_1_.refs_3_ = f32[80,8,128]{2,1,0:T(8,128)S(1)} all-gather(f32[20,8,128]{2,1,0:T(8,128)S(1)} %all_gather.24), channel_id=1, replica_groups=mesh['y'=2,'x'=2,'h'=2,'l'=2,'c'=2] {'y','x'}, dimensions={0}, use_global_device_ids=true | all-gather | bytes 409600 | tf_op jit(solution)/shard_map/all_gather | solution.py:997
  106.6 7.3 %recur.2 = (f32[320,1024]{1,0:T(8,128)S(1)}, f32[320,1024]{1,0:T(8,128)}, f32[320,1024]{1,0:T(8,128)}, f32[6,8,128]{2,1,0:T(8,128)S(1)}) custom-call(s32[8]{0:T(128)S(1)} %stack.124.place_ref, f32[320]{0:T(512)S(1)} %fusion.6.gate_ref, f32[320,1024]{1,0:T(8,128)} %get-tuple-element.144.refs_0_, f32[80,8,128]{2,1,0:T(8,128)S(1)} %all_gather.25.refs_1_.refs_3_, ...), custom_call_target="tpu_custom_call" | custom-call | flops 512000 | bytes 102400 | tf_op jit(solution)/shard_map/recur/pallas_call | solution.py:434
  115.7 6.6 %collective-permute-done.20 = f32[64,2048]{1,0:T(8,128)S(1)} collective-permute-done((f32[64,2048]{1,0:T(8,128)S(1)}, f32[64,2048]{1,0:T(8,128)S(1)}, u32[]{:S(2)}, u32[]{:S(2)}) %collective-permute-start.20) | collective-permute-done | bytes 524320 | tf_op jit(solution)/shard_map/ppermute | solution.py:1017
  129.1 3.8 prepare.4
  132.9 3.8 prepare.5
  136.6 5.2 %project.7.refs_3_ = f32[320,512]{1,0:T(8,128)} custom-call(s32[4]{0:T(128)S(1)} %pad_add_fusion.2.cols_ref, s32[8]{0:T(128)S(1)} %stack.124.place_ref, f32[320,1024]{1,0:T(8,128)S(1)} %get-tuple-element.160.refs_0_.own_ref.refs_5_, f32[2,256,2048]{2,1,0:T(8,128)} %refs_2_.1, ...), custom_call_target="tpu_custom_call" | custom-call | flops 15728640 | bytes 32768 | tf_op jit(solution)/shard_map/project/pallas_call | solution.py:288
  141.8 3.8 prepare.6
  145.6 4.7 %collective-permute-done.16.refs_0_.refs_1_.own_ref = f32[320,1024]{1,0:T(8,128)S(1)} collective-permute-done((f32[320,1024]{1,0:T(8,128)S(1)}, f32[320,1024]{1,0:T(8,128)S(1)}, u32[]{:S(2)}, u32[]{:S(2)}) %collective-permute-start.16) | collective-permute-done | bytes 1310752 | tf_op jit(solution)/shard_map/ppermute | solution.py:29
  153.1 5.7 %project.8 = (f32[320,512]{1,0:T(8,128)}, f32[3,8,128]{2,1,0:T(8,128)S(1)}) custom-call(s32[4]{0:T(128)S(1)} %pad_add_fusion.cols_ref, s32[8]{0:T(128)S(1)} %stack.124.place_ref, f32[320,1024]{1,0:T(8,128)S(1)} %collective-permute-done.16.refs_0_.refs_1_.own_ref, f32[2,256,2048]{2,1,0:T(8,128)} %refs_2_.1, ...), custom_call_target="tpu_custom_call" | custom-call | flops 15728640 | bytes 32768 | tf_op jit(solution)/shard_map/project/pallas_call | solution.py:288
  158.9 9.2 %project.9 = (f32[320,512]{1,0:T(8,128)}, f32[3,8,128]{2,1,0:T(8,128)S(1)}) custom-call(s32[8]{0:T(128)S(1)} %concatenate.12.cols_ref, s32[8]{0:T(128)S(1)} %stack.124.place_ref, f32[320,1024]{1,0:T(8,128)S(1)} %copy-done.1, f32[320,1024]{1,0:T(8,128)S(1)} %collective-permute-done.16.refs_0_.refs_1_.own_ref, ...), custom_call_target="tpu_custom_call" | custom-call | flops 31457280 | bytes 65536 | tf_op jit(solution)/shard_map/project/pallas_call | solution.py:288
  168.1 8.1 %all_gather.26 = f32[12,8,128]{2,1,0:T(8,128)S(1)} all-gather(f32[3,8,128]{2,1,0:T(8,128)S(1)} %get-tuple-element.168), channel_id=1, replica_groups=mesh['y'=2,'x'=2,'h'=2,'l'=2,'c'=2] {'y','x'}, dimensions={0}, use_global_device_ids=true | all-gather | bytes 61440 | tf_op jit(solution)/shard_map/all_gather | solution.py:997
  176.2 8.8 %all_gather.27.refs_2_.refs_4_ = f32[48,8,128]{2,1,0:T(8,128)S(1)} all-gather(f32[12,8,128]{2,1,0:T(8,128)S(1)} %all_gather.26), channel_id=1, replica_groups=mesh['y'=2,'x'=2,'h'=2,'l'=2,'c'=2] {'h','c'}, dimensions={0}, use_global_device_ids=true | all-gather | bytes 245760 | tf_op jit(solution)/shard_map/all_gather | solution.py:997
  185.3 7.4 %recur.3 = (f32[320,256]{1,0:T(8,128)}, f32[320,256]{1,0:T(8,128)}, f32[320,256]{1,0:T(8,128)}, f32[320,256]{1,0:T(8,128)}, f32[320,1024]{1,0:T(8,128)}, /*index=5*/f32[320,1024]{1,0:T(8,128)}) custom-call(s32[8]{0:T(128)S(1)} %stack.124.place_ref, f32[320]{0:T(512)S(1)} %fusion.6.gate_ref, f32[320,512]{1,0:T(8,128)} %get-tuple-element.156.refs_0_, ...), custom_call_target="tpu_custom_call" | custom-call | flops 512000 | bytes 102400 | tf_op jit(solution)/shard_map/recur/pallas_call | solution.py:434
  193.1 5.6 %back.2 = (f32[320,1024]{1,0:T(8,128)S(1)}, f32[3,8,128]{2,1,0:T(8,128)S(1)}) custom-call(s32[8]{0:T(128)S(1)} %stack.124.place_ref, f32[320]{0:T(512)S(1)} %fusion.6.gate_ref, f32[320,512]{1,0:T(8,128)} %get-tuple-element.156.refs_0_, f32[320,512]{1,0:T(8,128)} %get-tuple-element.167.refs_1_, f32[48,8,128]{2,1,0:T(8,128)S(1)} %all_gather.27.refs_2_.refs_4_, ...), custom_call_target="tpu_custom_call" | custom-call | flops 153600 | bytes 102400 | tf_op jit(solution)/shard_map/back/pallas_call | solution.py:541
  198.7 8.2 %all_gather.28 = f32[12,8,128]{2,1,0:T(8,128)S(1)} all-gather(f32[3,8,128]{2,1,0:T(8,128)S(1)} %get-tuple-element.177), channel_id=1, replica_groups=mesh['y'=2,'x'=2,'h'=2,'l'=2,'c'=2] {'y','x'}, dimensions={0}, use_global_device_ids=true | all-gather | bytes 61440 | tf_op jit(solution)/shard_map/all_gather | solution.py:997
  206.9 6.8 %all_gather.29.refs_5_ = f32[48,8,128]{2,1,0:T(8,128)S(1)} all-gather(f32[12,8,128]{2,1,0:T(8,128)S(1)} %all_gather.28), channel_id=1, replica_groups=mesh['y'=2,'x'=2,'h'=2,'l'=2,'c'=2] {'h','c'}, dimensions={0}, use_global_device_ids=true | all-gather | bytes 245760 | tf_op jit(solution)/shard_map/all_gather | solution.py:997
  213.7 7.7 %norm_back.2 = (f32[320,1024]{1,0:T(8,128)}, f32[320,512]{1,0:T(8,128)S(1)}, f32[320,1024]{1,0:T(8,128)}, f32[3,8,128]{2,1,0:T(8,128)S(1)}) custom-call(s32[2]{0:T(128)S(1)} %pad_add_fusion.4.cols_ref, s32[8]{0:T(128)S(1)} %stack.124.place_ref, f32[320,1024]{1,0:T(8,128)S(1)} %get-tuple-element.176.grad_ref, f32[320,512]{1,0:T(8,128)} %get-tuple-element.156.refs_0_, ...), custom_call_target="tpu_custom_call" | custom-call | flops 31457280 | bytes 65536 | tf_op jit(solution)/shard_map/norm_back/pallas_call | solution.py:646
  223.7 3.8 prepare.7
  228.2 7.2 %weight_rows.4 = (f32[2,2,64,1024]{3,2,1,0:T(8,128)}, f32[2,2,64,1024]{3,2,1,0:T(8,128)}, bf16[512,768]{1,0:T(8,128)(2,1)S(1)}, bf16[512,768]{1,0:T(8,128)(2,1)S(1)}) custom-call(s32[8]{0:T(128)S(1)} %stack.124.place_ref, f32[320,1024]{1,0:T(8,128)} %get-tuple-element.191.refs_0_.grad_ref, f32[320,512]{1,0:T(8,128)S(1)} %collective-permute-done.32.refs_1_, ...), custom_call_target="tpu_custom_call" | custom-call | flops 37748736 | bytes 32768 | tf_op jit(solution)/shard_map/weight_rows/pallas_call | solution.py:819
  236.2 6.1 %weight_rows.5 = (f32[2,2,64,1024]{3,2,1,0:T(8,128)}, f32[2,2,64,1024]{3,2,1,0:T(8,128)}) custom-call(s32[8]{0:T(128)S(1)} %stack.124.place_ref, bf16[512,768]{1,0:T(8,128)(2,1)S(1)} %get-tuple-element.187.refs_0_, bf16[512,768]{1,0:T(8,128)(2,1)S(1)} %get-tuple-element.188.refs_1_, bf16[768,1024]{1,0:T(8,128)(2,1)} %get-tuple-element.184.refs_2_, ...), custom_call_target="tpu_custom_call" | custom-call | flops 37748736 | bytes 32768 | tf_op jit(solution)/shard_map/weight_rows/pallas_call | solution.py:819
  243.7 6.1 %own_terms.2.refs_3_.refs_0_ = f32[320,1024]{1,0:T(8,128)S(1)} custom-call(s32[2]{0:T(128)S(1)} %pad_add_fusion.5.cols_ref, s32[8]{0:T(128)S(1)} %stack.124.place_ref, f32[320,1024]{1,0:T(8,128)} %get-tuple-element.191.refs_0_.grad_ref, f32[640,256]{1,0:T(8,128)S(1)} %copy-done.6, f32[640,256]{1,0:T(8,128)} %collective-permute-done.29.refs_5_.refs_1_, ...), custom_call_target="tpu_custom_call" | custom-call | flops 31457280 | bytes 65536 | tf_op jit(solution)/shard_map/own_terms/pallas_call | solution.py:704
  253.2 5.9 %back.3 = (f32[320,1024]{1,0:T(8,128)S(1)}, f32[3,8,128]{2,1,0:T(8,128)S(1)}) custom-call(s32[8]{0:T(128)S(1)} %stack.124.place_ref, f32[320]{0:T(512)S(1)} %fusion.6.gate_ref, f32[320,1024]{1,0:T(8,128)} %get-tuple-element.144.refs_0_, f32[80,8,128]{2,1,0:T(8,128)S(1)} %all_gather.25.refs_1_.refs_3_, ...), custom_call_target="tpu_custom_call" | custom-call | flops 153600 | bytes 102400 | tf_op jit(solution)/shard_map/back/pallas_call | solution.py:541
  259.1 7.5 %all_gather.30 = f32[12,8,128]{2,1,0:T(8,128)S(1)} all-gather(f32[3,8,128]{2,1,0:T(8,128)S(1)} %get-tuple-element.195), channel_id=1, replica_groups=mesh['y'=2,'x'=2,'h'=2,'l'=2,'c'=2] {'y','x'}, dimensions={0}, use_global_device_ids=true | all-gather | bytes 61440 | tf_op jit(solution)/shard_map/all_gather | solution.py:997
  271.9 6.9 %all_gather.31.refs_4_ = f32[48,8,128]{2,1,0:T(8,128)S(1)} all-gather(f32[12,8,128]{2,1,0:T(8,128)S(1)} %all_gather.30), channel_id=1, replica_groups=mesh['y'=2,'x'=2,'h'=2,'l'=2,'c'=2] {'h','c'}, dimensions={0}, use_global_device_ids=true | all-gather | bytes 245760 | tf_op jit(solution)/shard_map/all_gather | solution.py:997
  278.7 7.3 %norm_back.3 = (f32[320,1024]{1,0:T(8,128)}, f32[320,512]{1,0:T(8,128)S(1)}, f32[320,512]{1,0:T(8,128)S(1)}, f32[320,512]{1,0:T(8,128)S(1)}, f32[3,8,128]{2,1,0:T(8,128)S(1)}) custom-call(s32[2]{0:T(128)S(1)} %pad_add_fusion.4.cols_ref, s32[8]{0:T(128)S(1)} %stack.124.place_ref, f32[320,1024]{1,0:T(8,128)S(1)} %get-tuple-element.194.grad_ref, ...), custom_call_target="tpu_custom_call" | custom-call | flops 31457280 | bytes 65536 | tf_op jit(solution)/shard_map/norm_back/pallas_call | solution.py:646
  291.3 7.2 %weight_rows.6 = (f32[2,2,64,1024]{3,2,1,0:T(8,128)}, f32[2,2,64,1024]{3,2,1,0:T(8,128)}, bf16[512,768]{1,0:T(8,128)(2,1)S(1)}, bf16[512,768]{1,0:T(8,128)(2,1)S(1)}) custom-call(s32[8]{0:T(128)S(1)} %stack.124.place_ref, f32[320,1024]{1,0:T(8,128)} %get-tuple-element.221.refs_0_.grad_ref, f32[320,512]{1,0:T(8,128)S(1)} %collective-permute-done.41.refs_1_, ...), custom_call_target="tpu_custom_call" | custom-call | flops 37748736 | bytes 32768 | tf_op jit(solution)/shard_map/weight_rows/pallas_call | solution.py:819
  299.3 6.1 %weight_rows.7 = (f32[2,2,64,1024]{3,2,1,0:T(8,128)}, f32[2,2,64,1024]{3,2,1,0:T(8,128)}) custom-call(s32[8]{0:T(128)S(1)} %stack.124.place_ref, bf16[512,768]{1,0:T(8,128)(2,1)S(1)} %get-tuple-element.217.refs_0_, bf16[512,768]{1,0:T(8,128)(2,1)S(1)} %get-tuple-element.218.refs_1_, bf16[768,1024]{1,0:T(8,128)(2,1)} %get-tuple-element.154.refs_2_, ...), custom_call_target="tpu_custom_call" | custom-call | flops 37748736 | bytes 32768 | tf_op jit(solution)/shard_map/weight_rows/pallas_call | solution.py:819
  306.6 6.0 %own_terms.3.kept_ref = f32[320,1024]{1,0:T(8,128)S(1)} custom-call(s32[2]{0:T(128)S(1)} %pad_add_fusion.5.cols_ref, s32[8]{0:T(128)S(1)} %stack.124.place_ref, f32[320,1024]{1,0:T(8,128)} %get-tuple-element.221.refs_0_.grad_ref, f32[320,1024]{1,0:T(8,128)S(1)} %own_terms.2.refs_3_.refs_0_, f32[320,1024]{1,0:T(8,128)S(1)} %copy-done.4, ...), custom_call_target="tpu_custom_call" | custom-call | flops 31457280 | bytes 65536 | tf_op jit(solution)/shard_map/own_terms/pallas_call | solution.py:704
  312.7 2.6 collective-permute-done.45.come_ref
  319.1 5.6 %collective-permute-done.47.refs_3_ = f32[2,2,64,1024]{3,2,1,0:T(8,128)S(1)} collective-permute-done((f32[2,2,64,1024]{3,2,1,0:T(8,128)}, f32[2,2,64,1024]{3,2,1,0:T(8,128)S(1)}, u32[]{:S(2)}, u32[]{:S(2)}) %collective-permute-start.47) | collective-permute-done | bytes 1048608 | tf_op jit(solution)/shard_map/ppermute | solution.py:880
  327.4 7.5 %collective-permute-done.51 = f32[320,256]{1,0:T(8,128)S(1)} collective-permute-done((f32[320,256]{1,0:T(8,128)}, f32[320,256]{1,0:T(8,128)S(1)}, u32[]{:S(2)}, u32[]{:S(2)}) %collective-permute-start.51) | collective-permute-done | bytes 327712 | tf_op jit(solution)/shard_map/ppermute | solution.py:1106
  341.9 9.6 %collective-permute-done.58.refs_2_ = f32[64,2048]{1,0:T(8,128)S(1)} collective-permute-done((f32[64,2048]{1,0:T(8,128)S(1)}, f32[64,2048]{1,0:T(8,128)S(1)}, u32[]{:S(2)}, u32[]{:S(2)}) %collective-permute-start.58) | collective-permute-done | bytes 524320 | tf_op jit(solution)/shard_map/ppermute | solution.py:880
  352.6 3.6 collective-permute-done.48.refs_1_
  356.3 2.8 unpack.2
  359.1 7.0 %collective-permute-done.49.come_ref = f32[320,512]{1,0:T(8,128)S(1)} collective-permute-done((f32[320,512]{1,0:T(8,128)S(1)}, f32[320,512]{1,0:T(8,128)S(1)}, u32[]{:S(2)}, u32[]{:S(2)}) %collective-permute-start.49) | collective-permute-done | bytes 655392 | tf_op jit(solution)/shard_map/ppermute | solution.py:29
  369.4 10.2 %collective-permute-done.61.refs_2_ = f32[64,2048]{1,0:T(8,128)S(1)} collective-permute-done((f32[64,2048]{1,0:T(8,128)S(1)}, f32[64,2048]{1,0:T(8,128)S(1)}, u32[]{:S(2)}, u32[]{:S(2)}) %collective-permute-start.61) | collective-permute-done | bytes 524320 | tf_op jit(solution)/shard_map/ppermute | solution.py:880
  380.7 3.3 collective-permute-done.55
  384.0 3.0 assemble.2.refs_4_
  (214 shorter events, 77.7 us)
Async XLA Ops:
  0.6 36.5 %collective-permute-start.2 = (f32[2,256,2048]{2,1,0:T(8,128)}, f32[2,256,2048]{2,1,0:T(8,128)}, u32[]{:S(2)}, u32[]{:S(2)}) collective-permute-start(f32[2,256,2048]{2,1,0:T(8,128)} %refs_2_.1), channel_id=1, source_target_pairs={{0,1},{1,0},{2,3},{3,2},{4,5},{5,4},{6,7},{7,6},{8,9},{9,8},{10,11... | collective-permute-start | bytes 12582920 | tf_op jit(solution)/shard_map/ppermute | solution.py:961
  5.2 32.0 %collective-permute-start.3 = (f32[640,256]{1,0:T(8,128)S(1)}, f32[640,256]{1,0:T(8,128)S(1)}, u32[]{:S(2)}, u32[]{:S(2)}) collective-permute-start(f32[640,256]{1,0:T(8,128)S(1)} %get-tuple-element.137.refs_0_.refs_6_), channel_id=1, source_target_pairs={{0,2},{2,0},{1,3},{3,1},{4,6},{6,4},{5,7},{7,5},{8,10},{10,8},{9,1... | collective-permute-start | bytes 1966088 | tf_op jit(solution)/shard_map/ppermute | solution.py:29
  7.8 26.3 %collective-permute-start.1 = (f32[64,2048]{1,0:T(8,128)S(1)}, f32[64,2048]{1,0:T(8,128)}, u32[]{:S(2)}, u32[]{:S(2)}) collective-permute-start(f32[64,2048]{1,0:T(8,128)S(1)} %get-tuple-element.254), channel_id=1, source_target_pairs={{0,4},{4,0},{1,5},{5,1},{2,6},{6,2},{3,7},{7,3},{8,12},{12,8},{9,1... | collective-permute-start | bytes 1572872 | tf_op jit(solution)/shard_map/ppermute | solution.py:958
  10.4 51.7 %collective-permute-start = (f32[640,256]{1,0:T(8,128)S(1)}, f32[640,256]{1,0:T(8,128)S(1)}, u32[]{:S(2)}, u32[]{:S(2)}) collective-permute-start(f32[640,256]{1,0:T(8,128)S(1)} %get-tuple-element.131), channel_id=1, source_target_pairs={{0,4},{4,0},{1,5},{5,1},{2,6},{6,2},{3,7},{7,3},{8,12},{12,8},{9,1... | collective-permute-start | bytes 1966088 | tf_op jit(solution)/shard_map/ppermute | solution.py:958
  37.2 24.9 %collective-permute-start.6 = (f32[64,2048]{1,0:T(8,128)}, f32[64,2048]{1,0:T(8,128)}, u32[]{:S(2)}, u32[]{:S(2)}) collective-permute-start(f32[64,2048]{1,0:T(8,128)} %collective-permute-done.1.refs_12_.refs_8_.refs_7_.refs_4_), channel_id=1, source_target_pairs={{0,24},{8,16},{16,8},{24,0},{1,25},{9,17},{17,9},{25,1},{2,26},{10... | collective-permute-start | bytes 1572872 | tf_op jit(solution)/shard_map/ppermute | solution.py:975
  39.9 23.6 %collective-permute-start.5 = (f32[64,2048]{1,0:T(8,128)}, f32[64,2048]{1,0:T(8,128)}, u32[]{:S(2)}, u32[]{:S(2)}) collective-permute-start(f32[64,2048]{1,0:T(8,128)} %collective-permute-done.1.refs_12_.refs_8_.refs_7_.refs_4_), channel_id=1, source_target_pairs={{0,16},{16,0},{1,17},{17,1},{2,18},{18,2},{3,19},{19,3},{4,20},{20... | collective-permute-start | bytes 1572872 | tf_op jit(solution)/shard_map/ppermute | solution.py:976
  40.4 23.1 %collective-permute-start.4 = (f32[64,2048]{1,0:T(8,128)}, f32[64,2048]{1,0:T(8,128)S(1)}, u32[]{:S(2)}, u32[]{:S(2)}) collective-permute-start(f32[64,2048]{1,0:T(8,128)} %collective-permute-done.1.refs_12_.refs_8_.refs_7_.refs_4_), channel_id=1, source_target_pairs={{0,8},{8,0},{1,9},{9,1},{2,10},{10,2},{3,11},{11,3},{4,12},{12,4},... | collective-permute-start | bytes 1572872 | tf_op jit(solution)/shard_map/ppermute | solution.py:976
  40.8 23.7 %collective-permute-start.10 = (f32[640,256]{1,0:T(8,128)S(1)}, f32[640,256]{1,0:T(8,128)S(1)}, u32[]{:S(2)}, u32[]{:S(2)}) collective-permute-start(f32[640,256]{1,0:T(8,128)S(1)} %collective-permute-done.3.refs_4_.refs_2_), channel_id=1, source_target_pairs={{0,1},{1,0},{2,3},{3,2},{4,5},{5,4},{6,7},{7,6},{8,9},{9,8},{10,11... | collective-permute-start | bytes 1966088 | tf_op jit(solution)/shard_map/ppermute | solution.py:961
  64.5 16.7 %collective-permute-start.7 = (f32[640,256]{1,0:T(8,128)S(1)}, f32[640,256]{1,0:T(8,128)S(1)}, u32[]{:S(2)}, u32[]{:S(2)}) collective-permute-start(f32[640,256]{1,0:T(8,128)S(1)} %collective-permute-done.refs_2_.refs_8_), channel_id=1, source_target_pairs={{0,2},{2,0},{1,3},{3,1},{4,6},{6,4},{5,7},{7,5},{8,10},{10,8},{9,1... | collective-permute-start | bytes 1966088 | tf_op jit(solution)/shard_map/ppermute | solution.py:29
  89.4 34.9 %collective-permute-start.18 = (f32[320,1024]{1,0:T(8,128)S(1)}, f32[320,1024]{1,0:T(8,128)S(1)}, u32[]{:S(2)}, u32[]{:S(2)}) collective-permute-start(f32[320,1024]{1,0:T(8,128)S(1)} %copy-done.18), channel_id=1, source_target_pairs={{0,1},{1,0},{2,3},{3,2},{4,5},{5,4},{6,7},{7,6},{8,9},{9,8},{10,11... | collective-permute-start | bytes 3932168 | tf_op jit(solution)/shard_map/ppermute | solution.py:961
  89.6 35.9 %collective-permute-start.19 = (f32[320,1024]{1,0:T(8,128)}, f32[320,1024]{1,0:T(8,128)}, u32[]{:S(2)}, u32[]{:S(2)}) collective-permute-start(f32[320,1024]{1,0:T(8,128)} %get-tuple-element.153.own_ref), channel_id=1, source_target_pairs={{0,1},{1,0},{2,3},{3,2},{4,5},{5,4},{6,7},{7,6},{8,9},{9,8},{10,11... | collective-permute-start | bytes 3932168 | tf_op jit(solution)/shard_map/ppermute | solution.py:961
  96.1 26.1 %collective-permute-start.20 = (f32[64,2048]{1,0:T(8,128)S(1)}, f32[64,2048]{1,0:T(8,128)S(1)}, u32[]{:S(2)}, u32[]{:S(2)}) collective-permute-start(f32[64,2048]{1,0:T(8,128)S(1)} %copy-done.20), channel_id=1, source_target_pairs={{0,5},{1,4},{4,1},{5,0},{2,7},{3,6},{6,3},{7,2},{8,13},{9,12},{12,... | collective-permute-start | bytes 1572872 | tf_op jit(solution)/shard_map/ppermute | solution.py:1017
  113.8 15.3 %collective-permute-start.17 = (f32[320,1024]{1,0:T(8,128)S(1)}, f32[320,1024]{1,0:T(8,128)}, u32[]{:S(2)}, u32[]{:S(2)}) collective-permute-start(f32[320,1024]{1,0:T(8,128)S(1)} %get-tuple-element.160.refs_0_.own_ref.refs_5_), channel_id=1, source_target_pairs={{0,1},{1,0},{2,3},{3,2},{4,5},{5,4},{6,7},{7,6},{8,9},{9,8},{10,11... | collective-permute-start | bytes 3932168 | tf_op jit(solution)/shard_map/ppermute | solution.py:961
  113.8 36.5 %collective-permute-start.16 = (f32[320,1024]{1,0:T(8,128)S(1)}, f32[320,1024]{1,0:T(8,128)S(1)}, u32[]{:S(2)}, u32[]{:S(2)}) collective-permute-start(f32[320,1024]{1,0:T(8,128)S(1)} %get-tuple-element.160.refs_0_.own_ref.refs_5_), channel_id=1, source_target_pairs={{0,2},{2,0},{1,3},{3,1},{4,6},{6,4},{5,7},{7,5},{8,10},{10,8},{9,1... | collective-permute-start | bytes 3932168 | tf_op jit(solution)/shard_map/ppermute | solution.py:29
  125.4 25.4 %collective-permute-start.24 = (f32[64,2048]{1,0:T(8,128)}, f32[64,2048]{1,0:T(8,128)}, u32[]{:S(2)}, u32[]{:S(2)}) collective-permute-start(f32[64,2048]{1,0:T(8,128)} %collective-permute-done.21.refs_2_.refs_8_.refs_6_), channel_id=1, source_target_pairs={{0,24},{8,16},{16,8},{24,0},{1,25},{9,17},{17,9},{25,1},{2,26},{10... | collective-permute-start | bytes 1572872 | tf_op jit(solution)/shard_map/ppermute | solution.py:975
  127.2 24.7 %collective-permute-start.23 = (f32[64,2048]{1,0:T(8,128)}, f32[64,2048]{1,0:T(8,128)}, u32[]{:S(2)}, u32[]{:S(2)}) collective-permute-start(f32[64,2048]{1,0:T(8,128)} %collective-permute-done.21.refs_2_.refs_8_.refs_6_), channel_id=1, source_target_pairs={{0,16},{16,0},{1,17},{17,1},{2,18},{18,2},{3,19},{19,3},{4,20},{20... | collective-permute-start | bytes 1572872 | tf_op jit(solution)/shard_map/ppermute | solution.py:976
  128.4 23.6 %collective-permute-start.22 = (f32[64,2048]{1,0:T(8,128)}, f32[64,2048]{1,0:T(8,128)}, u32[]{:S(2)}, u32[]{:S(2)}) collective-permute-start(f32[64,2048]{1,0:T(8,128)} %collective-permute-done.21.refs_2_.refs_8_.refs_6_), channel_id=1, source_target_pairs={{0,8},{8,0},{1,9},{9,1},{2,10},{10,2},{3,11},{11,3},{4,12},{12,4},... | collective-permute-start | bytes 1572872 | tf_op jit(solution)/shard_map/ppermute | solution.py:976
  150.3 34.7 %collective-permute-start.30 = (f32[640,256]{1,0:T(8,128)}, f32[640,256]{1,0:T(8,128)}, u32[]{:S(2)}, u32[]{:S(2)}) collective-permute-start(f32[640,256]{1,0:T(8,128)} %get-tuple-element.172), channel_id=1, source_target_pairs={{0,4},{4,0},{1,5},{5,1},{2,6},{6,2},{3,7},{7,3},{8,12},{12,8},{9,1... | collective-permute-start | bytes 1966088 | tf_op jit(solution)/shard_map/ppermute | solution.py:958
  152.0 6.9 %collective-permute-start.25 = (f32[64,2048]{1,0:T(8,128)}, f32[64,2048]{1,0:T(8,128)}, u32[]{:S(2)}, u32[]{:S(2)}) collective-permute-start(f32[64,2048]{1,0:T(8,128)} %collective-permute-done.21.refs_2_.refs_8_.refs_6_), channel_id=1, source_target_pairs={{0,1},{1,0},{2,3},{3,2},{4,5},{5,4},{6,7},{7,6},{8,9},{9,8},{10,11... | collective-permute-start | bytes 1572872 | tf_op jit(solution)/shard_map/ppermute | solution.py:961
  152.0 6.9 %collective-permute-start.26 = (f32[64,2048]{1,0:T(8,128)}, f32[64,2048]{1,0:T(8,128)}, u32[]{:S(2)}, u32[]{:S(2)}) collective-permute-start(f32[64,2048]{1,0:T(8,128)} %collective-permute-done.22.refs_3_.refs_9_.refs_7_), channel_id=1, source_target_pairs={{0,1},{1,0},{2,3},{3,2},{4,5},{5,4},{6,7},{7,6},{8,9},{9,8},{10,11... | collective-permute-start | bytes 1572872 | tf_op jit(solution)/shard_map/ppermute | solution.py:961
  152.5 6.4 %collective-permute-start.27 = (f32[64,2048]{1,0:T(8,128)}, f32[64,2048]{1,0:T(8,128)}, u32[]{:S(2)}, u32[]{:S(2)}) collective-permute-start(f32[64,2048]{1,0:T(8,128)} %collective-permute-done.23.refs_4_.refs_10_.refs_8_), channel_id=1, source_target_pairs={{0,1},{1,0},{2,3},{3,2},{4,5},{5,4},{6,7},{7,6},{8,9},{9,8},{10,11... | collective-permute-start | bytes 1572872 | tf_op jit(solution)/shard_map/ppermute | solution.py:961
  152.5 6.4 %collective-permute-start.28 = (f32[64,2048]{1,0:T(8,128)}, f32[64,2048]{1,0:T(8,128)}, u32[]{:S(2)}, u32[]{:S(2)}) collective-permute-start(f32[64,2048]{1,0:T(8,128)} %collective-permute-done.24.refs_5_.refs_11_.refs_9_), channel_id=1, source_target_pairs={{0,1},{1,0},{2,3},{3,2},{4,5},{5,4},{6,7},{7,6},{8,9},{9,8},{10,11... | collective-permute-start | bytes 1572872 | tf_op jit(solution)/shard_map/ppermute | solution.py:961
  158.8 34.2 %collective-permute-start.29 = (f32[640,256]{1,0:T(8,128)S(1)}, f32[640,256]{1,0:T(8,128)}, u32[]{:S(2)}, u32[]{:S(2)}) collective-permute-start(f32[640,256]{1,0:T(8,128)S(1)} %copy-done.5), channel_id=1, source_target_pairs={{0,1},{1,0},{2,3},{3,2},{4,5},{5,4},{6,7},{7,6},{8,9},{9,8},{10,11... | collective-permute-start | bytes 1966088 | tf_op jit(solution)/shard_map/ppermute | solution.py:961
  185.0 8.1 %collective-permute-start.31 = (f32[640,256]{1,0:T(8,128)}, f32[640,256]{1,0:T(8,128)}, u32[]{:S(2)}, u32[]{:S(2)}) collective-permute-start(f32[640,256]{1,0:T(8,128)} %collective-permute-done.30.refs_6_.refs_2_), channel_id=1, source_target_pairs={{0,1},{1,0},{2,3},{3,2},{4,5},{5,4},{6,7},{7,6},{8,9},{9,8},{10,11... | collective-permute-start | bytes 1966088 | tf_op jit(solution)/shard_map/ppermute | solution.py:961
  192.7 31.0 %collective-permute-start.35 = (f32[320,1024]{1,0:T(8,128)S(1)}, f32[320,1024]{1,0:T(8,128)}, u32[]{:S(2)}, u32[]{:S(2)}) collective-permute-start(f32[320,1024]{1,0:T(8,128)S(1)} %collective-permute-done.16.refs_0_.refs_1_.own_ref), channel_id=1, source_target_pairs={{0,1},{1,0},{2,3},{3,2},{4,5},{5,4},{6,7},{7,6},{8,9},{9,8},{10,11... | collective-permute-start | bytes 3932168 | tf_op jit(solution)/shard_map/ppermute | solution.py:961
  193.0 28.8 %collective-permute-start.33 = (f32[320,256]{1,0:T(8,128)}, f32[320,256]{1,0:T(8,128)S(1)}, u32[]{:S(2)}, u32[]{:S(2)}) collective-permute-start(f32[320,256]{1,0:T(8,128)} %get-tuple-element.180), channel_id=1, source_target_pairs={{0,4},{4,0},{1,5},{5,1},{2,6},{6,2},{3,7},{7,3},{8,12},{12,8},{9,1... | collective-permute-start | bytes 983048 | tf_op jit(solution)/shard_map/ppermute | solution.py:958
  222.0 31.3 %collective-permute-start.36 = (f32[320,1024]{1,0:T(8,128)}, f32[320,1024]{1,0:T(8,128)S(1)}, u32[]{:S(2)}, u32[]{:S(2)}) collective-permute-start(f32[320,1024]{1,0:T(8,128)} %get-tuple-element.192), channel_id=1, source_target_pairs={{0,2},{2,0},{1,3},{3,1},{4,6},{6,4},{5,7},{7,5},{8,10},{10,8},{9,1... | collective-permute-start | bytes 3932168 | tf_op jit(solution)/shard_map/ppermute | solution.py:29
  235.4 32.4 %collective-permute-start.37 = (f32[2,2,64,1024]{3,2,1,0:T(8,128)}, f32[2,2,64,1024]{3,2,1,0:T(8,128)}, u32[]{:S(2)}, u32[]{:S(2)}) collective-permute-start(f32[2,2,64,1024]{3,2,1,0:T(8,128)} %get-tuple-element.197), channel_id=1, source_target_pairs={{0,8},{1,17},{8,0},{9,25},{16,24},{17,1},{24,16},{25,9},{2,10},{3,... | collective-permute-start | bytes 3145736 | tf_op jit(solution)/shard_map/ppermute | solution.py:880
  242.4 25.5 %collective-permute-start.40 = (f32[2,2,64,1024]{3,2,1,0:T(8,128)}, f32[2,2,64,1024]{3,2,1,0:T(8,128)}, u32[]{:S(2)}, u32[]{:S(2)}) collective-permute-start(f32[2,2,64,1024]{3,2,1,0:T(8,128)} %get-tuple-element.202), channel_id=1, source_target_pairs={{0,8},{1,17},{8,0},{9,25},{16,24},{17,1},{24,16},{25,9},{2,10},{3,... | collective-permute-start | bytes 3145736 | tf_op jit(solution)/shard_map/ppermute | solution.py:880
  243.7 23.0 %collective-permute-start.39 = (f32[320,256]{1,0:T(8,128)}, f32[320,256]{1,0:T(8,128)S(1)}, u32[]{:S(2)}, u32[]{:S(2)}) collective-permute-start(f32[320,256]{1,0:T(8,128)} %get-tuple-element.200), channel_id=1, source_target_pairs={{0,1},{1,0},{2,3},{3,2},{4,5},{5,4},{6,7},{7,6},{8,9},{9,8},{10,11... | collective-permute-start | bytes 983048 | tf_op jit(solution)/shard_map/ppermute | solution.py:961
  249.8 18.1 %collective-permute-start.38 = (f32[320,256]{1,0:T(8,128)S(1)}, f32[320,256]{1,0:T(8,128)S(1)}, u32[]{:S(2)}, u32[]{:S(2)}) collective-permute-start(f32[320,256]{1,0:T(8,128)S(1)} %copy-done.32), channel_id=1, source_target_pairs={{0,4},{4,0},{1,5},{5,1},{2,6},{6,2},{3,7},{7,3},{8,12},{12,8},{9,1... | collective-permute-start | bytes 983048 | tf_op jit(solution)/shard_map/ppermute | solution.py:958
  271.0 17.8 %collective-permute-start.42 = (f32[2,64,2048]{2,1,0:T(8,128)S(1)}, f32[2,64,2048]{2,1,0:T(8,128)S(1)}, u32[]{:S(2)}, u32[]{:S(2)}) collective-permute-start(f32[2,64,2048]{2,1,0:T(8,128)S(1)} %get-tuple-element.207), channel_id=1, source_target_pairs={{0,16},{1,9},{8,24},{9,1},{16,0},{17,25},{24,8},{25,17},{2,18},{3,... | collective-permute-start | bytes 3145736 | tf_op jit(solution)/shard_map/ppermute | solution.py:880
  287.3 28.0 %collective-permute-start.45 = (f32[320,512]{1,0:T(8,128)S(1)}, f32[320,512]{1,0:T(8,128)S(1)}, u32[]{:S(2)}, u32[]{:S(2)}) collective-permute-start(f32[320,512]{1,0:T(8,128)S(1)} %get-tuple-element.222), channel_id=1, source_target_pairs={{0,2},{2,0},{1,3},{3,1},{4,6},{6,4},{5,7},{7,5},{8,10},{10,8},{9,1... | collective-permute-start | bytes 1966088 | tf_op jit(solution)/shard_map/ppermute | solution.py:29
  289.7 26.5 %collective-permute-start.44 = (f32[64,2048]{1,0:T(8,128)S(1)}, f32[64,2048]{1,0:T(8,128)}, u32[]{:S(2)}, u32[]{:S(2)}) collective-permute-start(f32[64,2048]{1,0:T(8,128)S(1)} %get-tuple-element.216), channel_id=1, source_target_pairs={{0,5},{1,4},{4,1},{5,0},{2,7},{3,6},{6,3},{7,2},{8,13},{9,12},{12,... | collective-permute-start | bytes 1572872 | tf_op jit(solution)/shard_map/ppermute | solution.py:1082
  298.5 19.5 %collective-permute-start.43 = (f32[2,2,64,1024]{3,2,1,0:T(8,128)}, f32[2,2,64,1024]{3,2,1,0:T(8,128)S(1)}, u32[]{:S(2)}, u32[]{:S(2)}) collective-permute-start(f32[2,2,64,1024]{3,2,1,0:T(8,128)} %get-tuple-element.213), channel_id=1, source_target_pairs={{0,8},{1,17},{8,0},{9,25},{16,24},{17,1},{24,16},{25,9},{2,10},{3,... | collective-permute-start | bytes 3145736 | tf_op jit(solution)/shard_map/ppermute | solution.py:880
  305.4 19.3 %collective-permute-start.47 = (f32[2,2,64,1024]{3,2,1,0:T(8,128)}, f32[2,2,64,1024]{3,2,1,0:T(8,128)S(1)}, u32[]{:S(2)}, u32[]{:S(2)}) collective-permute-start(f32[2,2,64,1024]{3,2,1,0:T(8,128)} %get-tuple-element.226), channel_id=1, source_target_pairs={{0,8},{1,17},{8,0},{9,25},{16,24},{17,1},{24,16},{25,9},{2,10},{3,... | collective-permute-start | bytes 3145736 | tf_op jit(solution)/shard_map/ppermute | solution.py:880
  316.9 18.0 %collective-permute-start.51 = (f32[320,256]{1,0:T(8,128)}, f32[320,256]{1,0:T(8,128)S(1)}, u32[]{:S(2)}, u32[]{:S(2)}) collective-permute-start(f32[320,256]{1,0:T(8,128)} %copy-done.14), channel_id=1, source_target_pairs={{0,5},{1,4},{4,1},{5,0},{2,7},{3,6},{6,3},{7,2},{8,13},{9,12},{12,... | collective-permute-start | bytes 983048 | tf_op jit(solution)/shard_map/ppermute | solution.py:1106
  326.6 9.9 %collective-permute-start.53 = (f32[64,2048]{1,0:T(8,128)S(1)}, f32[64,2048]{1,0:T(8,128)S(1)}, u32[]{:S(2)}, u32[]{:S(2)}) collective-permute-start(f32[64,2048]{1,0:T(8,128)S(1)} %get-tuple-element.238), channel_id=1, source_target_pairs={{0,16},{1,9},{8,24},{9,1},{16,0},{17,25},{24,8},{25,17},{2,18},{3,... | collective-permute-start | bytes 1572872 | tf_op jit(solution)/shard_map/ppermute | solution.py:880
  336.6 14.9 %collective-permute-start.58 = (f32[64,2048]{1,0:T(8,128)S(1)}, f32[64,2048]{1,0:T(8,128)S(1)}, u32[]{:S(2)}, u32[]{:S(2)}) collective-permute-start(f32[64,2048]{1,0:T(8,128)S(1)} %reduction_step.12.refs_0_), channel_id=1, source_target_pairs={{0,8},{1,17},{8,0},{9,25},{16,24},{17,1},{24,16},{25,9},{2,10},{3,... | collective-permute-start | bytes 1572872 | tf_op jit(solution)/shard_map/ppermute | solution.py:880
  337.7 13.7 %collective-permute-start.57 = (f32[64,2048]{1,0:T(8,128)S(1)}, f32[64,2048]{1,0:T(8,128)S(1)}, u32[]{:S(2)}, u32[]{:S(2)}) collective-permute-start(f32[64,2048]{1,0:T(8,128)S(1)} %reduction_step.12.refs_0_), channel_id=1, source_target_pairs={{0,16},{1,9},{8,24},{9,1},{16,0},{17,25},{24,8},{25,17},{2,18},{3,... | collective-permute-start | bytes 1572872 | tf_op jit(solution)/shard_map/ppermute | solution.py:880
  338.7 27.4 %collective-permute-start.49 = (f32[320,512]{1,0:T(8,128)S(1)}, f32[320,512]{1,0:T(8,128)S(1)}, u32[]{:S(2)}, u32[]{:S(2)}) collective-permute-start(f32[320,512]{1,0:T(8,128)S(1)} %copy-done.11), channel_id=1, source_target_pairs={{0,2},{2,0},{1,3},{3,1},{4,6},{6,4},{5,7},{7,5},{8,10},{10,8},{9,1... | collective-permute-start | bytes 1966088 | tf_op jit(solution)/shard_map/ppermute | solution.py:29
  338.7 17.5 %collective-permute-start.48 = (f32[64,2048]{1,0:T(8,128)S(1)}, f32[64,2048]{1,0:T(8,128)S(1)}, u32[]{:S(2)}, u32[]{:S(2)}) collective-permute-start(f32[64,2048]{1,0:T(8,128)S(1)} %get-tuple-element.228), channel_id=1, source_target_pairs={{0,16},{1,9},{8,24},{9,1},{16,0},{17,25},{24,8},{25,17},{2,18},{3,... | collective-permute-start | bytes 1572872 | tf_op jit(solution)/shard_map/ppermute | solution.py:880
  339.8 26.4 %collective-permute-start.54 = (f32[64,2048]{1,0:T(8,128)S(1)}, f32[64,2048]{1,0:T(8,128)S(1)}, u32[]{:S(2)}, u32[]{:S(2)}) collective-permute-start(f32[64,2048]{1,0:T(8,128)S(1)} %reduction_step.11), channel_id=1, source_target_pairs={{0,4},{4,0},{1,5},{5,1},{2,6},{6,2},{3,7},{7,3},{8,12},{12,8},{9,1... | collective-permute-start | bytes 1572872 | tf_op jit(solution)/shard_map/ppermute | solution.py:958
  351.4 14.8 %collective-permute-start.59 = (f32[64,2048]{1,0:T(8,128)S(1)}, f32[64,2048]{1,0:T(8,128)S(1)}, u32[]{:S(2)}, u32[]{:S(2)}) collective-permute-start(f32[64,2048]{1,0:T(8,128)S(1)} %collective-permute-done.58.refs_2_), channel_id=1, source_target_pairs={{0,16},{1,9},{8,24},{9,1},{16,0},{17,25},{24,8},{25,17},{2,18},{3,... | collective-permute-start | bytes 1572872 | tf_op jit(solution)/shard_map/ppermute | solution.py:880
  366.3 13.4 %collective-permute-start.61 = (f32[64,2048]{1,0:T(8,128)S(1)}, f32[64,2048]{1,0:T(8,128)S(1)}, u32[]{:S(2)}, u32[]{:S(2)}) collective-permute-start(f32[64,2048]{1,0:T(8,128)S(1)} %reduction_step.13.refs_0_), channel_id=1, source_target_pairs={{0,8},{1,17},{8,0},{9,25},{16,24},{17,1},{24,16},{25,9},{2,10},{3,... | collective-permute-start | bytes 1572872 | tf_op jit(solution)/shard_map/ppermute | solution.py:880
  367.5 12.2 %collective-permute-start.60 = (f32[64,2048]{1,0:T(8,128)S(1)}, f32[64,2048]{1,0:T(8,128)S(1)}, u32[]{:S(2)}, u32[]{:S(2)}) collective-permute-start(f32[64,2048]{1,0:T(8,128)S(1)} %reduction_step.13.refs_0_), channel_id=1, source_target_pairs={{0,16},{1,9},{8,24},{9,1},{16,0},{17,25},{24,8},{25,17},{2,18},{3,... | collective-permute-start | bytes 1572872 | tf_op jit(solution)/shard_map/ppermute | solution.py:880
  368.4 15.6 %collective-permute-start.55 = (f32[320,256]{1,0:T(8,128)S(1)}, f32[320,256]{1,0:T(8,128)S(1)}, u32[]{:S(2)}, u32[]{:S(2)}) collective-permute-start(f32[320,256]{1,0:T(8,128)S(1)} %copy-done.13), channel_id=1, source_target_pairs={{0,4},{4,0},{1,5},{5,1},{2,6},{6,2},{3,7},{7,3},{8,12},{12,8},{9,1... | collective-permute-start | bytes 983048 | tf_op jit(solution)/shard_map/ppermute | solution.py:958
  379.7 9.4 %collective-permute-start.62 = (f32[64,2048]{1,0:T(8,128)S(1)}, f32[64,2048]{1,0:T(8,128)S(1)}, u32[]{:S(2)}, u32[]{:S(2)}) collective-permute-start(f32[64,2048]{1,0:T(8,128)S(1)} %collective-permute-done.61.refs_2_), channel_id=1, source_target_pairs={{0,16},{1,9},{8,24},{9,1},{16,0},{17,25},{24,8},{25,17},{2,18},{3,... | collective-permute-start | bytes 1572872 | tf_op jit(solution)/shard_map/ppermute | solution.py:880
  (49 other events, 405.6 us)

commit v2 on v0

--- a/solution.py
+++ b/solution.py
@@ -882,8 +882,8 @@
 
 def plane_gather(share, *before):
     first = plane_swap(share, 0)
-    second = plane_swap(share, 1)
-    return [share, second, first, plane_swap(after(first, second, *before), 1)]
+    second = plane_swap(after(share, first), 1)
+    return [share, second, first, plane_swap(after(first, *before), 1)]
 
 
 def assemble_body(place_ref, *refs):
@@ -1110,7 +1110,7 @@
     near_go, far_go = over_second(near_go), over_second(far_go)
     (go,) = step_of((far_sum, after(far_go, far_near)), cut=0)
     (later,) = step_of(later, cut=0)
-    later = after(later, go)
+    later = after(later, go, received[0])
     go = over_h(go)
     later = plane_gather(later)
     (total,) = step_of((near_sum, near_go), cut=0)
@@ -1118,10 +1118,10 @@
     close = merge(kept, 0, after(received[0], output))
     far = over_c(over_h(after(aways[1], go)))
     (share,) = step_of((total, after(go, close, *later[1:])), cut=0)
-    gathered = plane_gather(share, far)
+    grad_weights = assemble(place, after(later, share), 1)
+    gathered = plane_gather(share, grad_weights)
     grad_in = [(close, 0), (over_c(close[frames:]), 0), (far_near, 0), (far, 0)]
     grad_in = unpack(place, grad_in, frames)
-    grad_weights = assemble(place, after(later, share), 1)
     grad_weights = assemble(place, after(gathered, grad_in), 0, grad_weights)
     return (output, grad_in, grad_weights, *sums, sums[1])
 

time: 397 us -> 401 us (1.010)
    ppermute x7, waiting for transfers between devices: 61 us -> 50.9 us  [over_h(): return lax.ppermute(array, 'h', FLIP2)]
    ppermute x13, waiting for transfers between devices: 19.4 us -> 28.8 us  [plane_swap(): return lax.ppermute(array, ('y', 'x', 'c'), pairs)]
    ppermute x1, waiting for transfers between devices: 7.4 us -> 11.8 us  [half_features(): far_near = over_c(lax.ppermute(aways[0], ('h', 'c'), DIAGONAL))]
  transfers between devices with their start and end apart: 63 -> 63, of which waited for: 28 -> 30; matrix products, arithmetic and copies ran while one was open for 1% -> 1% of each run, Pallas kernels for 36% -> 35%
where the time goes in v2:
time: 401 us; the launch traced here: 399 us
  Pallas kernels  151 us (38%)
  waiting for transfers between devices  126 us (31%)
  blocking collectives  61.8 us (15%)
  starting transfers between devices  47.1 us (12%)
  local copies, waits for them, and re-layouts  10.3 us (3%)
    all_gather x8, blocking collectives, gather(): return lax.all_gather(array, axes, tiled=True)  61.8 us
    ppermute x7, waiting for transfers between devices, over_h(): return lax.ppermute(array, 'h', FLIP2)  50.9 us
    pallas_call x5, Pallas kernels, project(): call(partial(project_body, len(parts), len(flat), spots, len(weights), 0...  35.9 us
    ppermute x13, waiting for transfers between devices, plane_swap(): return lax.ppermute(array, ('y', 'x', 'c'), pairs)  28.8 us
    pallas_call x4, Pallas kernels, weight_rows(): call(partial(weight_body, turn), grid_spec=pltpu.PrefetchScalarGridSpec(n...  26.6 us
    pallas_call x4, Pallas kernels, prepare(): call(prepare_body, grid_spec=pltpu.PrefetchScalarGridSpec(num_scalar_pref...  15.1 us
    pallas_call x2, Pallas kernels, norm_back(): call(partial(norm_back_body, len(z), split_terms, layer), grid_spec=pltpu...  15 us
    pallas_call x2, Pallas kernels, recur(): call(partial(recur_body, len(z), last, layer, spread_params), grid=(CHUNK...  14.7 us
  transfers between devices with their start and end apart: 63, of which 30 were waited for; matrix products, arithmetic and copies ran while one was open for 1% of the time, Pallas kernels for 35%

profile of v2, /device:TPU:0, one launch (start us, length us, event | category | flops | bytes accessed | tf_op | source)
XLA Modules:
  0.0 399.4 jit_solution(9474685006345432348)
XLA Ops:
  5.2 2.7 collective-permute-start.3
  7.8 2.6 collective-permute-start.1
  10.8 2.9 pack.3
  15.6 18.6 %collective-permute-done.1.refs_12_.refs_8_.refs_7_.refs_4_ = f32[64,2048]{1,0:T(8,128)} collective-permute-done((f32[64,2048]{1,0:T(8,128)S(1)}, f32[64,2048]{1,0:T(8,128)}, u32[]{:S(2)}, u32[]{:S(2)}) %collective-permute-start.1) | collective-permute-done | bytes 524320 | tf_op jit(solution)/shard_map/ppermute | solution.py:958
  34.2 3.0 collective-permute-done.3.refs_4_.refs_2_
  37.2 2.7 collective-permute-start.6
  40.8 21.3 %collective-permute-done.refs_2_.refs_8_ = f32[640,256]{1,0:T(8,128)S(1)} collective-permute-done((f32[640,256]{1,0:T(8,128)S(1)}, f32[640,256]{1,0:T(8,128)S(1)}, u32[]{:S(2)}, u32[]{:S(2)}) %collective-permute-start) | collective-permute-done | bytes 655392 | tf_op jit(solution)/shard_map/ppermute | solution.py:958
  69.9 9.9 %project.5 = (f32[320,1024]{1,0:T(8,128)}, f32[320,1024]{1,0:T(8,128)}) custom-call(s32[6]{0:T(128)S(1)} %concatenate.11.cols_ref, s32[8]{0:T(128)S(1)} %stack.124.place_ref, f32[640,256]{1,0:T(8,128)S(1)} %get-tuple-element.138.refs_0_.refs_6_, f32[640,256]{1,0:T(8,128)} %collective-permute-done.8.refs_1_.refs_7_, ...), custom_call_target="tpu_custom_call" | custom-call | flops 47185920 | bytes 98304 | tf_op jit(solution)/shard_map/project/pallas_call | solution.py:288
  83.3 6.1 %project.6 = (f32[320,1024]{1,0:T(8,128)}, f32[5,8,128]{2,1,0:T(8,128)S(1)}, f32[320,1024]{1,0:T(8,128)}) custom-call(s32[2]{0:T(128)S(1)} %pad_add_fusion.1.cols_ref, s32[8]{0:T(128)S(1)} %stack.124.place_ref, f32[640,256]{1,0:T(8,128)S(1)} %collective-permute-done.7.refs_0_.refs_4_, f32[640,256]{1,0:T(8,128)S(1)} %collective-permute-done.15.refs_1_.refs_5_, ...), custom_call_target="tpu_custom_call" | custom-call | flops 15728640 | bytes 32768 | tf_op jit(solution)/shard_map/project/pallas_call | solution.py:288
  90.0 6.2 %all_gather.24 = f32[20,8,128]{2,1,0:T(8,128)S(1)} all-gather(f32[5,8,128]{2,1,0:T(8,128)S(1)} %get-tuple-element.146), channel_id=1, replica_groups=mesh['y'=2,'x'=2,'h'=2,'l'=2,'c'=2] {'h','c'}, dimensions={0}, use_global_device_ids=true | all-gather | bytes 102400 | tf_op jit(solution)/shard_map/all_gather | solution.py:997
  97.3 9.2 %all_gather.25.refs_1_.refs_3_ = f32[80,8,128]{2,1,0:T(8,128)S(1)} all-gather(f32[20,8,128]{2,1,0:T(8,128)S(1)} %all_gather.24), channel_id=1, replica_groups=mesh['y'=2,'x'=2,'h'=2,'l'=2,'c'=2] {'y','x'}, dimensions={0}, use_global_device_ids=true | all-gather | bytes 409600 | tf_op jit(solution)/shard_map/all_gather | solution.py:997
  106.6 7.3 %recur.2 = (f32[320,1024]{1,0:T(8,128)S(1)}, f32[320,1024]{1,0:T(8,128)}, f32[320,1024]{1,0:T(8,128)}, f32[6,8,128]{2,1,0:T(8,128)S(1)}) custom-call(s32[8]{0:T(128)S(1)} %stack.124.place_ref, f32[320]{0:T(512)S(1)} %fusion.6.gate_ref, f32[320,1024]{1,0:T(8,128)} %get-tuple-element.145.refs_0_, f32[80,8,128]{2,1,0:T(8,128)S(1)} %all_gather.25.refs_1_.refs_3_, ...), custom_call_target="tpu_custom_call" | custom-call | flops 512000 | bytes 102400 | tf_op jit(solution)/shard_map/recur/pallas_call | solution.py:434
  115.7 6.6 %collective-permute-done.20 = f32[64,2048]{1,0:T(8,128)S(1)} collective-permute-done((f32[64,2048]{1,0:T(8,128)S(1)}, f32[64,2048]{1,0:T(8,128)S(1)}, u32[]{:S(2)}, u32[]{:S(2)}) %collective-permute-start.20) | collective-permute-done | bytes 524320 | tf_op jit(solution)/shard_map/ppermute | solution.py:1017
  129.1 3.8 prepare.4
  132.9 3.8 prepare.5
  136.6 5.2 %project.7.refs_3_ = f32[320,512]{1,0:T(8,128)} custom-call(s32[4]{0:T(128)S(1)} %pad_add_fusion.2.cols_ref, s32[8]{0:T(128)S(1)} %stack.124.place_ref, f32[320,1024]{1,0:T(8,128)S(1)} %get-tuple-element.161.refs_0_.own_ref.refs_5_, f32[2,256,2048]{2,1,0:T(8,128)} %refs_2_.1, ...), custom_call_target="tpu_custom_call" | custom-call | flops 15728640 | bytes 32768 | tf_op jit(solution)/shard_map/project/pallas_call | solution.py:288
  141.8 3.8 prepare.6
  145.7 4.7 %collective-permute-done.16.refs_0_.refs_1_.own_ref = f32[320,1024]{1,0:T(8,128)S(1)} collective-permute-done((f32[320,1024]{1,0:T(8,128)S(1)}, f32[320,1024]{1,0:T(8,128)S(1)}, u32[]{:S(2)}, u32[]{:S(2)}) %collective-permute-start.16) | collective-permute-done | bytes 1310752 | tf_op jit(solution)/shard_map/ppermute | solution.py:29
  153.2 5.7 %project.8 = (f32[320,512]{1,0:T(8,128)}, f32[3,8,128]{2,1,0:T(8,128)S(1)}) custom-call(s32[4]{0:T(128)S(1)} %pad_add_fusion.cols_ref, s32[8]{0:T(128)S(1)} %stack.124.place_ref, f32[320,1024]{1,0:T(8,128)S(1)} %collective-permute-done.16.refs_0_.refs_1_.own_ref, f32[2,256,2048]{2,1,0:T(8,128)} %refs_2_.1, ...), custom_call_target="tpu_custom_call" | custom-call | flops 15728640 | bytes 32768 | tf_op jit(solution)/shard_map/project/pallas_call | solution.py:288
  158.9 9.1 %project.9 = (f32[320,512]{1,0:T(8,128)}, f32[3,8,128]{2,1,0:T(8,128)S(1)}) custom-call(s32[8]{0:T(128)S(1)} %concatenate.12.cols_ref, s32[8]{0:T(128)S(1)} %stack.124.place_ref, f32[320,1024]{1,0:T(8,128)S(1)} %copy-done.1, f32[320,1024]{1,0:T(8,128)S(1)} %collective-permute-done.16.refs_0_.refs_1_.own_ref, ...), custom_call_target="tpu_custom_call" | custom-call | flops 31457280 | bytes 65536 | tf_op jit(solution)/shard_map/project/pallas_call | solution.py:288
  168.1 8.1 %all_gather.26 = f32[12,8,128]{2,1,0:T(8,128)S(1)} all-gather(f32[3,8,128]{2,1,0:T(8,128)S(1)} %get-tuple-element.169), channel_id=1, replica_groups=mesh['y'=2,'x'=2,'h'=2,'l'=2,'c'=2] {'y','x'}, dimensions={0}, use_global_device_ids=true | all-gather | bytes 61440 | tf_op jit(solution)/shard_map/all_gather | solution.py:997
  176.2 8.8 %all_gather.27.refs_2_.refs_4_ = f32[48,8,128]{2,1,0:T(8,128)S(1)} all-gather(f32[12,8,128]{2,1,0:T(8,128)S(1)} %all_gather.26), channel_id=1, replica_groups=mesh['y'=2,'x'=2,'h'=2,'l'=2,'c'=2] {'h','c'}, dimensions={0}, use_global_device_ids=true | all-gather | bytes 245760 | tf_op jit(solution)/shard_map/all_gather | solution.py:997
  185.4 7.4 %recur.3 = (f32[320,256]{1,0:T(8,128)}, f32[320,256]{1,0:T(8,128)}, f32[320,256]{1,0:T(8,128)}, f32[320,256]{1,0:T(8,128)}, f32[320,1024]{1,0:T(8,128)}, /*index=5*/f32[320,1024]{1,0:T(8,128)}) custom-call(s32[8]{0:T(128)S(1)} %stack.124.place_ref, f32[320]{0:T(512)S(1)} %fusion.6.gate_ref, f32[320,512]{1,0:T(8,128)} %get-tuple-element.157.refs_0_, ...), custom_call_target="tpu_custom_call" | custom-call | flops 512000 | bytes 102400 | tf_op jit(solution)/shard_map/recur/pallas_call | solution.py:434
  193.1 5.6 %back.2 = (f32[320,1024]{1,0:T(8,128)S(1)}, f32[3,8,128]{2,1,0:T(8,128)S(1)}) custom-call(s32[8]{0:T(128)S(1)} %stack.124.place_ref, f32[320]{0:T(512)S(1)} %fusion.6.gate_ref, f32[320,512]{1,0:T(8,128)} %get-tuple-element.157.refs_0_, f32[320,512]{1,0:T(8,128)} %get-tuple-element.168.refs_1_, f32[48,8,128]{2,1,0:T(8,128)S(1)} %all_gather.27.refs_2_.refs_4_, ...), custom_call_target="tpu_custom_call" | custom-call | flops 153600 | bytes 102400 | tf_op jit(solution)/shard_map/back/pallas_call | solution.py:541
  198.7 8.2 %all_gather.28 = f32[12,8,128]{2,1,0:T(8,128)S(1)} all-gather(f32[3,8,128]{2,1,0:T(8,128)S(1)} %get-tuple-element.178), channel_id=1, replica_groups=mesh['y'=2,'x'=2,'h'=2,'l'=2,'c'=2] {'y','x'}, dimensions={0}, use_global_device_ids=true | all-gather | bytes 61440 | tf_op jit(solution)/shard_map/all_gather | solution.py:997
  206.9 6.8 %all_gather.29.refs_5_ = f32[48,8,128]{2,1,0:T(8,128)S(1)} all-gather(f32[12,8,128]{2,1,0:T(8,128)S(1)} %all_gather.28), channel_id=1, replica_groups=mesh['y'=2,'x'=2,'h'=2,'l'=2,'c'=2] {'h','c'}, dimensions={0}, use_global_device_ids=true | all-gather | bytes 245760 | tf_op jit(solution)/shard_map/all_gather | solution.py:997
  213.7 7.7 %norm_back.2 = (f32[320,1024]{1,0:T(8,128)}, f32[320,512]{1,0:T(8,128)S(1)}, f32[320,1024]{1,0:T(8,128)}, f32[3,8,128]{2,1,0:T(8,128)S(1)}) custom-call(s32[2]{0:T(128)S(1)} %pad_add_fusion.4.cols_ref, s32[8]{0:T(128)S(1)} %stack.124.place_ref, f32[320,1024]{1,0:T(8,128)S(1)} %get-tuple-element.177.grad_ref, f32[320,512]{1,0:T(8,128)} %get-tuple-element.157.refs_0_, ...), custom_call_target="tpu_custom_call" | custom-call | flops 31457280 | bytes 65536 | tf_op jit(solution)/shard_map/norm_back/pallas_call | solution.py:646
  223.8 3.8 prepare.7
  228.2 7.2 %weight_rows.4 = (f32[2,2,64,1024]{3,2,1,0:T(8,128)}, f32[2,2,64,1024]{3,2,1,0:T(8,128)}, bf16[512,768]{1,0:T(8,128)(2,1)S(1)}, bf16[512,768]{1,0:T(8,128)(2,1)S(1)}) custom-call(s32[8]{0:T(128)S(1)} %stack.124.place_ref, f32[320,1024]{1,0:T(8,128)} %get-tuple-element.192.refs_0_.grad_ref, f32[320,512]{1,0:T(8,128)S(1)} %collective-permute-done.32.refs_1_, ...), custom_call_target="tpu_custom_call" | custom-call | flops 37748736 | bytes 32768 | tf_op jit(solution)/shard_map/weight_rows/pallas_call | solution.py:819
  236.2 6.1 %weight_rows.5 = (f32[2,2,64,1024]{3,2,1,0:T(8,128)}, f32[2,2,64,1024]{3,2,1,0:T(8,128)}) custom-call(s32[8]{0:T(128)S(1)} %stack.124.place_ref, bf16[512,768]{1,0:T(8,128)(2,1)S(1)} %get-tuple-element.188.refs_0_, bf16[512,768]{1,0:T(8,128)(2,1)S(1)} %get-tuple-element.189.refs_1_, bf16[768,1024]{1,0:T(8,128)(2,1)} %get-tuple-element.185.refs_2_, ...), custom_call_target="tpu_custom_call" | custom-call | flops 37748736 | bytes 32768 | tf_op jit(solution)/shard_map/weight_rows/pallas_call | solution.py:819
  243.7 6.1 %own_terms.2.refs_3_.refs_0_ = f32[320,1024]{1,0:T(8,128)S(1)} custom-call(s32[2]{0:T(128)S(1)} %pad_add_fusion.5.cols_ref, s32[8]{0:T(128)S(1)} %stack.124.place_ref, f32[320,1024]{1,0:T(8,128)} %get-tuple-element.192.refs_0_.grad_ref, f32[640,256]{1,0:T(8,128)S(1)} %copy-done.6, f32[640,256]{1,0:T(8,128)} %collective-permute-done.29.refs_5_.refs_1_, ...), custom_call_target="tpu_custom_call" | custom-call | flops 31457280 | bytes 65536 | tf_op jit(solution)/shard_map/own_terms/pallas_call | solution.py:704
  253.2 5.9 %back.3 = (f32[320,1024]{1,0:T(8,128)S(1)}, f32[3,8,128]{2,1,0:T(8,128)S(1)}) custom-call(s32[8]{0:T(128)S(1)} %stack.124.place_ref, f32[320]{0:T(512)S(1)} %fusion.6.gate_ref, f32[320,1024]{1,0:T(8,128)} %get-tuple-element.145.refs_0_, f32[80,8,128]{2,1,0:T(8,128)S(1)} %all_gather.25.refs_1_.refs_3_, ...), custom_call_target="tpu_custom_call" | custom-call | flops 153600 | bytes 102400 | tf_op jit(solution)/shard_map/back/pallas_call | solution.py:541
  259.1 7.5 %all_gather.30 = f32[12,8,128]{2,1,0:T(8,128)S(1)} all-gather(f32[3,8,128]{2,1,0:T(8,128)S(1)} %get-tuple-element.196), channel_id=1, replica_groups=mesh['y'=2,'x'=2,'h'=2,'l'=2,'c'=2] {'y','x'}, dimensions={0}, use_global_device_ids=true | all-gather | bytes 61440 | tf_op jit(solution)/shard_map/all_gather | solution.py:997
  271.8 6.9 %all_gather.31.refs_4_ = f32[48,8,128]{2,1,0:T(8,128)S(1)} all-gather(f32[12,8,128]{2,1,0:T(8,128)S(1)} %all_gather.30), channel_id=1, replica_groups=mesh['y'=2,'x'=2,'h'=2,'l'=2,'c'=2] {'h','c'}, dimensions={0}, use_global_device_ids=true | all-gather | bytes 245760 | tf_op jit(solution)/shard_map/all_gather | solution.py:997
  278.7 7.3 %norm_back.3 = (f32[320,1024]{1,0:T(8,128)}, f32[320,512]{1,0:T(8,128)S(1)}, f32[320,512]{1,0:T(8,128)S(1)}, f32[320,512]{1,0:T(8,128)S(1)}, f32[3,8,128]{2,1,0:T(8,128)S(1)}) custom-call(s32[2]{0:T(128)S(1)} %pad_add_fusion.4.cols_ref, s32[8]{0:T(128)S(1)} %stack.124.place_ref, f32[320,1024]{1,0:T(8,128)S(1)} %get-tuple-element.195.grad_ref, ...), custom_call_target="tpu_custom_call" | custom-call | flops 31457280 | bytes 65536 | tf_op jit(solution)/shard_map/norm_back/pallas_call | solution.py:646
  291.3 7.2 %weight_rows.6 = (f32[2,2,64,1024]{3,2,1,0:T(8,128)}, f32[2,2,64,1024]{3,2,1,0:T(8,128)}, bf16[512,768]{1,0:T(8,128)(2,1)S(1)}, bf16[512,768]{1,0:T(8,128)(2,1)S(1)}) custom-call(s32[8]{0:T(128)S(1)} %stack.124.place_ref, f32[320,1024]{1,0:T(8,128)} %get-tuple-element.222.refs_0_.grad_ref, f32[320,512]{1,0:T(8,128)S(1)} %collective-permute-done.41.refs_1_, ...), custom_call_target="tpu_custom_call" | custom-call | flops 37748736 | bytes 32768 | tf_op jit(solution)/shard_map/weight_rows/pallas_call | solution.py:819
  299.3 6.1 %weight_rows.7 = (f32[2,2,64,1024]{3,2,1,0:T(8,128)}, f32[2,2,64,1024]{3,2,1,0:T(8,128)}) custom-call(s32[8]{0:T(128)S(1)} %stack.124.place_ref, bf16[512,768]{1,0:T(8,128)(2,1)S(1)} %get-tuple-element.218.refs_0_, bf16[512,768]{1,0:T(8,128)(2,1)S(1)} %get-tuple-element.219.refs_1_, bf16[768,1024]{1,0:T(8,128)(2,1)} %get-tuple-element.155.refs_2_, ...), custom_call_target="tpu_custom_call" | custom-call | flops 37748736 | bytes 32768 | tf_op jit(solution)/shard_map/weight_rows/pallas_call | solution.py:819
  306.7 6.0 %own_terms.3.kept_ref = f32[320,1024]{1,0:T(8,128)S(1)} custom-call(s32[2]{0:T(128)S(1)} %pad_add_fusion.5.cols_ref, s32[8]{0:T(128)S(1)} %stack.124.place_ref, f32[320,1024]{1,0:T(8,128)} %get-tuple-element.222.refs_0_.grad_ref, f32[320,1024]{1,0:T(8,128)S(1)} %own_terms.2.refs_3_.refs_0_, f32[320,1024]{1,0:T(8,128)S(1)} %copy-done.4, ...), custom_call_target="tpu_custom_call" | custom-call | flops 31457280 | bytes 65536 | tf_op jit(solution)/shard_map/own_terms/pallas_call | solution.py:704
  312.7 2.6 collective-permute-done.45.come_ref
  320.1 4.7 %collective-permute-done.47.refs_3_ = f32[2,2,64,1024]{3,2,1,0:T(8,128)S(1)} collective-permute-done((f32[2,2,64,1024]{3,2,1,0:T(8,128)}, f32[2,2,64,1024]{3,2,1,0:T(8,128)S(1)}, u32[]{:S(2)}, u32[]{:S(2)}) %collective-permute-start.47) | collective-permute-done | bytes 1048608 | tf_op jit(solution)/shard_map/ppermute | solution.py:880
  327.4 11.8 %collective-permute-done.51 = f32[320,256]{1,0:T(8,128)S(1)} collective-permute-done((f32[320,256]{1,0:T(8,128)}, f32[320,256]{1,0:T(8,128)S(1)}, u32[]{:S(2)}, u32[]{:S(2)}) %collective-permute-start.51) | collective-permute-done | bytes 327712 | tf_op jit(solution)/shard_map/ppermute | solution.py:1106
  345.8 10.3 %collective-permute-done.57.refs_2_ = f32[64,2048]{1,0:T(8,128)S(1)} collective-permute-done((f32[64,2048]{1,0:T(8,128)S(1)}, f32[64,2048]{1,0:T(8,128)S(1)}, u32[]{:S(2)}, u32[]{:S(2)}) %collective-permute-start.57) | collective-permute-done | bytes 524320 | tf_op jit(solution)/shard_map/ppermute | solution.py:880
  358.1 2.8 unpack.2
  361.1 7.8 %collective-permute-done.54.refs_1_ = f32[64,2048]{1,0:T(8,128)S(1)} collective-permute-done((f32[64,2048]{1,0:T(8,128)S(1)}, f32[64,2048]{1,0:T(8,128)S(1)}, u32[]{:S(2)}, u32[]{:S(2)}) %collective-permute-start.54) | collective-permute-done | bytes 524320 | tf_op jit(solution)/shard_map/ppermute | solution.py:958
  371.9 2.6 collective-permute-start.55
  374.6 3.0 assemble.2.refs_4_
  377.5 4.5 %collective-permute-done.60.refs_2_ = f32[64,2048]{1,0:T(8,128)S(1)} collective-permute-done((f32[64,2048]{1,0:T(8,128)S(1)}, f32[64,2048]{1,0:T(8,128)S(1)}, u32[]{:S(2)}, u32[]{:S(2)}) %collective-permute-start.60) | collective-permute-done | bytes 524320 | tf_op jit(solution)/shard_map/ppermute | solution.py:880
  391.2 5.6 %collective-permute-done.62.refs_3_ = f32[64,2048]{1,0:T(8,128)S(1)} collective-permute-done((f32[64,2048]{1,0:T(8,128)S(1)}, f32[64,2048]{1,0:T(8,128)S(1)}, u32[]{:S(2)}, u32[]{:S(2)}) %collective-permute-start.62) | collective-permute-done | bytes 524320 | tf_op jit(solution)/shard_map/ppermute | solution.py:880
  (212 shorter events, 84.9 us)
Async XLA Ops:
  0.6 36.5 %collective-permute-start.2 = (f32[2,256,2048]{2,1,0:T(8,128)}, f32[2,256,2048]{2,1,0:T(8,128)}, u32[]{:S(2)}, u32[]{:S(2)}) collective-permute-start(f32[2,256,2048]{2,1,0:T(8,128)} %refs_2_.1), channel_id=1, source_target_pairs={{0,1},{1,0},{2,3},{3,2},{4,5},{5,4},{6,7},{7,6},{8,9},{9,8},{10,11... | collective-permute-start | bytes 12582920 | tf_op jit(solution)/shard_map/ppermute | solution.py:961
  5.2 32.0 %collective-permute-start.3 = (f32[640,256]{1,0:T(8,128)S(1)}, f32[640,256]{1,0:T(8,128)S(1)}, u32[]{:S(2)}, u32[]{:S(2)}) collective-permute-start(f32[640,256]{1,0:T(8,128)S(1)} %get-tuple-element.138.refs_0_.refs_6_), channel_id=1, source_target_pairs={{0,2},{2,0},{1,3},{3,1},{4,6},{6,4},{5,7},{7,5},{8,10},{10,8},{9,1... | collective-permute-start | bytes 1966088 | tf_op jit(solution)/shard_map/ppermute | solution.py:29
  7.8 26.3 %collective-permute-start.1 = (f32[64,2048]{1,0:T(8,128)S(1)}, f32[64,2048]{1,0:T(8,128)}, u32[]{:S(2)}, u32[]{:S(2)}) collective-permute-start(f32[64,2048]{1,0:T(8,128)S(1)} %get-tuple-element.256), channel_id=1, source_target_pairs={{0,4},{4,0},{1,5},{5,1},{2,6},{6,2},{3,7},{7,3},{8,12},{12,8},{9,1... | collective-permute-start | bytes 1572872 | tf_op jit(solution)/shard_map/ppermute | solution.py:958
  10.4 51.7 %collective-permute-start = (f32[640,256]{1,0:T(8,128)S(1)}, f32[640,256]{1,0:T(8,128)S(1)}, u32[]{:S(2)}, u32[]{:S(2)}) collective-permute-start(f32[640,256]{1,0:T(8,128)S(1)} %get-tuple-element.132), channel_id=1, source_target_pairs={{0,4},{4,0},{1,5},{5,1},{2,6},{6,2},{3,7},{7,3},{8,12},{12,8},{9,1... | collective-permute-start | bytes 1966088 | tf_op jit(solution)/shard_map/ppermute | solution.py:958
  37.2 24.9 %collective-permute-start.6 = (f32[64,2048]{1,0:T(8,128)}, f32[64,2048]{1,0:T(8,128)}, u32[]{:S(2)}, u32[]{:S(2)}) collective-permute-start(f32[64,2048]{1,0:T(8,128)} %collective-permute-done.1.refs_12_.refs_8_.refs_7_.refs_4_), channel_id=1, source_target_pairs={{0,24},{8,16},{16,8},{24,0},{1,25},{9,17},{17,9},{25,1},{2,26},{10... | collective-permute-start | bytes 1572872 | tf_op jit(solution)/shard_map/ppermute | solution.py:975
  39.9 23.6 %collective-permute-start.5 = (f32[64,2048]{1,0:T(8,128)}, f32[64,2048]{1,0:T(8,128)}, u32[]{:S(2)}, u32[]{:S(2)}) collective-permute-start(f32[64,2048]{1,0:T(8,128)} %collective-permute-done.1.refs_12_.refs_8_.refs_7_.refs_4_), channel_id=1, source_target_pairs={{0,16},{16,0},{1,17},{17,1},{2,18},{18,2},{3,19},{19,3},{4,20},{20... | collective-permute-start | bytes 1572872 | tf_op jit(solution)/shard_map/ppermute | solution.py:976
  40.4 23.1 %collective-permute-start.4 = (f32[64,2048]{1,0:T(8,128)}, f32[64,2048]{1,0:T(8,128)S(1)}, u32[]{:S(2)}, u32[]{:S(2)}) collective-permute-start(f32[64,2048]{1,0:T(8,128)} %collective-permute-done.1.refs_12_.refs_8_.refs_7_.refs_4_), channel_id=1, source_target_pairs={{0,8},{8,0},{1,9},{9,1},{2,10},{10,2},{3,11},{11,3},{4,12},{12,4},... | collective-permute-start | bytes 1572872 | tf_op jit(solution)/shard_map/ppermute | solution.py:976
  40.8 23.7 %collective-permute-start.10 = (f32[640,256]{1,0:T(8,128)S(1)}, f32[640,256]{1,0:T(8,128)S(1)}, u32[]{:S(2)}, u32[]{:S(2)}) collective-permute-start(f32[640,256]{1,0:T(8,128)S(1)} %collective-permute-done.3.refs_4_.refs_2_), channel_id=1, source_target_pairs={{0,1},{1,0},{2,3},{3,2},{4,5},{5,4},{6,7},{7,6},{8,9},{9,8},{10,11... | collective-permute-start | bytes 1966088 | tf_op jit(solution)/shard_map/ppermute | solution.py:961
  64.5 16.7 %collective-permute-start.7 = (f32[640,256]{1,0:T(8,128)S(1)}, f32[640,256]{1,0:T(8,128)S(1)}, u32[]{:S(2)}, u32[]{:S(2)}) collective-permute-start(f32[640,256]{1,0:T(8,128)S(1)} %collective-permute-done.refs_2_.refs_8_), channel_id=1, source_target_pairs={{0,2},{2,0},{1,3},{3,1},{4,6},{6,4},{5,7},{7,5},{8,10},{10,8},{9,1... | collective-permute-start | bytes 1966088 | tf_op jit(solution)/shard_map/ppermute | solution.py:29
  89.4 34.9 %collective-permute-start.18 = (f32[320,1024]{1,0:T(8,128)S(1)}, f32[320,1024]{1,0:T(8,128)S(1)}, u32[]{:S(2)}, u32[]{:S(2)}) collective-permute-start(f32[320,1024]{1,0:T(8,128)S(1)} %copy-done.17), channel_id=1, source_target_pairs={{0,1},{1,0},{2,3},{3,2},{4,5},{5,4},{6,7},{7,6},{8,9},{9,8},{10,11... | collective-permute-start | bytes 3932168 | tf_op jit(solution)/shard_map/ppermute | solution.py:961
  89.6 35.9 %collective-permute-start.19 = (f32[320,1024]{1,0:T(8,128)}, f32[320,1024]{1,0:T(8,128)}, u32[]{:S(2)}, u32[]{:S(2)}) collective-permute-start(f32[320,1024]{1,0:T(8,128)} %get-tuple-element.154.own_ref), channel_id=1, source_target_pairs={{0,1},{1,0},{2,3},{3,2},{4,5},{5,4},{6,7},{7,6},{8,9},{9,8},{10,11... | collective-permute-start | bytes 3932168 | tf_op jit(solution)/shard_map/ppermute | solution.py:961
  96.1 26.1 %collective-permute-start.20 = (f32[64,2048]{1,0:T(8,128)S(1)}, f32[64,2048]{1,0:T(8,128)S(1)}, u32[]{:S(2)}, u32[]{:S(2)}) collective-permute-start(f32[64,2048]{1,0:T(8,128)S(1)} %copy-done.19), channel_id=1, source_target_pairs={{0,5},{1,4},{4,1},{5,0},{2,7},{3,6},{6,3},{7,2},{8,13},{9,12},{12,... | collective-permute-start | bytes 1572872 | tf_op jit(solution)/shard_map/ppermute | solution.py:1017
  113.8 15.3 %collective-permute-start.17 = (f32[320,1024]{1,0:T(8,128)S(1)}, f32[320,1024]{1,0:T(8,128)}, u32[]{:S(2)}, u32[]{:S(2)}) collective-permute-start(f32[320,1024]{1,0:T(8,128)S(1)} %get-tuple-element.161.refs_0_.own_ref.refs_5_), channel_id=1, source_target_pairs={{0,1},{1,0},{2,3},{3,2},{4,5},{5,4},{6,7},{7,6},{8,9},{9,8},{10,11... | collective-permute-start | bytes 3932168 | tf_op jit(solution)/shard_map/ppermute | solution.py:961
  113.9 36.5 %collective-permute-start.16 = (f32[320,1024]{1,0:T(8,128)S(1)}, f32[320,1024]{1,0:T(8,128)S(1)}, u32[]{:S(2)}, u32[]{:S(2)}) collective-permute-start(f32[320,1024]{1,0:T(8,128)S(1)} %get-tuple-element.161.refs_0_.own_ref.refs_5_), channel_id=1, source_target_pairs={{0,2},{2,0},{1,3},{3,1},{4,6},{6,4},{5,7},{7,5},{8,10},{10,8},{9,1... | collective-permute-start | bytes 3932168 | tf_op jit(solution)/shard_map/ppermute | solution.py:29
  125.5 25.4 %collective-permute-start.24 = (f32[64,2048]{1,0:T(8,128)}, f32[64,2048]{1,0:T(8,128)}, u32[]{:S(2)}, u32[]{:S(2)}) collective-permute-start(f32[64,2048]{1,0:T(8,128)} %collective-permute-done.21.refs_2_.refs_8_.refs_6_), channel_id=1, source_target_pairs={{0,24},{8,16},{16,8},{24,0},{1,25},{9,17},{17,9},{25,1},{2,26},{10... | collective-permute-start | bytes 1572872 | tf_op jit(solution)/shard_map/ppermute | solution.py:975
  127.2 24.7 %collective-permute-start.23 = (f32[64,2048]{1,0:T(8,128)}, f32[64,2048]{1,0:T(8,128)}, u32[]{:S(2)}, u32[]{:S(2)}) collective-permute-start(f32[64,2048]{1,0:T(8,128)} %collective-permute-done.21.refs_2_.refs_8_.refs_6_), channel_id=1, source_target_pairs={{0,16},{16,0},{1,17},{17,1},{2,18},{18,2},{3,19},{19,3},{4,20},{20... | collective-permute-start | bytes 1572872 | tf_op jit(solution)/shard_map/ppermute | solution.py:976
  128.4 23.6 %collective-permute-start.22 = (f32[64,2048]{1,0:T(8,128)}, f32[64,2048]{1,0:T(8,128)}, u32[]{:S(2)}, u32[]{:S(2)}) collective-permute-start(f32[64,2048]{1,0:T(8,128)} %collective-permute-done.21.refs_2_.refs_8_.refs_6_), channel_id=1, source_target_pairs={{0,8},{8,0},{1,9},{9,1},{2,10},{10,2},{3,11},{11,3},{4,12},{12,4},... | collective-permute-start | bytes 1572872 | tf_op jit(solution)/shard_map/ppermute | solution.py:976
  150.3 34.7 %collective-permute-start.30 = (f32[640,256]{1,0:T(8,128)}, f32[640,256]{1,0:T(8,128)}, u32[]{:S(2)}, u32[]{:S(2)}) collective-permute-start(f32[640,256]{1,0:T(8,128)} %get-tuple-element.173), channel_id=1, source_target_pairs={{0,4},{4,0},{1,5},{5,1},{2,6},{6,2},{3,7},{7,3},{8,12},{12,8},{9,1... | collective-permute-start | bytes 1966088 | tf_op jit(solution)/shard_map/ppermute | solution.py:958
  152.0 6.8 %collective-permute-start.25 = (f32[64,2048]{1,0:T(8,128)}, f32[64,2048]{1,0:T(8,128)}, u32[]{:S(2)}, u32[]{:S(2)}) collective-permute-start(f32[64,2048]{1,0:T(8,128)} %collective-permute-done.21.refs_2_.refs_8_.refs_6_), channel_id=1, source_target_pairs={{0,1},{1,0},{2,3},{3,2},{4,5},{5,4},{6,7},{7,6},{8,9},{9,8},{10,11... | collective-permute-start | bytes 1572872 | tf_op jit(solution)/shard_map/ppermute | solution.py:961
  152.0 6.9 %collective-permute-start.26 = (f32[64,2048]{1,0:T(8,128)}, f32[64,2048]{1,0:T(8,128)}, u32[]{:S(2)}, u32[]{:S(2)}) collective-permute-start(f32[64,2048]{1,0:T(8,128)} %collective-permute-done.22.refs_3_.refs_9_.refs_7_), channel_id=1, source_target_pairs={{0,1},{1,0},{2,3},{3,2},{4,5},{5,4},{6,7},{7,6},{8,9},{9,8},{10,11... | collective-permute-start | bytes 1572872 | tf_op jit(solution)/shard_map/ppermute | solution.py:961
  152.5 6.4 %collective-permute-start.27 = (f32[64,2048]{1,0:T(8,128)}, f32[64,2048]{1,0:T(8,128)}, u32[]{:S(2)}, u32[]{:S(2)}) collective-permute-start(f32[64,2048]{1,0:T(8,128)} %collective-permute-done.23.refs_4_.refs_10_.refs_8_), channel_id=1, source_target_pairs={{0,1},{1,0},{2,3},{3,2},{4,5},{5,4},{6,7},{7,6},{8,9},{9,8},{10,11... | collective-permute-start | bytes 1572872 | tf_op jit(solution)/shard_map/ppermute | solution.py:961
  152.5 6.4 %collective-permute-start.28 = (f32[64,2048]{1,0:T(8,128)}, f32[64,2048]{1,0:T(8,128)}, u32[]{:S(2)}, u32[]{:S(2)}) collective-permute-start(f32[64,2048]{1,0:T(8,128)} %collective-permute-done.24.refs_5_.refs_11_.refs_9_), channel_id=1, source_target_pairs={{0,1},{1,0},{2,3},{3,2},{4,5},{5,4},{6,7},{7,6},{8,9},{9,8},{10,11... | collective-permute-start | bytes 1572872 | tf_op jit(solution)/shard_map/ppermute | solution.py:961
  158.8 34.2 %collective-permute-start.29 = (f32[640,256]{1,0:T(8,128)S(1)}, f32[640,256]{1,0:T(8,128)}, u32[]{:S(2)}, u32[]{:S(2)}) collective-permute-start(f32[640,256]{1,0:T(8,128)S(1)} %copy-done.5), channel_id=1, source_target_pairs={{0,1},{1,0},{2,3},{3,2},{4,5},{5,4},{6,7},{7,6},{8,9},{9,8},{10,11... | collective-permute-start | bytes 1966088 | tf_op jit(solution)/shard_map/ppermute | solution.py:961
  185.0 8.1 %collective-permute-start.31 = (f32[640,256]{1,0:T(8,128)}, f32[640,256]{1,0:T(8,128)}, u32[]{:S(2)}, u32[]{:S(2)}) collective-permute-start(f32[640,256]{1,0:T(8,128)} %collective-permute-done.30.refs_6_.refs_2_), channel_id=1, source_target_pairs={{0,1},{1,0},{2,3},{3,2},{4,5},{5,4},{6,7},{7,6},{8,9},{9,8},{10,11... | collective-permute-start | bytes 1966088 | tf_op jit(solution)/shard_map/ppermute | solution.py:961
  192.8 31.0 %collective-permute-start.35 = (f32[320,1024]{1,0:T(8,128)S(1)}, f32[320,1024]{1,0:T(8,128)}, u32[]{:S(2)}, u32[]{:S(2)}) collective-permute-start(f32[320,1024]{1,0:T(8,128)S(1)} %collective-permute-done.16.refs_0_.refs_1_.own_ref), channel_id=1, source_target_pairs={{0,1},{1,0},{2,3},{3,2},{4,5},{5,4},{6,7},{7,6},{8,9},{9,8},{10,11... | collective-permute-start | bytes 3932168 | tf_op jit(solution)/shard_map/ppermute | solution.py:961
  193.1 28.8 %collective-permute-start.33 = (f32[320,256]{1,0:T(8,128)}, f32[320,256]{1,0:T(8,128)S(1)}, u32[]{:S(2)}, u32[]{:S(2)}) collective-permute-start(f32[320,256]{1,0:T(8,128)} %get-tuple-element.181), channel_id=1, source_target_pairs={{0,4},{4,0},{1,5},{5,1},{2,6},{6,2},{3,7},{7,3},{8,12},{12,8},{9,1... | collective-permute-start | bytes 983048 | tf_op jit(solution)/shard_map/ppermute | solution.py:958
  222.0 31.3 %collective-permute-start.36 = (f32[320,1024]{1,0:T(8,128)}, f32[320,1024]{1,0:T(8,128)S(1)}, u32[]{:S(2)}, u32[]{:S(2)}) collective-permute-start(f32[320,1024]{1,0:T(8,128)} %get-tuple-element.193), channel_id=1, source_target_pairs={{0,2},{2,0},{1,3},{3,1},{4,6},{6,4},{5,7},{7,5},{8,10},{10,8},{9,1... | collective-permute-start | bytes 3932168 | tf_op jit(solution)/shard_map/ppermute | solution.py:29
  235.4 32.4 %collective-permute-start.37 = (f32[2,2,64,1024]{3,2,1,0:T(8,128)}, f32[2,2,64,1024]{3,2,1,0:T(8,128)}, u32[]{:S(2)}, u32[]{:S(2)}) collective-permute-start(f32[2,2,64,1024]{3,2,1,0:T(8,128)} %get-tuple-element.198), channel_id=1, source_target_pairs={{0,8},{1,17},{8,0},{9,25},{16,24},{17,1},{24,16},{25,9},{2,10},{3,... | collective-permute-start | bytes 3145736 | tf_op jit(solution)/shard_map/ppermute | solution.py:880
  242.3 25.5 %collective-permute-start.40 = (f32[2,2,64,1024]{3,2,1,0:T(8,128)}, f32[2,2,64,1024]{3,2,1,0:T(8,128)}, u32[]{:S(2)}, u32[]{:S(2)}) collective-permute-start(f32[2,2,64,1024]{3,2,1,0:T(8,128)} %get-tuple-element.203), channel_id=1, source_target_pairs={{0,8},{1,17},{8,0},{9,25},{16,24},{17,1},{24,16},{25,9},{2,10},{3,... | collective-permute-start | bytes 3145736 | tf_op jit(solution)/shard_map/ppermute | solution.py:880
  243.6 23.0 %collective-permute-start.39 = (f32[320,256]{1,0:T(8,128)}, f32[320,256]{1,0:T(8,128)S(1)}, u32[]{:S(2)}, u32[]{:S(2)}) collective-permute-start(f32[320,256]{1,0:T(8,128)} %get-tuple-element.201), channel_id=1, source_target_pairs={{0,1},{1,0},{2,3},{3,2},{4,5},{5,4},{6,7},{7,6},{8,9},{9,8},{10,11... | collective-permute-start | bytes 983048 | tf_op jit(solution)/shard_map/ppermute | solution.py:961
  249.8 18.1 %collective-permute-start.38 = (f32[320,256]{1,0:T(8,128)S(1)}, f32[320,256]{1,0:T(8,128)S(1)}, u32[]{:S(2)}, u32[]{:S(2)}) collective-permute-start(f32[320,256]{1,0:T(8,128)S(1)} %copy-done.31), channel_id=1, source_target_pairs={{0,4},{4,0},{1,5},{5,1},{2,6},{6,2},{3,7},{7,3},{8,12},{12,8},{9,1... | collective-permute-start | bytes 983048 | tf_op jit(solution)/shard_map/ppermute | solution.py:958
  271.0 17.8 %collective-permute-start.42 = (f32[2,64,2048]{2,1,0:T(8,128)S(1)}, f32[2,64,2048]{2,1,0:T(8,128)S(1)}, u32[]{:S(2)}, u32[]{:S(2)}) collective-permute-start(f32[2,64,2048]{2,1,0:T(8,128)S(1)} %get-tuple-element.208), channel_id=1, source_target_pairs={{0,16},{1,9},{8,24},{9,1},{16,0},{17,25},{24,8},{25,17},{2,18},{3,... | collective-permute-start | bytes 3145736 | tf_op jit(solution)/shard_map/ppermute | solution.py:880
  287.3 28.0 %collective-permute-start.45 = (f32[320,512]{1,0:T(8,128)S(1)}, f32[320,512]{1,0:T(8,128)S(1)}, u32[]{:S(2)}, u32[]{:S(2)}) collective-permute-start(f32[320,512]{1,0:T(8,128)S(1)} %get-tuple-element.223), channel_id=1, source_target_pairs={{0,2},{2,0},{1,3},{3,1},{4,6},{6,4},{5,7},{7,5},{8,10},{10,8},{9,1... | collective-permute-start | bytes 1966088 | tf_op jit(solution)/shard_map/ppermute | solution.py:29
  289.7 26.5 %collective-permute-start.44 = (f32[64,2048]{1,0:T(8,128)S(1)}, f32[64,2048]{1,0:T(8,128)}, u32[]{:S(2)}, u32[]{:S(2)}) collective-permute-start(f32[64,2048]{1,0:T(8,128)S(1)} %get-tuple-element.217), channel_id=1, source_target_pairs={{0,5},{1,4},{4,1},{5,0},{2,7},{3,6},{6,3},{7,2},{8,13},{9,12},{12,... | collective-permute-start | bytes 1572872 | tf_op jit(solution)/shard_map/ppermute | solution.py:1082
  298.5 21.5 %collective-permute-start.43 = (f32[2,2,64,1024]{3,2,1,0:T(8,128)}, f32[2,2,64,1024]{3,2,1,0:T(8,128)S(1)}, u32[]{:S(2)}, u32[]{:S(2)}) collective-permute-start(f32[2,2,64,1024]{3,2,1,0:T(8,128)} %get-tuple-element.214), channel_id=1, source_target_pairs={{0,8},{1,17},{8,0},{9,25},{16,24},{17,1},{24,16},{25,9},{2,10},{3,... | collective-permute-start | bytes 3145736 | tf_op jit(solution)/shard_map/ppermute | solution.py:880
  305.4 19.3 %collective-permute-start.47 = (f32[2,2,64,1024]{3,2,1,0:T(8,128)}, f32[2,2,64,1024]{3,2,1,0:T(8,128)S(1)}, u32[]{:S(2)}, u32[]{:S(2)}) collective-permute-start(f32[2,2,64,1024]{3,2,1,0:T(8,128)} %get-tuple-element.227), channel_id=1, source_target_pairs={{0,8},{1,17},{8,0},{9,25},{16,24},{17,1},{24,16},{25,9},{2,10},{3,... | collective-permute-start | bytes 3145736 | tf_op jit(solution)/shard_map/ppermute | solution.py:880
  316.9 24.4 %collective-permute-start.49 = (f32[320,512]{1,0:T(8,128)}, f32[320,512]{1,0:T(8,128)S(1)}, u32[]{:S(2)}, u32[]{:S(2)}) collective-permute-start(f32[320,512]{1,0:T(8,128)} %copy-done.10), channel_id=1, source_target_pairs={{0,2},{2,0},{1,3},{3,1},{4,6},{6,4},{5,7},{7,5},{8,10},{10,8},{9,1... | collective-permute-start | bytes 1966088 | tf_op jit(solution)/shard_map/ppermute | solution.py:29
  317.7 21.6 %collective-permute-start.51 = (f32[320,256]{1,0:T(8,128)}, f32[320,256]{1,0:T(8,128)S(1)}, u32[]{:S(2)}, u32[]{:S(2)}) collective-permute-start(f32[320,256]{1,0:T(8,128)} %copy-done.13), channel_id=1, source_target_pairs={{0,5},{1,4},{4,1},{5,0},{2,7},{3,6},{6,3},{7,2},{8,13},{9,12},{12,... | collective-permute-start | bytes 983048 | tf_op jit(solution)/shard_map/ppermute | solution.py:1106
  326.6 14.3 %collective-permute-start.53 = (f32[64,2048]{1,0:T(8,128)S(1)}, f32[64,2048]{1,0:T(8,128)S(1)}, u32[]{:S(2)}, u32[]{:S(2)}) collective-permute-start(f32[64,2048]{1,0:T(8,128)S(1)} %get-tuple-element.239), channel_id=1, source_target_pairs={{0,16},{1,9},{8,24},{9,1},{16,0},{17,25},{24,8},{25,17},{2,18},{3,... | collective-permute-start | bytes 1572872 | tf_op jit(solution)/shard_map/ppermute | solution.py:880
  341.3 14.7 %collective-permute-start.57 = (f32[64,2048]{1,0:T(8,128)S(1)}, f32[64,2048]{1,0:T(8,128)S(1)}, u32[]{:S(2)}, u32[]{:S(2)}) collective-permute-start(f32[64,2048]{1,0:T(8,128)S(1)} %reduction_step.12.refs_0_), channel_id=1, source_target_pairs={{0,8},{1,17},{8,0},{9,25},{16,24},{17,1},{24,16},{25,9},{2,10},{3,... | collective-permute-start | bytes 1572872 | tf_op jit(solution)/shard_map/ppermute | solution.py:880
  342.4 15.7 %collective-permute-start.48 = (f32[64,2048]{1,0:T(8,128)S(1)}, f32[64,2048]{1,0:T(8,128)S(1)}, u32[]{:S(2)}, u32[]{:S(2)}) collective-permute-start(f32[64,2048]{1,0:T(8,128)S(1)} %get-tuple-element.229), channel_id=1, source_target_pairs={{0,16},{1,9},{8,24},{9,1},{16,0},{17,25},{24,8},{25,17},{2,18},{3,... | collective-permute-start | bytes 1572872 | tf_op jit(solution)/shard_map/ppermute | solution.py:880
  343.4 25.5 %collective-permute-start.54 = (f32[64,2048]{1,0:T(8,128)S(1)}, f32[64,2048]{1,0:T(8,128)S(1)}, u32[]{:S(2)}, u32[]{:S(2)}) collective-permute-start(f32[64,2048]{1,0:T(8,128)S(1)} %reduction_step.11), channel_id=1, source_target_pairs={{0,4},{4,0},{1,5},{5,1},{2,6},{6,2},{3,7},{7,3},{8,12},{12,8},{9,1... | collective-permute-start | bytes 1572872 | tf_op jit(solution)/shard_map/ppermute | solution.py:958
  356.1 12.9 %collective-permute-start.58 = (f32[64,2048]{1,0:T(8,128)S(1)}, f32[64,2048]{1,0:T(8,128)S(1)}, u32[]{:S(2)}, u32[]{:S(2)}) collective-permute-start(f32[64,2048]{1,0:T(8,128)S(1)} %reduction_step.12.refs_0_), channel_id=1, source_target_pairs={{0,16},{1,9},{8,24},{9,1},{16,0},{17,25},{24,8},{25,17},{2,18},{3,... | collective-permute-start | bytes 1572872 | tf_op jit(solution)/shard_map/ppermute | solution.py:880
  356.8 14.5 %collective-permute-start.59 = (f32[64,2048]{1,0:T(8,128)S(1)}, f32[64,2048]{1,0:T(8,128)S(1)}, u32[]{:S(2)}, u32[]{:S(2)}) collective-permute-start(f32[64,2048]{1,0:T(8,128)S(1)} %collective-permute-done.57.refs_2_), channel_id=1, source_target_pairs={{0,16},{1,9},{8,24},{9,1},{16,0},{17,25},{24,8},{25,17},{2,18},{3,... | collective-permute-start | bytes 1572872 | tf_op jit(solution)/shard_map/ppermute | solution.py:880
  371.4 10.6 %collective-permute-start.60 = (f32[64,2048]{1,0:T(8,128)S(1)}, f32[64,2048]{1,0:T(8,128)S(1)}, u32[]{:S(2)}, u32[]{:S(2)}) collective-permute-start(f32[64,2048]{1,0:T(8,128)S(1)} %reduction_step.13.refs_0_), channel_id=1, source_target_pairs={{0,8},{1,17},{8,0},{9,25},{16,24},{17,1},{24,16},{25,9},{2,10},{3,... | collective-permute-start | bytes 1572872 | tf_op jit(solution)/shard_map/ppermute | solution.py:880
  371.9 14.3 %collective-permute-start.55 = (f32[320,256]{1,0:T(8,128)S(1)}, f32[320,256]{1,0:T(8,128)S(1)}, u32[]{:S(2)}, u32[]{:S(2)}) collective-permute-start(f32[320,256]{1,0:T(8,128)S(1)} %copy-done.12), channel_id=1, source_target_pairs={{0,4},{4,0},{1,5},{5,1},{2,6},{6,2},{3,7},{7,3},{8,12},{12,8},{9,1... | collective-permute-start | bytes 983048 | tf_op jit(solution)/shard_map/ppermute | solution.py:958
  382.0 9.2 %collective-permute-start.61 = (f32[64,2048]{1,0:T(8,128)S(1)}, f32[64,2048]{1,0:T(8,128)S(1)}, u32[]{:S(2)}, u32[]{:S(2)}) collective-permute-start(f32[64,2048]{1,0:T(8,128)S(1)} %reduction_step.13.refs_0_), channel_id=1, source_target_pairs={{0,16},{1,9},{8,24},{9,1},{16,0},{17,25},{24,8},{25,17},{2,18},{3,... | collective-permute-start | bytes 1572872 | tf_op jit(solution)/shard_map/ppermute | solution.py:880
  382.2 14.6 %collective-permute-start.62 = (f32[64,2048]{1,0:T(8,128)S(1)}, f32[64,2048]{1,0:T(8,128)S(1)}, u32[]{:S(2)}, u32[]{:S(2)}) collective-permute-start(f32[64,2048]{1,0:T(8,128)S(1)} %collective-permute-done.60.refs_2_), channel_id=1, source_target_pairs={{0,16},{1,9},{8,24},{9,1},{16,0},{17,25},{24,8},{25,17},{2,18},{3,... | collective-permute-start | bytes 1572872 | tf_op jit(solution)/shard_map/ppermute | solution.py:880
  (48 other events, 385.4 us)

commit v3 on v0

--- a/solution.py
+++ b/solution.py
@@ -146,6 +146,7 @@
     rows, n = (frames, 2) if apart else (2 * frames, 1)
     outs = call(
         merge_body,
+        hbm_outs=(0, 1) if apart else (),
         grid=(1,),
         out_shape=[jax.ShapeDtypeStruct((rows, columns // 2), F32)] * n,
         in_specs=[
@@ -659,7 +660,7 @@
             ],
         ),
         out_shape=out_shape,
-        hbm_outs=(0,),
+        hbm_outs=(0, 2) if split_terms else (0,),
         cost_estimate=cost(6 * frames * features * features, 4 * features * features),
         name="norm_back",
     )(columns, place, *operands, *[in_hbm(w) for w in weights])
@@ -852,7 +853,7 @@
         column = end
 
 
-def step_of(*pairs, cut=1, widths=None):
+def step_of(*pairs, cut=1, widths=None, hbm_outs=()):
     shape = list(pairs[0][0].shape)
     widths = widths or [sum(pair[0].shape[-1] for pair in pairs)]
     outs = []
@@ -867,6 +868,7 @@
         in_specs=[whole(a) for a in operands],
         out_specs=[whole(a) for a in outs],
         out_shape=outs,
+        hbm_outs=hbm_outs,
         cost_estimate=cost(0, 4 * sum(a.size for a in operands)),
         name="reduction_step",
     )(*operands)
@@ -1077,7 +1079,7 @@
             leaving = after(leaving, diagonal, other_split[0])
         else:
             received = [None, swap_half(terms[1])]
-            later, go = step_of((later, after(go, grad_z)))
+            later, go = step_of((later, after(go, grad_z)), hbm_outs=(0,))
             leaving = after(leaving, later)
             go = lax.ppermute(go, ("h", "c"), DIAGONAL)
             later = (later, go)
@@ -1101,7 +1103,7 @@
     sums = jnp.stack(results)
     sums = [sums[:, 0], sums[:, 1], sums[:, 2]]
     aways = merge(kept, 1, received[1], apart=True)
-    later = (later[0], over_c(after(later[1], aways[0])))
+    later = (in_hbm(later[0]), over_c(after(later[1], aways[0])))
     come[0] = after(come[0], sums, later[1])
     far_near = over_c(lax.ppermute(aways[0], ("h", "c"), DIAGONAL))
     near_sum, far_sum, near_go, far_go = step_of(
@@ -1118,10 +1120,10 @@
     close = merge(kept, 0, after(received[0], output))
     far = over_c(over_h(after(aways[1], go)))
     (share,) = step_of((total, after(go, close, *later[1:])), cut=0)
-    gathered = plane_gather(share, far)
+    grad_weights = assemble(place, after(later, share), 1)
+    gathered = plane_gather(share, grad_weights)
     grad_in = [(close, 0), (over_c(close[frames:]), 0), (far_near, 0), (far, 0)]
     grad_in = unpack(place, grad_in, frames)
-    grad_weights = assemble(place, after(later, share), 1)
     grad_weights = assemble(place, after(gathered, grad_in), 0, grad_weights)
     return (output, grad_in, grad_weights, *sums, sums[1])
 

time: 397 us -> 392 us (0.987)
  waiting for transfers between devices: 123 us -> 119 us
    ppermute x7, waiting for transfers between devices: 61 us -> 44.4 us  [over_h(): return lax.ppermute(array, 'h', FLIP2)]
    ppermute x13, waiting for transfers between devices: 19.4 us -> 27.7 us  [plane_swap(): return lax.ppermute(array, ('y', 'x', 'c'), pairs)]
    ppermute x6, waiting for transfers between devices: 14.3 us -> 21.3 us  [swap_half(): return lax.ppermute(array, 'l', FLIP2)]
  transfers between devices with their start and end apart: 63 -> 63, of which waited for: 28 -> 29; matrix products, arithmetic and copies ran while one was open for 1% -> 1% of each run, Pallas kernels for 36% -> 37%
where the time goes in v3:
time: 392 us; the launch traced here: 390 us
  Pallas kernels  153 us (39%)
  waiting for transfers between devices  119 us (30%)
  blocking collectives  61.8 us (16%)
  starting transfers between devices  45.3 us (12%)
  local copies, waits for them, and re-layouts  7.14 us (2%)
    all_gather x8, blocking collectives, gather(): return lax.all_gather(array, axes, tiled=True)  61.8 us
    ppermute x7, waiting for transfers between devices, over_h(): return lax.ppermute(array, 'h', FLIP2)  44.4 us
    pallas_call x5, Pallas kernels, project(): call(partial(project_body, len(parts), len(flat), spots, len(weights), 0...  35.9 us
    ppermute x13, waiting for transfers between devices, plane_swap(): return lax.ppermute(array, ('y', 'x', 'c'), pairs)  27.7 us
    pallas_call x4, Pallas kernels, weight_rows(): call(partial(weight_body, turn), grid_spec=pltpu.PrefetchScalarGridSpec(n...  26.5 us
    ppermute x6, waiting for transfers between devices, swap_half(): return lax.ppermute(array, 'l', FLIP2)  21.3 us
    pallas_call x2, Pallas kernels, norm_back(): call(partial(norm_back_body, len(z), split_terms, layer), grid_spec=pltpu...  15.3 us
    pallas_call x4, Pallas kernels, prepare(): call(prepare_body, grid_spec=pltpu.PrefetchScalarGridSpec(num_scalar_pref...  15.1 us
  transfers between devices with their start and end apart: 63, of which 29 were waited for; matrix products, arithmetic and copies ran while one was open for 1% of the time, Pallas kernels for 37%

profile of v3, /device:TPU:0, one launch (start us, length us, event | category | flops | bytes accessed | tf_op | source)
XLA Modules:
  0.0 390.3 jit_solution(14564786999467255358)
XLA Ops:
  5.2 2.7 collective-permute-start.3
  7.8 2.6 collective-permute-start.1
  10.8 2.9 pack.3
  15.6 18.6 %collective-permute-done.1.refs_12_.refs_8_.refs_7_.refs_4_ = f32[64,2048]{1,0:T(8,128)} collective-permute-done((f32[64,2048]{1,0:T(8,128)S(1)}, f32[64,2048]{1,0:T(8,128)}, u32[]{:S(2)}, u32[]{:S(2)}) %collective-permute-start.1) | collective-permute-done | bytes 524320 | tf_op jit(solution)/shard_map/ppermute | solution.py:960
  34.2 3.0 collective-permute-done.3.refs_4_.refs_2_
  37.2 2.7 collective-permute-start.6
  40.8 21.3 %collective-permute-done.refs_2_.refs_8_ = f32[640,256]{1,0:T(8,128)S(1)} collective-permute-done((f32[640,256]{1,0:T(8,128)S(1)}, f32[640,256]{1,0:T(8,128)S(1)}, u32[]{:S(2)}, u32[]{:S(2)}) %collective-permute-start) | collective-permute-done | bytes 655392 | tf_op jit(solution)/shard_map/ppermute | solution.py:960
  69.9 9.9 %project.5 = (f32[320,1024]{1,0:T(8,128)}, f32[320,1024]{1,0:T(8,128)}) custom-call(s32[6]{0:T(128)S(1)} %concatenate.11.cols_ref, s32[8]{0:T(128)S(1)} %stack.124.place_ref, f32[640,256]{1,0:T(8,128)S(1)} %get-tuple-element.137.refs_0_.refs_6_, f32[640,256]{1,0:T(8,128)} %collective-permute-done.8.refs_1_.refs_7_, ...), custom_call_target="tpu_custom_call" | custom-call | flops 47185920 | bytes 98304 | tf_op jit(solution)/shard_map/project/pallas_call | solution.py:289
  83.3 6.1 %project.6 = (f32[320,1024]{1,0:T(8,128)}, f32[5,8,128]{2,1,0:T(8,128)S(1)}, f32[320,1024]{1,0:T(8,128)}) custom-call(s32[2]{0:T(128)S(1)} %pad_add_fusion.1.cols_ref, s32[8]{0:T(128)S(1)} %stack.124.place_ref, f32[640,256]{1,0:T(8,128)S(1)} %collective-permute-done.7.refs_0_.refs_4_, f32[640,256]{1,0:T(8,128)S(1)} %collective-permute-done.15.refs_1_.refs_5_, ...), custom_call_target="tpu_custom_call" | custom-call | flops 15728640 | bytes 32768 | tf_op jit(solution)/shard_map/project/pallas_call | solution.py:289
  89.9 6.2 %all_gather.24 = f32[20,8,128]{2,1,0:T(8,128)S(1)} all-gather(f32[5,8,128]{2,1,0:T(8,128)S(1)} %get-tuple-element.145), channel_id=1, replica_groups=mesh['y'=2,'x'=2,'h'=2,'l'=2,'c'=2] {'h','c'}, dimensions={0}, use_global_device_ids=true | all-gather | bytes 102400 | tf_op jit(solution)/shard_map/all_gather | solution.py:999
  97.3 9.2 %all_gather.25.refs_1_.refs_3_ = f32[80,8,128]{2,1,0:T(8,128)S(1)} all-gather(f32[20,8,128]{2,1,0:T(8,128)S(1)} %all_gather.24), channel_id=1, replica_groups=mesh['y'=2,'x'=2,'h'=2,'l'=2,'c'=2] {'y','x'}, dimensions={0}, use_global_device_ids=true | all-gather | bytes 409600 | tf_op jit(solution)/shard_map/all_gather | solution.py:999
  106.6 7.3 %recur.2 = (f32[320,1024]{1,0:T(8,128)S(1)}, f32[320,1024]{1,0:T(8,128)}, f32[320,1024]{1,0:T(8,128)}, f32[6,8,128]{2,1,0:T(8,128)S(1)}) custom-call(s32[8]{0:T(128)S(1)} %stack.124.place_ref, f32[320]{0:T(512)S(1)} %fusion.6.gate_ref, f32[320,1024]{1,0:T(8,128)} %get-tuple-element.144.refs_0_, f32[80,8,128]{2,1,0:T(8,128)S(1)} %all_gather.25.refs_1_.refs_3_, ...), custom_call_target="tpu_custom_call" | custom-call | flops 512000 | bytes 102400 | tf_op jit(solution)/shard_map/recur/pallas_call | solution.py:435
  115.7 6.6 %collective-permute-done.20 = f32[64,2048]{1,0:T(8,128)S(1)} collective-permute-done((f32[64,2048]{1,0:T(8,128)S(1)}, f32[64,2048]{1,0:T(8,128)S(1)}, u32[]{:S(2)}, u32[]{:S(2)}) %collective-permute-start.20) | collective-permute-done | bytes 524320 | tf_op jit(solution)/shard_map/ppermute | solution.py:1019
  129.1 3.8 prepare.4
  132.9 3.8 prepare.5
  136.6 5.2 %project.7.refs_3_ = f32[320,512]{1,0:T(8,128)} custom-call(s32[4]{0:T(128)S(1)} %pad_add_fusion.2.cols_ref, s32[8]{0:T(128)S(1)} %stack.124.place_ref, f32[320,1024]{1,0:T(8,128)S(1)} %get-tuple-element.160.refs_0_.own_ref.refs_5_, f32[2,256,2048]{2,1,0:T(8,128)} %refs_2_.1, ...), custom_call_target="tpu_custom_call" | custom-call | flops 15728640 | bytes 32768 | tf_op jit(solution)/shard_map/project/pallas_call | solution.py:289
  141.8 3.8 prepare.6
  145.6 4.7 %collective-permute-done.16.refs_0_.refs_1_.own_ref = f32[320,1024]{1,0:T(8,128)S(1)} collective-permute-done((f32[320,1024]{1,0:T(8,128)S(1)}, f32[320,1024]{1,0:T(8,128)S(1)}, u32[]{:S(2)}, u32[]{:S(2)}) %collective-permute-start.16) | collective-permute-done | bytes 1310752 | tf_op jit(solution)/shard_map/ppermute | solution.py:29
  153.1 5.7 %project.8 = (f32[320,512]{1,0:T(8,128)}, f32[3,8,128]{2,1,0:T(8,128)S(1)}) custom-call(s32[4]{0:T(128)S(1)} %pad_add_fusion.cols_ref, s32[8]{0:T(128)S(1)} %stack.124.place_ref, f32[320,1024]{1,0:T(8,128)S(1)} %collective-permute-done.16.refs_0_.refs_1_.own_ref, f32[2,256,2048]{2,1,0:T(8,128)} %refs_2_.1, ...), custom_call_target="tpu_custom_call" | custom-call | flops 15728640 | bytes 32768 | tf_op jit(solution)/shard_map/project/pallas_call | solution.py:289
  158.9 9.1 %project.9 = (f32[320,512]{1,0:T(8,128)}, f32[3,8,128]{2,1,0:T(8,128)S(1)}) custom-call(s32[8]{0:T(128)S(1)} %concatenate.12.cols_ref, s32[8]{0:T(128)S(1)} %stack.124.place_ref, f32[320,1024]{1,0:T(8,128)S(1)} %copy-done.1, f32[320,1024]{1,0:T(8,128)S(1)} %collective-permute-done.16.refs_0_.refs_1_.own_ref, ...), custom_call_target="tpu_custom_call" | custom-call | flops 31457280 | bytes 65536 | tf_op jit(solution)/shard_map/project/pallas_call | solution.py:289
  168.1 8.2 %all_gather.26 = f32[12,8,128]{2,1,0:T(8,128)S(1)} all-gather(f32[3,8,128]{2,1,0:T(8,128)S(1)} %get-tuple-element.168), channel_id=1, replica_groups=mesh['y'=2,'x'=2,'h'=2,'l'=2,'c'=2] {'y','x'}, dimensions={0}, use_global_device_ids=true | all-gather | bytes 61440 | tf_op jit(solution)/shard_map/all_gather | solution.py:999
  176.2 8.8 %all_gather.27.refs_2_.refs_4_ = f32[48,8,128]{2,1,0:T(8,128)S(1)} all-gather(f32[12,8,128]{2,1,0:T(8,128)S(1)} %all_gather.26), channel_id=1, replica_groups=mesh['y'=2,'x'=2,'h'=2,'l'=2,'c'=2] {'h','c'}, dimensions={0}, use_global_device_ids=true | all-gather | bytes 245760 | tf_op jit(solution)/shard_map/all_gather | solution.py:999
  185.3 7.4 %recur.3 = (f32[320,256]{1,0:T(8,128)}, f32[320,256]{1,0:T(8,128)}, f32[320,256]{1,0:T(8,128)}, f32[320,256]{1,0:T(8,128)}, f32[320,1024]{1,0:T(8,128)}, /*index=5*/f32[320,1024]{1,0:T(8,128)}) custom-call(s32[8]{0:T(128)S(1)} %stack.124.place_ref, f32[320]{0:T(512)S(1)} %fusion.6.gate_ref, f32[320,512]{1,0:T(8,128)} %get-tuple-element.156.refs_0_, ...), custom_call_target="tpu_custom_call" | custom-call | flops 512000 | bytes 102400 | tf_op jit(solution)/shard_map/recur/pallas_call | solution.py:435
  193.1 5.6 %back.2 = (f32[320,1024]{1,0:T(8,128)S(1)}, f32[3,8,128]{2,1,0:T(8,128)S(1)}) custom-call(s32[8]{0:T(128)S(1)} %stack.124.place_ref, f32[320]{0:T(512)S(1)} %fusion.6.gate_ref, f32[320,512]{1,0:T(8,128)} %get-tuple-element.156.refs_0_, f32[320,512]{1,0:T(8,128)} %get-tuple-element.167.refs_1_, f32[48,8,128]{2,1,0:T(8,128)S(1)} %all_gather.27.refs_2_.refs_4_, ...), custom_call_target="tpu_custom_call" | custom-call | flops 153600 | bytes 102400 | tf_op jit(solution)/shard_map/back/pallas_call | solution.py:542
  198.7 8.2 %all_gather.28 = f32[12,8,128]{2,1,0:T(8,128)S(1)} all-gather(f32[3,8,128]{2,1,0:T(8,128)S(1)} %get-tuple-element.177), channel_id=1, replica_groups=mesh['y'=2,'x'=2,'h'=2,'l'=2,'c'=2] {'y','x'}, dimensions={0}, use_global_device_ids=true | all-gather | bytes 61440 | tf_op jit(solution)/shard_map/all_gather | solution.py:999
  206.9 6.8 %all_gather.29.refs_5_ = f32[48,8,128]{2,1,0:T(8,128)S(1)} all-gather(f32[12,8,128]{2,1,0:T(8,128)S(1)} %all_gather.28), channel_id=1, replica_groups=mesh['y'=2,'x'=2,'h'=2,'l'=2,'c'=2] {'h','c'}, dimensions={0}, use_global_device_ids=true | all-gather | bytes 245760 | tf_op jit(solution)/shard_map/all_gather | solution.py:999
  213.7 7.7 %norm_back.2 = (f32[320,1024]{1,0:T(8,128)}, f32[320,512]{1,0:T(8,128)S(1)}, f32[320,1024]{1,0:T(8,128)}, f32[3,8,128]{2,1,0:T(8,128)S(1)}) custom-call(s32[2]{0:T(128)S(1)} %pad_add_fusion.4.cols_ref, s32[8]{0:T(128)S(1)} %stack.124.place_ref, f32[320,1024]{1,0:T(8,128)S(1)} %get-tuple-element.176.grad_ref, f32[320,512]{1,0:T(8,128)} %get-tuple-element.156.refs_0_, ...), custom_call_target="tpu_custom_call" | custom-call | flops 31457280 | bytes 65536 | tf_op jit(solution)/shard_map/norm_back/pallas_call | solution.py:647
  223.7 3.8 prepare.7
  228.2 7.2 %weight_rows.4 = (f32[2,2,64,1024]{3,2,1,0:T(8,128)}, f32[2,2,64,1024]{3,2,1,0:T(8,128)}, bf16[512,768]{1,0:T(8,128)(2,1)S(1)}, bf16[512,768]{1,0:T(8,128)(2,1)S(1)}) custom-call(s32[8]{0:T(128)S(1)} %stack.124.place_ref, f32[320,1024]{1,0:T(8,128)} %get-tuple-element.191.refs_0_.grad_ref, f32[320,512]{1,0:T(8,128)S(1)} %collective-permute-done.32.refs_1_, ...), custom_call_target="tpu_custom_call" | custom-call | flops 37748736 | bytes 32768 | tf_op jit(solution)/shard_map/weight_rows/pallas_call | solution.py:820
  236.2 6.1 %weight_rows.5 = (f32[2,2,64,1024]{3,2,1,0:T(8,128)}, f32[2,2,64,1024]{3,2,1,0:T(8,128)}) custom-call(s32[8]{0:T(128)S(1)} %stack.124.place_ref, bf16[512,768]{1,0:T(8,128)(2,1)S(1)} %get-tuple-element.187.refs_0_, bf16[512,768]{1,0:T(8,128)(2,1)S(1)} %get-tuple-element.188.refs_1_, bf16[768,1024]{1,0:T(8,128)(2,1)} %get-tuple-element.184.refs_2_, ...), custom_call_target="tpu_custom_call" | custom-call | flops 37748736 | bytes 32768 | tf_op jit(solution)/shard_map/weight_rows/pallas_call | solution.py:820
  243.7 6.1 %own_terms.2.refs_3_.refs_0_ = f32[320,1024]{1,0:T(8,128)S(1)} custom-call(s32[2]{0:T(128)S(1)} %pad_add_fusion.5.cols_ref, s32[8]{0:T(128)S(1)} %stack.124.place_ref, f32[320,1024]{1,0:T(8,128)} %get-tuple-element.191.refs_0_.grad_ref, f32[640,256]{1,0:T(8,128)S(1)} %copy-done.6, f32[640,256]{1,0:T(8,128)} %collective-permute-done.29.refs_5_.refs_1_, ...), custom_call_target="tpu_custom_call" | custom-call | flops 31457280 | bytes 65536 | tf_op jit(solution)/shard_map/own_terms/pallas_call | solution.py:705
  253.2 5.9 %back.3 = (f32[320,1024]{1,0:T(8,128)S(1)}, f32[3,8,128]{2,1,0:T(8,128)S(1)}) custom-call(s32[8]{0:T(128)S(1)} %stack.124.place_ref, f32[320]{0:T(512)S(1)} %fusion.6.gate_ref, f32[320,1024]{1,0:T(8,128)} %get-tuple-element.144.refs_0_, f32[80,8,128]{2,1,0:T(8,128)S(1)} %all_gather.25.refs_1_.refs_3_, ...), custom_call_target="tpu_custom_call" | custom-call | flops 153600 | bytes 102400 | tf_op jit(solution)/shard_map/back/pallas_call | solution.py:542
  259.1 7.5 %all_gather.30 = f32[12,8,128]{2,1,0:T(8,128)S(1)} all-gather(f32[3,8,128]{2,1,0:T(8,128)S(1)} %get-tuple-element.195), channel_id=1, replica_groups=mesh['y'=2,'x'=2,'h'=2,'l'=2,'c'=2] {'y','x'}, dimensions={0}, use_global_device_ids=true | all-gather | bytes 61440 | tf_op jit(solution)/shard_map/all_gather | solution.py:999
  271.8 6.9 %all_gather.31.refs_4_ = f32[48,8,128]{2,1,0:T(8,128)S(1)} all-gather(f32[12,8,128]{2,1,0:T(8,128)S(1)} %all_gather.30), channel_id=1, replica_groups=mesh['y'=2,'x'=2,'h'=2,'l'=2,'c'=2] {'h','c'}, dimensions={0}, use_global_device_ids=true | all-gather | bytes 245760 | tf_op jit(solution)/shard_map/all_gather | solution.py:999
  278.8 7.6 %norm_back.3 = (f32[320,1024]{1,0:T(8,128)}, f32[320,512]{1,0:T(8,128)S(1)}, f32[320,512]{1,0:T(8,128)}, f32[320,512]{1,0:T(8,128)S(1)}, f32[3,8,128]{2,1,0:T(8,128)S(1)}) custom-call(s32[2]{0:T(128)S(1)} %pad_add_fusion.4.cols_ref, s32[8]{0:T(128)S(1)} %stack.124.place_ref, f32[320,1024]{1,0:T(8,128)S(1)} %get-tuple-element.194.grad_ref, ...), custom_call_target="tpu_custom_call" | custom-call | flops 31457280 | bytes 65536 | tf_op jit(solution)/shard_map/norm_back/pallas_call | solution.py:647
  290.7 7.2 %weight_rows.6 = (f32[2,2,64,1024]{3,2,1,0:T(8,128)}, f32[2,2,64,1024]{3,2,1,0:T(8,128)}, bf16[512,768]{1,0:T(8,128)(2,1)S(1)}, bf16[512,768]{1,0:T(8,128)(2,1)S(1)}) custom-call(s32[8]{0:T(128)S(1)} %stack.124.place_ref, f32[320,1024]{1,0:T(8,128)} %get-tuple-element.221.refs_0_.grad_ref, f32[320,512]{1,0:T(8,128)S(1)} %collective-permute-done.41.refs_1_, ...), custom_call_target="tpu_custom_call" | custom-call | flops 37748736 | bytes 32768 | tf_op jit(solution)/shard_map/weight_rows/pallas_call | solution.py:820
  298.7 6.1 %weight_rows.7 = (f32[2,2,64,1024]{3,2,1,0:T(8,128)}, f32[2,2,64,1024]{3,2,1,0:T(8,128)}) custom-call(s32[8]{0:T(128)S(1)} %stack.124.place_ref, bf16[512,768]{1,0:T(8,128)(2,1)S(1)} %get-tuple-element.217.refs_0_, bf16[512,768]{1,0:T(8,128)(2,1)S(1)} %get-tuple-element.218.refs_1_, bf16[768,1024]{1,0:T(8,128)(2,1)} %get-tuple-element.154.refs_2_, ...), custom_call_target="tpu_custom_call" | custom-call | flops 37748736 | bytes 32768 | tf_op jit(solution)/shard_map/weight_rows/pallas_call | solution.py:820
  306.0 6.0 %own_terms.3.kept_ref = f32[320,1024]{1,0:T(8,128)S(1)} custom-call(s32[2]{0:T(128)S(1)} %pad_add_fusion.5.cols_ref, s32[8]{0:T(128)S(1)} %stack.124.place_ref, f32[320,1024]{1,0:T(8,128)} %get-tuple-element.221.refs_0_.grad_ref, f32[320,1024]{1,0:T(8,128)S(1)} %own_terms.2.refs_3_.refs_0_, f32[320,1024]{1,0:T(8,128)S(1)} %copy-done.4, ...), custom_call_target="tpu_custom_call" | custom-call | flops 31457280 | bytes 65536 | tf_op jit(solution)/shard_map/own_terms/pallas_call | solution.py:705
  312.0 2.7 collective-permute-done.45.come_ref
  317.9 6.2 %collective-permute-done.47.refs_3_ = f32[2,2,64,1024]{3,2,1,0:T(8,128)S(1)} collective-permute-done((f32[2,2,64,1024]{3,2,1,0:T(8,128)}, f32[2,2,64,1024]{3,2,1,0:T(8,128)S(1)}, u32[]{:S(2)}, u32[]{:S(2)}) %collective-permute-start.47) | collective-permute-done | bytes 1048608 | tf_op jit(solution)/shard_map/ppermute | solution.py:882
  326.7 6.5 %collective-permute-done.51 = f32[320,256]{1,0:T(8,128)S(1)} collective-permute-done((f32[320,256]{1,0:T(8,128)}, f32[320,256]{1,0:T(8,128)S(1)}, u32[]{:S(2)}, u32[]{:S(2)}) %collective-permute-start.51) | collective-permute-done | bytes 327712 | tf_op jit(solution)/shard_map/ppermute | solution.py:1108
  341.2 8.8 %collective-permute-done.58.refs_2_ = f32[64,2048]{1,0:T(8,128)S(1)} collective-permute-done((f32[64,2048]{1,0:T(8,128)S(1)}, f32[64,2048]{1,0:T(8,128)S(1)}, u32[]{:S(2)}, u32[]{:S(2)}) %collective-permute-start.58) | collective-permute-done | bytes 524320 | tf_op jit(solution)/shard_map/ppermute | solution.py:882
  350.9 4.0 %collective-permute-done.48.refs_1_ = f32[64,2048]{1,0:T(8,128)S(1)} collective-permute-done((f32[64,2048]{1,0:T(8,128)S(1)}, f32[64,2048]{1,0:T(8,128)S(1)}, u32[]{:S(2)}, u32[]{:S(2)}) %collective-permute-start.48) | collective-permute-done | bytes 524320 | tf_op jit(solution)/shard_map/ppermute | solution.py:882
  355.0 2.8 unpack.2
  357.8 7.0 %collective-permute-done.49.come_ref = f32[320,512]{1,0:T(8,128)S(1)} collective-permute-done((f32[320,512]{1,0:T(8,128)S(1)}, f32[320,512]{1,0:T(8,128)S(1)}, u32[]{:S(2)}, u32[]{:S(2)}) %collective-permute-start.49) | collective-permute-done | bytes 655392 | tf_op jit(solution)/shard_map/ppermute | solution.py:29
  368.1 3.0 assemble.2.refs_4_
  371.1 7.4 %collective-permute-done.61.refs_2_ = f32[64,2048]{1,0:T(8,128)S(1)} collective-permute-done((f32[64,2048]{1,0:T(8,128)S(1)}, f32[64,2048]{1,0:T(8,128)S(1)}, u32[]{:S(2)}, u32[]{:S(2)}) %collective-permute-start.61) | collective-permute-done | bytes 524320 | tf_op jit(solution)/shard_map/ppermute | solution.py:882
  379.5 3.3 collective-permute-done.55
  (204 shorter events, 79.6 us)
Async XLA Ops:
  0.6 36.5 %collective-permute-start.2 = (f32[2,256,2048]{2,1,0:T(8,128)}, f32[2,256,2048]{2,1,0:T(8,128)}, u32[]{:S(2)}, u32[]{:S(2)}) collective-permute-start(f32[2,256,2048]{2,1,0:T(8,128)} %refs_2_.1), channel_id=1, source_target_pairs={{0,1},{1,0},{2,3},{3,2},{4,5},{5,4},{6,7},{7,6},{8,9},{9,8},{10,11... | collective-permute-start | bytes 12582920 | tf_op jit(solution)/shard_map/ppermute | solution.py:963
  5.2 32.0 %collective-permute-start.3 = (f32[640,256]{1,0:T(8,128)S(1)}, f32[640,256]{1,0:T(8,128)S(1)}, u32[]{:S(2)}, u32[]{:S(2)}) collective-permute-start(f32[640,256]{1,0:T(8,128)S(1)} %get-tuple-element.137.refs_0_.refs_6_), channel_id=1, source_target_pairs={{0,2},{2,0},{1,3},{3,1},{4,6},{6,4},{5,7},{7,5},{8,10},{10,8},{9,1... | collective-permute-start | bytes 1966088 | tf_op jit(solution)/shard_map/ppermute | solution.py:29
  7.8 26.3 %collective-permute-start.1 = (f32[64,2048]{1,0:T(8,128)S(1)}, f32[64,2048]{1,0:T(8,128)}, u32[]{:S(2)}, u32[]{:S(2)}) collective-permute-start(f32[64,2048]{1,0:T(8,128)S(1)} %get-tuple-element.254), channel_id=1, source_target_pairs={{0,4},{4,0},{1,5},{5,1},{2,6},{6,2},{3,7},{7,3},{8,12},{12,8},{9,1... | collective-permute-start | bytes 1572872 | tf_op jit(solution)/shard_map/ppermute | solution.py:960
  10.4 51.7 %collective-permute-start = (f32[640,256]{1,0:T(8,128)S(1)}, f32[640,256]{1,0:T(8,128)S(1)}, u32[]{:S(2)}, u32[]{:S(2)}) collective-permute-start(f32[640,256]{1,0:T(8,128)S(1)} %get-tuple-element.131), channel_id=1, source_target_pairs={{0,4},{4,0},{1,5},{5,1},{2,6},{6,2},{3,7},{7,3},{8,12},{12,8},{9,1... | collective-permute-start | bytes 1966088 | tf_op jit(solution)/shard_map/ppermute | solution.py:960
  37.2 24.9 %collective-permute-start.6 = (f32[64,2048]{1,0:T(8,128)}, f32[64,2048]{1,0:T(8,128)}, u32[]{:S(2)}, u32[]{:S(2)}) collective-permute-start(f32[64,2048]{1,0:T(8,128)} %collective-permute-done.1.refs_12_.refs_8_.refs_7_.refs_4_), channel_id=1, source_target_pairs={{0,24},{8,16},{16,8},{24,0},{1,25},{9,17},{17,9},{25,1},{2,26},{10... | collective-permute-start | bytes 1572872 | tf_op jit(solution)/shard_map/ppermute | solution.py:977
  39.9 23.6 %collective-permute-start.5 = (f32[64,2048]{1,0:T(8,128)}, f32[64,2048]{1,0:T(8,128)}, u32[]{:S(2)}, u32[]{:S(2)}) collective-permute-start(f32[64,2048]{1,0:T(8,128)} %collective-permute-done.1.refs_12_.refs_8_.refs_7_.refs_4_), channel_id=1, source_target_pairs={{0,16},{16,0},{1,17},{17,1},{2,18},{18,2},{3,19},{19,3},{4,20},{20... | collective-permute-start | bytes 1572872 | tf_op jit(solution)/shard_map/ppermute | solution.py:978
  40.4 23.1 %collective-permute-start.4 = (f32[64,2048]{1,0:T(8,128)}, f32[64,2048]{1,0:T(8,128)S(1)}, u32[]{:S(2)}, u32[]{:S(2)}) collective-permute-start(f32[64,2048]{1,0:T(8,128)} %collective-permute-done.1.refs_12_.refs_8_.refs_7_.refs_4_), channel_id=1, source_target_pairs={{0,8},{8,0},{1,9},{9,1},{2,10},{10,2},{3,11},{11,3},{4,12},{12,4},... | collective-permute-start | bytes 1572872 | tf_op jit(solution)/shard_map/ppermute | solution.py:978
  40.8 23.7 %collective-permute-start.10 = (f32[640,256]{1,0:T(8,128)S(1)}, f32[640,256]{1,0:T(8,128)S(1)}, u32[]{:S(2)}, u32[]{:S(2)}) collective-permute-start(f32[640,256]{1,0:T(8,128)S(1)} %collective-permute-done.3.refs_4_.refs_2_), channel_id=1, source_target_pairs={{0,1},{1,0},{2,3},{3,2},{4,5},{5,4},{6,7},{7,6},{8,9},{9,8},{10,11... | collective-permute-start | bytes 1966088 | tf_op jit(solution)/shard_map/ppermute | solution.py:963
  64.5 16.7 %collective-permute-start.7 = (f32[640,256]{1,0:T(8,128)S(1)}, f32[640,256]{1,0:T(8,128)S(1)}, u32[]{:S(2)}, u32[]{:S(2)}) collective-permute-start(f32[640,256]{1,0:T(8,128)S(1)} %collective-permute-done.refs_2_.refs_8_), channel_id=1, source_target_pairs={{0,2},{2,0},{1,3},{3,1},{4,6},{6,4},{5,7},{7,5},{8,10},{10,8},{9,1... | collective-permute-start | bytes 1966088 | tf_op jit(solution)/shard_map/ppermute | solution.py:29
  89.4 34.9 %collective-permute-start.18 = (f32[320,1024]{1,0:T(8,128)S(1)}, f32[320,1024]{1,0:T(8,128)S(1)}, u32[]{:S(2)}, u32[]{:S(2)}) collective-permute-start(f32[320,1024]{1,0:T(8,128)S(1)} %copy-done.11), channel_id=1, source_target_pairs={{0,1},{1,0},{2,3},{3,2},{4,5},{5,4},{6,7},{7,6},{8,9},{9,8},{10,11... | collective-permute-start | bytes 3932168 | tf_op jit(solution)/shard_map/ppermute | solution.py:963
  89.6 35.9 %collective-permute-start.19 = (f32[320,1024]{1,0:T(8,128)}, f32[320,1024]{1,0:T(8,128)}, u32[]{:S(2)}, u32[]{:S(2)}) collective-permute-start(f32[320,1024]{1,0:T(8,128)} %get-tuple-element.153.own_ref), channel_id=1, source_target_pairs={{0,1},{1,0},{2,3},{3,2},{4,5},{5,4},{6,7},{7,6},{8,9},{9,8},{10,11... | collective-permute-start | bytes 3932168 | tf_op jit(solution)/shard_map/ppermute | solution.py:963
  96.1 26.1 %collective-permute-start.20 = (f32[64,2048]{1,0:T(8,128)S(1)}, f32[64,2048]{1,0:T(8,128)S(1)}, u32[]{:S(2)}, u32[]{:S(2)}) collective-permute-start(f32[64,2048]{1,0:T(8,128)S(1)} %copy-done.13), channel_id=1, source_target_pairs={{0,5},{1,4},{4,1},{5,0},{2,7},{3,6},{6,3},{7,2},{8,13},{9,12},{12,... | collective-permute-start | bytes 1572872 | tf_op jit(solution)/shard_map/ppermute | solution.py:1019
  113.8 15.3 %collective-permute-start.17 = (f32[320,1024]{1,0:T(8,128)S(1)}, f32[320,1024]{1,0:T(8,128)}, u32[]{:S(2)}, u32[]{:S(2)}) collective-permute-start(f32[320,1024]{1,0:T(8,128)S(1)} %get-tuple-element.160.refs_0_.own_ref.refs_5_), channel_id=1, source_target_pairs={{0,1},{1,0},{2,3},{3,2},{4,5},{5,4},{6,7},{7,6},{8,9},{9,8},{10,11... | collective-permute-start | bytes 3932168 | tf_op jit(solution)/shard_map/ppermute | solution.py:963
  113.8 36.5 %collective-permute-start.16 = (f32[320,1024]{1,0:T(8,128)S(1)}, f32[320,1024]{1,0:T(8,128)S(1)}, u32[]{:S(2)}, u32[]{:S(2)}) collective-permute-start(f32[320,1024]{1,0:T(8,128)S(1)} %get-tuple-element.160.refs_0_.own_ref.refs_5_), channel_id=1, source_target_pairs={{0,2},{2,0},{1,3},{3,1},{4,6},{6,4},{5,7},{7,5},{8,10},{10,8},{9,1... | collective-permute-start | bytes 3932168 | tf_op jit(solution)/shard_map/ppermute | solution.py:29
  125.4 25.4 %collective-permute-start.24 = (f32[64,2048]{1,0:T(8,128)}, f32[64,2048]{1,0:T(8,128)}, u32[]{:S(2)}, u32[]{:S(2)}) collective-permute-start(f32[64,2048]{1,0:T(8,128)} %collective-permute-done.21.refs_2_.refs_8_.refs_6_), channel_id=1, source_target_pairs={{0,24},{8,16},{16,8},{24,0},{1,25},{9,17},{17,9},{25,1},{2,26},{10... | collective-permute-start | bytes 1572872 | tf_op jit(solution)/shard_map/ppermute | solution.py:977
  127.2 24.7 %collective-permute-start.23 = (f32[64,2048]{1,0:T(8,128)}, f32[64,2048]{1,0:T(8,128)}, u32[]{:S(2)}, u32[]{:S(2)}) collective-permute-start(f32[64,2048]{1,0:T(8,128)} %collective-permute-done.21.refs_2_.refs_8_.refs_6_), channel_id=1, source_target_pairs={{0,16},{16,0},{1,17},{17,1},{2,18},{18,2},{3,19},{19,3},{4,20},{20... | collective-permute-start | bytes 1572872 | tf_op jit(solution)/shard_map/ppermute | solution.py:978
  128.4 23.6 %collective-permute-start.22 = (f32[64,2048]{1,0:T(8,128)}, f32[64,2048]{1,0:T(8,128)}, u32[]{:S(2)}, u32[]{:S(2)}) collective-permute-start(f32[64,2048]{1,0:T(8,128)} %collective-permute-done.21.refs_2_.refs_8_.refs_6_), channel_id=1, source_target_pairs={{0,8},{8,0},{1,9},{9,1},{2,10},{10,2},{3,11},{11,3},{4,12},{12,4},... | collective-permute-start | bytes 1572872 | tf_op jit(solution)/shard_map/ppermute | solution.py:978
  150.3 34.7 %collective-permute-start.30 = (f32[640,256]{1,0:T(8,128)}, f32[640,256]{1,0:T(8,128)}, u32[]{:S(2)}, u32[]{:S(2)}) collective-permute-start(f32[640,256]{1,0:T(8,128)} %get-tuple-element.172), channel_id=1, source_target_pairs={{0,4},{4,0},{1,5},{5,1},{2,6},{6,2},{3,7},{7,3},{8,12},{12,8},{9,1... | collective-permute-start | bytes 1966088 | tf_op jit(solution)/shard_map/ppermute | solution.py:960
  152.0 6.8 %collective-permute-start.25 = (f32[64,2048]{1,0:T(8,128)}, f32[64,2048]{1,0:T(8,128)}, u32[]{:S(2)}, u32[]{:S(2)}) collective-permute-start(f32[64,2048]{1,0:T(8,128)} %collective-permute-done.21.refs_2_.refs_8_.refs_6_), channel_id=1, source_target_pairs={{0,1},{1,0},{2,3},{3,2},{4,5},{5,4},{6,7},{7,6},{8,9},{9,8},{10,11... | collective-permute-start | bytes 1572872 | tf_op jit(solution)/shard_map/ppermute | solution.py:963
  152.0 6.9 %collective-permute-start.26 = (f32[64,2048]{1,0:T(8,128)}, f32[64,2048]{1,0:T(8,128)}, u32[]{:S(2)}, u32[]{:S(2)}) collective-permute-start(f32[64,2048]{1,0:T(8,128)} %collective-permute-done.22.refs_3_.refs_9_.refs_7_), channel_id=1, source_target_pairs={{0,1},{1,0},{2,3},{3,2},{4,5},{5,4},{6,7},{7,6},{8,9},{9,8},{10,11... | collective-permute-start | bytes 1572872 | tf_op jit(solution)/shard_map/ppermute | solution.py:963
  152.5 6.4 %collective-permute-start.27 = (f32[64,2048]{1,0:T(8,128)}, f32[64,2048]{1,0:T(8,128)}, u32[]{:S(2)}, u32[]{:S(2)}) collective-permute-start(f32[64,2048]{1,0:T(8,128)} %collective-permute-done.23.refs_4_.refs_10_.refs_8_), channel_id=1, source_target_pairs={{0,1},{1,0},{2,3},{3,2},{4,5},{5,4},{6,7},{7,6},{8,9},{9,8},{10,11... | collective-permute-start | bytes 1572872 | tf_op jit(solution)/shard_map/ppermute | solution.py:963
  152.5 6.4 %collective-permute-start.28 = (f32[64,2048]{1,0:T(8,128)}, f32[64,2048]{1,0:T(8,128)}, u32[]{:S(2)}, u32[]{:S(2)}) collective-permute-start(f32[64,2048]{1,0:T(8,128)} %collective-permute-done.24.refs_5_.refs_11_.refs_9_), channel_id=1, source_target_pairs={{0,1},{1,0},{2,3},{3,2},{4,5},{5,4},{6,7},{7,6},{8,9},{9,8},{10,11... | collective-permute-start | bytes 1572872 | tf_op jit(solution)/shard_map/ppermute | solution.py:963
  158.8 34.3 %collective-permute-start.29 = (f32[640,256]{1,0:T(8,128)S(1)}, f32[640,256]{1,0:T(8,128)}, u32[]{:S(2)}, u32[]{:S(2)}) collective-permute-start(f32[640,256]{1,0:T(8,128)S(1)} %copy-done.5), channel_id=1, source_target_pairs={{0,1},{1,0},{2,3},{3,2},{4,5},{5,4},{6,7},{7,6},{8,9},{9,8},{10,11... | collective-permute-start | bytes 1966088 | tf_op jit(solution)/shard_map/ppermute | solution.py:963
  185.0 8.1 %collective-permute-start.31 = (f32[640,256]{1,0:T(8,128)}, f32[640,256]{1,0:T(8,128)}, u32[]{:S(2)}, u32[]{:S(2)}) collective-permute-start(f32[640,256]{1,0:T(8,128)} %collective-permute-done.30.refs_6_.refs_2_), channel_id=1, source_target_pairs={{0,1},{1,0},{2,3},{3,2},{4,5},{5,4},{6,7},{7,6},{8,9},{9,8},{10,11... | collective-permute-start | bytes 1966088 | tf_op jit(solution)/shard_map/ppermute | solution.py:963
  192.7 31.0 %collective-permute-start.35 = (f32[320,1024]{1,0:T(8,128)S(1)}, f32[320,1024]{1,0:T(8,128)}, u32[]{:S(2)}, u32[]{:S(2)}) collective-permute-start(f32[320,1024]{1,0:T(8,128)S(1)} %collective-permute-done.16.refs_0_.refs_1_.own_ref), channel_id=1, source_target_pairs={{0,1},{1,0},{2,3},{3,2},{4,5},{5,4},{6,7},{7,6},{8,9},{9,8},{10,11... | collective-permute-start | bytes 3932168 | tf_op jit(solution)/shard_map/ppermute | solution.py:963
  193.1 28.8 %collective-permute-start.33 = (f32[320,256]{1,0:T(8,128)}, f32[320,256]{1,0:T(8,128)S(1)}, u32[]{:S(2)}, u32[]{:S(2)}) collective-permute-start(f32[320,256]{1,0:T(8,128)} %get-tuple-element.180), channel_id=1, source_target_pairs={{0,4},{4,0},{1,5},{5,1},{2,6},{6,2},{3,7},{7,3},{8,12},{12,8},{9,1... | collective-permute-start | bytes 983048 | tf_op jit(solution)/shard_map/ppermute | solution.py:960
  222.0 31.3 %collective-permute-start.36 = (f32[320,1024]{1,0:T(8,128)}, f32[320,1024]{1,0:T(8,128)S(1)}, u32[]{:S(2)}, u32[]{:S(2)}) collective-permute-start(f32[320,1024]{1,0:T(8,128)} %get-tuple-element.192), channel_id=1, source_target_pairs={{0,2},{2,0},{1,3},{3,1},{4,6},{6,4},{5,7},{7,5},{8,10},{10,8},{9,1... | collective-permute-start | bytes 3932168 | tf_op jit(solution)/shard_map/ppermute | solution.py:29
  235.4 32.4 %collective-permute-start.37 = (f32[2,2,64,1024]{3,2,1,0:T(8,128)}, f32[2,2,64,1024]{3,2,1,0:T(8,128)}, u32[]{:S(2)}, u32[]{:S(2)}) collective-permute-start(f32[2,2,64,1024]{3,2,1,0:T(8,128)} %get-tuple-element.197), channel_id=1, source_target_pairs={{0,8},{1,17},{8,0},{9,25},{16,24},{17,1},{24,16},{25,9},{2,10},{3,... | collective-permute-start | bytes 3145736 | tf_op jit(solution)/shard_map/ppermute | solution.py:882
  242.3 25.5 %collective-permute-start.40 = (f32[2,2,64,1024]{3,2,1,0:T(8,128)}, f32[2,2,64,1024]{3,2,1,0:T(8,128)}, u32[]{:S(2)}, u32[]{:S(2)}) collective-permute-start(f32[2,2,64,1024]{3,2,1,0:T(8,128)} %get-tuple-element.202), channel_id=1, source_target_pairs={{0,8},{1,17},{8,0},{9,25},{16,24},{17,1},{24,16},{25,9},{2,10},{3,... | collective-permute-start | bytes 3145736 | tf_op jit(solution)/shard_map/ppermute | solution.py:882
  243.6 23.0 %collective-permute-start.39 = (f32[320,256]{1,0:T(8,128)}, f32[320,256]{1,0:T(8,128)S(1)}, u32[]{:S(2)}, u32[]{:S(2)}) collective-permute-start(f32[320,256]{1,0:T(8,128)} %get-tuple-element.200), channel_id=1, source_target_pairs={{0,1},{1,0},{2,3},{3,2},{4,5},{5,4},{6,7},{7,6},{8,9},{9,8},{10,11... | collective-permute-start | bytes 983048 | tf_op jit(solution)/shard_map/ppermute | solution.py:963
  249.8 18.1 %collective-permute-start.38 = (f32[320,256]{1,0:T(8,128)S(1)}, f32[320,256]{1,0:T(8,128)S(1)}, u32[]{:S(2)}, u32[]{:S(2)}) collective-permute-start(f32[320,256]{1,0:T(8,128)S(1)} %copy-done.27), channel_id=1, source_target_pairs={{0,4},{4,0},{1,5},{5,1},{2,6},{6,2},{3,7},{7,3},{8,12},{12,8},{9,1... | collective-permute-start | bytes 983048 | tf_op jit(solution)/shard_map/ppermute | solution.py:960
  271.0 17.2 %collective-permute-start.42 = (f32[2,64,2048]{2,1,0:T(8,128)S(1)}, f32[2,64,2048]{2,1,0:T(8,128)S(1)}, u32[]{:S(2)}, u32[]{:S(2)}) collective-permute-start(f32[2,64,2048]{2,1,0:T(8,128)S(1)} %get-tuple-element.207), channel_id=1, source_target_pairs={{0,16},{1,9},{8,24},{9,1},{16,0},{17,25},{24,8},{25,17},{2,18},{3,... | collective-permute-start | bytes 3145736 | tf_op jit(solution)/shard_map/ppermute | solution.py:882
  286.7 28.0 %collective-permute-start.45 = (f32[320,512]{1,0:T(8,128)S(1)}, f32[320,512]{1,0:T(8,128)S(1)}, u32[]{:S(2)}, u32[]{:S(2)}) collective-permute-start(f32[320,512]{1,0:T(8,128)S(1)} %get-tuple-element.222), channel_id=1, source_target_pairs={{0,2},{2,0},{1,3},{3,1},{4,6},{6,4},{5,7},{7,5},{8,10},{10,8},{9,1... | collective-permute-start | bytes 1966088 | tf_op jit(solution)/shard_map/ppermute | solution.py:29
  289.1 26.6 %collective-permute-start.44 = (f32[64,2048]{1,0:T(8,128)S(1)}, f32[64,2048]{1,0:T(8,128)}, u32[]{:S(2)}, u32[]{:S(2)}) collective-permute-start(f32[64,2048]{1,0:T(8,128)S(1)} %get-tuple-element.216), channel_id=1, source_target_pairs={{0,5},{1,4},{4,1},{5,0},{2,7},{3,6},{6,3},{7,2},{8,13},{9,12},{12,... | collective-permute-start | bytes 1572872 | tf_op jit(solution)/shard_map/ppermute | solution.py:1084
  297.9 19.5 %collective-permute-start.43 = (f32[2,2,64,1024]{3,2,1,0:T(8,128)}, f32[2,2,64,1024]{3,2,1,0:T(8,128)S(1)}, u32[]{:S(2)}, u32[]{:S(2)}) collective-permute-start(f32[2,2,64,1024]{3,2,1,0:T(8,128)} %get-tuple-element.213), channel_id=1, source_target_pairs={{0,8},{1,17},{8,0},{9,25},{16,24},{17,1},{24,16},{25,9},{2,10},{3,... | collective-permute-start | bytes 3145736 | tf_op jit(solution)/shard_map/ppermute | solution.py:882
  304.8 19.3 %collective-permute-start.47 = (f32[2,2,64,1024]{3,2,1,0:T(8,128)}, f32[2,2,64,1024]{3,2,1,0:T(8,128)S(1)}, u32[]{:S(2)}, u32[]{:S(2)}) collective-permute-start(f32[2,2,64,1024]{3,2,1,0:T(8,128)} %get-tuple-element.226), channel_id=1, source_target_pairs={{0,8},{1,17},{8,0},{9,25},{16,24},{17,1},{24,16},{25,9},{2,10},{3,... | collective-permute-start | bytes 3145736 | tf_op jit(solution)/shard_map/ppermute | solution.py:882
  315.7 17.6 %collective-permute-start.51 = (f32[320,256]{1,0:T(8,128)}, f32[320,256]{1,0:T(8,128)S(1)}, u32[]{:S(2)}, u32[]{:S(2)}) collective-permute-start(f32[320,256]{1,0:T(8,128)} %get-tuple-element.223), channel_id=1, source_target_pairs={{0,5},{1,4},{4,1},{5,0},{2,7},{3,6},{6,3},{7,2},{8,13},{9,12},{12,... | collective-permute-start | bytes 983048 | tf_op jit(solution)/shard_map/ppermute | solution.py:1108
  325.9 9.2 %collective-permute-start.53 = (f32[64,2048]{1,0:T(8,128)S(1)}, f32[64,2048]{1,0:T(8,128)S(1)}, u32[]{:S(2)}, u32[]{:S(2)}) collective-permute-start(f32[64,2048]{1,0:T(8,128)S(1)} %get-tuple-element.238), channel_id=1, source_target_pairs={{0,16},{1,9},{8,24},{9,1},{16,0},{17,25},{24,8},{25,17},{2,18},{3,... | collective-permute-start | bytes 1572872 | tf_op jit(solution)/shard_map/ppermute | solution.py:882
  335.2 14.9 %collective-permute-start.58 = (f32[64,2048]{1,0:T(8,128)S(1)}, f32[64,2048]{1,0:T(8,128)S(1)}, u32[]{:S(2)}, u32[]{:S(2)}) collective-permute-start(f32[64,2048]{1,0:T(8,128)S(1)} %reduction_step.12.refs_0_), channel_id=1, source_target_pairs={{0,8},{1,17},{8,0},{9,25},{16,24},{17,1},{24,16},{25,9},{2,10},{3,... | collective-permute-start | bytes 1572872 | tf_op jit(solution)/shard_map/ppermute | solution.py:882
  336.1 13.9 %collective-permute-start.57 = (f32[64,2048]{1,0:T(8,128)S(1)}, f32[64,2048]{1,0:T(8,128)S(1)}, u32[]{:S(2)}, u32[]{:S(2)}) collective-permute-start(f32[64,2048]{1,0:T(8,128)S(1)} %reduction_step.12.refs_0_), channel_id=1, source_target_pairs={{0,16},{1,9},{8,24},{9,1},{16,0},{17,25},{24,8},{25,17},{2,18},{3,... | collective-permute-start | bytes 1572872 | tf_op jit(solution)/shard_map/ppermute | solution.py:882
  337.3 27.5 %collective-permute-start.49 = (f32[320,512]{1,0:T(8,128)S(1)}, f32[320,512]{1,0:T(8,128)S(1)}, u32[]{:S(2)}, u32[]{:S(2)}) collective-permute-start(f32[320,512]{1,0:T(8,128)S(1)} %copy-done.25), channel_id=1, source_target_pairs={{0,2},{2,0},{1,3},{3,1},{4,6},{6,4},{5,7},{7,5},{8,10},{10,8},{9,1... | collective-permute-start | bytes 1966088 | tf_op jit(solution)/shard_map/ppermute | solution.py:29
  338.0 16.9 %collective-permute-start.48 = (f32[64,2048]{1,0:T(8,128)S(1)}, f32[64,2048]{1,0:T(8,128)S(1)}, u32[]{:S(2)}, u32[]{:S(2)}) collective-permute-start(f32[64,2048]{1,0:T(8,128)S(1)} %get-tuple-element.228), channel_id=1, source_target_pairs={{0,16},{1,9},{8,24},{9,1},{16,0},{17,25},{24,8},{25,17},{2,18},{3,... | collective-permute-start | bytes 1572872 | tf_op jit(solution)/shard_map/ppermute | solution.py:882
  338.8 26.1 %collective-permute-start.54 = (f32[64,2048]{1,0:T(8,128)S(1)}, f32[64,2048]{1,0:T(8,128)S(1)}, u32[]{:S(2)}, u32[]{:S(2)}) collective-permute-start(f32[64,2048]{1,0:T(8,128)S(1)} %reduction_step.11), channel_id=1, source_target_pairs={{0,4},{4,0},{1,5},{5,1},{2,6},{6,2},{3,7},{7,3},{8,12},{12,8},{9,1... | collective-permute-start | bytes 1572872 | tf_op jit(solution)/shard_map/ppermute | solution.py:960
  350.0 14.9 %collective-permute-start.59 = (f32[64,2048]{1,0:T(8,128)S(1)}, f32[64,2048]{1,0:T(8,128)S(1)}, u32[]{:S(2)}, u32[]{:S(2)}) collective-permute-start(f32[64,2048]{1,0:T(8,128)S(1)} %collective-permute-done.58.refs_2_), channel_id=1, source_target_pairs={{0,16},{1,9},{8,24},{9,1},{16,0},{17,25},{24,8},{25,17},{2,18},{3,... | collective-permute-start | bytes 1572872 | tf_op jit(solution)/shard_map/ppermute | solution.py:882
  365.0 13.5 %collective-permute-start.61 = (f32[64,2048]{1,0:T(8,128)S(1)}, f32[64,2048]{1,0:T(8,128)S(1)}, u32[]{:S(2)}, u32[]{:S(2)}) collective-permute-start(f32[64,2048]{1,0:T(8,128)S(1)} %reduction_step.13.refs_0_), channel_id=1, source_target_pairs={{0,8},{1,17},{8,0},{9,25},{16,24},{17,1},{24,16},{25,9},{2,10},{3,... | collective-permute-start | bytes 1572872 | tf_op jit(solution)/shard_map/ppermute | solution.py:882
  366.1 12.5 %collective-permute-start.60 = (f32[64,2048]{1,0:T(8,128)S(1)}, f32[64,2048]{1,0:T(8,128)S(1)}, u32[]{:S(2)}, u32[]{:S(2)}) collective-permute-start(f32[64,2048]{1,0:T(8,128)S(1)} %reduction_step.13.refs_0_), channel_id=1, source_target_pairs={{0,16},{1,9},{8,24},{9,1},{16,0},{17,25},{24,8},{25,17},{2,18},{3,... | collective-permute-start | bytes 1572872 | tf_op jit(solution)/shard_map/ppermute | solution.py:882
  367.1 15.7 %collective-permute-start.55 = (f32[320,256]{1,0:T(8,128)S(1)}, f32[320,256]{1,0:T(8,128)S(1)}, u32[]{:S(2)}, u32[]{:S(2)}) collective-permute-start(f32[320,256]{1,0:T(8,128)S(1)} %copy-done.26), channel_id=1, source_target_pairs={{0,4},{4,0},{1,5},{5,1},{2,6},{6,2},{3,7},{7,3},{8,12},{12,8},{9,1... | collective-permute-start | bytes 983048 | tf_op jit(solution)/shard_map/ppermute | solution.py:960
  378.5 9.2 %collective-permute-start.62 = (f32[64,2048]{1,0:T(8,128)S(1)}, f32[64,2048]{1,0:T(8,128)S(1)}, u32[]{:S(2)}, u32[]{:S(2)}) collective-permute-start(f32[64,2048]{1,0:T(8,128)S(1)} %collective-permute-done.61.refs_2_), channel_id=1, source_target_pairs={{0,16},{1,9},{8,24},{9,1},{16,0},{17,25},{24,8},{25,17},{2,18},{3,... | collective-permute-start | bytes 1572872 | tf_op jit(solution)/shard_map/ppermute | solution.py:882
  (44 other events, 371.8 us)

commit v4 on v3

--- a/solution.py
+++ b/solution.py
@@ -984,9 +984,9 @@
     away = over_h(away)
     other_close = swap_half(close)
     up_close, up_away = pack(place, after(grad_out, close), frames, waits=True)
-    share = after(share, up_close, valid, near, other_close)
+    share = after(share, up_close, valid, near)
     pieces = four_of_plane(share)
-    away = after(away, pieces[1:])
+    away = after(away, pieces[1:], other_close)
     half_weights = [[weights, near, *pieces, *map(over_c, after(pieces, away))]]
     own = four_of(after(close, away), away)
     other_away = swap_half(away)

time: 392 us -> 389 us (level)
  waiting for transfers between devices: 119 us -> 114 us
    ppermute x7, waiting for transfers between devices: 44.4 us -> 38.3 us  [over_h(): return lax.ppermute(array, 'h', FLIP2)]
  transfers between devices with their start and end apart: 63 -> 63, of which waited for: 29 -> 27; matrix products, arithmetic and copies ran while one was open for 1% -> 1% of each run, Pallas kernels for 37% -> 37%
where the time goes in v4:
time: 389 us; the launch traced here: 387 us
  Pallas kernels  153 us (39%)
  waiting for transfers between devices  114 us (29%)
  blocking collectives  62.8 us (16%)
  starting transfers between devices  46.7 us (12%)
  local copies, waits for them, and re-layouts  7.14 us (2%)
    all_gather x8, blocking collectives, gather(): return lax.all_gather(array, axes, tiled=True)  62.8 us
    ppermute x7, waiting for transfers between devices, over_h(): return lax.ppermute(array, 'h', FLIP2)  38.3 us
    pallas_call x5, Pallas kernels, project(): call(partial(project_body, len(parts), len(flat), spots, len(weights), 0...  35.9 us
    ppermute x13, waiting for transfers between devices, plane_swap(): return lax.ppermute(array, ('y', 'x', 'c'), pairs)  27.5 us
    pallas_call x4, Pallas kernels, weight_rows(): call(partial(weight_body, turn), grid_spec=pltpu.PrefetchScalarGridSpec(n...  26.5 us
    ppermute x6, waiting for transfers between devices, swap_half(): return lax.ppermute(array, 'l', FLIP2)  25.1 us
    pallas_call x2, Pallas kernels, norm_back(): call(partial(norm_back_body, len(z), split_terms, layer), grid_spec=pltpu...  15.3 us
    pallas_call x4, Pallas kernels, prepare(): call(prepare_body, grid_spec=pltpu.PrefetchScalarGridSpec(num_scalar_pref...  15.1 us
  transfers between devices with their start and end apart: 63, of which 27 were waited for; matrix products, arithmetic and copies ran while one was open for 1% of the time, Pallas kernels for 37%

profile of v4, /device:TPU:0, one launch (start us, length us, event | category | flops | bytes accessed | tf_op | source)
XLA Modules:
  0.0 387.0 jit_solution(1610710475115107642)
XLA Ops:
  3.2 3.6 collective-permute-start.1
  10.7 2.9 pack.3
  15.6 15.5 %collective-permute-done.1.refs_12_.refs_8_.refs_7_.refs_4_ = f32[64,2048]{1,0:T(8,128)} collective-permute-done((f32[64,2048]{1,0:T(8,128)S(1)}, f32[64,2048]{1,0:T(8,128)}, u32[]{:S(2)}, u32[]{:S(2)}) %collective-permute-start.1) | collective-permute-done | bytes 524320 | tf_op jit(solution)/shard_map/ppermute | solution.py:960
  31.2 2.8 collective-permute-start.5
  34.7 5.0 %collective-permute-done.6.refs_4_.refs_2_ = f32[640,256]{1,0:T(8,128)S(1)} collective-permute-done((f32[640,256]{1,0:T(8,128)S(1)}, f32[640,256]{1,0:T(8,128)S(1)}, u32[]{:S(2)}, u32[]{:S(2)}) %collective-permute-start.6) | collective-permute-done | bytes 655392 | tf_op jit(solution)/shard_map/ppermute | solution.py:29
  39.7 19.1 %collective-permute-done.refs_2_.refs_8_ = f32[640,256]{1,0:T(8,128)S(1)} collective-permute-done((f32[640,256]{1,0:T(8,128)S(1)}, f32[640,256]{1,0:T(8,128)S(1)}, u32[]{:S(2)}, u32[]{:S(2)}) %collective-permute-start) | collective-permute-done | bytes 655392 | tf_op jit(solution)/shard_map/ppermute | solution.py:960
  65.3 9.9 %project.5 = (f32[320,1024]{1,0:T(8,128)}, f32[320,1024]{1,0:T(8,128)}) custom-call(s32[6]{0:T(128)S(1)} %concatenate.11.cols_ref, s32[8]{0:T(128)S(1)} %stack.124.place_ref, f32[640,256]{1,0:T(8,128)S(1)} %get-tuple-element.137.refs_0_.refs_6_, f32[640,256]{1,0:T(8,128)} %collective-permute-done.8.refs_1_.refs_7_, ...), custom_call_target="tpu_custom_call" | custom-call | flops 47185920 | bytes 98304 | tf_op jit(solution)/shard_map/project/pallas_call | solution.py:289
  78.7 6.0 %project.6 = (f32[320,1024]{1,0:T(8,128)}, f32[5,8,128]{2,1,0:T(8,128)S(1)}, f32[320,1024]{1,0:T(8,128)}) custom-call(s32[2]{0:T(128)S(1)} %pad_add_fusion.1.cols_ref, s32[8]{0:T(128)S(1)} %stack.124.place_ref, f32[640,256]{1,0:T(8,128)S(1)} %collective-permute-done.7.refs_0_.refs_4_, f32[640,256]{1,0:T(8,128)S(1)} %collective-permute-done.15.refs_1_.refs_5_, ...), custom_call_target="tpu_custom_call" | custom-call | flops 15728640 | bytes 32768 | tf_op jit(solution)/shard_map/project/pallas_call | solution.py:289
  85.3 6.2 %all_gather.24 = f32[20,8,128]{2,1,0:T(8,128)S(1)} all-gather(f32[5,8,128]{2,1,0:T(8,128)S(1)} %get-tuple-element.145), channel_id=1, replica_groups=mesh['y'=2,'x'=2,'h'=2,'l'=2,'c'=2] {'h','c'}, dimensions={0}, use_global_device_ids=true | all-gather | bytes 102400 | tf_op jit(solution)/shard_map/all_gather | solution.py:999
  93.8 9.3 %all_gather.25.refs_1_.refs_3_ = f32[80,8,128]{2,1,0:T(8,128)S(1)} all-gather(f32[20,8,128]{2,1,0:T(8,128)S(1)} %all_gather.24), channel_id=1, replica_groups=mesh['y'=2,'x'=2,'h'=2,'l'=2,'c'=2] {'y','x'}, dimensions={0}, use_global_device_ids=true | all-gather | bytes 409600 | tf_op jit(solution)/shard_map/all_gather | solution.py:999
  103.1 7.3 %recur.2 = (f32[320,1024]{1,0:T(8,128)S(1)}, f32[320,1024]{1,0:T(8,128)}, f32[320,1024]{1,0:T(8,128)}, f32[6,8,128]{2,1,0:T(8,128)S(1)}) custom-call(s32[8]{0:T(128)S(1)} %stack.124.place_ref, f32[320]{0:T(512)S(1)} %fusion.6.gate_ref, f32[320,1024]{1,0:T(8,128)} %get-tuple-element.144.refs_0_, f32[80,8,128]{2,1,0:T(8,128)S(1)} %all_gather.25.refs_1_.refs_3_, ...), custom_call_target="tpu_custom_call" | custom-call | flops 512000 | bytes 102400 | tf_op jit(solution)/shard_map/recur/pallas_call | solution.py:435
  112.2 5.4 %collective-permute-done.20 = f32[64,2048]{1,0:T(8,128)S(1)} collective-permute-done((f32[64,2048]{1,0:T(8,128)S(1)}, f32[64,2048]{1,0:T(8,128)S(1)}, u32[]{:S(2)}, u32[]{:S(2)}) %collective-permute-start.20) | collective-permute-done | bytes 524320 | tf_op jit(solution)/shard_map/ppermute | solution.py:1019
  124.4 3.8 prepare.4
  128.1 3.8 prepare.5
  131.9 5.2 %project.7.refs_3_ = f32[320,512]{1,0:T(8,128)} custom-call(s32[4]{0:T(128)S(1)} %pad_add_fusion.2.cols_ref, s32[8]{0:T(128)S(1)} %stack.124.place_ref, f32[320,1024]{1,0:T(8,128)S(1)} %get-tuple-element.160.refs_0_.own_ref.refs_5_, f32[2,256,2048]{2,1,0:T(8,128)} %refs_2_.1, ...), custom_call_target="tpu_custom_call" | custom-call | flops 15728640 | bytes 32768 | tf_op jit(solution)/shard_map/project/pallas_call | solution.py:289
  137.1 3.8 prepare.6
  140.9 5.1 %collective-permute-done.16.refs_0_.refs_1_.own_ref = f32[320,1024]{1,0:T(8,128)S(1)} collective-permute-done((f32[320,1024]{1,0:T(8,128)S(1)}, f32[320,1024]{1,0:T(8,128)S(1)}, u32[]{:S(2)}, u32[]{:S(2)}) %collective-permute-start.16) | collective-permute-done | bytes 1310752 | tf_op jit(solution)/shard_map/ppermute | solution.py:29
  148.6 5.7 %project.8 = (f32[320,512]{1,0:T(8,128)}, f32[3,8,128]{2,1,0:T(8,128)S(1)}) custom-call(s32[4]{0:T(128)S(1)} %pad_add_fusion.cols_ref, s32[8]{0:T(128)S(1)} %stack.124.place_ref, f32[320,1024]{1,0:T(8,128)S(1)} %collective-permute-done.16.refs_0_.refs_1_.own_ref, f32[2,256,2048]{2,1,0:T(8,128)} %refs_2_.1, ...), custom_call_target="tpu_custom_call" | custom-call | flops 15728640 | bytes 32768 | tf_op jit(solution)/shard_map/project/pallas_call | solution.py:289
  154.4 9.2 %project.9 = (f32[320,512]{1,0:T(8,128)}, f32[3,8,128]{2,1,0:T(8,128)S(1)}) custom-call(s32[8]{0:T(128)S(1)} %concatenate.12.cols_ref, s32[8]{0:T(128)S(1)} %stack.124.place_ref, f32[320,1024]{1,0:T(8,128)S(1)} %copy-done.1, f32[320,1024]{1,0:T(8,128)S(1)} %collective-permute-done.16.refs_0_.refs_1_.own_ref, ...), custom_call_target="tpu_custom_call" | custom-call | flops 31457280 | bytes 65536 | tf_op jit(solution)/shard_map/project/pallas_call | solution.py:289
  163.6 8.2 %all_gather.26 = f32[12,8,128]{2,1,0:T(8,128)S(1)} all-gather(f32[3,8,128]{2,1,0:T(8,128)S(1)} %get-tuple-element.168), channel_id=1, replica_groups=mesh['y'=2,'x'=2,'h'=2,'l'=2,'c'=2] {'y','x'}, dimensions={0}, use_global_device_ids=true | all-gather | bytes 61440 | tf_op jit(solution)/shard_map/all_gather | solution.py:999
  171.8 9.0 %all_gather.27.refs_2_.refs_4_ = f32[48,8,128]{2,1,0:T(8,128)S(1)} all-gather(f32[12,8,128]{2,1,0:T(8,128)S(1)} %all_gather.26), channel_id=1, replica_groups=mesh['y'=2,'x'=2,'h'=2,'l'=2,'c'=2] {'h','c'}, dimensions={0}, use_global_device_ids=true | all-gather | bytes 245760 | tf_op jit(solution)/shard_map/all_gather | solution.py:999
  181.2 7.4 %recur.3 = (f32[320,256]{1,0:T(8,128)}, f32[320,256]{1,0:T(8,128)}, f32[320,256]{1,0:T(8,128)}, f32[320,256]{1,0:T(8,128)}, f32[320,1024]{1,0:T(8,128)}, /*index=5*/f32[320,1024]{1,0:T(8,128)}) custom-call(s32[8]{0:T(128)S(1)} %stack.124.place_ref, f32[320]{0:T(512)S(1)} %fusion.6.gate_ref, f32[320,512]{1,0:T(8,128)} %get-tuple-element.156.refs_0_, ...), custom_call_target="tpu_custom_call" | custom-call | flops 512000 | bytes 102400 | tf_op jit(solution)/shard_map/recur/pallas_call | solution.py:435
  189.0 5.6 %back.2 = (f32[320,1024]{1,0:T(8,128)S(1)}, f32[3,8,128]{2,1,0:T(8,128)S(1)}) custom-call(s32[8]{0:T(128)S(1)} %stack.124.place_ref, f32[320]{0:T(512)S(1)} %fusion.6.gate_ref, f32[320,512]{1,0:T(8,128)} %get-tuple-element.156.refs_0_, f32[320,512]{1,0:T(8,128)} %get-tuple-element.167.refs_1_, f32[48,8,128]{2,1,0:T(8,128)S(1)} %all_gather.27.refs_2_.refs_4_, ...), custom_call_target="tpu_custom_call" | custom-call | flops 153600 | bytes 102400 | tf_op jit(solution)/shard_map/back/pallas_call | solution.py:542
  194.6 8.3 %all_gather.28 = f32[12,8,128]{2,1,0:T(8,128)S(1)} all-gather(f32[3,8,128]{2,1,0:T(8,128)S(1)} %get-tuple-element.177), channel_id=1, replica_groups=mesh['y'=2,'x'=2,'h'=2,'l'=2,'c'=2] {'y','x'}, dimensions={0}, use_global_device_ids=true | all-gather | bytes 61440 | tf_op jit(solution)/shard_map/all_gather | solution.py:999
  202.9 6.8 %all_gather.29.refs_5_ = f32[48,8,128]{2,1,0:T(8,128)S(1)} all-gather(f32[12,8,128]{2,1,0:T(8,128)S(1)} %all_gather.28), channel_id=1, replica_groups=mesh['y'=2,'x'=2,'h'=2,'l'=2,'c'=2] {'h','c'}, dimensions={0}, use_global_device_ids=true | all-gather | bytes 245760 | tf_op jit(solution)/shard_map/all_gather | solution.py:999
  209.7 7.7 %norm_back.2 = (f32[320,1024]{1,0:T(8,128)}, f32[320,512]{1,0:T(8,128)S(1)}, f32[320,1024]{1,0:T(8,128)}, f32[3,8,128]{2,1,0:T(8,128)S(1)}) custom-call(s32[2]{0:T(128)S(1)} %pad_add_fusion.4.cols_ref, s32[8]{0:T(128)S(1)} %stack.124.place_ref, f32[320,1024]{1,0:T(8,128)S(1)} %get-tuple-element.176.grad_ref, f32[320,512]{1,0:T(8,128)} %get-tuple-element.156.refs_0_, ...), custom_call_target="tpu_custom_call" | custom-call | flops 31457280 | bytes 65536 | tf_op jit(solution)/shard_map/norm_back/pallas_call | solution.py:647
  220.3 3.8 prepare.7
  224.8 7.2 %weight_rows.4 = (f32[2,2,64,1024]{3,2,1,0:T(8,128)}, f32[2,2,64,1024]{3,2,1,0:T(8,128)}, bf16[512,768]{1,0:T(8,128)(2,1)S(1)}, bf16[512,768]{1,0:T(8,128)(2,1)S(1)}) custom-call(s32[8]{0:T(128)S(1)} %stack.124.place_ref, f32[320,1024]{1,0:T(8,128)} %get-tuple-element.191.refs_0_.grad_ref, f32[320,512]{1,0:T(8,128)S(1)} %collective-permute-done.32.refs_1_, ...), custom_call_target="tpu_custom_call" | custom-call | flops 37748736 | bytes 32768 | tf_op jit(solution)/shard_map/weight_rows/pallas_call | solution.py:820
  233.4 6.1 %weight_rows.5 = (f32[2,2,64,1024]{3,2,1,0:T(8,128)}, f32[2,2,64,1024]{3,2,1,0:T(8,128)}) custom-call(s32[8]{0:T(128)S(1)} %stack.124.place_ref, bf16[512,768]{1,0:T(8,128)(2,1)S(1)} %get-tuple-element.187.refs_0_, bf16[512,768]{1,0:T(8,128)(2,1)S(1)} %get-tuple-element.188.refs_1_, bf16[768,1024]{1,0:T(8,128)(2,1)} %get-tuple-element.184.refs_2_, ...), custom_call_target="tpu_custom_call" | custom-call | flops 37748736 | bytes 32768 | tf_op jit(solution)/shard_map/weight_rows/pallas_call | solution.py:820
  240.2 6.1 %own_terms.2.refs_3_.refs_0_ = f32[320,1024]{1,0:T(8,128)S(1)} custom-call(s32[2]{0:T(128)S(1)} %pad_add_fusion.5.cols_ref, s32[8]{0:T(128)S(1)} %stack.124.place_ref, f32[320,1024]{1,0:T(8,128)} %get-tuple-element.191.refs_0_.grad_ref, f32[640,256]{1,0:T(8,128)S(1)} %copy-done.6, f32[640,256]{1,0:T(8,128)} %collective-permute-done.29.refs_5_.refs_1_, ...), custom_call_target="tpu_custom_call" | custom-call | flops 31457280 | bytes 65536 | tf_op jit(solution)/shard_map/own_terms/pallas_call | solution.py:705
  246.7 3.1 collective-permute-done.36.refs_4_.refs_1_
  249.8 5.9 %back.3 = (f32[320,1024]{1,0:T(8,128)S(1)}, f32[3,8,128]{2,1,0:T(8,128)S(1)}) custom-call(s32[8]{0:T(128)S(1)} %stack.124.place_ref, f32[320]{0:T(512)S(1)} %fusion.6.gate_ref, f32[320,1024]{1,0:T(8,128)} %get-tuple-element.144.refs_0_, f32[80,8,128]{2,1,0:T(8,128)S(1)} %all_gather.25.refs_1_.refs_3_, ...), custom_call_target="tpu_custom_call" | custom-call | flops 153600 | bytes 102400 | tf_op jit(solution)/shard_map/back/pallas_call | solution.py:542
  255.7 8.2 %all_gather.30 = f32[12,8,128]{2,1,0:T(8,128)S(1)} all-gather(f32[3,8,128]{2,1,0:T(8,128)S(1)} %get-tuple-element.195), channel_id=1, replica_groups=mesh['y'=2,'x'=2,'h'=2,'l'=2,'c'=2] {'y','x'}, dimensions={0}, use_global_device_ids=true | all-gather | bytes 61440 | tf_op jit(solution)/shard_map/all_gather | solution.py:999
  269.0 6.7 %all_gather.31.refs_4_ = f32[48,8,128]{2,1,0:T(8,128)S(1)} all-gather(f32[12,8,128]{2,1,0:T(8,128)S(1)} %all_gather.30), channel_id=1, replica_groups=mesh['y'=2,'x'=2,'h'=2,'l'=2,'c'=2] {'h','c'}, dimensions={0}, use_global_device_ids=true | all-gather | bytes 245760 | tf_op jit(solution)/shard_map/all_gather | solution.py:999
  275.8 7.6 %norm_back.3 = (f32[320,1024]{1,0:T(8,128)}, f32[320,512]{1,0:T(8,128)S(1)}, f32[320,512]{1,0:T(8,128)}, f32[320,512]{1,0:T(8,128)S(1)}, f32[3,8,128]{2,1,0:T(8,128)S(1)}) custom-call(s32[2]{0:T(128)S(1)} %pad_add_fusion.4.cols_ref, s32[8]{0:T(128)S(1)} %stack.124.place_ref, f32[320,1024]{1,0:T(8,128)S(1)} %get-tuple-element.194.grad_ref, ...), custom_call_target="tpu_custom_call" | custom-call | flops 31457280 | bytes 65536 | tf_op jit(solution)/shard_map/norm_back/pallas_call | solution.py:647
  286.7 7.2 %weight_rows.6 = (f32[2,2,64,1024]{3,2,1,0:T(8,128)}, f32[2,2,64,1024]{3,2,1,0:T(8,128)}, bf16[512,768]{1,0:T(8,128)(2,1)S(1)}, bf16[512,768]{1,0:T(8,128)(2,1)S(1)}) custom-call(s32[8]{0:T(128)S(1)} %stack.124.place_ref, f32[320,1024]{1,0:T(8,128)} %get-tuple-element.221.refs_0_.grad_ref, f32[320,512]{1,0:T(8,128)S(1)} %collective-permute-done.41.refs_1_, ...), custom_call_target="tpu_custom_call" | custom-call | flops 37748736 | bytes 32768 | tf_op jit(solution)/shard_map/weight_rows/pallas_call | solution.py:820
  295.3 6.1 %weight_rows.7 = (f32[2,2,64,1024]{3,2,1,0:T(8,128)}, f32[2,2,64,1024]{3,2,1,0:T(8,128)}) custom-call(s32[8]{0:T(128)S(1)} %stack.124.place_ref, bf16[512,768]{1,0:T(8,128)(2,1)S(1)} %get-tuple-element.217.refs_0_, bf16[512,768]{1,0:T(8,128)(2,1)S(1)} %get-tuple-element.218.refs_1_, bf16[768,1024]{1,0:T(8,128)(2,1)} %get-tuple-element.154.refs_2_, ...), custom_call_target="tpu_custom_call" | custom-call | flops 37748736 | bytes 32768 | tf_op jit(solution)/shard_map/weight_rows/pallas_call | solution.py:820
  302.0 6.0 %own_terms.3.kept_ref = f32[320,1024]{1,0:T(8,128)S(1)} custom-call(s32[2]{0:T(128)S(1)} %pad_add_fusion.5.cols_ref, s32[8]{0:T(128)S(1)} %stack.124.place_ref, f32[320,1024]{1,0:T(8,128)} %get-tuple-element.221.refs_0_.grad_ref, f32[320,1024]{1,0:T(8,128)S(1)} %own_terms.2.refs_3_.refs_0_, f32[320,1024]{1,0:T(8,128)S(1)} %copy-done.4, ...), custom_call_target="tpu_custom_call" | custom-call | flops 31457280 | bytes 65536 | tf_op jit(solution)/shard_map/own_terms/pallas_call | solution.py:705
  308.1 3.6 collective-permute-done.45.come_ref
  314.9 5.3 %collective-permute-done.47.refs_3_ = f32[2,2,64,1024]{3,2,1,0:T(8,128)S(1)} collective-permute-done((f32[2,2,64,1024]{3,2,1,0:T(8,128)}, f32[2,2,64,1024]{3,2,1,0:T(8,128)S(1)}, u32[]{:S(2)}, u32[]{:S(2)}) %collective-permute-start.47) | collective-permute-done | bytes 1048608 | tf_op jit(solution)/shard_map/ppermute | solution.py:882
  323.4 7.2 %collective-permute-done.51 = f32[320,256]{1,0:T(8,128)S(1)} collective-permute-done((f32[320,256]{1,0:T(8,128)}, f32[320,256]{1,0:T(8,128)S(1)}, u32[]{:S(2)}, u32[]{:S(2)}) %collective-permute-start.51) | collective-permute-done | bytes 327712 | tf_op jit(solution)/shard_map/ppermute | solution.py:1108
  337.4 9.7 %collective-permute-done.58.refs_2_ = f32[64,2048]{1,0:T(8,128)S(1)} collective-permute-done((f32[64,2048]{1,0:T(8,128)S(1)}, f32[64,2048]{1,0:T(8,128)S(1)}, u32[]{:S(2)}, u32[]{:S(2)}) %collective-permute-start.58) | collective-permute-done | bytes 524320 | tf_op jit(solution)/shard_map/ppermute | solution.py:882
  347.3 4.6 %collective-permute-done.48.refs_1_ = f32[64,2048]{1,0:T(8,128)S(1)} collective-permute-done((f32[64,2048]{1,0:T(8,128)S(1)}, f32[64,2048]{1,0:T(8,128)S(1)}, u32[]{:S(2)}, u32[]{:S(2)}) %collective-permute-start.48) | collective-permute-done | bytes 524320 | tf_op jit(solution)/shard_map/ppermute | solution.py:882
  352.0 2.8 unpack.2
  354.9 7.0 %collective-permute-done.49.come_ref = f32[320,512]{1,0:T(8,128)S(1)} collective-permute-done((f32[320,512]{1,0:T(8,128)S(1)}, f32[320,512]{1,0:T(8,128)S(1)}, u32[]{:S(2)}, u32[]{:S(2)}) %collective-permute-start.49) | collective-permute-done | bytes 655392 | tf_op jit(solution)/shard_map/ppermute | solution.py:29
  365.2 3.0 assemble.2.refs_4_
  368.2 7.0 %collective-permute-done.61.refs_2_ = f32[64,2048]{1,0:T(8,128)S(1)} collective-permute-done((f32[64,2048]{1,0:T(8,128)S(1)}, f32[64,2048]{1,0:T(8,128)S(1)}, u32[]{:S(2)}, u32[]{:S(2)}) %collective-permute-start.61) | collective-permute-done | bytes 524320 | tf_op jit(solution)/shard_map/ppermute | solution.py:882
  376.5 3.3 collective-permute-done.55
  (204 shorter events, 76.1 us)
Async XLA Ops:
  0.6 30.4 %collective-permute-start.2 = (f32[2,256,2048]{2,1,0:T(8,128)}, f32[2,256,2048]{2,1,0:T(8,128)}, u32[]{:S(2)}, u32[]{:S(2)}) collective-permute-start(f32[2,256,2048]{2,1,0:T(8,128)} %refs_2_.1), channel_id=1, source_target_pairs={{0,1},{1,0},{2,3},{3,2},{4,5},{5,4},{6,7},{7,6},{8,9},{9,8},{10,11... | collective-permute-start | bytes 12582920 | tf_op jit(solution)/shard_map/ppermute | solution.py:963
  3.2 27.8 %collective-permute-start.1 = (f32[64,2048]{1,0:T(8,128)S(1)}, f32[64,2048]{1,0:T(8,128)}, u32[]{:S(2)}, u32[]{:S(2)}) collective-permute-start(f32[64,2048]{1,0:T(8,128)S(1)} %get-tuple-element.254), channel_id=1, source_target_pairs={{0,4},{4,0},{1,5},{5,1},{2,6},{6,2},{3,7},{7,3},{8,12},{12,8},{9,1... | collective-permute-start | bytes 1572872 | tf_op jit(solution)/shard_map/ppermute | solution.py:960
  8.8 30.9 %collective-permute-start.6 = (f32[640,256]{1,0:T(8,128)S(1)}, f32[640,256]{1,0:T(8,128)S(1)}, u32[]{:S(2)}, u32[]{:S(2)}) collective-permute-start(f32[640,256]{1,0:T(8,128)S(1)} %get-tuple-element.137.refs_0_.refs_6_), channel_id=1, source_target_pairs={{0,2},{2,0},{1,3},{3,1},{4,6},{6,4},{5,7},{7,5},{8,10},{10,8},{9,1... | collective-permute-start | bytes 1966088 | tf_op jit(solution)/shard_map/ppermute | solution.py:29
  10.4 48.4 %collective-permute-start = (f32[640,256]{1,0:T(8,128)S(1)}, f32[640,256]{1,0:T(8,128)S(1)}, u32[]{:S(2)}, u32[]{:S(2)}) collective-permute-start(f32[640,256]{1,0:T(8,128)S(1)} %get-tuple-element.131), channel_id=1, source_target_pairs={{0,4},{4,0},{1,5},{5,1},{2,6},{6,2},{3,7},{7,3},{8,12},{12,8},{9,1... | collective-permute-start | bytes 1966088 | tf_op jit(solution)/shard_map/ppermute | solution.py:960
  31.2 27.6 %collective-permute-start.5 = (f32[64,2048]{1,0:T(8,128)}, f32[64,2048]{1,0:T(8,128)}, u32[]{:S(2)}, u32[]{:S(2)}) collective-permute-start(f32[64,2048]{1,0:T(8,128)} %collective-permute-done.1.refs_12_.refs_8_.refs_7_.refs_4_), channel_id=1, source_target_pairs={{0,24},{8,16},{16,8},{24,0},{1,25},{9,17},{17,9},{25,1},{2,26},{10... | collective-permute-start | bytes 1572872 | tf_op jit(solution)/shard_map/ppermute | solution.py:977
  33.9 24.8 %collective-permute-start.4 = (f32[64,2048]{1,0:T(8,128)}, f32[64,2048]{1,0:T(8,128)}, u32[]{:S(2)}, u32[]{:S(2)}) collective-permute-start(f32[64,2048]{1,0:T(8,128)} %collective-permute-done.1.refs_12_.refs_8_.refs_7_.refs_4_), channel_id=1, source_target_pairs={{0,16},{16,0},{1,17},{17,1},{2,18},{18,2},{3,19},{19,3},{4,20},{20... | collective-permute-start | bytes 1572872 | tf_op jit(solution)/shard_map/ppermute | solution.py:978
  34.5 24.3 %collective-permute-start.3 = (f32[64,2048]{1,0:T(8,128)}, f32[64,2048]{1,0:T(8,128)S(1)}, u32[]{:S(2)}, u32[]{:S(2)}) collective-permute-start(f32[64,2048]{1,0:T(8,128)} %collective-permute-done.1.refs_12_.refs_8_.refs_7_.refs_4_), channel_id=1, source_target_pairs={{0,8},{8,0},{1,9},{9,1},{2,10},{10,2},{3,11},{11,3},{4,12},{12,4},... | collective-permute-start | bytes 1572872 | tf_op jit(solution)/shard_map/ppermute | solution.py:978
  39.7 20.2 %collective-permute-start.10 = (f32[640,256]{1,0:T(8,128)S(1)}, f32[640,256]{1,0:T(8,128)S(1)}, u32[]{:S(2)}, u32[]{:S(2)}) collective-permute-start(f32[640,256]{1,0:T(8,128)S(1)} %collective-permute-done.6.refs_4_.refs_2_), channel_id=1, source_target_pairs={{0,1},{1,0},{2,3},{3,2},{4,5},{5,4},{6,7},{7,6},{8,9},{9,8},{10,11... | collective-permute-start | bytes 1966088 | tf_op jit(solution)/shard_map/ppermute | solution.py:963
  59.9 16.7 %collective-permute-start.7 = (f32[640,256]{1,0:T(8,128)S(1)}, f32[640,256]{1,0:T(8,128)S(1)}, u32[]{:S(2)}, u32[]{:S(2)}) collective-permute-start(f32[640,256]{1,0:T(8,128)S(1)} %collective-permute-done.refs_2_.refs_8_), channel_id=1, source_target_pairs={{0,2},{2,0},{1,3},{3,1},{4,6},{6,4},{5,7},{7,5},{8,10},{10,8},{9,1... | collective-permute-start | bytes 1966088 | tf_op jit(solution)/shard_map/ppermute | solution.py:29
  84.8 34.8 %collective-permute-start.18 = (f32[320,1024]{1,0:T(8,128)S(1)}, f32[320,1024]{1,0:T(8,128)S(1)}, u32[]{:S(2)}, u32[]{:S(2)}) collective-permute-start(f32[320,1024]{1,0:T(8,128)S(1)} %copy-done.11), channel_id=1, source_target_pairs={{0,1},{1,0},{2,3},{3,2},{4,5},{5,4},{6,7},{7,6},{8,9},{9,8},{10,11... | collective-permute-start | bytes 3932168 | tf_op jit(solution)/shard_map/ppermute | solution.py:963
  85.0 35.7 %collective-permute-start.19 = (f32[320,1024]{1,0:T(8,128)}, f32[320,1024]{1,0:T(8,128)}, u32[]{:S(2)}, u32[]{:S(2)}) collective-permute-start(f32[320,1024]{1,0:T(8,128)} %get-tuple-element.153.own_ref), channel_id=1, source_target_pairs={{0,1},{1,0},{2,3},{3,2},{4,5},{5,4},{6,7},{7,6},{8,9},{9,8},{10,11... | collective-permute-start | bytes 3932168 | tf_op jit(solution)/shard_map/ppermute | solution.py:963
  91.5 26.0 %collective-permute-start.20 = (f32[64,2048]{1,0:T(8,128)S(1)}, f32[64,2048]{1,0:T(8,128)S(1)}, u32[]{:S(2)}, u32[]{:S(2)}) collective-permute-start(f32[64,2048]{1,0:T(8,128)S(1)} %copy-done.13), channel_id=1, source_target_pairs={{0,5},{1,4},{4,1},{5,0},{2,7},{3,6},{6,3},{7,2},{8,13},{9,12},{12,... | collective-permute-start | bytes 1572872 | tf_op jit(solution)/shard_map/ppermute | solution.py:1019
  110.4 14.0 %collective-permute-start.17 = (f32[320,1024]{1,0:T(8,128)S(1)}, f32[320,1024]{1,0:T(8,128)}, u32[]{:S(2)}, u32[]{:S(2)}) collective-permute-start(f32[320,1024]{1,0:T(8,128)S(1)} %get-tuple-element.160.refs_0_.own_ref.refs_5_), channel_id=1, source_target_pairs={{0,1},{1,0},{2,3},{3,2},{4,5},{5,4},{6,7},{7,6},{8,9},{9,8},{10,11... | collective-permute-start | bytes 3932168 | tf_op jit(solution)/shard_map/ppermute | solution.py:963
  110.4 35.6 %collective-permute-start.16 = (f32[320,1024]{1,0:T(8,128)S(1)}, f32[320,1024]{1,0:T(8,128)S(1)}, u32[]{:S(2)}, u32[]{:S(2)}) collective-permute-start(f32[320,1024]{1,0:T(8,128)S(1)} %get-tuple-element.160.refs_0_.own_ref.refs_5_), channel_id=1, source_target_pairs={{0,2},{2,0},{1,3},{3,1},{4,6},{6,4},{5,7},{7,5},{8,10},{10,8},{9,1... | collective-permute-start | bytes 3932168 | tf_op jit(solution)/shard_map/ppermute | solution.py:29
  120.7 26.6 %collective-permute-start.24 = (f32[64,2048]{1,0:T(8,128)}, f32[64,2048]{1,0:T(8,128)}, u32[]{:S(2)}, u32[]{:S(2)}) collective-permute-start(f32[64,2048]{1,0:T(8,128)} %collective-permute-done.21.refs_2_.refs_8_.refs_6_), channel_id=1, source_target_pairs={{0,24},{8,16},{16,8},{24,0},{1,25},{9,17},{17,9},{25,1},{2,26},{10... | collective-permute-start | bytes 1572872 | tf_op jit(solution)/shard_map/ppermute | solution.py:977
  123.2 24.1 %collective-permute-start.23 = (f32[64,2048]{1,0:T(8,128)}, f32[64,2048]{1,0:T(8,128)}, u32[]{:S(2)}, u32[]{:S(2)}) collective-permute-start(f32[64,2048]{1,0:T(8,128)} %collective-permute-done.21.refs_2_.refs_8_.refs_6_), channel_id=1, source_target_pairs={{0,16},{16,0},{1,17},{17,1},{2,18},{18,2},{3,19},{19,3},{4,20},{20... | collective-permute-start | bytes 1572872 | tf_op jit(solution)/shard_map/ppermute | solution.py:978
  123.7 23.7 %collective-permute-start.22 = (f32[64,2048]{1,0:T(8,128)}, f32[64,2048]{1,0:T(8,128)}, u32[]{:S(2)}, u32[]{:S(2)}) collective-permute-start(f32[64,2048]{1,0:T(8,128)} %collective-permute-done.21.refs_2_.refs_8_.refs_6_), channel_id=1, source_target_pairs={{0,8},{8,0},{1,9},{9,1},{2,10},{10,2},{3,11},{11,3},{4,12},{12,4},... | collective-permute-start | bytes 1572872 | tf_op jit(solution)/shard_map/ppermute | solution.py:978
  146.0 34.9 %collective-permute-start.30 = (f32[640,256]{1,0:T(8,128)}, f32[640,256]{1,0:T(8,128)}, u32[]{:S(2)}, u32[]{:S(2)}) collective-permute-start(f32[640,256]{1,0:T(8,128)} %get-tuple-element.172), channel_id=1, source_target_pairs={{0,4},{4,0},{1,5},{5,1},{2,6},{6,2},{3,7},{7,3},{8,12},{12,8},{9,1... | collective-permute-start | bytes 1966088 | tf_op jit(solution)/shard_map/ppermute | solution.py:960
  147.4 6.8 %collective-permute-start.25 = (f32[64,2048]{1,0:T(8,128)}, f32[64,2048]{1,0:T(8,128)}, u32[]{:S(2)}, u32[]{:S(2)}) collective-permute-start(f32[64,2048]{1,0:T(8,128)} %collective-permute-done.21.refs_2_.refs_8_.refs_6_), channel_id=1, source_target_pairs={{0,1},{1,0},{2,3},{3,2},{4,5},{5,4},{6,7},{7,6},{8,9},{9,8},{10,11... | collective-permute-start | bytes 1572872 | tf_op jit(solution)/shard_map/ppermute | solution.py:963
  147.4 7.0 %collective-permute-start.26 = (f32[64,2048]{1,0:T(8,128)}, f32[64,2048]{1,0:T(8,128)}, u32[]{:S(2)}, u32[]{:S(2)}) collective-permute-start(f32[64,2048]{1,0:T(8,128)} %collective-permute-done.22.refs_3_.refs_9_.refs_7_), channel_id=1, source_target_pairs={{0,1},{1,0},{2,3},{3,2},{4,5},{5,4},{6,7},{7,6},{8,9},{9,8},{10,11... | collective-permute-start | bytes 1572872 | tf_op jit(solution)/shard_map/ppermute | solution.py:963
  147.9 6.5 %collective-permute-start.27 = (f32[64,2048]{1,0:T(8,128)}, f32[64,2048]{1,0:T(8,128)}, u32[]{:S(2)}, u32[]{:S(2)}) collective-permute-start(f32[64,2048]{1,0:T(8,128)} %collective-permute-done.23.refs_4_.refs_10_.refs_8_), channel_id=1, source_target_pairs={{0,1},{1,0},{2,3},{3,2},{4,5},{5,4},{6,7},{7,6},{8,9},{9,8},{10,11... | collective-permute-start | bytes 1572872 | tf_op jit(solution)/shard_map/ppermute | solution.py:963
  154.3 34.7 %collective-permute-start.29 = (f32[640,256]{1,0:T(8,128)S(1)}, f32[640,256]{1,0:T(8,128)}, u32[]{:S(2)}, u32[]{:S(2)}) collective-permute-start(f32[640,256]{1,0:T(8,128)S(1)} %copy-done.5), channel_id=1, source_target_pairs={{0,1},{1,0},{2,3},{3,2},{4,5},{5,4},{6,7},{7,6},{8,9},{9,8},{10,11... | collective-permute-start | bytes 1966088 | tf_op jit(solution)/shard_map/ppermute | solution.py:963
  180.9 8.1 %collective-permute-start.31 = (f32[640,256]{1,0:T(8,128)}, f32[640,256]{1,0:T(8,128)}, u32[]{:S(2)}, u32[]{:S(2)}) collective-permute-start(f32[640,256]{1,0:T(8,128)} %collective-permute-done.30.refs_6_.refs_2_), channel_id=1, source_target_pairs={{0,1},{1,0},{2,3},{3,2},{4,5},{5,4},{6,7},{7,6},{8,9},{9,8},{10,11... | collective-permute-start | bytes 1966088 | tf_op jit(solution)/shard_map/ppermute | solution.py:963
  188.6 31.6 %collective-permute-start.35 = (f32[320,1024]{1,0:T(8,128)S(1)}, f32[320,1024]{1,0:T(8,128)}, u32[]{:S(2)}, u32[]{:S(2)}) collective-permute-start(f32[320,1024]{1,0:T(8,128)S(1)} %collective-permute-done.16.refs_0_.refs_1_.own_ref), channel_id=1, source_target_pairs={{0,1},{1,0},{2,3},{3,2},{4,5},{5,4},{6,7},{7,6},{8,9},{9,8},{10,11... | collective-permute-start | bytes 3932168 | tf_op jit(solution)/shard_map/ppermute | solution.py:963
  188.9 28.9 %collective-permute-start.33 = (f32[320,256]{1,0:T(8,128)}, f32[320,256]{1,0:T(8,128)S(1)}, u32[]{:S(2)}, u32[]{:S(2)}) collective-permute-start(f32[320,256]{1,0:T(8,128)} %get-tuple-element.180), channel_id=1, source_target_pairs={{0,4},{4,0},{1,5},{5,1},{2,6},{6,2},{3,7},{7,3},{8,12},{12,8},{9,1... | collective-permute-start | bytes 983048 | tf_op jit(solution)/shard_map/ppermute | solution.py:960
  217.4 6.6 %collective-permute-start.32 = (f32[320,512]{1,0:T(8,128)S(1)}, f32[320,512]{1,0:T(8,128)S(1)}, u32[]{:S(2)}, u32[]{:S(2)}) collective-permute-start(f32[320,512]{1,0:T(8,128)S(1)} %get-tuple-element.179), channel_id=1, source_target_pairs={{0,1},{1,0},{2,3},{3,2},{4,5},{5,4},{6,7},{7,6},{8,9},{9,8},{10,11... | collective-permute-start | bytes 1966088 | tf_op jit(solution)/shard_map/ppermute | solution.py:963
  218.0 31.8 %collective-permute-start.36 = (f32[320,1024]{1,0:T(8,128)}, f32[320,1024]{1,0:T(8,128)S(1)}, u32[]{:S(2)}, u32[]{:S(2)}) collective-permute-start(f32[320,1024]{1,0:T(8,128)} %get-tuple-element.192), channel_id=1, source_target_pairs={{0,2},{2,0},{1,3},{3,1},{4,6},{6,4},{5,7},{7,5},{8,10},{10,8},{9,1... | collective-permute-start | bytes 3932168 | tf_op jit(solution)/shard_map/ppermute | solution.py:29
  231.9 32.4 %collective-permute-start.37 = (f32[2,2,64,1024]{3,2,1,0:T(8,128)}, f32[2,2,64,1024]{3,2,1,0:T(8,128)}, u32[]{:S(2)}, u32[]{:S(2)}) collective-permute-start(f32[2,2,64,1024]{3,2,1,0:T(8,128)} %get-tuple-element.197), channel_id=1, source_target_pairs={{0,8},{1,17},{8,0},{9,25},{16,24},{17,1},{24,16},{25,9},{2,10},{3,... | collective-permute-start | bytes 3145736 | tf_op jit(solution)/shard_map/ppermute | solution.py:882
  239.5 24.8 %collective-permute-start.40 = (f32[2,2,64,1024]{3,2,1,0:T(8,128)}, f32[2,2,64,1024]{3,2,1,0:T(8,128)}, u32[]{:S(2)}, u32[]{:S(2)}) collective-permute-start(f32[2,2,64,1024]{3,2,1,0:T(8,128)} %get-tuple-element.202), channel_id=1, source_target_pairs={{0,8},{1,17},{8,0},{9,25},{16,24},{17,1},{24,16},{25,9},{2,10},{3,... | collective-permute-start | bytes 3145736 | tf_op jit(solution)/shard_map/ppermute | solution.py:882
  240.1 23.7 %collective-permute-start.39 = (f32[320,256]{1,0:T(8,128)}, f32[320,256]{1,0:T(8,128)S(1)}, u32[]{:S(2)}, u32[]{:S(2)}) collective-permute-start(f32[320,256]{1,0:T(8,128)} %get-tuple-element.200), channel_id=1, source_target_pairs={{0,1},{1,0},{2,3},{3,2},{4,5},{5,4},{6,7},{7,6},{8,9},{9,8},{10,11... | collective-permute-start | bytes 983048 | tf_op jit(solution)/shard_map/ppermute | solution.py:963
  246.3 18.1 %collective-permute-start.38 = (f32[320,256]{1,0:T(8,128)S(1)}, f32[320,256]{1,0:T(8,128)S(1)}, u32[]{:S(2)}, u32[]{:S(2)}) collective-permute-start(f32[320,256]{1,0:T(8,128)S(1)} %copy-done.27), channel_id=1, source_target_pairs={{0,4},{4,0},{1,5},{5,1},{2,6},{6,2},{3,7},{7,3},{8,12},{12,8},{9,1... | collective-permute-start | bytes 983048 | tf_op jit(solution)/shard_map/ppermute | solution.py:960
  267.5 17.3 %collective-permute-start.42 = (f32[2,64,2048]{2,1,0:T(8,128)S(1)}, f32[2,64,2048]{2,1,0:T(8,128)S(1)}, u32[]{:S(2)}, u32[]{:S(2)}) collective-permute-start(f32[2,64,2048]{2,1,0:T(8,128)S(1)} %get-tuple-element.207), channel_id=1, source_target_pairs={{0,16},{1,9},{8,24},{9,1},{16,0},{17,25},{24,8},{25,17},{2,18},{3,... | collective-permute-start | bytes 3145736 | tf_op jit(solution)/shard_map/ppermute | solution.py:882
  283.7 28.0 %collective-permute-start.45 = (f32[320,512]{1,0:T(8,128)S(1)}, f32[320,512]{1,0:T(8,128)S(1)}, u32[]{:S(2)}, u32[]{:S(2)}) collective-permute-start(f32[320,512]{1,0:T(8,128)S(1)} %get-tuple-element.222), channel_id=1, source_target_pairs={{0,2},{2,0},{1,3},{3,1},{4,6},{6,4},{5,7},{7,5},{8,10},{10,8},{9,1... | collective-permute-start | bytes 1966088 | tf_op jit(solution)/shard_map/ppermute | solution.py:29
  285.7 27.0 %collective-permute-start.44 = (f32[64,2048]{1,0:T(8,128)S(1)}, f32[64,2048]{1,0:T(8,128)}, u32[]{:S(2)}, u32[]{:S(2)}) collective-permute-start(f32[64,2048]{1,0:T(8,128)S(1)} %get-tuple-element.216), channel_id=1, source_target_pairs={{0,5},{1,4},{4,1},{5,0},{2,7},{3,6},{6,3},{7,2},{8,13},{9,12},{12,... | collective-permute-start | bytes 1572872 | tf_op jit(solution)/shard_map/ppermute | solution.py:1084
  293.9 20.0 %collective-permute-start.43 = (f32[2,2,64,1024]{3,2,1,0:T(8,128)}, f32[2,2,64,1024]{3,2,1,0:T(8,128)S(1)}, u32[]{:S(2)}, u32[]{:S(2)}) collective-permute-start(f32[2,2,64,1024]{3,2,1,0:T(8,128)} %get-tuple-element.213), channel_id=1, source_target_pairs={{0,8},{1,17},{8,0},{9,25},{16,24},{17,1},{24,16},{25,9},{2,10},{3,... | collective-permute-start | bytes 3145736 | tf_op jit(solution)/shard_map/ppermute | solution.py:882
  301.4 18.7 %collective-permute-start.47 = (f32[2,2,64,1024]{3,2,1,0:T(8,128)}, f32[2,2,64,1024]{3,2,1,0:T(8,128)S(1)}, u32[]{:S(2)}, u32[]{:S(2)}) collective-permute-start(f32[2,2,64,1024]{3,2,1,0:T(8,128)} %get-tuple-element.226), channel_id=1, source_target_pairs={{0,8},{1,17},{8,0},{9,25},{16,24},{17,1},{24,16},{25,9},{2,10},{3,... | collective-permute-start | bytes 3145736 | tf_op jit(solution)/shard_map/ppermute | solution.py:882
  312.7 17.9 %collective-permute-start.51 = (f32[320,256]{1,0:T(8,128)}, f32[320,256]{1,0:T(8,128)S(1)}, u32[]{:S(2)}, u32[]{:S(2)}) collective-permute-start(f32[320,256]{1,0:T(8,128)} %get-tuple-element.223), channel_id=1, source_target_pairs={{0,5},{1,4},{4,1},{5,0},{2,7},{3,6},{6,3},{7,2},{8,13},{9,12},{12,... | collective-permute-start | bytes 983048 | tf_op jit(solution)/shard_map/ppermute | solution.py:1108
  321.9 10.3 %collective-permute-start.53 = (f32[64,2048]{1,0:T(8,128)S(1)}, f32[64,2048]{1,0:T(8,128)S(1)}, u32[]{:S(2)}, u32[]{:S(2)}) collective-permute-start(f32[64,2048]{1,0:T(8,128)S(1)} %get-tuple-element.238), channel_id=1, source_target_pairs={{0,16},{1,9},{8,24},{9,1},{16,0},{17,25},{24,8},{25,17},{2,18},{3,... | collective-permute-start | bytes 1572872 | tf_op jit(solution)/shard_map/ppermute | solution.py:882
  332.3 14.8 %collective-permute-start.58 = (f32[64,2048]{1,0:T(8,128)S(1)}, f32[64,2048]{1,0:T(8,128)S(1)}, u32[]{:S(2)}, u32[]{:S(2)}) collective-permute-start(f32[64,2048]{1,0:T(8,128)S(1)} %reduction_step.12.refs_0_), channel_id=1, source_target_pairs={{0,8},{1,17},{8,0},{9,25},{16,24},{17,1},{24,16},{25,9},{2,10},{3,... | collective-permute-start | bytes 1572872 | tf_op jit(solution)/shard_map/ppermute | solution.py:882
  332.9 14.2 %collective-permute-start.57 = (f32[64,2048]{1,0:T(8,128)S(1)}, f32[64,2048]{1,0:T(8,128)S(1)}, u32[]{:S(2)}, u32[]{:S(2)}) collective-permute-start(f32[64,2048]{1,0:T(8,128)S(1)} %reduction_step.12.refs_0_), channel_id=1, source_target_pairs={{0,16},{1,9},{8,24},{9,1},{16,0},{17,25},{24,8},{25,17},{2,18},{3,... | collective-permute-start | bytes 1572872 | tf_op jit(solution)/shard_map/ppermute | solution.py:882
  334.4 27.5 %collective-permute-start.49 = (f32[320,512]{1,0:T(8,128)S(1)}, f32[320,512]{1,0:T(8,128)S(1)}, u32[]{:S(2)}, u32[]{:S(2)}) collective-permute-start(f32[320,512]{1,0:T(8,128)S(1)} %copy-done.25), channel_id=1, source_target_pairs={{0,2},{2,0},{1,3},{3,1},{4,6},{6,4},{5,7},{7,5},{8,10},{10,8},{9,1... | collective-permute-start | bytes 1966088 | tf_op jit(solution)/shard_map/ppermute | solution.py:29
  334.4 17.6 %collective-permute-start.48 = (f32[64,2048]{1,0:T(8,128)S(1)}, f32[64,2048]{1,0:T(8,128)S(1)}, u32[]{:S(2)}, u32[]{:S(2)}) collective-permute-start(f32[64,2048]{1,0:T(8,128)S(1)} %get-tuple-element.228), channel_id=1, source_target_pairs={{0,16},{1,9},{8,24},{9,1},{16,0},{17,25},{24,8},{25,17},{2,18},{3,... | collective-permute-start | bytes 1572872 | tf_op jit(solution)/shard_map/ppermute | solution.py:882
  335.4 26.5 %collective-permute-start.54 = (f32[64,2048]{1,0:T(8,128)S(1)}, f32[64,2048]{1,0:T(8,128)S(1)}, u32[]{:S(2)}, u32[]{:S(2)}) collective-permute-start(f32[64,2048]{1,0:T(8,128)S(1)} %reduction_step.11), channel_id=1, source_target_pairs={{0,4},{4,0},{1,5},{5,1},{2,6},{6,2},{3,7},{7,3},{8,12},{12,8},{9,1... | collective-permute-start | bytes 1572872 | tf_op jit(solution)/shard_map/ppermute | solution.py:960
  347.1 14.9 %collective-permute-start.59 = (f32[64,2048]{1,0:T(8,128)S(1)}, f32[64,2048]{1,0:T(8,128)S(1)}, u32[]{:S(2)}, u32[]{:S(2)}) collective-permute-start(f32[64,2048]{1,0:T(8,128)S(1)} %collective-permute-done.58.refs_2_), channel_id=1, source_target_pairs={{0,16},{1,9},{8,24},{9,1},{16,0},{17,25},{24,8},{25,17},{2,18},{3,... | collective-permute-start | bytes 1572872 | tf_op jit(solution)/shard_map/ppermute | solution.py:882
  362.1 13.1 %collective-permute-start.61 = (f32[64,2048]{1,0:T(8,128)S(1)}, f32[64,2048]{1,0:T(8,128)S(1)}, u32[]{:S(2)}, u32[]{:S(2)}) collective-permute-start(f32[64,2048]{1,0:T(8,128)S(1)} %reduction_step.13.refs_0_), channel_id=1, source_target_pairs={{0,8},{1,17},{8,0},{9,25},{16,24},{17,1},{24,16},{25,9},{2,10},{3,... | collective-permute-start | bytes 1572872 | tf_op jit(solution)/shard_map/ppermute | solution.py:882
  362.8 12.4 %collective-permute-start.60 = (f32[64,2048]{1,0:T(8,128)S(1)}, f32[64,2048]{1,0:T(8,128)S(1)}, u32[]{:S(2)}, u32[]{:S(2)}) collective-permute-start(f32[64,2048]{1,0:T(8,128)S(1)} %reduction_step.13.refs_0_), channel_id=1, source_target_pairs={{0,16},{1,9},{8,24},{9,1},{16,0},{17,25},{24,8},{25,17},{2,18},{3,... | collective-permute-start | bytes 1572872 | tf_op jit(solution)/shard_map/ppermute | solution.py:882
  364.2 15.7 %collective-permute-start.55 = (f32[320,256]{1,0:T(8,128)S(1)}, f32[320,256]{1,0:T(8,128)S(1)}, u32[]{:S(2)}, u32[]{:S(2)}) collective-permute-start(f32[320,256]{1,0:T(8,128)S(1)} %copy-done.26), channel_id=1, source_target_pairs={{0,4},{4,0},{1,5},{5,1},{2,6},{6,2},{3,7},{7,3},{8,12},{12,8},{9,1... | collective-permute-start | bytes 983048 | tf_op jit(solution)/shard_map/ppermute | solution.py:960
  375.2 9.2 %collective-permute-start.62 = (f32[64,2048]{1,0:T(8,128)S(1)}, f32[64,2048]{1,0:T(8,128)S(1)}, u32[]{:S(2)}, u32[]{:S(2)}) collective-permute-start(f32[64,2048]{1,0:T(8,128)S(1)} %collective-permute-done.61.refs_2_), channel_id=1, source_target_pairs={{0,16},{1,9},{8,24},{9,1},{16,0},{17,25},{24,8},{25,17},{2,18},{3,... | collective-permute-start | bytes 1572872 | tf_op jit(solution)/shard_map/ppermute | solution.py:882
  (44 other events, 367.3 us)

commit v5 on v4

--- a/solution.py
+++ b/solution.py
@@ -1001,7 +1001,7 @@
     weight = half_weights[0]
     early = jnp.concatenate([own_blocks, other_blocks[:2]])
     z, own_flat = project(place, frames, own + others, early, weight, 0, flat=own)
-    others += [(other_away, 0), (over_c(after(other_away, z)), 1)]
+    others += [(other_away, 0), (over_c(after(other_away, z)[frames:]), 0)]
     z, stats, other_flat = project(
         place,
         frames,
@@ -1032,7 +1032,7 @@
     z, *_ = project(place, frames, [(x_own, None)], own_blocks, near, 1)
     own_split = prepare(place, after(x, z), x_near)
     far = [*pieces, *map(over_c, after(pieces, own_split[0]))]
-    up_away = over_h(after(up_away, other, own_split[0]))
+    up_away = over_h(after(up_away, own_split[0]))
     half_weights.append(near + far)
     z, stats = project(place, frames, [(other, None)], other_blocks, near, 1, z, valid)
     both = jnp.concatenate([own_blocks, other_blocks])

time: 389 us -> 386 us (level)
    ppermute x2, waiting for transfers between devices: 0.01 us -> 6.36 us  [four_of_plane(): lax.ppermute(share, 'y', FLIP2)]
    ppermute x6, waiting for transfers between devices: 25.1 us -> 20.3 us  [swap_half(): return lax.ppermute(array, 'l', FLIP2)]
where the time goes in v5:
time: 386 us; the launch traced here: 385 us
  Pallas kernels  153 us (40%)
  waiting for transfers between devices  114 us (30%)
  blocking collectives  60.9 us (16%)
  starting transfers between devices  46 us (12%)
  local copies, waits for them, and re-layouts  7.17 us (2%)
    all_gather x8, blocking collectives, gather(): return lax.all_gather(array, axes, tiled=True)  60.9 us
    ppermute x7, waiting for transfers between devices, over_h(): return lax.ppermute(array, 'h', FLIP2)  38 us
    pallas_call x5, Pallas kernels, project(): call(partial(project_body, len(parts), len(flat), spots, len(weights), 0...  35.9 us
    ppermute x13, waiting for transfers between devices, plane_swap(): return lax.ppermute(array, ('y', 'x', 'c'), pairs)  27.1 us
    pallas_call x4, Pallas kernels, weight_rows(): call(partial(weight_body, turn), grid_spec=pltpu.PrefetchScalarGridSpec(n...  26.5 us
    ppermute x6, waiting for transfers between devices, swap_half(): return lax.ppermute(array, 'l', FLIP2)  20.3 us
    pallas_call x2, Pallas kernels, norm_back(): call(partial(norm_back_body, len(z), split_terms, layer), grid_spec=pltpu...  15.3 us
    pallas_call x4, Pallas kernels, prepare(): call(prepare_body, grid_spec=pltpu.PrefetchScalarGridSpec(num_scalar_pref...  15.1 us
  transfers between devices with their start and end apart: 63, of which 27 were waited for; matrix products, arithmetic and copies ran while one was open for 1% of the time, Pallas kernels for 37%

profile of v5, /device:TPU:0, one launch (start us, length us, event | category | flops | bytes accessed | tf_op | source)
XLA Modules:
  0.0 384.7 jit_solution(15174906829932109597)
XLA Ops:
  3.2 3.6 collective-permute-start.1
  10.7 2.9 pack.3
  15.6 15.5 %collective-permute-done.1.refs_12_.refs_8_.refs_7_.refs_4_ = f32[64,2048]{1,0:T(8,128)} collective-permute-done((f32[64,2048]{1,0:T(8,128)S(1)}, f32[64,2048]{1,0:T(8,128)}, u32[]{:S(2)}, u32[]{:S(2)}) %collective-permute-start.1) | collective-permute-done | bytes 524320 | tf_op jit(solution)/shard_map/ppermute | solution.py:960
  31.2 2.8 collective-permute-start.5
  34.7 5.0 %collective-permute-done.6.refs_4_.refs_2_ = f32[640,256]{1,0:T(8,128)S(1)} collective-permute-done((f32[640,256]{1,0:T(8,128)S(1)}, f32[640,256]{1,0:T(8,128)S(1)}, u32[]{:S(2)}, u32[]{:S(2)}) %collective-permute-start.6) | collective-permute-done | bytes 655392 | tf_op jit(solution)/shard_map/ppermute | solution.py:29
  39.7 19.1 %collective-permute-done.refs_2_.refs_8_ = f32[640,256]{1,0:T(8,128)S(1)} collective-permute-done((f32[640,256]{1,0:T(8,128)S(1)}, f32[640,256]{1,0:T(8,128)S(1)}, u32[]{:S(2)}, u32[]{:S(2)}) %collective-permute-start) | collective-permute-done | bytes 655392 | tf_op jit(solution)/shard_map/ppermute | solution.py:960
  65.3 9.9 %project.5 = (f32[320,1024]{1,0:T(8,128)}, f32[320,1024]{1,0:T(8,128)}) custom-call(s32[6]{0:T(128)S(1)} %concatenate.11.cols_ref, s32[8]{0:T(128)S(1)} %stack.124.place_ref, f32[640,256]{1,0:T(8,128)S(1)} %get-tuple-element.137.refs_0_.refs_6_, f32[640,256]{1,0:T(8,128)} %collective-permute-done.8.refs_1_.refs_7_, ...), custom_call_target="tpu_custom_call" | custom-call | flops 47185920 | bytes 98304 | tf_op jit(solution)/shard_map/project/pallas_call | solution.py:289
  78.3 6.0 %project.6 = (f32[320,1024]{1,0:T(8,128)}, f32[5,8,128]{2,1,0:T(8,128)S(1)}, f32[320,1024]{1,0:T(8,128)}) custom-call(s32[2]{0:T(128)S(1)} %pad_add_fusion.1.cols_ref, s32[8]{0:T(128)S(1)} %stack.124.place_ref, f32[640,256]{1,0:T(8,128)S(1)} %collective-permute-done.7.refs_0_.refs_4_, f32[320,256]{1,0:T(8,128)S(1)} %collective-permute-done.15.refs_1_.refs_5_, ...), custom_call_target="tpu_custom_call" | custom-call | flops 15728640 | bytes 32768 | tf_op jit(solution)/shard_map/project/pallas_call | solution.py:289
  85.0 6.2 %all_gather.24 = f32[20,8,128]{2,1,0:T(8,128)S(1)} all-gather(f32[5,8,128]{2,1,0:T(8,128)S(1)} %get-tuple-element.145), channel_id=1, replica_groups=mesh['y'=2,'x'=2,'h'=2,'l'=2,'c'=2] {'h','c'}, dimensions={0}, use_global_device_ids=true | all-gather | bytes 102400 | tf_op jit(solution)/shard_map/all_gather | solution.py:999
  93.5 9.2 %all_gather.25.refs_1_.refs_3_ = f32[80,8,128]{2,1,0:T(8,128)S(1)} all-gather(f32[20,8,128]{2,1,0:T(8,128)S(1)} %all_gather.24), channel_id=1, replica_groups=mesh['y'=2,'x'=2,'h'=2,'l'=2,'c'=2] {'y','x'}, dimensions={0}, use_global_device_ids=true | all-gather | bytes 409600 | tf_op jit(solution)/shard_map/all_gather | solution.py:999
  102.7 7.3 %recur.2 = (f32[320,1024]{1,0:T(8,128)S(1)}, f32[320,1024]{1,0:T(8,128)}, f32[320,1024]{1,0:T(8,128)}, f32[6,8,128]{2,1,0:T(8,128)S(1)}) custom-call(s32[8]{0:T(128)S(1)} %stack.124.place_ref, f32[320]{0:T(512)S(1)} %fusion.6.gate_ref, f32[320,1024]{1,0:T(8,128)} %get-tuple-element.144.refs_0_, f32[80,8,128]{2,1,0:T(8,128)S(1)} %all_gather.25.refs_1_.refs_3_, ...), custom_call_target="tpu_custom_call" | custom-call | flops 512000 | bytes 102400 | tf_op jit(solution)/shard_map/recur/pallas_call | solution.py:435
  111.8 5.4 %collective-permute-done.20 = f32[64,2048]{1,0:T(8,128)S(1)} collective-permute-done((f32[64,2048]{1,0:T(8,128)S(1)}, f32[64,2048]{1,0:T(8,128)S(1)}, u32[]{:S(2)}, u32[]{:S(2)}) %collective-permute-start.20) | collective-permute-done | bytes 524320 | tf_op jit(solution)/shard_map/ppermute | solution.py:1019
  124.0 3.8 prepare.4
  127.8 3.8 prepare.5
  131.5 5.2 %project.7.refs_3_ = f32[320,512]{1,0:T(8,128)} custom-call(s32[4]{0:T(128)S(1)} %pad_add_fusion.2.cols_ref, s32[8]{0:T(128)S(1)} %stack.124.place_ref, f32[320,1024]{1,0:T(8,128)S(1)} %get-tuple-element.160.refs_0_.own_ref.refs_5_, f32[2,256,2048]{2,1,0:T(8,128)} %refs_2_.1, ...), custom_call_target="tpu_custom_call" | custom-call | flops 15728640 | bytes 32768 | tf_op jit(solution)/shard_map/project/pallas_call | solution.py:289
  136.7 3.8 prepare.6
  140.5 6.4 %collective-permute-done.23.refs_4_.refs_10_.refs_8_ = f32[64,2048]{1,0:T(8,128)} collective-permute-done((f32[64,2048]{1,0:T(8,128)}, f32[64,2048]{1,0:T(8,128)}, u32[]{:S(2)}, u32[]{:S(2)}) %collective-permute-start.23) | collective-permute-done | bytes 524320 | tf_op jit(solution)/shard_map/ppermute | solution.py:978
  148.2 5.6 %project.8 = (f32[320,512]{1,0:T(8,128)}, f32[3,8,128]{2,1,0:T(8,128)S(1)}) custom-call(s32[4]{0:T(128)S(1)} %pad_add_fusion.cols_ref, s32[8]{0:T(128)S(1)} %stack.124.place_ref, f32[320,1024]{1,0:T(8,128)S(1)} %collective-permute-done.16.refs_0_.refs_1_.own_ref, f32[2,256,2048]{2,1,0:T(8,128)} %refs_2_.1, ...), custom_call_target="tpu_custom_call" | custom-call | flops 15728640 | bytes 32768 | tf_op jit(solution)/shard_map/project/pallas_call | solution.py:289
  154.3 9.2 %project.9 = (f32[320,512]{1,0:T(8,128)}, f32[3,8,128]{2,1,0:T(8,128)S(1)}) custom-call(s32[8]{0:T(128)S(1)} %concatenate.12.cols_ref, s32[8]{0:T(128)S(1)} %stack.124.place_ref, f32[320,1024]{1,0:T(8,128)S(1)} %copy-done.1, f32[320,1024]{1,0:T(8,128)S(1)} %collective-permute-done.16.refs_0_.refs_1_.own_ref, ...), custom_call_target="tpu_custom_call" | custom-call | flops 31457280 | bytes 65536 | tf_op jit(solution)/shard_map/project/pallas_call | solution.py:289
  163.4 8.2 %all_gather.26 = f32[12,8,128]{2,1,0:T(8,128)S(1)} all-gather(f32[3,8,128]{2,1,0:T(8,128)S(1)} %get-tuple-element.168), channel_id=1, replica_groups=mesh['y'=2,'x'=2,'h'=2,'l'=2,'c'=2] {'y','x'}, dimensions={0}, use_global_device_ids=true | all-gather | bytes 61440 | tf_op jit(solution)/shard_map/all_gather | solution.py:999
  171.6 7.7 %all_gather.27.refs_2_.refs_4_ = f32[48,8,128]{2,1,0:T(8,128)S(1)} all-gather(f32[12,8,128]{2,1,0:T(8,128)S(1)} %all_gather.26), channel_id=1, replica_groups=mesh['y'=2,'x'=2,'h'=2,'l'=2,'c'=2] {'h','c'}, dimensions={0}, use_global_device_ids=true | all-gather | bytes 245760 | tf_op jit(solution)/shard_map/all_gather | solution.py:999
  179.7 7.4 %recur.3 = (f32[320,256]{1,0:T(8,128)}, f32[320,256]{1,0:T(8,128)}, f32[320,256]{1,0:T(8,128)}, f32[320,256]{1,0:T(8,128)}, f32[320,1024]{1,0:T(8,128)}, /*index=5*/f32[320,1024]{1,0:T(8,128)}) custom-call(s32[8]{0:T(128)S(1)} %stack.124.place_ref, f32[320]{0:T(512)S(1)} %fusion.6.gate_ref, f32[320,512]{1,0:T(8,128)} %get-tuple-element.156.refs_0_, ...), custom_call_target="tpu_custom_call" | custom-call | flops 512000 | bytes 102400 | tf_op jit(solution)/shard_map/recur/pallas_call | solution.py:435
  187.4 5.6 %back.2 = (f32[320,1024]{1,0:T(8,128)S(1)}, f32[3,8,128]{2,1,0:T(8,128)S(1)}) custom-call(s32[8]{0:T(128)S(1)} %stack.124.place_ref, f32[320]{0:T(512)S(1)} %fusion.6.gate_ref, f32[320,512]{1,0:T(8,128)} %get-tuple-element.156.refs_0_, f32[320,512]{1,0:T(8,128)} %get-tuple-element.167.refs_1_, f32[48,8,128]{2,1,0:T(8,128)S(1)} %all_gather.27.refs_2_.refs_4_, ...), custom_call_target="tpu_custom_call" | custom-call | flops 153600 | bytes 102400 | tf_op jit(solution)/shard_map/back/pallas_call | solution.py:542
  193.1 7.4 %all_gather.28 = f32[12,8,128]{2,1,0:T(8,128)S(1)} all-gather(f32[3,8,128]{2,1,0:T(8,128)S(1)} %get-tuple-element.177), channel_id=1, replica_groups=mesh['y'=2,'x'=2,'h'=2,'l'=2,'c'=2] {'y','x'}, dimensions={0}, use_global_device_ids=true | all-gather | bytes 61440 | tf_op jit(solution)/shard_map/all_gather | solution.py:999
  200.5 7.4 %all_gather.29.refs_5_ = f32[48,8,128]{2,1,0:T(8,128)S(1)} all-gather(f32[12,8,128]{2,1,0:T(8,128)S(1)} %all_gather.28), channel_id=1, replica_groups=mesh['y'=2,'x'=2,'h'=2,'l'=2,'c'=2] {'h','c'}, dimensions={0}, use_global_device_ids=true | all-gather | bytes 245760 | tf_op jit(solution)/shard_map/all_gather | solution.py:999
  207.8 7.7 %norm_back.2 = (f32[320,1024]{1,0:T(8,128)}, f32[320,512]{1,0:T(8,128)S(1)}, f32[320,1024]{1,0:T(8,128)}, f32[3,8,128]{2,1,0:T(8,128)S(1)}) custom-call(s32[2]{0:T(128)S(1)} %pad_add_fusion.4.cols_ref, s32[8]{0:T(128)S(1)} %stack.124.place_ref, f32[320,1024]{1,0:T(8,128)S(1)} %get-tuple-element.176.grad_ref, f32[320,512]{1,0:T(8,128)} %get-tuple-element.156.refs_0_, ...), custom_call_target="tpu_custom_call" | custom-call | flops 31457280 | bytes 65536 | tf_op jit(solution)/shard_map/norm_back/pallas_call | solution.py:647
  218.2 3.8 prepare.7
  222.7 7.2 %weight_rows.4 = (f32[2,2,64,1024]{3,2,1,0:T(8,128)}, f32[2,2,64,1024]{3,2,1,0:T(8,128)}, bf16[512,768]{1,0:T(8,128)(2,1)S(1)}, bf16[512,768]{1,0:T(8,128)(2,1)S(1)}) custom-call(s32[8]{0:T(128)S(1)} %stack.124.place_ref, f32[320,1024]{1,0:T(8,128)} %get-tuple-element.191.refs_0_.grad_ref, f32[320,512]{1,0:T(8,128)S(1)} %collective-permute-done.32.refs_1_, ...), custom_call_target="tpu_custom_call" | custom-call | flops 37748736 | bytes 32768 | tf_op jit(solution)/shard_map/weight_rows/pallas_call | solution.py:820
  231.2 6.1 %weight_rows.5 = (f32[2,2,64,1024]{3,2,1,0:T(8,128)}, f32[2,2,64,1024]{3,2,1,0:T(8,128)}) custom-call(s32[8]{0:T(128)S(1)} %stack.124.place_ref, bf16[512,768]{1,0:T(8,128)(2,1)S(1)} %get-tuple-element.187.refs_0_, bf16[512,768]{1,0:T(8,128)(2,1)S(1)} %get-tuple-element.188.refs_1_, bf16[768,1024]{1,0:T(8,128)(2,1)} %get-tuple-element.184.refs_2_, ...), custom_call_target="tpu_custom_call" | custom-call | flops 37748736 | bytes 32768 | tf_op jit(solution)/shard_map/weight_rows/pallas_call | solution.py:820
  238.1 6.1 %own_terms.2.refs_3_.refs_0_ = f32[320,1024]{1,0:T(8,128)S(1)} custom-call(s32[2]{0:T(128)S(1)} %pad_add_fusion.5.cols_ref, s32[8]{0:T(128)S(1)} %stack.124.place_ref, f32[320,1024]{1,0:T(8,128)} %get-tuple-element.191.refs_0_.grad_ref, f32[640,256]{1,0:T(8,128)S(1)} %copy-done.6, f32[640,256]{1,0:T(8,128)} %collective-permute-done.29.refs_5_.refs_1_, ...), custom_call_target="tpu_custom_call" | custom-call | flops 31457280 | bytes 65536 | tf_op jit(solution)/shard_map/own_terms/pallas_call | solution.py:705
  244.7 3.0 collective-permute-done.36.refs_4_.refs_1_
  247.7 5.9 %back.3 = (f32[320,1024]{1,0:T(8,128)S(1)}, f32[3,8,128]{2,1,0:T(8,128)S(1)}) custom-call(s32[8]{0:T(128)S(1)} %stack.124.place_ref, f32[320]{0:T(512)S(1)} %fusion.6.gate_ref, f32[320,1024]{1,0:T(8,128)} %get-tuple-element.144.refs_0_, f32[80,8,128]{2,1,0:T(8,128)S(1)} %all_gather.25.refs_1_.refs_3_, ...), custom_call_target="tpu_custom_call" | custom-call | flops 153600 | bytes 102400 | tf_op jit(solution)/shard_map/back/pallas_call | solution.py:542
  253.6 8.0 %all_gather.30 = f32[12,8,128]{2,1,0:T(8,128)S(1)} all-gather(f32[3,8,128]{2,1,0:T(8,128)S(1)} %get-tuple-element.195), channel_id=1, replica_groups=mesh['y'=2,'x'=2,'h'=2,'l'=2,'c'=2] {'y','x'}, dimensions={0}, use_global_device_ids=true | all-gather | bytes 61440 | tf_op jit(solution)/shard_map/all_gather | solution.py:999
  266.8 6.7 %all_gather.31.refs_4_ = f32[48,8,128]{2,1,0:T(8,128)S(1)} all-gather(f32[12,8,128]{2,1,0:T(8,128)S(1)} %all_gather.30), channel_id=1, replica_groups=mesh['y'=2,'x'=2,'h'=2,'l'=2,'c'=2] {'h','c'}, dimensions={0}, use_global_device_ids=true | all-gather | bytes 245760 | tf_op jit(solution)/shard_map/all_gather | solution.py:999
  273.5 7.6 %norm_back.3 = (f32[320,1024]{1,0:T(8,128)}, f32[320,512]{1,0:T(8,128)S(1)}, f32[320,512]{1,0:T(8,128)}, f32[320,512]{1,0:T(8,128)S(1)}, f32[3,8,128]{2,1,0:T(8,128)S(1)}) custom-call(s32[2]{0:T(128)S(1)} %pad_add_fusion.4.cols_ref, s32[8]{0:T(128)S(1)} %stack.124.place_ref, f32[320,1024]{1,0:T(8,128)S(1)} %get-tuple-element.194.grad_ref, ...), custom_call_target="tpu_custom_call" | custom-call | flops 31457280 | bytes 65536 | tf_op jit(solution)/shard_map/norm_back/pallas_call | solution.py:647
  284.2 7.2 %weight_rows.6 = (f32[2,2,64,1024]{3,2,1,0:T(8,128)}, f32[2,2,64,1024]{3,2,1,0:T(8,128)}, bf16[512,768]{1,0:T(8,128)(2,1)S(1)}, bf16[512,768]{1,0:T(8,128)(2,1)S(1)}) custom-call(s32[8]{0:T(128)S(1)} %stack.124.place_ref, f32[320,1024]{1,0:T(8,128)} %get-tuple-element.221.refs_0_.grad_ref, f32[320,512]{1,0:T(8,128)S(1)} %collective-permute-done.41.refs_1_, ...), custom_call_target="tpu_custom_call" | custom-call | flops 37748736 | bytes 32768 | tf_op jit(solution)/shard_map/weight_rows/pallas_call | solution.py:820
  292.7 6.1 %weight_rows.7 = (f32[2,2,64,1024]{3,2,1,0:T(8,128)}, f32[2,2,64,1024]{3,2,1,0:T(8,128)}) custom-call(s32[8]{0:T(128)S(1)} %stack.124.place_ref, bf16[512,768]{1,0:T(8,128)(2,1)S(1)} %get-tuple-element.217.refs_0_, bf16[512,768]{1,0:T(8,128)(2,1)S(1)} %get-tuple-element.218.refs_1_, bf16[768,1024]{1,0:T(8,128)(2,1)} %get-tuple-element.154.refs_2_, ...), custom_call_target="tpu_custom_call" | custom-call | flops 37748736 | bytes 32768 | tf_op jit(solution)/shard_map/weight_rows/pallas_call | solution.py:820
  299.5 6.0 %own_terms.3.kept_ref = f32[320,1024]{1,0:T(8,128)S(1)} custom-call(s32[2]{0:T(128)S(1)} %pad_add_fusion.5.cols_ref, s32[8]{0:T(128)S(1)} %stack.124.place_ref, f32[320,1024]{1,0:T(8,128)} %get-tuple-element.221.refs_0_.grad_ref, f32[320,1024]{1,0:T(8,128)S(1)} %own_terms.2.refs_3_.refs_0_, f32[320,1024]{1,0:T(8,128)S(1)} %copy-done.4, ...), custom_call_target="tpu_custom_call" | custom-call | flops 31457280 | bytes 65536 | tf_op jit(solution)/shard_map/own_terms/pallas_call | solution.py:705
  305.6 3.9 %collective-permute-done.45.come_ref = f32[320,512]{1,0:T(8,128)S(1)} collective-permute-done((f32[320,512]{1,0:T(8,128)S(1)}, f32[320,512]{1,0:T(8,128)S(1)}, u32[]{:S(2)}, u32[]{:S(2)}) %collective-permute-start.45) | collective-permute-done | bytes 655392 | tf_op jit(solution)/shard_map/ppermute | solution.py:29
  312.7 5.0 %collective-permute-done.47.refs_3_ = f32[2,2,64,1024]{3,2,1,0:T(8,128)S(1)} collective-permute-done((f32[2,2,64,1024]{3,2,1,0:T(8,128)}, f32[2,2,64,1024]{3,2,1,0:T(8,128)S(1)}, u32[]{:S(2)}, u32[]{:S(2)}) %collective-permute-start.47) | collective-permute-done | bytes 1048608 | tf_op jit(solution)/shard_map/ppermute | solution.py:882
  320.8 7.3 %collective-permute-done.51 = f32[320,256]{1,0:T(8,128)S(1)} collective-permute-done((f32[320,256]{1,0:T(8,128)}, f32[320,256]{1,0:T(8,128)S(1)}, u32[]{:S(2)}, u32[]{:S(2)}) %collective-permute-start.51) | collective-permute-done | bytes 327712 | tf_op jit(solution)/shard_map/ppermute | solution.py:1108
  335.1 9.5 %collective-permute-done.58.refs_2_ = f32[64,2048]{1,0:T(8,128)S(1)} collective-permute-done((f32[64,2048]{1,0:T(8,128)S(1)}, f32[64,2048]{1,0:T(8,128)S(1)}, u32[]{:S(2)}, u32[]{:S(2)}) %collective-permute-start.58) | collective-permute-done | bytes 524320 | tf_op jit(solution)/shard_map/ppermute | solution.py:882
  345.8 3.7 collective-permute-done.48.refs_1_
  349.5 2.8 unpack.2
  352.4 7.0 %collective-permute-done.49.come_ref = f32[320,512]{1,0:T(8,128)S(1)} collective-permute-done((f32[320,512]{1,0:T(8,128)S(1)}, f32[320,512]{1,0:T(8,128)S(1)}, u32[]{:S(2)}, u32[]{:S(2)}) %collective-permute-start.49) | collective-permute-done | bytes 655392 | tf_op jit(solution)/shard_map/ppermute | solution.py:29
  362.7 3.0 assemble.2.refs_4_
  365.7 7.3 %collective-permute-done.61.refs_2_ = f32[64,2048]{1,0:T(8,128)S(1)} collective-permute-done((f32[64,2048]{1,0:T(8,128)S(1)}, f32[64,2048]{1,0:T(8,128)S(1)}, u32[]{:S(2)}, u32[]{:S(2)}) %collective-permute-start.61) | collective-permute-done | bytes 524320 | tf_op jit(solution)/shard_map/ppermute | solution.py:882
  374.0 2.8 collective-permute-done.55
  (205 shorter events, 75.9 us)
Async XLA Ops:
  0.6 30.4 %collective-permute-start.2 = (f32[2,256,2048]{2,1,0:T(8,128)}, f32[2,256,2048]{2,1,0:T(8,128)}, u32[]{:S(2)}, u32[]{:S(2)}) collective-permute-start(f32[2,256,2048]{2,1,0:T(8,128)} %refs_2_.1), channel_id=1, source_target_pairs={{0,1},{1,0},{2,3},{3,2},{4,5},{5,4},{6,7},{7,6},{8,9},{9,8},{10,11... | collective-permute-start | bytes 12582920 | tf_op jit(solution)/shard_map/ppermute | solution.py:963
  3.2 27.8 %collective-permute-start.1 = (f32[64,2048]{1,0:T(8,128)S(1)}, f32[64,2048]{1,0:T(8,128)}, u32[]{:S(2)}, u32[]{:S(2)}) collective-permute-start(f32[64,2048]{1,0:T(8,128)S(1)} %get-tuple-element.254), channel_id=1, source_target_pairs={{0,4},{4,0},{1,5},{5,1},{2,6},{6,2},{3,7},{7,3},{8,12},{12,8},{9,1... | collective-permute-start | bytes 1572872 | tf_op jit(solution)/shard_map/ppermute | solution.py:960
  8.8 30.9 %collective-permute-start.6 = (f32[640,256]{1,0:T(8,128)S(1)}, f32[640,256]{1,0:T(8,128)S(1)}, u32[]{:S(2)}, u32[]{:S(2)}) collective-permute-start(f32[640,256]{1,0:T(8,128)S(1)} %get-tuple-element.137.refs_0_.refs_6_), channel_id=1, source_target_pairs={{0,2},{2,0},{1,3},{3,1},{4,6},{6,4},{5,7},{7,5},{8,10},{10,8},{9,1... | collective-permute-start | bytes 1966088 | tf_op jit(solution)/shard_map/ppermute | solution.py:29
  10.4 48.4 %collective-permute-start = (f32[640,256]{1,0:T(8,128)S(1)}, f32[640,256]{1,0:T(8,128)S(1)}, u32[]{:S(2)}, u32[]{:S(2)}) collective-permute-start(f32[640,256]{1,0:T(8,128)S(1)} %get-tuple-element.131), channel_id=1, source_target_pairs={{0,4},{4,0},{1,5},{5,1},{2,6},{6,2},{3,7},{7,3},{8,12},{12,8},{9,1... | collective-permute-start | bytes 1966088 | tf_op jit(solution)/shard_map/ppermute | solution.py:960
  31.2 27.6 %collective-permute-start.5 = (f32[64,2048]{1,0:T(8,128)}, f32[64,2048]{1,0:T(8,128)}, u32[]{:S(2)}, u32[]{:S(2)}) collective-permute-start(f32[64,2048]{1,0:T(8,128)} %collective-permute-done.1.refs_12_.refs_8_.refs_7_.refs_4_), channel_id=1, source_target_pairs={{0,24},{8,16},{16,8},{24,0},{1,25},{9,17},{17,9},{25,1},{2,26},{10... | collective-permute-start | bytes 1572872 | tf_op jit(solution)/shard_map/ppermute | solution.py:977
  33.9 24.8 %collective-permute-start.4 = (f32[64,2048]{1,0:T(8,128)}, f32[64,2048]{1,0:T(8,128)}, u32[]{:S(2)}, u32[]{:S(2)}) collective-permute-start(f32[64,2048]{1,0:T(8,128)} %collective-permute-done.1.refs_12_.refs_8_.refs_7_.refs_4_), channel_id=1, source_target_pairs={{0,16},{16,0},{1,17},{17,1},{2,18},{18,2},{3,19},{19,3},{4,20},{20... | collective-permute-start | bytes 1572872 | tf_op jit(solution)/shard_map/ppermute | solution.py:978
  34.5 24.3 %collective-permute-start.3 = (f32[64,2048]{1,0:T(8,128)}, f32[64,2048]{1,0:T(8,128)S(1)}, u32[]{:S(2)}, u32[]{:S(2)}) collective-permute-start(f32[64,2048]{1,0:T(8,128)} %collective-permute-done.1.refs_12_.refs_8_.refs_7_.refs_4_), channel_id=1, source_target_pairs={{0,8},{8,0},{1,9},{9,1},{2,10},{10,2},{3,11},{11,3},{4,12},{12,4},... | collective-permute-start | bytes 1572872 | tf_op jit(solution)/shard_map/ppermute | solution.py:978
  39.7 20.2 %collective-permute-start.10 = (f32[640,256]{1,0:T(8,128)S(1)}, f32[640,256]{1,0:T(8,128)S(1)}, u32[]{:S(2)}, u32[]{:S(2)}) collective-permute-start(f32[640,256]{1,0:T(8,128)S(1)} %collective-permute-done.6.refs_4_.refs_2_), channel_id=1, source_target_pairs={{0,1},{1,0},{2,3},{3,2},{4,5},{5,4},{6,7},{7,6},{8,9},{9,8},{10,11... | collective-permute-start | bytes 1966088 | tf_op jit(solution)/shard_map/ppermute | solution.py:963
  59.9 16.7 %collective-permute-start.7 = (f32[640,256]{1,0:T(8,128)S(1)}, f32[640,256]{1,0:T(8,128)S(1)}, u32[]{:S(2)}, u32[]{:S(2)}) collective-permute-start(f32[640,256]{1,0:T(8,128)S(1)} %collective-permute-done.refs_2_.refs_8_), channel_id=1, source_target_pairs={{0,2},{2,0},{1,3},{3,1},{4,6},{6,4},{5,7},{7,5},{8,10},{10,8},{9,1... | collective-permute-start | bytes 1966088 | tf_op jit(solution)/shard_map/ppermute | solution.py:29
  84.4 34.8 %collective-permute-start.18 = (f32[320,1024]{1,0:T(8,128)S(1)}, f32[320,1024]{1,0:T(8,128)S(1)}, u32[]{:S(2)}, u32[]{:S(2)}) collective-permute-start(f32[320,1024]{1,0:T(8,128)S(1)} %copy-done.11), channel_id=1, source_target_pairs={{0,1},{1,0},{2,3},{3,2},{4,5},{5,4},{6,7},{7,6},{8,9},{9,8},{10,11... | collective-permute-start | bytes 3932168 | tf_op jit(solution)/shard_map/ppermute | solution.py:963
  84.6 35.7 %collective-permute-start.19 = (f32[320,1024]{1,0:T(8,128)}, f32[320,1024]{1,0:T(8,128)}, u32[]{:S(2)}, u32[]{:S(2)}) collective-permute-start(f32[320,1024]{1,0:T(8,128)} %get-tuple-element.153.own_ref), channel_id=1, source_target_pairs={{0,1},{1,0},{2,3},{3,2},{4,5},{5,4},{6,7},{7,6},{8,9},{9,8},{10,11... | collective-permute-start | bytes 3932168 | tf_op jit(solution)/shard_map/ppermute | solution.py:963
  91.1 26.0 %collective-permute-start.20 = (f32[64,2048]{1,0:T(8,128)S(1)}, f32[64,2048]{1,0:T(8,128)S(1)}, u32[]{:S(2)}, u32[]{:S(2)}) collective-permute-start(f32[64,2048]{1,0:T(8,128)S(1)} %copy-done.13), channel_id=1, source_target_pairs={{0,5},{1,4},{4,1},{5,0},{2,7},{3,6},{6,3},{7,2},{8,13},{9,12},{12,... | collective-permute-start | bytes 1572872 | tf_op jit(solution)/shard_map/ppermute | solution.py:1019
  110.0 14.0 %collective-permute-start.17 = (f32[320,1024]{1,0:T(8,128)S(1)}, f32[320,1024]{1,0:T(8,128)}, u32[]{:S(2)}, u32[]{:S(2)}) collective-permute-start(f32[320,1024]{1,0:T(8,128)S(1)} %get-tuple-element.160.refs_0_.own_ref.refs_5_), channel_id=1, source_target_pairs={{0,1},{1,0},{2,3},{3,2},{4,5},{5,4},{6,7},{7,6},{8,9},{9,8},{10,11... | collective-permute-start | bytes 3932168 | tf_op jit(solution)/shard_map/ppermute | solution.py:963
  110.0 37.6 %collective-permute-start.16 = (f32[320,1024]{1,0:T(8,128)S(1)}, f32[320,1024]{1,0:T(8,128)S(1)}, u32[]{:S(2)}, u32[]{:S(2)}) collective-permute-start(f32[320,1024]{1,0:T(8,128)S(1)} %get-tuple-element.160.refs_0_.own_ref.refs_5_), channel_id=1, source_target_pairs={{0,2},{2,0},{1,3},{3,1},{4,6},{6,4},{5,7},{7,5},{8,10},{10,8},{9,1... | collective-permute-start | bytes 3932168 | tf_op jit(solution)/shard_map/ppermute | solution.py:29
  120.3 20.2 %collective-permute-start.24 = (f32[64,2048]{1,0:T(8,128)}, f32[64,2048]{1,0:T(8,128)}, u32[]{:S(2)}, u32[]{:S(2)}) collective-permute-start(f32[64,2048]{1,0:T(8,128)} %collective-permute-done.21.refs_2_.refs_8_.refs_6_), channel_id=1, source_target_pairs={{0,24},{8,16},{16,8},{24,0},{1,25},{9,17},{17,9},{25,1},{2,26},{10... | collective-permute-start | bytes 1572872 | tf_op jit(solution)/shard_map/ppermute | solution.py:977
  122.8 24.1 %collective-permute-start.23 = (f32[64,2048]{1,0:T(8,128)}, f32[64,2048]{1,0:T(8,128)}, u32[]{:S(2)}, u32[]{:S(2)}) collective-permute-start(f32[64,2048]{1,0:T(8,128)} %collective-permute-done.21.refs_2_.refs_8_.refs_6_), channel_id=1, source_target_pairs={{0,16},{16,0},{1,17},{17,1},{2,18},{18,2},{3,19},{19,3},{4,20},{20... | collective-permute-start | bytes 1572872 | tf_op jit(solution)/shard_map/ppermute | solution.py:978
  123.3 23.7 %collective-permute-start.22 = (f32[64,2048]{1,0:T(8,128)}, f32[64,2048]{1,0:T(8,128)}, u32[]{:S(2)}, u32[]{:S(2)}) collective-permute-start(f32[64,2048]{1,0:T(8,128)} %collective-permute-done.21.refs_2_.refs_8_.refs_6_), channel_id=1, source_target_pairs={{0,8},{8,0},{1,9},{9,1},{2,10},{10,2},{3,11},{11,3},{4,12},{12,4},... | collective-permute-start | bytes 1572872 | tf_op jit(solution)/shard_map/ppermute | solution.py:978
  140.5 38.8 %collective-permute-start.30 = (f32[640,256]{1,0:T(8,128)}, f32[640,256]{1,0:T(8,128)}, u32[]{:S(2)}, u32[]{:S(2)}) collective-permute-start(f32[640,256]{1,0:T(8,128)} %get-tuple-element.172), channel_id=1, source_target_pairs={{0,4},{4,0},{1,5},{5,1},{2,6},{6,2},{3,7},{7,3},{8,12},{12,8},{9,1... | collective-permute-start | bytes 1966088 | tf_op jit(solution)/shard_map/ppermute | solution.py:960
  147.0 6.8 %collective-permute-start.25 = (f32[64,2048]{1,0:T(8,128)}, f32[64,2048]{1,0:T(8,128)}, u32[]{:S(2)}, u32[]{:S(2)}) collective-permute-start(f32[64,2048]{1,0:T(8,128)} %collective-permute-done.21.refs_2_.refs_8_.refs_6_), channel_id=1, source_target_pairs={{0,1},{1,0},{2,3},{3,2},{4,5},{5,4},{6,7},{7,6},{8,9},{9,8},{10,11... | collective-permute-start | bytes 1572872 | tf_op jit(solution)/shard_map/ppermute | solution.py:963
  147.0 7.2 %collective-permute-start.26 = (f32[64,2048]{1,0:T(8,128)}, f32[64,2048]{1,0:T(8,128)}, u32[]{:S(2)}, u32[]{:S(2)}) collective-permute-start(f32[64,2048]{1,0:T(8,128)} %collective-permute-done.22.refs_3_.refs_9_.refs_7_), channel_id=1, source_target_pairs={{0,1},{1,0},{2,3},{3,2},{4,5},{5,4},{6,7},{7,6},{8,9},{9,8},{10,11... | collective-permute-start | bytes 1572872 | tf_op jit(solution)/shard_map/ppermute | solution.py:963
  147.6 6.7 %collective-permute-start.27 = (f32[64,2048]{1,0:T(8,128)}, f32[64,2048]{1,0:T(8,128)}, u32[]{:S(2)}, u32[]{:S(2)}) collective-permute-start(f32[64,2048]{1,0:T(8,128)} %collective-permute-done.23.refs_4_.refs_10_.refs_8_), channel_id=1, source_target_pairs={{0,1},{1,0},{2,3},{3,2},{4,5},{5,4},{6,7},{7,6},{8,9},{9,8},{10,11... | collective-permute-start | bytes 1572872 | tf_op jit(solution)/shard_map/ppermute | solution.py:963
  147.6 6.7 %collective-permute-start.28 = (f32[64,2048]{1,0:T(8,128)}, f32[64,2048]{1,0:T(8,128)}, u32[]{:S(2)}, u32[]{:S(2)}) collective-permute-start(f32[64,2048]{1,0:T(8,128)} %collective-permute-done.24.refs_5_.refs_11_.refs_9_), channel_id=1, source_target_pairs={{0,1},{1,0},{2,3},{3,2},{4,5},{5,4},{6,7},{7,6},{8,9},{9,8},{10,11... | collective-permute-start | bytes 1572872 | tf_op jit(solution)/shard_map/ppermute | solution.py:963
  153.9 33.5 %collective-permute-start.29 = (f32[640,256]{1,0:T(8,128)S(1)}, f32[640,256]{1,0:T(8,128)}, u32[]{:S(2)}, u32[]{:S(2)}) collective-permute-start(f32[640,256]{1,0:T(8,128)S(1)} %copy-done.5), channel_id=1, source_target_pairs={{0,1},{1,0},{2,3},{3,2},{4,5},{5,4},{6,7},{7,6},{8,9},{9,8},{10,11... | collective-permute-start | bytes 1966088 | tf_op jit(solution)/shard_map/ppermute | solution.py:963
  179.4 8.1 %collective-permute-start.31 = (f32[640,256]{1,0:T(8,128)}, f32[640,256]{1,0:T(8,128)}, u32[]{:S(2)}, u32[]{:S(2)}) collective-permute-start(f32[640,256]{1,0:T(8,128)} %collective-permute-done.30.refs_6_.refs_2_), channel_id=1, source_target_pairs={{0,1},{1,0},{2,3},{3,2},{4,5},{5,4},{6,7},{7,6},{8,9},{9,8},{10,11... | collective-permute-start | bytes 1966088 | tf_op jit(solution)/shard_map/ppermute | solution.py:963
  187.1 31.1 %collective-permute-start.35 = (f32[320,1024]{1,0:T(8,128)S(1)}, f32[320,1024]{1,0:T(8,128)}, u32[]{:S(2)}, u32[]{:S(2)}) collective-permute-start(f32[320,1024]{1,0:T(8,128)S(1)} %collective-permute-done.16.refs_0_.refs_1_.own_ref), channel_id=1, source_target_pairs={{0,1},{1,0},{2,3},{3,2},{4,5},{5,4},{6,7},{7,6},{8,9},{9,8},{10,11... | collective-permute-start | bytes 3932168 | tf_op jit(solution)/shard_map/ppermute | solution.py:963
  187.4 28.5 %collective-permute-start.33 = (f32[320,256]{1,0:T(8,128)}, f32[320,256]{1,0:T(8,128)S(1)}, u32[]{:S(2)}, u32[]{:S(2)}) collective-permute-start(f32[320,256]{1,0:T(8,128)} %get-tuple-element.180), channel_id=1, source_target_pairs={{0,4},{4,0},{1,5},{5,1},{2,6},{6,2},{3,7},{7,3},{8,12},{12,8},{9,1... | collective-permute-start | bytes 983048 | tf_op jit(solution)/shard_map/ppermute | solution.py:960
  216.1 31.6 %collective-permute-start.36 = (f32[320,1024]{1,0:T(8,128)}, f32[320,1024]{1,0:T(8,128)S(1)}, u32[]{:S(2)}, u32[]{:S(2)}) collective-permute-start(f32[320,1024]{1,0:T(8,128)} %get-tuple-element.192), channel_id=1, source_target_pairs={{0,2},{2,0},{1,3},{3,1},{4,6},{6,4},{5,7},{7,5},{8,10},{10,8},{9,1... | collective-permute-start | bytes 3932168 | tf_op jit(solution)/shard_map/ppermute | solution.py:29
  229.9 32.4 %collective-permute-start.37 = (f32[2,2,64,1024]{3,2,1,0:T(8,128)}, f32[2,2,64,1024]{3,2,1,0:T(8,128)}, u32[]{:S(2)}, u32[]{:S(2)}) collective-permute-start(f32[2,2,64,1024]{3,2,1,0:T(8,128)} %get-tuple-element.197), channel_id=1, source_target_pairs={{0,8},{1,17},{8,0},{9,25},{16,24},{17,1},{24,16},{25,9},{2,10},{3,... | collective-permute-start | bytes 3145736 | tf_op jit(solution)/shard_map/ppermute | solution.py:882
  237.3 25.0 %collective-permute-start.40 = (f32[2,2,64,1024]{3,2,1,0:T(8,128)}, f32[2,2,64,1024]{3,2,1,0:T(8,128)}, u32[]{:S(2)}, u32[]{:S(2)}) collective-permute-start(f32[2,2,64,1024]{3,2,1,0:T(8,128)} %get-tuple-element.202), channel_id=1, source_target_pairs={{0,8},{1,17},{8,0},{9,25},{16,24},{17,1},{24,16},{25,9},{2,10},{3,... | collective-permute-start | bytes 3145736 | tf_op jit(solution)/shard_map/ppermute | solution.py:882
  238.1 23.5 %collective-permute-start.39 = (f32[320,256]{1,0:T(8,128)}, f32[320,256]{1,0:T(8,128)S(1)}, u32[]{:S(2)}, u32[]{:S(2)}) collective-permute-start(f32[320,256]{1,0:T(8,128)} %get-tuple-element.200), channel_id=1, source_target_pairs={{0,1},{1,0},{2,3},{3,2},{4,5},{5,4},{6,7},{7,6},{8,9},{9,8},{10,11... | collective-permute-start | bytes 983048 | tf_op jit(solution)/shard_map/ppermute | solution.py:963
  244.2 18.0 %collective-permute-start.38 = (f32[320,256]{1,0:T(8,128)S(1)}, f32[320,256]{1,0:T(8,128)S(1)}, u32[]{:S(2)}, u32[]{:S(2)}) collective-permute-start(f32[320,256]{1,0:T(8,128)S(1)} %copy-done.27), channel_id=1, source_target_pairs={{0,4},{4,0},{1,5},{5,1},{2,6},{6,2},{3,7},{7,3},{8,12},{12,8},{9,1... | collective-permute-start | bytes 983048 | tf_op jit(solution)/shard_map/ppermute | solution.py:960
  265.4 17.2 %collective-permute-start.42 = (f32[2,64,2048]{2,1,0:T(8,128)S(1)}, f32[2,64,2048]{2,1,0:T(8,128)S(1)}, u32[]{:S(2)}, u32[]{:S(2)}) collective-permute-start(f32[2,64,2048]{2,1,0:T(8,128)S(1)} %get-tuple-element.207), channel_id=1, source_target_pairs={{0,16},{1,9},{8,24},{9,1},{16,0},{17,25},{24,8},{25,17},{2,18},{3,... | collective-permute-start | bytes 3145736 | tf_op jit(solution)/shard_map/ppermute | solution.py:882
  281.4 28.0 %collective-permute-start.45 = (f32[320,512]{1,0:T(8,128)S(1)}, f32[320,512]{1,0:T(8,128)S(1)}, u32[]{:S(2)}, u32[]{:S(2)}) collective-permute-start(f32[320,512]{1,0:T(8,128)S(1)} %get-tuple-element.222), channel_id=1, source_target_pairs={{0,2},{2,0},{1,3},{3,1},{4,6},{6,4},{5,7},{7,5},{8,10},{10,8},{9,1... | collective-permute-start | bytes 1966088 | tf_op jit(solution)/shard_map/ppermute | solution.py:29
  283.5 26.9 %collective-permute-start.44 = (f32[64,2048]{1,0:T(8,128)S(1)}, f32[64,2048]{1,0:T(8,128)}, u32[]{:S(2)}, u32[]{:S(2)}) collective-permute-start(f32[64,2048]{1,0:T(8,128)S(1)} %get-tuple-element.216), channel_id=1, source_target_pairs={{0,5},{1,4},{4,1},{5,0},{2,7},{3,6},{6,3},{7,2},{8,13},{9,12},{12,... | collective-permute-start | bytes 1572872 | tf_op jit(solution)/shard_map/ppermute | solution.py:1084
  291.4 20.4 %collective-permute-start.43 = (f32[2,2,64,1024]{3,2,1,0:T(8,128)}, f32[2,2,64,1024]{3,2,1,0:T(8,128)S(1)}, u32[]{:S(2)}, u32[]{:S(2)}) collective-permute-start(f32[2,2,64,1024]{3,2,1,0:T(8,128)} %get-tuple-element.213), channel_id=1, source_target_pairs={{0,8},{1,17},{8,0},{9,25},{16,24},{17,1},{24,16},{25,9},{2,10},{3,... | collective-permute-start | bytes 3145736 | tf_op jit(solution)/shard_map/ppermute | solution.py:882
  298.8 18.8 %collective-permute-start.47 = (f32[2,2,64,1024]{3,2,1,0:T(8,128)}, f32[2,2,64,1024]{3,2,1,0:T(8,128)S(1)}, u32[]{:S(2)}, u32[]{:S(2)}) collective-permute-start(f32[2,2,64,1024]{3,2,1,0:T(8,128)} %get-tuple-element.226), channel_id=1, source_target_pairs={{0,8},{1,17},{8,0},{9,25},{16,24},{17,1},{24,16},{25,9},{2,10},{3,... | collective-permute-start | bytes 3145736 | tf_op jit(solution)/shard_map/ppermute | solution.py:882
  310.4 17.7 %collective-permute-start.51 = (f32[320,256]{1,0:T(8,128)}, f32[320,256]{1,0:T(8,128)S(1)}, u32[]{:S(2)}, u32[]{:S(2)}) collective-permute-start(f32[320,256]{1,0:T(8,128)} %get-tuple-element.223), channel_id=1, source_target_pairs={{0,5},{1,4},{4,1},{5,0},{2,7},{3,6},{6,3},{7,2},{8,13},{9,12},{12,... | collective-permute-start | bytes 983048 | tf_op jit(solution)/shard_map/ppermute | solution.py:1108
  319.4 10.3 %collective-permute-start.53 = (f32[64,2048]{1,0:T(8,128)S(1)}, f32[64,2048]{1,0:T(8,128)S(1)}, u32[]{:S(2)}, u32[]{:S(2)}) collective-permute-start(f32[64,2048]{1,0:T(8,128)S(1)} %get-tuple-element.238), channel_id=1, source_target_pairs={{0,16},{1,9},{8,24},{9,1},{16,0},{17,25},{24,8},{25,17},{2,18},{3,... | collective-permute-start | bytes 1572872 | tf_op jit(solution)/shard_map/ppermute | solution.py:882
  329.8 14.9 %collective-permute-start.58 = (f32[64,2048]{1,0:T(8,128)S(1)}, f32[64,2048]{1,0:T(8,128)S(1)}, u32[]{:S(2)}, u32[]{:S(2)}) collective-permute-start(f32[64,2048]{1,0:T(8,128)S(1)} %reduction_step.12.refs_0_), channel_id=1, source_target_pairs={{0,8},{1,17},{8,0},{9,25},{16,24},{17,1},{24,16},{25,9},{2,10},{3,... | collective-permute-start | bytes 1572872 | tf_op jit(solution)/shard_map/ppermute | solution.py:882
  330.9 13.7 %collective-permute-start.57 = (f32[64,2048]{1,0:T(8,128)S(1)}, f32[64,2048]{1,0:T(8,128)S(1)}, u32[]{:S(2)}, u32[]{:S(2)}) collective-permute-start(f32[64,2048]{1,0:T(8,128)S(1)} %reduction_step.12.refs_0_), channel_id=1, source_target_pairs={{0,16},{1,9},{8,24},{9,1},{16,0},{17,25},{24,8},{25,17},{2,18},{3,... | collective-permute-start | bytes 1572872 | tf_op jit(solution)/shard_map/ppermute | solution.py:882
  331.9 27.5 %collective-permute-start.49 = (f32[320,512]{1,0:T(8,128)S(1)}, f32[320,512]{1,0:T(8,128)S(1)}, u32[]{:S(2)}, u32[]{:S(2)}) collective-permute-start(f32[320,512]{1,0:T(8,128)S(1)} %copy-done.25), channel_id=1, source_target_pairs={{0,2},{2,0},{1,3},{3,1},{4,6},{6,4},{5,7},{7,5},{8,10},{10,8},{9,1... | collective-permute-start | bytes 1966088 | tf_op jit(solution)/shard_map/ppermute | solution.py:29
  331.9 17.6 %collective-permute-start.48 = (f32[64,2048]{1,0:T(8,128)S(1)}, f32[64,2048]{1,0:T(8,128)S(1)}, u32[]{:S(2)}, u32[]{:S(2)}) collective-permute-start(f32[64,2048]{1,0:T(8,128)S(1)} %get-tuple-element.228), channel_id=1, source_target_pairs={{0,16},{1,9},{8,24},{9,1},{16,0},{17,25},{24,8},{25,17},{2,18},{3,... | collective-permute-start | bytes 1572872 | tf_op jit(solution)/shard_map/ppermute | solution.py:882
  333.0 26.5 %collective-permute-start.54 = (f32[64,2048]{1,0:T(8,128)S(1)}, f32[64,2048]{1,0:T(8,128)S(1)}, u32[]{:S(2)}, u32[]{:S(2)}) collective-permute-start(f32[64,2048]{1,0:T(8,128)S(1)} %reduction_step.11), channel_id=1, source_target_pairs={{0,4},{4,0},{1,5},{5,1},{2,6},{6,2},{3,7},{7,3},{8,12},{12,8},{9,1... | collective-permute-start | bytes 1572872 | tf_op jit(solution)/shard_map/ppermute | solution.py:960
  344.7 14.8 %collective-permute-start.59 = (f32[64,2048]{1,0:T(8,128)S(1)}, f32[64,2048]{1,0:T(8,128)S(1)}, u32[]{:S(2)}, u32[]{:S(2)}) collective-permute-start(f32[64,2048]{1,0:T(8,128)S(1)} %collective-permute-done.58.refs_2_), channel_id=1, source_target_pairs={{0,16},{1,9},{8,24},{9,1},{16,0},{17,25},{24,8},{25,17},{2,18},{3,... | collective-permute-start | bytes 1572872 | tf_op jit(solution)/shard_map/ppermute | solution.py:882
  359.6 13.4 %collective-permute-start.61 = (f32[64,2048]{1,0:T(8,128)S(1)}, f32[64,2048]{1,0:T(8,128)S(1)}, u32[]{:S(2)}, u32[]{:S(2)}) collective-permute-start(f32[64,2048]{1,0:T(8,128)S(1)} %reduction_step.13.refs_0_), channel_id=1, source_target_pairs={{0,8},{1,17},{8,0},{9,25},{16,24},{17,1},{24,16},{25,9},{2,10},{3,... | collective-permute-start | bytes 1572872 | tf_op jit(solution)/shard_map/ppermute | solution.py:882
  360.7 12.3 %collective-permute-start.60 = (f32[64,2048]{1,0:T(8,128)S(1)}, f32[64,2048]{1,0:T(8,128)S(1)}, u32[]{:S(2)}, u32[]{:S(2)}) collective-permute-start(f32[64,2048]{1,0:T(8,128)S(1)} %reduction_step.13.refs_0_), channel_id=1, source_target_pairs={{0,16},{1,9},{8,24},{9,1},{16,0},{17,25},{24,8},{25,17},{2,18},{3,... | collective-permute-start | bytes 1572872 | tf_op jit(solution)/shard_map/ppermute | solution.py:882
  361.7 15.2 %collective-permute-start.55 = (f32[320,256]{1,0:T(8,128)S(1)}, f32[320,256]{1,0:T(8,128)S(1)}, u32[]{:S(2)}, u32[]{:S(2)}) collective-permute-start(f32[320,256]{1,0:T(8,128)S(1)} %copy-done.26), channel_id=1, source_target_pairs={{0,4},{4,0},{1,5},{5,1},{2,6},{6,2},{3,7},{7,3},{8,12},{12,8},{9,1... | collective-permute-start | bytes 983048 | tf_op jit(solution)/shard_map/ppermute | solution.py:960
  373.0 9.2 %collective-permute-start.62 = (f32[64,2048]{1,0:T(8,128)S(1)}, f32[64,2048]{1,0:T(8,128)S(1)}, u32[]{:S(2)}, u32[]{:S(2)}) collective-permute-start(f32[64,2048]{1,0:T(8,128)S(1)} %collective-permute-done.61.refs_2_), channel_id=1, source_target_pairs={{0,16},{1,9},{8,24},{9,1},{16,0},{17,25},{24,8},{25,17},{2,18},{3,... | collective-permute-start | bytes 1572872 | tf_op jit(solution)/shard_map/ppermute | solution.py:882
  (44 other events, 362.9 us)

commit v6 on v5

--- a/solution.py
+++ b/solution.py
@@ -1104,14 +1104,14 @@
     sums = [sums[:, 0], sums[:, 1], sums[:, 2]]
     aways = merge(kept, 1, received[1], apart=True)
     later = (in_hbm(later[0]), over_c(after(later[1], aways[0])))
-    come[0] = after(come[0], sums, later[1])
+    (later,) = step_of(later, cut=0, hbm_outs=(0,))
+    come[0] = after(come[0], sums, later)
     far_near = over_c(lax.ppermute(aways[0], ("h", "c"), DIAGONAL))
     near_sum, far_sum, near_go, far_go = step_of(
         (in_hbm(stay[0]), come[0]), (in_hbm(stay[1]), come[1]), cut=2
     )
     near_go, far_go = over_second(near_go), over_second(far_go)
     (go,) = step_of((far_sum, after(far_go, far_near)), cut=0)
-    (later,) = step_of(later, cut=0)
     later = after(later, go)
     go = over_h(go)
     later = plane_gather(later)

time: 386 us -> 386 us (level)
  no operation moved by 1% of the time
where the time goes in v6:
time: 386 us; the launch traced here: 385 us
  Pallas kernels  154 us (40%)
  waiting for transfers between devices  113 us (29%)
  blocking collectives  60.9 us (16%)
  starting transfers between devices  46 us (12%)
  local copies, waits for them, and re-layouts  7.17 us (2%)
    all_gather x8, blocking collectives, gather(): return lax.all_gather(array, axes, tiled=True)  60.9 us
    ppermute x7, waiting for transfers between devices, over_h(): return lax.ppermute(array, 'h', FLIP2)  38 us
    pallas_call x5, Pallas kernels, project(): call(partial(project_body, len(parts), len(flat), spots, len(weights), 0...  35.9 us
    pallas_call x4, Pallas kernels, weight_rows(): call(partial(weight_body, turn), grid_spec=pltpu.PrefetchScalarGridSpec(n...  26.5 us
    ppermute x13, waiting for transfers between devices, plane_swap(): return lax.ppermute(array, ('y', 'x', 'c'), pairs)  24.9 us
    ppermute x6, waiting for transfers between devices, swap_half(): return lax.ppermute(array, 'l', FLIP2)  20.3 us
    pallas_call x2, Pallas kernels, norm_back(): call(partial(norm_back_body, len(z), split_terms, layer), grid_spec=pltpu...  15.3 us
    pallas_call x4, Pallas kernels, prepare(): call(prepare_body, grid_spec=pltpu.PrefetchScalarGridSpec(num_scalar_pref...  15.1 us
  transfers between devices with their start and end apart: 63, of which 27 were waited for; matrix products, arithmetic and copies ran while one was open for 1% of the time, Pallas kernels for 37%

profile of v6, /device:TPU:0, one launch (start us, length us, event | category | flops | bytes accessed | tf_op | source)
XLA Modules:
  0.0 384.7 jit_solution(17243220486993467652)
XLA Ops:
  3.2 3.6 collective-permute-start.1
  10.7 2.9 pack.3
  15.6 15.5 %collective-permute-done.1.refs_12_.refs_8_.refs_7_.refs_4_ = f32[64,2048]{1,0:T(8,128)} collective-permute-done((f32[64,2048]{1,0:T(8,128)S(1)}, f32[64,2048]{1,0:T(8,128)}, u32[]{:S(2)}, u32[]{:S(2)}) %collective-permute-start.1) | collective-permute-done | bytes 524320 | tf_op jit(solution)/shard_map/ppermute | solution.py:960
  31.2 2.8 collective-permute-start.5
  34.7 5.0 %collective-permute-done.6.refs_4_.refs_2_ = f32[640,256]{1,0:T(8,128)S(1)} collective-permute-done((f32[640,256]{1,0:T(8,128)S(1)}, f32[640,256]{1,0:T(8,128)S(1)}, u32[]{:S(2)}, u32[]{:S(2)}) %collective-permute-start.6) | collective-permute-done | bytes 655392 | tf_op jit(solution)/shard_map/ppermute | solution.py:29
  39.7 19.1 %collective-permute-done.refs_2_.refs_8_ = f32[640,256]{1,0:T(8,128)S(1)} collective-permute-done((f32[640,256]{1,0:T(8,128)S(1)}, f32[640,256]{1,0:T(8,128)S(1)}, u32[]{:S(2)}, u32[]{:S(2)}) %collective-permute-start) | collective-permute-done | bytes 655392 | tf_op jit(solution)/shard_map/ppermute | solution.py:960
  65.3 9.9 %project.5 = (f32[320,1024]{1,0:T(8,128)}, f32[320,1024]{1,0:T(8,128)}) custom-call(s32[6]{0:T(128)S(1)} %concatenate.11.cols_ref, s32[8]{0:T(128)S(1)} %stack.124.place_ref, f32[640,256]{1,0:T(8,128)S(1)} %get-tuple-element.137.refs_0_.refs_6_, f32[640,256]{1,0:T(8,128)} %collective-permute-done.8.refs_1_.refs_7_, ...), custom_call_target="tpu_custom_call" | custom-call | flops 47185920 | bytes 98304 | tf_op jit(solution)/shard_map/project/pallas_call | solution.py:289
  78.3 6.0 %project.6 = (f32[320,1024]{1,0:T(8,128)}, f32[5,8,128]{2,1,0:T(8,128)S(1)}, f32[320,1024]{1,0:T(8,128)}) custom-call(s32[2]{0:T(128)S(1)} %pad_add_fusion.1.cols_ref, s32[8]{0:T(128)S(1)} %stack.124.place_ref, f32[640,256]{1,0:T(8,128)S(1)} %collective-permute-done.7.refs_0_.refs_4_, f32[320,256]{1,0:T(8,128)S(1)} %collective-permute-done.15.refs_1_.refs_5_, ...), custom_call_target="tpu_custom_call" | custom-call | flops 15728640 | bytes 32768 | tf_op jit(solution)/shard_map/project/pallas_call | solution.py:289
  85.0 6.2 %all_gather.24 = f32[20,8,128]{2,1,0:T(8,128)S(1)} all-gather(f32[5,8,128]{2,1,0:T(8,128)S(1)} %get-tuple-element.145), channel_id=1, replica_groups=mesh['y'=2,'x'=2,'h'=2,'l'=2,'c'=2] {'h','c'}, dimensions={0}, use_global_device_ids=true | all-gather | bytes 102400 | tf_op jit(solution)/shard_map/all_gather | solution.py:999
  93.5 9.2 %all_gather.25.refs_1_.refs_3_ = f32[80,8,128]{2,1,0:T(8,128)S(1)} all-gather(f32[20,8,128]{2,1,0:T(8,128)S(1)} %all_gather.24), channel_id=1, replica_groups=mesh['y'=2,'x'=2,'h'=2,'l'=2,'c'=2] {'y','x'}, dimensions={0}, use_global_device_ids=true | all-gather | bytes 409600 | tf_op jit(solution)/shard_map/all_gather | solution.py:999
  102.7 7.3 %recur.2 = (f32[320,1024]{1,0:T(8,128)S(1)}, f32[320,1024]{1,0:T(8,128)}, f32[320,1024]{1,0:T(8,128)}, f32[6,8,128]{2,1,0:T(8,128)S(1)}) custom-call(s32[8]{0:T(128)S(1)} %stack.124.place_ref, f32[320]{0:T(512)S(1)} %fusion.6.gate_ref, f32[320,1024]{1,0:T(8,128)} %get-tuple-element.144.refs_0_, f32[80,8,128]{2,1,0:T(8,128)S(1)} %all_gather.25.refs_1_.refs_3_, ...), custom_call_target="tpu_custom_call" | custom-call | flops 512000 | bytes 102400 | tf_op jit(solution)/shard_map/recur/pallas_call | solution.py:435
  111.8 5.4 %collective-permute-done.20 = f32[64,2048]{1,0:T(8,128)S(1)} collective-permute-done((f32[64,2048]{1,0:T(8,128)S(1)}, f32[64,2048]{1,0:T(8,128)S(1)}, u32[]{:S(2)}, u32[]{:S(2)}) %collective-permute-start.20) | collective-permute-done | bytes 524320 | tf_op jit(solution)/shard_map/ppermute | solution.py:1019
  124.0 3.8 prepare.4
  127.8 3.8 prepare.5
  131.5 5.2 %project.7.refs_3_ = f32[320,512]{1,0:T(8,128)} custom-call(s32[4]{0:T(128)S(1)} %pad_add_fusion.2.cols_ref, s32[8]{0:T(128)S(1)} %stack.124.place_ref, f32[320,1024]{1,0:T(8,128)S(1)} %get-tuple-element.160.refs_0_.own_ref.refs_5_, f32[2,256,2048]{2,1,0:T(8,128)} %refs_2_.1, ...), custom_call_target="tpu_custom_call" | custom-call | flops 15728640 | bytes 32768 | tf_op jit(solution)/shard_map/project/pallas_call | solution.py:289
  136.7 3.8 prepare.6
  140.5 6.4 %collective-permute-done.23.refs_4_.refs_10_.refs_8_ = f32[64,2048]{1,0:T(8,128)} collective-permute-done((f32[64,2048]{1,0:T(8,128)}, f32[64,2048]{1,0:T(8,128)}, u32[]{:S(2)}, u32[]{:S(2)}) %collective-permute-start.23) | collective-permute-done | bytes 524320 | tf_op jit(solution)/shard_map/ppermute | solution.py:978
  148.2 5.6 %project.8 = (f32[320,512]{1,0:T(8,128)}, f32[3,8,128]{2,1,0:T(8,128)S(1)}) custom-call(s32[4]{0:T(128)S(1)} %pad_add_fusion.cols_ref, s32[8]{0:T(128)S(1)} %stack.124.place_ref, f32[320,1024]{1,0:T(8,128)S(1)} %collective-permute-done.16.refs_0_.refs_1_.own_ref, f32[2,256,2048]{2,1,0:T(8,128)} %refs_2_.1, ...), custom_call_target="tpu_custom_call" | custom-call | flops 15728640 | bytes 32768 | tf_op jit(solution)/shard_map/project/pallas_call | solution.py:289
  154.3 9.2 %project.9 = (f32[320,512]{1,0:T(8,128)}, f32[3,8,128]{2,1,0:T(8,128)S(1)}) custom-call(s32[8]{0:T(128)S(1)} %concatenate.12.cols_ref, s32[8]{0:T(128)S(1)} %stack.124.place_ref, f32[320,1024]{1,0:T(8,128)S(1)} %copy-done.1, f32[320,1024]{1,0:T(8,128)S(1)} %collective-permute-done.16.refs_0_.refs_1_.own_ref, ...), custom_call_target="tpu_custom_call" | custom-call | flops 31457280 | bytes 65536 | tf_op jit(solution)/shard_map/project/pallas_call | solution.py:289
  163.4 8.2 %all_gather.26 = f32[12,8,128]{2,1,0:T(8,128)S(1)} all-gather(f32[3,8,128]{2,1,0:T(8,128)S(1)} %get-tuple-element.168), channel_id=1, replica_groups=mesh['y'=2,'x'=2,'h'=2,'l'=2,'c'=2] {'y','x'}, dimensions={0}, use_global_device_ids=true | all-gather | bytes 61440 | tf_op jit(solution)/shard_map/all_gather | solution.py:999
  171.6 7.7 %all_gather.27.refs_2_.refs_4_ = f32[48,8,128]{2,1,0:T(8,128)S(1)} all-gather(f32[12,8,128]{2,1,0:T(8,128)S(1)} %all_gather.26), channel_id=1, replica_groups=mesh['y'=2,'x'=2,'h'=2,'l'=2,'c'=2] {'h','c'}, dimensions={0}, use_global_device_ids=true | all-gather | bytes 245760 | tf_op jit(solution)/shard_map/all_gather | solution.py:999
  179.7 7.4 %recur.3 = (f32[320,256]{1,0:T(8,128)}, f32[320,256]{1,0:T(8,128)}, f32[320,256]{1,0:T(8,128)}, f32[320,256]{1,0:T(8,128)}, f32[320,1024]{1,0:T(8,128)}, /*index=5*/f32[320,1024]{1,0:T(8,128)}) custom-call(s32[8]{0:T(128)S(1)} %stack.124.place_ref, f32[320]{0:T(512)S(1)} %fusion.6.gate_ref, f32[320,512]{1,0:T(8,128)} %get-tuple-element.156.refs_0_, ...), custom_call_target="tpu_custom_call" | custom-call | flops 512000 | bytes 102400 | tf_op jit(solution)/shard_map/recur/pallas_call | solution.py:435
  187.4 5.6 %back.2 = (f32[320,1024]{1,0:T(8,128)S(1)}, f32[3,8,128]{2,1,0:T(8,128)S(1)}) custom-call(s32[8]{0:T(128)S(1)} %stack.124.place_ref, f32[320]{0:T(512)S(1)} %fusion.6.gate_ref, f32[320,512]{1,0:T(8,128)} %get-tuple-element.156.refs_0_, f32[320,512]{1,0:T(8,128)} %get-tuple-element.167.refs_1_, f32[48,8,128]{2,1,0:T(8,128)S(1)} %all_gather.27.refs_2_.refs_4_, ...), custom_call_target="tpu_custom_call" | custom-call | flops 153600 | bytes 102400 | tf_op jit(solution)/shard_map/back/pallas_call | solution.py:542
  193.1 7.4 %all_gather.28 = f32[12,8,128]{2,1,0:T(8,128)S(1)} all-gather(f32[3,8,128]{2,1,0:T(8,128)S(1)} %get-tuple-element.177), channel_id=1, replica_groups=mesh['y'=2,'x'=2,'h'=2,'l'=2,'c'=2] {'y','x'}, dimensions={0}, use_global_device_ids=true | all-gather | bytes 61440 | tf_op jit(solution)/shard_map/all_gather | solution.py:999
  200.5 7.4 %all_gather.29.refs_5_ = f32[48,8,128]{2,1,0:T(8,128)S(1)} all-gather(f32[12,8,128]{2,1,0:T(8,128)S(1)} %all_gather.28), channel_id=1, replica_groups=mesh['y'=2,'x'=2,'h'=2,'l'=2,'c'=2] {'h','c'}, dimensions={0}, use_global_device_ids=true | all-gather | bytes 245760 | tf_op jit(solution)/shard_map/all_gather | solution.py:999
  207.8 7.7 %norm_back.2 = (f32[320,1024]{1,0:T(8,128)}, f32[320,512]{1,0:T(8,128)S(1)}, f32[320,1024]{1,0:T(8,128)}, f32[3,8,128]{2,1,0:T(8,128)S(1)}) custom-call(s32[2]{0:T(128)S(1)} %pad_add_fusion.4.cols_ref, s32[8]{0:T(128)S(1)} %stack.124.place_ref, f32[320,1024]{1,0:T(8,128)S(1)} %get-tuple-element.176.grad_ref, f32[320,512]{1,0:T(8,128)} %get-tuple-element.156.refs_0_, ...), custom_call_target="tpu_custom_call" | custom-call | flops 31457280 | bytes 65536 | tf_op jit(solution)/shard_map/norm_back/pallas_call | solution.py:647
  218.2 3.8 prepare.7
  222.7 7.2 %weight_rows.4 = (f32[2,2,64,1024]{3,2,1,0:T(8,128)}, f32[2,2,64,1024]{3,2,1,0:T(8,128)}, bf16[512,768]{1,0:T(8,128)(2,1)S(1)}, bf16[512,768]{1,0:T(8,128)(2,1)S(1)}) custom-call(s32[8]{0:T(128)S(1)} %stack.124.place_ref, f32[320,1024]{1,0:T(8,128)} %get-tuple-element.191.refs_0_.grad_ref, f32[320,512]{1,0:T(8,128)S(1)} %collective-permute-done.32.refs_1_, ...), custom_call_target="tpu_custom_call" | custom-call | flops 37748736 | bytes 32768 | tf_op jit(solution)/shard_map/weight_rows/pallas_call | solution.py:820
  231.2 6.1 %weight_rows.5 = (f32[2,2,64,1024]{3,2,1,0:T(8,128)}, f32[2,2,64,1024]{3,2,1,0:T(8,128)}) custom-call(s32[8]{0:T(128)S(1)} %stack.124.place_ref, bf16[512,768]{1,0:T(8,128)(2,1)S(1)} %get-tuple-element.187.refs_0_, bf16[512,768]{1,0:T(8,128)(2,1)S(1)} %get-tuple-element.188.refs_1_, bf16[768,1024]{1,0:T(8,128)(2,1)} %get-tuple-element.184.refs_2_, ...), custom_call_target="tpu_custom_call" | custom-call | flops 37748736 | bytes 32768 | tf_op jit(solution)/shard_map/weight_rows/pallas_call | solution.py:820
  238.1 6.1 %own_terms.2.refs_3_.refs_0_ = f32[320,1024]{1,0:T(8,128)S(1)} custom-call(s32[2]{0:T(128)S(1)} %pad_add_fusion.5.cols_ref, s32[8]{0:T(128)S(1)} %stack.124.place_ref, f32[320,1024]{1,0:T(8,128)} %get-tuple-element.191.refs_0_.grad_ref, f32[640,256]{1,0:T(8,128)S(1)} %copy-done.6, f32[640,256]{1,0:T(8,128)} %collective-permute-done.29.refs_5_.refs_1_, ...), custom_call_target="tpu_custom_call" | custom-call | flops 31457280 | bytes 65536 | tf_op jit(solution)/shard_map/own_terms/pallas_call | solution.py:705
  244.7 3.0 collective-permute-done.36.refs_4_.refs_1_
  247.7 5.9 %back.3 = (f32[320,1024]{1,0:T(8,128)S(1)}, f32[3,8,128]{2,1,0:T(8,128)S(1)}) custom-call(s32[8]{0:T(128)S(1)} %stack.124.place_ref, f32[320]{0:T(512)S(1)} %fusion.6.gate_ref, f32[320,1024]{1,0:T(8,128)} %get-tuple-element.144.refs_0_, f32[80,8,128]{2,1,0:T(8,128)S(1)} %all_gather.25.refs_1_.refs_3_, ...), custom_call_target="tpu_custom_call" | custom-call | flops 153600 | bytes 102400 | tf_op jit(solution)/shard_map/back/pallas_call | solution.py:542
  253.6 8.0 %all_gather.30 = f32[12,8,128]{2,1,0:T(8,128)S(1)} all-gather(f32[3,8,128]{2,1,0:T(8,128)S(1)} %get-tuple-element.195), channel_id=1, replica_groups=mesh['y'=2,'x'=2,'h'=2,'l'=2,'c'=2] {'y','x'}, dimensions={0}, use_global_device_ids=true | all-gather | bytes 61440 | tf_op jit(solution)/shard_map/all_gather | solution.py:999
  266.8 6.7 %all_gather.31.refs_4_ = f32[48,8,128]{2,1,0:T(8,128)S(1)} all-gather(f32[12,8,128]{2,1,0:T(8,128)S(1)} %all_gather.30), channel_id=1, replica_groups=mesh['y'=2,'x'=2,'h'=2,'l'=2,'c'=2] {'h','c'}, dimensions={0}, use_global_device_ids=true | all-gather | bytes 245760 | tf_op jit(solution)/shard_map/all_gather | solution.py:999
  273.5 7.6 %norm_back.3 = (f32[320,1024]{1,0:T(8,128)}, f32[320,512]{1,0:T(8,128)S(1)}, f32[320,512]{1,0:T(8,128)}, f32[320,512]{1,0:T(8,128)S(1)}, f32[3,8,128]{2,1,0:T(8,128)S(1)}) custom-call(s32[2]{0:T(128)S(1)} %pad_add_fusion.4.cols_ref, s32[8]{0:T(128)S(1)} %stack.124.place_ref, f32[320,1024]{1,0:T(8,128)S(1)} %get-tuple-element.194.grad_ref, ...), custom_call_target="tpu_custom_call" | custom-call | flops 31457280 | bytes 65536 | tf_op jit(solution)/shard_map/norm_back/pallas_call | solution.py:647
  284.2 7.2 %weight_rows.6 = (f32[2,2,64,1024]{3,2,1,0:T(8,128)}, f32[2,2,64,1024]{3,2,1,0:T(8,128)}, bf16[512,768]{1,0:T(8,128)(2,1)S(1)}, bf16[512,768]{1,0:T(8,128)(2,1)S(1)}) custom-call(s32[8]{0:T(128)S(1)} %stack.124.place_ref, f32[320,1024]{1,0:T(8,128)} %get-tuple-element.221.refs_0_.grad_ref, f32[320,512]{1,0:T(8,128)S(1)} %collective-permute-done.41.refs_1_, ...), custom_call_target="tpu_custom_call" | custom-call | flops 37748736 | bytes 32768 | tf_op jit(solution)/shard_map/weight_rows/pallas_call | solution.py:820
  292.7 6.1 %weight_rows.7 = (f32[2,2,64,1024]{3,2,1,0:T(8,128)}, f32[2,2,64,1024]{3,2,1,0:T(8,128)}) custom-call(s32[8]{0:T(128)S(1)} %stack.124.place_ref, bf16[512,768]{1,0:T(8,128)(2,1)S(1)} %get-tuple-element.217.refs_0_, bf16[512,768]{1,0:T(8,128)(2,1)S(1)} %get-tuple-element.218.refs_1_, bf16[768,1024]{1,0:T(8,128)(2,1)} %get-tuple-element.154.refs_2_, ...), custom_call_target="tpu_custom_call" | custom-call | flops 37748736 | bytes 32768 | tf_op jit(solution)/shard_map/weight_rows/pallas_call | solution.py:820
  299.5 6.0 %own_terms.3.kept_ref = f32[320,1024]{1,0:T(8,128)S(1)} custom-call(s32[2]{0:T(128)S(1)} %pad_add_fusion.5.cols_ref, s32[8]{0:T(128)S(1)} %stack.124.place_ref, f32[320,1024]{1,0:T(8,128)} %get-tuple-element.221.refs_0_.grad_ref, f32[320,1024]{1,0:T(8,128)S(1)} %own_terms.2.refs_3_.refs_0_, f32[320,1024]{1,0:T(8,128)S(1)} %copy-done.4, ...), custom_call_target="tpu_custom_call" | custom-call | flops 31457280 | bytes 65536 | tf_op jit(solution)/shard_map/own_terms/pallas_call | solution.py:705
  305.6 3.9 %collective-permute-done.45.come_ref = f32[320,512]{1,0:T(8,128)S(1)} collective-permute-done((f32[320,512]{1,0:T(8,128)S(1)}, f32[320,512]{1,0:T(8,128)S(1)}, u32[]{:S(2)}, u32[]{:S(2)}) %collective-permute-start.45) | collective-permute-done | bytes 655392 | tf_op jit(solution)/shard_map/ppermute | solution.py:29
  314.7 2.9 collective-permute-done.47.refs_3_
  320.8 7.3 %collective-permute-done.51 = f32[320,256]{1,0:T(8,128)S(1)} collective-permute-done((f32[320,256]{1,0:T(8,128)}, f32[320,256]{1,0:T(8,128)S(1)}, u32[]{:S(2)}, u32[]{:S(2)}) %collective-permute-start.51) | collective-permute-done | bytes 327712 | tf_op jit(solution)/shard_map/ppermute | solution.py:1109
  335.2 9.5 %collective-permute-done.58.refs_2_ = f32[64,2048]{1,0:T(8,128)S(1)} collective-permute-done((f32[64,2048]{1,0:T(8,128)S(1)}, f32[64,2048]{1,0:T(8,128)S(1)}, u32[]{:S(2)}, u32[]{:S(2)}) %collective-permute-start.58) | collective-permute-done | bytes 524320 | tf_op jit(solution)/shard_map/ppermute | solution.py:882
  345.8 3.6 collective-permute-done.48.refs_1_
  349.5 2.8 unpack.2
  352.3 7.0 %collective-permute-done.49.come_ref = f32[320,512]{1,0:T(8,128)S(1)} collective-permute-done((f32[320,512]{1,0:T(8,128)S(1)}, f32[320,512]{1,0:T(8,128)S(1)}, u32[]{:S(2)}, u32[]{:S(2)}) %collective-permute-start.49) | collective-permute-done | bytes 655392 | tf_op jit(solution)/shard_map/ppermute | solution.py:29
  362.7 3.0 assemble.2.refs_4_
  365.7 7.2 %collective-permute-done.61.refs_2_ = f32[64,2048]{1,0:T(8,128)S(1)} collective-permute-done((f32[64,2048]{1,0:T(8,128)S(1)}, f32[64,2048]{1,0:T(8,128)S(1)}, u32[]{:S(2)}, u32[]{:S(2)}) %collective-permute-start.61) | collective-permute-done | bytes 524320 | tf_op jit(solution)/shard_map/ppermute | solution.py:882
  373.9 2.9 collective-permute-done.55
  (205 shorter events, 77.9 us)
Async XLA Ops:
  0.6 30.4 %collective-permute-start.2 = (f32[2,256,2048]{2,1,0:T(8,128)}, f32[2,256,2048]{2,1,0:T(8,128)}, u32[]{:S(2)}, u32[]{:S(2)}) collective-permute-start(f32[2,256,2048]{2,1,0:T(8,128)} %refs_2_.1), channel_id=1, source_target_pairs={{0,1},{1,0},{2,3},{3,2},{4,5},{5,4},{6,7},{7,6},{8,9},{9,8},{10,11... | collective-permute-start | bytes 12582920 | tf_op jit(solution)/shard_map/ppermute | solution.py:963
  3.2 27.8 %collective-permute-start.1 = (f32[64,2048]{1,0:T(8,128)S(1)}, f32[64,2048]{1,0:T(8,128)}, u32[]{:S(2)}, u32[]{:S(2)}) collective-permute-start(f32[64,2048]{1,0:T(8,128)S(1)} %get-tuple-element.254), channel_id=1, source_target_pairs={{0,4},{4,0},{1,5},{5,1},{2,6},{6,2},{3,7},{7,3},{8,12},{12,8},{9,1... | collective-permute-start | bytes 1572872 | tf_op jit(solution)/shard_map/ppermute | solution.py:960
  8.8 30.9 %collective-permute-start.6 = (f32[640,256]{1,0:T(8,128)S(1)}, f32[640,256]{1,0:T(8,128)S(1)}, u32[]{:S(2)}, u32[]{:S(2)}) collective-permute-start(f32[640,256]{1,0:T(8,128)S(1)} %get-tuple-element.137.refs_0_.refs_6_), channel_id=1, source_target_pairs={{0,2},{2,0},{1,3},{3,1},{4,6},{6,4},{5,7},{7,5},{8,10},{10,8},{9,1... | collective-permute-start | bytes 1966088 | tf_op jit(solution)/shard_map/ppermute | solution.py:29
  10.4 48.4 %collective-permute-start = (f32[640,256]{1,0:T(8,128)S(1)}, f32[640,256]{1,0:T(8,128)S(1)}, u32[]{:S(2)}, u32[]{:S(2)}) collective-permute-start(f32[640,256]{1,0:T(8,128)S(1)} %get-tuple-element.131), channel_id=1, source_target_pairs={{0,4},{4,0},{1,5},{5,1},{2,6},{6,2},{3,7},{7,3},{8,12},{12,8},{9,1... | collective-permute-start | bytes 1966088 | tf_op jit(solution)/shard_map/ppermute | solution.py:960
  31.2 27.6 %collective-permute-start.5 = (f32[64,2048]{1,0:T(8,128)}, f32[64,2048]{1,0:T(8,128)}, u32[]{:S(2)}, u32[]{:S(2)}) collective-permute-start(f32[64,2048]{1,0:T(8,128)} %collective-permute-done.1.refs_12_.refs_8_.refs_7_.refs_4_), channel_id=1, source_target_pairs={{0,24},{8,16},{16,8},{24,0},{1,25},{9,17},{17,9},{25,1},{2,26},{10... | collective-permute-start | bytes 1572872 | tf_op jit(solution)/shard_map/ppermute | solution.py:977
  33.9 24.8 %collective-permute-start.4 = (f32[64,2048]{1,0:T(8,128)}, f32[64,2048]{1,0:T(8,128)}, u32[]{:S(2)}, u32[]{:S(2)}) collective-permute-start(f32[64,2048]{1,0:T(8,128)} %collective-permute-done.1.refs_12_.refs_8_.refs_7_.refs_4_), channel_id=1, source_target_pairs={{0,16},{16,0},{1,17},{17,1},{2,18},{18,2},{3,19},{19,3},{4,20},{20... | collective-permute-start | bytes 1572872 | tf_op jit(solution)/shard_map/ppermute | solution.py:978
  34.5 24.3 %collective-permute-start.3 = (f32[64,2048]{1,0:T(8,128)}, f32[64,2048]{1,0:T(8,128)S(1)}, u32[]{:S(2)}, u32[]{:S(2)}) collective-permute-start(f32[64,2048]{1,0:T(8,128)} %collective-permute-done.1.refs_12_.refs_8_.refs_7_.refs_4_), channel_id=1, source_target_pairs={{0,8},{8,0},{1,9},{9,1},{2,10},{10,2},{3,11},{11,3},{4,12},{12,4},... | collective-permute-start | bytes 1572872 | tf_op jit(solution)/shard_map/ppermute | solution.py:978
  39.7 20.2 %collective-permute-start.10 = (f32[640,256]{1,0:T(8,128)S(1)}, f32[640,256]{1,0:T(8,128)S(1)}, u32[]{:S(2)}, u32[]{:S(2)}) collective-permute-start(f32[640,256]{1,0:T(8,128)S(1)} %collective-permute-done.6.refs_4_.refs_2_), channel_id=1, source_target_pairs={{0,1},{1,0},{2,3},{3,2},{4,5},{5,4},{6,7},{7,6},{8,9},{9,8},{10,11... | collective-permute-start | bytes 1966088 | tf_op jit(solution)/shard_map/ppermute | solution.py:963
  59.9 16.7 %collective-permute-start.7 = (f32[640,256]{1,0:T(8,128)S(1)}, f32[640,256]{1,0:T(8,128)S(1)}, u32[]{:S(2)}, u32[]{:S(2)}) collective-permute-start(f32[640,256]{1,0:T(8,128)S(1)} %collective-permute-done.refs_2_.refs_8_), channel_id=1, source_target_pairs={{0,2},{2,0},{1,3},{3,1},{4,6},{6,4},{5,7},{7,5},{8,10},{10,8},{9,1... | collective-permute-start | bytes 1966088 | tf_op jit(solution)/shard_map/ppermute | solution.py:29
  84.4 34.8 %collective-permute-start.18 = (f32[320,1024]{1,0:T(8,128)S(1)}, f32[320,1024]{1,0:T(8,128)S(1)}, u32[]{:S(2)}, u32[]{:S(2)}) collective-permute-start(f32[320,1024]{1,0:T(8,128)S(1)} %copy-done.10), channel_id=1, source_target_pairs={{0,1},{1,0},{2,3},{3,2},{4,5},{5,4},{6,7},{7,6},{8,9},{9,8},{10,11... | collective-permute-start | bytes 3932168 | tf_op jit(solution)/shard_map/ppermute | solution.py:963
  84.6 35.7 %collective-permute-start.19 = (f32[320,1024]{1,0:T(8,128)}, f32[320,1024]{1,0:T(8,128)}, u32[]{:S(2)}, u32[]{:S(2)}) collective-permute-start(f32[320,1024]{1,0:T(8,128)} %get-tuple-element.153.own_ref), channel_id=1, source_target_pairs={{0,1},{1,0},{2,3},{3,2},{4,5},{5,4},{6,7},{7,6},{8,9},{9,8},{10,11... | collective-permute-start | bytes 3932168 | tf_op jit(solution)/shard_map/ppermute | solution.py:963
  91.1 26.0 %collective-permute-start.20 = (f32[64,2048]{1,0:T(8,128)S(1)}, f32[64,2048]{1,0:T(8,128)S(1)}, u32[]{:S(2)}, u32[]{:S(2)}) collective-permute-start(f32[64,2048]{1,0:T(8,128)S(1)} %copy-done.13), channel_id=1, source_target_pairs={{0,5},{1,4},{4,1},{5,0},{2,7},{3,6},{6,3},{7,2},{8,13},{9,12},{12,... | collective-permute-start | bytes 1572872 | tf_op jit(solution)/shard_map/ppermute | solution.py:1019
  110.0 14.0 %collective-permute-start.17 = (f32[320,1024]{1,0:T(8,128)S(1)}, f32[320,1024]{1,0:T(8,128)}, u32[]{:S(2)}, u32[]{:S(2)}) collective-permute-start(f32[320,1024]{1,0:T(8,128)S(1)} %get-tuple-element.160.refs_0_.own_ref.refs_5_), channel_id=1, source_target_pairs={{0,1},{1,0},{2,3},{3,2},{4,5},{5,4},{6,7},{7,6},{8,9},{9,8},{10,11... | collective-permute-start | bytes 3932168 | tf_op jit(solution)/shard_map/ppermute | solution.py:963
  110.0 37.6 %collective-permute-start.16 = (f32[320,1024]{1,0:T(8,128)S(1)}, f32[320,1024]{1,0:T(8,128)S(1)}, u32[]{:S(2)}, u32[]{:S(2)}) collective-permute-start(f32[320,1024]{1,0:T(8,128)S(1)} %get-tuple-element.160.refs_0_.own_ref.refs_5_), channel_id=1, source_target_pairs={{0,2},{2,0},{1,3},{3,1},{4,6},{6,4},{5,7},{7,5},{8,10},{10,8},{9,1... | collective-permute-start | bytes 3932168 | tf_op jit(solution)/shard_map/ppermute | solution.py:29
  120.3 20.2 %collective-permute-start.24 = (f32[64,2048]{1,0:T(8,128)}, f32[64,2048]{1,0:T(8,128)}, u32[]{:S(2)}, u32[]{:S(2)}) collective-permute-start(f32[64,2048]{1,0:T(8,128)} %collective-permute-done.21.refs_2_.refs_8_.refs_6_), channel_id=1, source_target_pairs={{0,24},{8,16},{16,8},{24,0},{1,25},{9,17},{17,9},{25,1},{2,26},{10... | collective-permute-start | bytes 1572872 | tf_op jit(solution)/shard_map/ppermute | solution.py:977
  122.8 24.1 %collective-permute-start.23 = (f32[64,2048]{1,0:T(8,128)}, f32[64,2048]{1,0:T(8,128)}, u32[]{:S(2)}, u32[]{:S(2)}) collective-permute-start(f32[64,2048]{1,0:T(8,128)} %collective-permute-done.21.refs_2_.refs_8_.refs_6_), channel_id=1, source_target_pairs={{0,16},{16,0},{1,17},{17,1},{2,18},{18,2},{3,19},{19,3},{4,20},{20... | collective-permute-start | bytes 1572872 | tf_op jit(solution)/shard_map/ppermute | solution.py:978
  123.3 23.7 %collective-permute-start.22 = (f32[64,2048]{1,0:T(8,128)}, f32[64,2048]{1,0:T(8,128)}, u32[]{:S(2)}, u32[]{:S(2)}) collective-permute-start(f32[64,2048]{1,0:T(8,128)} %collective-permute-done.21.refs_2_.refs_8_.refs_6_), channel_id=1, source_target_pairs={{0,8},{8,0},{1,9},{9,1},{2,10},{10,2},{3,11},{11,3},{4,12},{12,4},... | collective-permute-start | bytes 1572872 | tf_op jit(solution)/shard_map/ppermute | solution.py:978
  140.5 38.8 %collective-permute-start.30 = (f32[640,256]{1,0:T(8,128)}, f32[640,256]{1,0:T(8,128)}, u32[]{:S(2)}, u32[]{:S(2)}) collective-permute-start(f32[640,256]{1,0:T(8,128)} %get-tuple-element.172), channel_id=1, source_target_pairs={{0,4},{4,0},{1,5},{5,1},{2,6},{6,2},{3,7},{7,3},{8,12},{12,8},{9,1... | collective-permute-start | bytes 1966088 | tf_op jit(solution)/shard_map/ppermute | solution.py:960
  147.0 6.8 %collective-permute-start.25 = (f32[64,2048]{1,0:T(8,128)}, f32[64,2048]{1,0:T(8,128)}, u32[]{:S(2)}, u32[]{:S(2)}) collective-permute-start(f32[64,2048]{1,0:T(8,128)} %collective-permute-done.21.refs_2_.refs_8_.refs_6_), channel_id=1, source_target_pairs={{0,1},{1,0},{2,3},{3,2},{4,5},{5,4},{6,7},{7,6},{8,9},{9,8},{10,11... | collective-permute-start | bytes 1572872 | tf_op jit(solution)/shard_map/ppermute | solution.py:963
  147.0 7.2 %collective-permute-start.26 = (f32[64,2048]{1,0:T(8,128)}, f32[64,2048]{1,0:T(8,128)}, u32[]{:S(2)}, u32[]{:S(2)}) collective-permute-start(f32[64,2048]{1,0:T(8,128)} %collective-permute-done.22.refs_3_.refs_9_.refs_7_), channel_id=1, source_target_pairs={{0,1},{1,0},{2,3},{3,2},{4,5},{5,4},{6,7},{7,6},{8,9},{9,8},{10,11... | collective-permute-start | bytes 1572872 | tf_op jit(solution)/shard_map/ppermute | solution.py:963
  147.6 6.7 %collective-permute-start.27 = (f32[64,2048]{1,0:T(8,128)}, f32[64,2048]{1,0:T(8,128)}, u32[]{:S(2)}, u32[]{:S(2)}) collective-permute-start(f32[64,2048]{1,0:T(8,128)} %collective-permute-done.23.refs_4_.refs_10_.refs_8_), channel_id=1, source_target_pairs={{0,1},{1,0},{2,3},{3,2},{4,5},{5,4},{6,7},{7,6},{8,9},{9,8},{10,11... | collective-permute-start | bytes 1572872 | tf_op jit(solution)/shard_map/ppermute | solution.py:963
  147.6 6.7 %collective-permute-start.28 = (f32[64,2048]{1,0:T(8,128)}, f32[64,2048]{1,0:T(8,128)}, u32[]{:S(2)}, u32[]{:S(2)}) collective-permute-start(f32[64,2048]{1,0:T(8,128)} %collective-permute-done.24.refs_5_.refs_11_.refs_9_), channel_id=1, source_target_pairs={{0,1},{1,0},{2,3},{3,2},{4,5},{5,4},{6,7},{7,6},{8,9},{9,8},{10,11... | collective-permute-start | bytes 1572872 | tf_op jit(solution)/shard_map/ppermute | solution.py:963
  153.9 33.5 %collective-permute-start.29 = (f32[640,256]{1,0:T(8,128)S(1)}, f32[640,256]{1,0:T(8,128)}, u32[]{:S(2)}, u32[]{:S(2)}) collective-permute-start(f32[640,256]{1,0:T(8,128)S(1)} %copy-done.5), channel_id=1, source_target_pairs={{0,1},{1,0},{2,3},{3,2},{4,5},{5,4},{6,7},{7,6},{8,9},{9,8},{10,11... | collective-permute-start | bytes 1966088 | tf_op jit(solution)/shard_map/ppermute | solution.py:963
  179.4 8.1 %collective-permute-start.31 = (f32[640,256]{1,0:T(8,128)}, f32[640,256]{1,0:T(8,128)}, u32[]{:S(2)}, u32[]{:S(2)}) collective-permute-start(f32[640,256]{1,0:T(8,128)} %collective-permute-done.30.refs_6_.refs_2_), channel_id=1, source_target_pairs={{0,1},{1,0},{2,3},{3,2},{4,5},{5,4},{6,7},{7,6},{8,9},{9,8},{10,11... | collective-permute-start | bytes 1966088 | tf_op jit(solution)/shard_map/ppermute | solution.py:963
  187.1 31.1 %collective-permute-start.35 = (f32[320,1024]{1,0:T(8,128)S(1)}, f32[320,1024]{1,0:T(8,128)}, u32[]{:S(2)}, u32[]{:S(2)}) collective-permute-start(f32[320,1024]{1,0:T(8,128)S(1)} %collective-permute-done.16.refs_0_.refs_1_.own_ref), channel_id=1, source_target_pairs={{0,1},{1,0},{2,3},{3,2},{4,5},{5,4},{6,7},{7,6},{8,9},{9,8},{10,11... | collective-permute-start | bytes 3932168 | tf_op jit(solution)/shard_map/ppermute | solution.py:963
  187.4 28.5 %collective-permute-start.33 = (f32[320,256]{1,0:T(8,128)}, f32[320,256]{1,0:T(8,128)S(1)}, u32[]{:S(2)}, u32[]{:S(2)}) collective-permute-start(f32[320,256]{1,0:T(8,128)} %get-tuple-element.180), channel_id=1, source_target_pairs={{0,4},{4,0},{1,5},{5,1},{2,6},{6,2},{3,7},{7,3},{8,12},{12,8},{9,1... | collective-permute-start | bytes 983048 | tf_op jit(solution)/shard_map/ppermute | solution.py:960
  216.1 31.6 %collective-permute-start.36 = (f32[320,1024]{1,0:T(8,128)}, f32[320,1024]{1,0:T(8,128)S(1)}, u32[]{:S(2)}, u32[]{:S(2)}) collective-permute-start(f32[320,1024]{1,0:T(8,128)} %get-tuple-element.192), channel_id=1, source_target_pairs={{0,2},{2,0},{1,3},{3,1},{4,6},{6,4},{5,7},{7,5},{8,10},{10,8},{9,1... | collective-permute-start | bytes 3932168 | tf_op jit(solution)/shard_map/ppermute | solution.py:29
  229.9 32.4 %collective-permute-start.37 = (f32[2,2,64,1024]{3,2,1,0:T(8,128)}, f32[2,2,64,1024]{3,2,1,0:T(8,128)}, u32[]{:S(2)}, u32[]{:S(2)}) collective-permute-start(f32[2,2,64,1024]{3,2,1,0:T(8,128)} %get-tuple-element.197), channel_id=1, source_target_pairs={{0,8},{1,17},{8,0},{9,25},{16,24},{17,1},{24,16},{25,9},{2,10},{3,... | collective-permute-start | bytes 3145736 | tf_op jit(solution)/shard_map/ppermute | solution.py:882
  237.3 25.0 %collective-permute-start.40 = (f32[2,2,64,1024]{3,2,1,0:T(8,128)}, f32[2,2,64,1024]{3,2,1,0:T(8,128)}, u32[]{:S(2)}, u32[]{:S(2)}) collective-permute-start(f32[2,2,64,1024]{3,2,1,0:T(8,128)} %get-tuple-element.202), channel_id=1, source_target_pairs={{0,8},{1,17},{8,0},{9,25},{16,24},{17,1},{24,16},{25,9},{2,10},{3,... | collective-permute-start | bytes 3145736 | tf_op jit(solution)/shard_map/ppermute | solution.py:882
  238.1 23.5 %collective-permute-start.39 = (f32[320,256]{1,0:T(8,128)}, f32[320,256]{1,0:T(8,128)S(1)}, u32[]{:S(2)}, u32[]{:S(2)}) collective-permute-start(f32[320,256]{1,0:T(8,128)} %get-tuple-element.200), channel_id=1, source_target_pairs={{0,1},{1,0},{2,3},{3,2},{4,5},{5,4},{6,7},{7,6},{8,9},{9,8},{10,11... | collective-permute-start | bytes 983048 | tf_op jit(solution)/shard_map/ppermute | solution.py:963
  244.2 18.0 %collective-permute-start.38 = (f32[320,256]{1,0:T(8,128)S(1)}, f32[320,256]{1,0:T(8,128)S(1)}, u32[]{:S(2)}, u32[]{:S(2)}) collective-permute-start(f32[320,256]{1,0:T(8,128)S(1)} %copy-done.27), channel_id=1, source_target_pairs={{0,4},{4,0},{1,5},{5,1},{2,6},{6,2},{3,7},{7,3},{8,12},{12,8},{9,1... | collective-permute-start | bytes 983048 | tf_op jit(solution)/shard_map/ppermute | solution.py:960
  265.4 17.2 %collective-permute-start.42 = (f32[2,64,2048]{2,1,0:T(8,128)S(1)}, f32[2,64,2048]{2,1,0:T(8,128)S(1)}, u32[]{:S(2)}, u32[]{:S(2)}) collective-permute-start(f32[2,64,2048]{2,1,0:T(8,128)S(1)} %get-tuple-element.207), channel_id=1, source_target_pairs={{0,16},{1,9},{8,24},{9,1},{16,0},{17,25},{24,8},{25,17},{2,18},{3,... | collective-permute-start | bytes 3145736 | tf_op jit(solution)/shard_map/ppermute | solution.py:882
  281.4 28.0 %collective-permute-start.45 = (f32[320,512]{1,0:T(8,128)S(1)}, f32[320,512]{1,0:T(8,128)S(1)}, u32[]{:S(2)}, u32[]{:S(2)}) collective-permute-start(f32[320,512]{1,0:T(8,128)S(1)} %get-tuple-element.222), channel_id=1, source_target_pairs={{0,2},{2,0},{1,3},{3,1},{4,6},{6,4},{5,7},{7,5},{8,10},{10,8},{9,1... | collective-permute-start | bytes 1966088 | tf_op jit(solution)/shard_map/ppermute | solution.py:29
  283.5 26.9 %collective-permute-start.44 = (f32[64,2048]{1,0:T(8,128)S(1)}, f32[64,2048]{1,0:T(8,128)}, u32[]{:S(2)}, u32[]{:S(2)}) collective-permute-start(f32[64,2048]{1,0:T(8,128)S(1)} %get-tuple-element.216), channel_id=1, source_target_pairs={{0,5},{1,4},{4,1},{5,0},{2,7},{3,6},{6,3},{7,2},{8,13},{9,12},{12,... | collective-permute-start | bytes 1572872 | tf_op jit(solution)/shard_map/ppermute | solution.py:1084
  291.4 23.3 %collective-permute-start.43 = (f32[2,2,64,1024]{3,2,1,0:T(8,128)}, f32[2,2,64,1024]{3,2,1,0:T(8,128)S(1)}, u32[]{:S(2)}, u32[]{:S(2)}) collective-permute-start(f32[2,2,64,1024]{3,2,1,0:T(8,128)} %get-tuple-element.213), channel_id=1, source_target_pairs={{0,8},{1,17},{8,0},{9,25},{16,24},{17,1},{24,16},{25,9},{2,10},{3,... | collective-permute-start | bytes 3145736 | tf_op jit(solution)/shard_map/ppermute | solution.py:882
  298.8 18.8 %collective-permute-start.47 = (f32[2,2,64,1024]{3,2,1,0:T(8,128)}, f32[2,2,64,1024]{3,2,1,0:T(8,128)S(1)}, u32[]{:S(2)}, u32[]{:S(2)}) collective-permute-start(f32[2,2,64,1024]{3,2,1,0:T(8,128)} %get-tuple-element.226), channel_id=1, source_target_pairs={{0,8},{1,17},{8,0},{9,25},{16,24},{17,1},{24,16},{25,9},{2,10},{3,... | collective-permute-start | bytes 3145736 | tf_op jit(solution)/shard_map/ppermute | solution.py:882
  310.4 17.7 %collective-permute-start.51 = (f32[320,256]{1,0:T(8,128)}, f32[320,256]{1,0:T(8,128)S(1)}, u32[]{:S(2)}, u32[]{:S(2)}) collective-permute-start(f32[320,256]{1,0:T(8,128)} %get-tuple-element.223), channel_id=1, source_target_pairs={{0,5},{1,4},{4,1},{5,0},{2,7},{3,6},{6,3},{7,2},{8,13},{9,12},{12,... | collective-permute-start | bytes 983048 | tf_op jit(solution)/shard_map/ppermute | solution.py:1109
  319.4 10.3 %collective-permute-start.53 = (f32[64,2048]{1,0:T(8,128)S(1)}, f32[64,2048]{1,0:T(8,128)S(1)}, u32[]{:S(2)}, u32[]{:S(2)}) collective-permute-start(f32[64,2048]{1,0:T(8,128)S(1)} %get-tuple-element.238), channel_id=1, source_target_pairs={{0,16},{1,9},{8,24},{9,1},{16,0},{17,25},{24,8},{25,17},{2,18},{3,... | collective-permute-start | bytes 1572872 | tf_op jit(solution)/shard_map/ppermute | solution.py:882
  329.8 14.9 %collective-permute-start.58 = (f32[64,2048]{1,0:T(8,128)S(1)}, f32[64,2048]{1,0:T(8,128)S(1)}, u32[]{:S(2)}, u32[]{:S(2)}) collective-permute-start(f32[64,2048]{1,0:T(8,128)S(1)} %copy-done.11), channel_id=1, source_target_pairs={{0,8},{1,17},{8,0},{9,25},{16,24},{17,1},{24,16},{25,9},{2,10},{3,... | collective-permute-start | bytes 1572872 | tf_op jit(solution)/shard_map/ppermute | solution.py:882
  330.9 13.7 %collective-permute-start.57 = (f32[64,2048]{1,0:T(8,128)S(1)}, f32[64,2048]{1,0:T(8,128)S(1)}, u32[]{:S(2)}, u32[]{:S(2)}) collective-permute-start(f32[64,2048]{1,0:T(8,128)S(1)} %copy-done.11), channel_id=1, source_target_pairs={{0,16},{1,9},{8,24},{9,1},{16,0},{17,25},{24,8},{25,17},{2,18},{3,... | collective-permute-start | bytes 1572872 | tf_op jit(solution)/shard_map/ppermute | solution.py:882
  331.9 27.4 %collective-permute-start.49 = (f32[320,512]{1,0:T(8,128)S(1)}, f32[320,512]{1,0:T(8,128)S(1)}, u32[]{:S(2)}, u32[]{:S(2)}) collective-permute-start(f32[320,512]{1,0:T(8,128)S(1)} %copy-done.25), channel_id=1, source_target_pairs={{0,2},{2,0},{1,3},{3,1},{4,6},{6,4},{5,7},{7,5},{8,10},{10,8},{9,1... | collective-permute-start | bytes 1966088 | tf_op jit(solution)/shard_map/ppermute | solution.py:29
  331.9 17.5 %collective-permute-start.48 = (f32[64,2048]{1,0:T(8,128)S(1)}, f32[64,2048]{1,0:T(8,128)S(1)}, u32[]{:S(2)}, u32[]{:S(2)}) collective-permute-start(f32[64,2048]{1,0:T(8,128)S(1)} %get-tuple-element.228), channel_id=1, source_target_pairs={{0,16},{1,9},{8,24},{9,1},{16,0},{17,25},{24,8},{25,17},{2,18},{3,... | collective-permute-start | bytes 1572872 | tf_op jit(solution)/shard_map/ppermute | solution.py:882
  333.0 26.5 %collective-permute-start.54 = (f32[64,2048]{1,0:T(8,128)S(1)}, f32[64,2048]{1,0:T(8,128)S(1)}, u32[]{:S(2)}, u32[]{:S(2)}) collective-permute-start(f32[64,2048]{1,0:T(8,128)S(1)} %reduction_step.12), channel_id=1, source_target_pairs={{0,4},{4,0},{1,5},{5,1},{2,6},{6,2},{3,7},{7,3},{8,12},{12,8},{9,1... | collective-permute-start | bytes 1572872 | tf_op jit(solution)/shard_map/ppermute | solution.py:960
  344.7 14.8 %collective-permute-start.59 = (f32[64,2048]{1,0:T(8,128)S(1)}, f32[64,2048]{1,0:T(8,128)S(1)}, u32[]{:S(2)}, u32[]{:S(2)}) collective-permute-start(f32[64,2048]{1,0:T(8,128)S(1)} %collective-permute-done.58.refs_2_), channel_id=1, source_target_pairs={{0,16},{1,9},{8,24},{9,1},{16,0},{17,25},{24,8},{25,17},{2,18},{3,... | collective-permute-start | bytes 1572872 | tf_op jit(solution)/shard_map/ppermute | solution.py:882
  359.5 13.4 %collective-permute-start.61 = (f32[64,2048]{1,0:T(8,128)S(1)}, f32[64,2048]{1,0:T(8,128)S(1)}, u32[]{:S(2)}, u32[]{:S(2)}) collective-permute-start(f32[64,2048]{1,0:T(8,128)S(1)} %reduction_step.13.refs_0_), channel_id=1, source_target_pairs={{0,8},{1,17},{8,0},{9,25},{16,24},{17,1},{24,16},{25,9},{2,10},{3,... | collective-permute-start | bytes 1572872 | tf_op jit(solution)/shard_map/ppermute | solution.py:882
  360.7 12.2 %collective-permute-start.60 = (f32[64,2048]{1,0:T(8,128)S(1)}, f32[64,2048]{1,0:T(8,128)S(1)}, u32[]{:S(2)}, u32[]{:S(2)}) collective-permute-start(f32[64,2048]{1,0:T(8,128)S(1)} %reduction_step.13.refs_0_), channel_id=1, source_target_pairs={{0,16},{1,9},{8,24},{9,1},{16,0},{17,25},{24,8},{25,17},{2,18},{3,... | collective-permute-start | bytes 1572872 | tf_op jit(solution)/shard_map/ppermute | solution.py:882
  361.6 15.2 %collective-permute-start.55 = (f32[320,256]{1,0:T(8,128)S(1)}, f32[320,256]{1,0:T(8,128)S(1)}, u32[]{:S(2)}, u32[]{:S(2)}) collective-permute-start(f32[320,256]{1,0:T(8,128)S(1)} %copy-done.26), channel_id=1, source_target_pairs={{0,4},{4,0},{1,5},{5,1},{2,6},{6,2},{3,7},{7,3},{8,12},{12,8},{9,1... | collective-permute-start | bytes 983048 | tf_op jit(solution)/shard_map/ppermute | solution.py:960
  372.9 9.2 %collective-permute-start.62 = (f32[64,2048]{1,0:T(8,128)S(1)}, f32[64,2048]{1,0:T(8,128)S(1)}, u32[]{:S(2)}, u32[]{:S(2)}) collective-permute-start(f32[64,2048]{1,0:T(8,128)S(1)} %collective-permute-done.61.refs_2_), channel_id=1, source_target_pairs={{0,16},{1,9},{8,24},{9,1},{16,0},{17,25},{24,8},{25,17},{2,18},{3,... | collective-permute-start | bytes 1572872 | tf_op jit(solution)/shard_map/ppermute | solution.py:882
  (44 other events, 353.1 us)

commit v7 on v6

--- a/solution.py
+++ b/solution.py
@@ -1102,6 +1102,7 @@
 
     sums = jnp.stack(results)
     sums = [sums[:, 0], sums[:, 1], sums[:, 2]]
+    sums.append(jnp.stack(after(results, kept))[:, 1])
     aways = merge(kept, 1, received[1], apart=True)
     later = (in_hbm(later[0]), over_c(after(later[1], aways[0])))
     (later,) = step_of(later, cut=0, hbm_outs=(0,))
@@ -1125,7 +1126,7 @@
     grad_in = [(close, 0), (over_c(close[frames:]), 0), (far_near, 0), (far, 0)]
     grad_in = unpack(place, grad_in, frames)
     grad_weights = assemble(place, after(gathered, grad_in), 0, grad_weights)
-    return (output, grad_in, grad_weights, *sums, sums[1])
+    return (output, grad_in, grad_weights, *sums)
 
 
 def gelu_slope(value):

time: 386 us -> 386 us (level)
  transfers between devices with their start and end apart: 63 -> 63, of which waited for: 27 -> 28; matrix products, arithmetic and copies ran while one was open for 1% -> 1% of each run, Pallas kernels for 37% -> 38%
where the time goes in v7:
time: 386 us; the launch traced here: 384 us
  Pallas kernels  155 us (40%)
  waiting for transfers between devices  110 us (28%)
  blocking collectives  61.2 us (16%)
  starting transfers between devices  48.6 us (13%)
  local copies, waits for them, and re-layouts  5.91 us (2%)
    all_gather x8, blocking collectives, gather(): return lax.all_gather(array, axes, tiled=True)  61.2 us
    ppermute x7, waiting for transfers between devices, over_h(): return lax.ppermute(array, 'h', FLIP2)  38 us
    pallas_call x5, Pallas kernels, project(): call(partial(project_body, len(parts), len(flat), spots, len(weights), 0...  35.7 us
    pallas_call x4, Pallas kernels, weight_rows(): call(partial(weight_body, turn), grid_spec=pltpu.PrefetchScalarGridSpec(n...  26.6 us
    ppermute x13, waiting for transfers between devices, plane_swap(): return lax.ppermute(array, ('y', 'x', 'c'), pairs)  23.2 us
    ppermute x6, waiting for transfers between devices, swap_half(): return lax.ppermute(array, 'l', FLIP2)  20.1 us
    pallas_call x2, Pallas kernels, norm_back(): call(partial(norm_back_body, len(z), split_terms, layer), grid_spec=pltpu...  15.4 us
    ppermute x13, starting transfers between devices, plane_swap(): return lax.ppermute(array, ('y', 'x', 'c'), pairs)  15.3 us
  transfers between devices with their start and end apart: 63, of which 28 were waited for; matrix products, arithmetic and copies ran while one was open for 1% of the time, Pallas kernels for 38%

profile of v7, /device:TPU:0, one launch (start us, length us, event | category | flops | bytes accessed | tf_op | source)
XLA Modules:
  0.0 383.8 jit_solution(5848978062302857143)
XLA Ops:
  3.2 3.6 collective-permute-start.1
  10.7 3.0 pack.3
  15.7 15.4 %collective-permute-done.1.refs_12_.refs_8_.refs_7_.refs_4_ = f32[64,2048]{1,0:T(8,128)} collective-permute-done((f32[64,2048]{1,0:T(8,128)S(1)}, f32[64,2048]{1,0:T(8,128)}, u32[]{:S(2)}, u32[]{:S(2)}) %collective-permute-start.1) | collective-permute-done | bytes 524320 | tf_op jit(solution)/shard_map/ppermute | solution.py:960
  31.2 2.8 collective-permute-start.5
  34.7 5.0 %collective-permute-done.6.refs_4_.refs_2_ = f32[640,256]{1,0:T(8,128)S(1)} collective-permute-done((f32[640,256]{1,0:T(8,128)S(1)}, f32[640,256]{1,0:T(8,128)S(1)}, u32[]{:S(2)}, u32[]{:S(2)}) %collective-permute-start.6) | collective-permute-done | bytes 655392 | tf_op jit(solution)/shard_map/ppermute | solution.py:29
  39.7 19.1 %collective-permute-done.refs_2_.refs_8_ = f32[640,256]{1,0:T(8,128)S(1)} collective-permute-done((f32[640,256]{1,0:T(8,128)S(1)}, f32[640,256]{1,0:T(8,128)S(1)}, u32[]{:S(2)}, u32[]{:S(2)}) %collective-permute-start) | collective-permute-done | bytes 655392 | tf_op jit(solution)/shard_map/ppermute | solution.py:960
  65.4 9.7 %project.5 = (f32[320,1024]{1,0:T(8,128)}, f32[320,1024]{1,0:T(8,128)}) custom-call(s32[6]{0:T(128)S(1)} %concatenate.11.cols_ref, s32[8]{0:T(128)S(1)} %stack.133.place_ref, f32[640,256]{1,0:T(8,128)S(1)} %get-tuple-element.139.refs_0_.refs_6_, f32[640,256]{1,0:T(8,128)} %collective-permute-done.8.refs_1_.refs_7_, ...), custom_call_target="tpu_custom_call" | custom-call | flops 47185920 | bytes 98304 | tf_op jit(solution)/shard_map/project/pallas_call | solution.py:289
  78.3 6.0 %project.6 = (f32[320,1024]{1,0:T(8,128)}, f32[5,8,128]{2,1,0:T(8,128)S(1)}, f32[320,1024]{1,0:T(8,128)}) custom-call(s32[2]{0:T(128)S(1)} %pad_add_fusion.1.cols_ref, s32[8]{0:T(128)S(1)} %stack.133.place_ref, f32[640,256]{1,0:T(8,128)S(1)} %collective-permute-done.7.refs_0_.refs_4_, f32[320,256]{1,0:T(8,128)S(1)} %collective-permute-done.15.refs_1_.refs_5_, ...), custom_call_target="tpu_custom_call" | custom-call | flops 15728640 | bytes 32768 | tf_op jit(solution)/shard_map/project/pallas_call | solution.py:289
  85.0 6.2 %all_gather.24 = f32[20,8,128]{2,1,0:T(8,128)S(1)} all-gather(f32[5,8,128]{2,1,0:T(8,128)S(1)} %get-tuple-element.147), channel_id=1, replica_groups=mesh['y'=2,'x'=2,'h'=2,'l'=2,'c'=2] {'h','c'}, dimensions={0}, use_global_device_ids=true | all-gather | bytes 102400 | tf_op jit(solution)/shard_map/all_gather | solution.py:999
  93.4 9.2 %all_gather.25.refs_1_.refs_3_ = f32[80,8,128]{2,1,0:T(8,128)S(1)} all-gather(f32[20,8,128]{2,1,0:T(8,128)S(1)} %all_gather.24), channel_id=1, replica_groups=mesh['y'=2,'x'=2,'h'=2,'l'=2,'c'=2] {'y','x'}, dimensions={0}, use_global_device_ids=true | all-gather | bytes 409600 | tf_op jit(solution)/shard_map/all_gather | solution.py:999
  102.7 7.3 %recur.2 = (f32[320,1024]{1,0:T(8,128)S(1)}, f32[320,1024]{1,0:T(8,128)}, f32[320,1024]{1,0:T(8,128)}, f32[6,8,128]{2,1,0:T(8,128)S(1)}) custom-call(s32[8]{0:T(128)S(1)} %stack.133.place_ref, f32[320]{0:T(512)S(1)} %fusion.7.gate_ref, f32[320,1024]{1,0:T(8,128)} %get-tuple-element.146.refs_0_, f32[80,8,128]{2,1,0:T(8,128)S(1)} %all_gather.25.refs_1_.refs_3_, ...), custom_call_target="tpu_custom_call" | custom-call | flops 512000 | bytes 102400 | tf_op jit(solution)/shard_map/recur/pallas_call | solution.py:435
  111.8 5.3 %collective-permute-done.20 = f32[64,2048]{1,0:T(8,128)S(1)} collective-permute-done((f32[64,2048]{1,0:T(8,128)S(1)}, f32[64,2048]{1,0:T(8,128)S(1)}, u32[]{:S(2)}, u32[]{:S(2)}) %collective-permute-start.20) | collective-permute-done | bytes 524320 | tf_op jit(solution)/shard_map/ppermute | solution.py:1019
  124.0 3.7 prepare.4
  127.7 3.8 prepare.5
  131.5 5.2 %project.7.refs_3_ = f32[320,512]{1,0:T(8,128)} custom-call(s32[4]{0:T(128)S(1)} %pad_add_fusion.2.cols_ref, s32[8]{0:T(128)S(1)} %stack.133.place_ref, f32[320,1024]{1,0:T(8,128)S(1)} %get-tuple-element.162.refs_0_.own_ref.refs_5_, f32[2,256,2048]{2,1,0:T(8,128)} %refs_2_.1, ...), custom_call_target="tpu_custom_call" | custom-call | flops 15728640 | bytes 32768 | tf_op jit(solution)/shard_map/project/pallas_call | solution.py:289
  136.7 3.8 prepare.6
  140.5 6.4 %collective-permute-done.23.refs_4_.refs_10_.refs_8_ = f32[64,2048]{1,0:T(8,128)} collective-permute-done((f32[64,2048]{1,0:T(8,128)}, f32[64,2048]{1,0:T(8,128)}, u32[]{:S(2)}, u32[]{:S(2)}) %collective-permute-start.23) | collective-permute-done | bytes 524320 | tf_op jit(solution)/shard_map/ppermute | solution.py:978
  148.2 5.6 %project.8 = (f32[320,512]{1,0:T(8,128)}, f32[3,8,128]{2,1,0:T(8,128)S(1)}) custom-call(s32[4]{0:T(128)S(1)} %pad_add_fusion.cols_ref, s32[8]{0:T(128)S(1)} %stack.133.place_ref, f32[320,1024]{1,0:T(8,128)S(1)} %collective-permute-done.16.refs_0_.refs_1_.own_ref, f32[2,256,2048]{2,1,0:T(8,128)} %refs_2_.1, ...), custom_call_target="tpu_custom_call" | custom-call | flops 15728640 | bytes 32768 | tf_op jit(solution)/shard_map/project/pallas_call | solution.py:289
  154.3 9.1 %project.9 = (f32[320,512]{1,0:T(8,128)}, f32[3,8,128]{2,1,0:T(8,128)S(1)}) custom-call(s32[8]{0:T(128)S(1)} %concatenate.12.cols_ref, s32[8]{0:T(128)S(1)} %stack.133.place_ref, f32[320,1024]{1,0:T(8,128)S(1)} %copy-done.1, f32[320,1024]{1,0:T(8,128)S(1)} %collective-permute-done.16.refs_0_.refs_1_.own_ref, ...), custom_call_target="tpu_custom_call" | custom-call | flops 31457280 | bytes 65536 | tf_op jit(solution)/shard_map/project/pallas_call | solution.py:289
  163.4 8.2 %all_gather.26 = f32[12,8,128]{2,1,0:T(8,128)S(1)} all-gather(f32[3,8,128]{2,1,0:T(8,128)S(1)} %get-tuple-element.170), channel_id=1, replica_groups=mesh['y'=2,'x'=2,'h'=2,'l'=2,'c'=2] {'y','x'}, dimensions={0}, use_global_device_ids=true | all-gather | bytes 61440 | tf_op jit(solution)/shard_map/all_gather | solution.py:999
  171.6 7.7 %all_gather.27.refs_2_.refs_4_ = f32[48,8,128]{2,1,0:T(8,128)S(1)} all-gather(f32[12,8,128]{2,1,0:T(8,128)S(1)} %all_gather.26), channel_id=1, replica_groups=mesh['y'=2,'x'=2,'h'=2,'l'=2,'c'=2] {'h','c'}, dimensions={0}, use_global_device_ids=true | all-gather | bytes 245760 | tf_op jit(solution)/shard_map/all_gather | solution.py:999
  179.7 7.4 %recur.3 = (f32[320,256]{1,0:T(8,128)}, f32[320,256]{1,0:T(8,128)}, f32[320,256]{1,0:T(8,128)}, f32[320,256]{1,0:T(8,128)}, f32[320,1024]{1,0:T(8,128)}, /*index=5*/f32[320,1024]{1,0:T(8,128)}) custom-call(s32[8]{0:T(128)S(1)} %stack.133.place_ref, f32[320]{0:T(512)S(1)} %fusion.7.gate_ref, f32[320,512]{1,0:T(8,128)} %get-tuple-element.158.refs_0_, ...), custom_call_target="tpu_custom_call" | custom-call | flops 512000 | bytes 102400 | tf_op jit(solution)/shard_map/recur/pallas_call | solution.py:435
  187.4 5.6 %back.2 = (f32[320,1024]{1,0:T(8,128)S(1)}, f32[3,8,128]{2,1,0:T(8,128)S(1)}) custom-call(s32[8]{0:T(128)S(1)} %stack.133.place_ref, f32[320]{0:T(512)S(1)} %fusion.7.gate_ref, f32[320,512]{1,0:T(8,128)} %get-tuple-element.158.refs_0_, f32[320,512]{1,0:T(8,128)} %get-tuple-element.169.refs_1_, f32[48,8,128]{2,1,0:T(8,128)S(1)} %all_gather.27.refs_2_.refs_4_, ...), custom_call_target="tpu_custom_call" | custom-call | flops 153600 | bytes 102400 | tf_op jit(solution)/shard_map/back/pallas_call | solution.py:542
  193.1 7.4 %all_gather.28 = f32[12,8,128]{2,1,0:T(8,128)S(1)} all-gather(f32[3,8,128]{2,1,0:T(8,128)S(1)} %get-tuple-element.179), channel_id=1, replica_groups=mesh['y'=2,'x'=2,'h'=2,'l'=2,'c'=2] {'y','x'}, dimensions={0}, use_global_device_ids=true | all-gather | bytes 61440 | tf_op jit(solution)/shard_map/all_gather | solution.py:999
  200.5 7.4 %all_gather.29.refs_5_ = f32[48,8,128]{2,1,0:T(8,128)S(1)} all-gather(f32[12,8,128]{2,1,0:T(8,128)S(1)} %all_gather.28), channel_id=1, replica_groups=mesh['y'=2,'x'=2,'h'=2,'l'=2,'c'=2] {'h','c'}, dimensions={0}, use_global_device_ids=true | all-gather | bytes 245760 | tf_op jit(solution)/shard_map/all_gather | solution.py:999
  207.8 7.7 %norm_back.2 = (f32[320,1024]{1,0:T(8,128)}, f32[320,512]{1,0:T(8,128)S(1)}, f32[320,1024]{1,0:T(8,128)}, f32[3,8,128]{2,1,0:T(8,128)S(1)}) custom-call(s32[2]{0:T(128)S(1)} %pad_add_fusion.4.cols_ref, s32[8]{0:T(128)S(1)} %stack.133.place_ref, f32[320,1024]{1,0:T(8,128)S(1)} %get-tuple-element.178.grad_ref, f32[320,512]{1,0:T(8,128)} %get-tuple-element.158.refs_0_, ...), custom_call_target="tpu_custom_call" | custom-call | flops 31457280 | bytes 65536 | tf_op jit(solution)/shard_map/norm_back/pallas_call | solution.py:647
  218.2 3.8 prepare.7
  222.0 7.2 %weight_rows.4 = (f32[2,2,64,1024]{3,2,1,0:T(8,128)}, f32[2,2,64,1024]{3,2,1,0:T(8,128)}, bf16[512,768]{1,0:T(8,128)(2,1)S(1)}, bf16[512,768]{1,0:T(8,128)(2,1)S(1)}) custom-call(s32[8]{0:T(128)S(1)} %stack.133.place_ref, f32[320,1024]{1,0:T(8,128)} %get-tuple-element.193.refs_0_.grad_ref, f32[320,512]{1,0:T(8,128)S(1)} %collective-permute-done.32.refs_1_, ...), custom_call_target="tpu_custom_call" | custom-call | flops 37748736 | bytes 32768 | tf_op jit(solution)/shard_map/weight_rows/pallas_call | solution.py:820
  230.6 6.1 %weight_rows.5 = (f32[2,2,64,1024]{3,2,1,0:T(8,128)}, f32[2,2,64,1024]{3,2,1,0:T(8,128)}) custom-call(s32[8]{0:T(128)S(1)} %stack.133.place_ref, bf16[512,768]{1,0:T(8,128)(2,1)S(1)} %get-tuple-element.189.refs_0_, bf16[512,768]{1,0:T(8,128)(2,1)S(1)} %get-tuple-element.190.refs_1_, bf16[768,1024]{1,0:T(8,128)(2,1)} %get-tuple-element.186.refs_2_, ...), custom_call_target="tpu_custom_call" | custom-call | flops 37748736 | bytes 32768 | tf_op jit(solution)/shard_map/weight_rows/pallas_call | solution.py:820
  237.5 6.1 %own_terms.2.refs_3_.refs_0_ = f32[320,1024]{1,0:T(8,128)S(1)} custom-call(s32[2]{0:T(128)S(1)} %pad_add_fusion.5.cols_ref, s32[8]{0:T(128)S(1)} %stack.133.place_ref, f32[320,1024]{1,0:T(8,128)} %get-tuple-element.193.refs_0_.grad_ref, f32[640,256]{1,0:T(8,128)S(1)} %copy-done.4, f32[640,256]{1,0:T(8,128)} %collective-permute-done.29.refs_5_.refs_1_, ...), custom_call_target="tpu_custom_call" | custom-call | flops 31457280 | bytes 65536 | tf_op jit(solution)/shard_map/own_terms/pallas_call | solution.py:705
  244.0 3.8 collective-permute-done.36.refs_4_.refs_1_
  247.8 5.6 %back.3 = (f32[320,1024]{1,0:T(8,128)S(1)}, f32[3,8,128]{2,1,0:T(8,128)S(1)}) custom-call(s32[8]{0:T(128)S(1)} %stack.133.place_ref, f32[320]{0:T(512)S(1)} %fusion.7.gate_ref, f32[320,1024]{1,0:T(8,128)} %get-tuple-element.146.refs_0_, f32[80,8,128]{2,1,0:T(8,128)S(1)} %all_gather.25.refs_1_.refs_3_, ...), custom_call_target="tpu_custom_call" | custom-call | flops 153600 | bytes 102400 | tf_op jit(solution)/shard_map/back/pallas_call | solution.py:542
  253.4 8.0 %all_gather.30 = f32[12,8,128]{2,1,0:T(8,128)S(1)} all-gather(f32[3,8,128]{2,1,0:T(8,128)S(1)} %get-tuple-element.197), channel_id=1, replica_groups=mesh['y'=2,'x'=2,'h'=2,'l'=2,'c'=2] {'y','x'}, dimensions={0}, use_global_device_ids=true | all-gather | bytes 61440 | tf_op jit(solution)/shard_map/all_gather | solution.py:999
  266.2 7.1 %all_gather.31.refs_4_ = f32[48,8,128]{2,1,0:T(8,128)S(1)} all-gather(f32[12,8,128]{2,1,0:T(8,128)S(1)} %all_gather.30), channel_id=1, replica_groups=mesh['y'=2,'x'=2,'h'=2,'l'=2,'c'=2] {'h','c'}, dimensions={0}, use_global_device_ids=true | all-gather | bytes 245760 | tf_op jit(solution)/shard_map/all_gather | solution.py:999
  273.2 7.7 %norm_back.3 = (f32[320,1024]{1,0:T(8,128)}, f32[320,512]{1,0:T(8,128)S(1)}, f32[320,512]{1,0:T(8,128)}, f32[320,512]{1,0:T(8,128)}, f32[3,8,128]{2,1,0:T(8,128)S(1)}) custom-call(s32[2]{0:T(128)S(1)} %pad_add_fusion.4.cols_ref, s32[8]{0:T(128)S(1)} %stack.133.place_ref, f32[320,1024]{1,0:T(8,128)S(1)} %get-tuple-element.196.grad_ref, ...), custom_call_target="tpu_custom_call" | custom-call | flops 31457280 | bytes 65536 | tf_op jit(solution)/shard_map/norm_back/pallas_call | solution.py:647
  285.1 7.2 %weight_rows.6 = (f32[2,2,64,1024]{3,2,1,0:T(8,128)}, f32[2,2,64,1024]{3,2,1,0:T(8,128)}, bf16[512,768]{1,0:T(8,128)(2,1)S(1)}, bf16[512,768]{1,0:T(8,128)(2,1)S(1)}) custom-call(s32[8]{0:T(128)S(1)} %stack.133.place_ref, f32[320,1024]{1,0:T(8,128)} %get-tuple-element.222.refs_0_.grad_ref, f32[320,512]{1,0:T(8,128)S(1)} %collective-permute-done.41.refs_1_, ...), custom_call_target="tpu_custom_call" | custom-call | flops 37748736 | bytes 32768 | tf_op jit(solution)/shard_map/weight_rows/pallas_call | solution.py:820
  293.7 6.1 %weight_rows.7 = (f32[2,2,64,1024]{3,2,1,0:T(8,128)}, f32[2,2,64,1024]{3,2,1,0:T(8,128)}) custom-call(s32[8]{0:T(128)S(1)} %stack.133.place_ref, bf16[512,768]{1,0:T(8,128)(2,1)S(1)} %get-tuple-element.218.refs_0_, bf16[512,768]{1,0:T(8,128)(2,1)S(1)} %get-tuple-element.219.refs_1_, bf16[768,1024]{1,0:T(8,128)(2,1)} %get-tuple-element.156.refs_2_, ...), custom_call_target="tpu_custom_call" | custom-call | flops 37748736 | bytes 32768 | tf_op jit(solution)/shard_map/weight_rows/pallas_call | solution.py:820
  300.5 6.3 %own_terms.3.kept_ref = f32[320,1024]{1,0:T(8,128)S(1)} custom-call(s32[2]{0:T(128)S(1)} %pad_add_fusion.5.cols_ref, s32[8]{0:T(128)S(1)} %stack.133.place_ref, f32[320,1024]{1,0:T(8,128)} %get-tuple-element.222.refs_0_.grad_ref, f32[320,1024]{1,0:T(8,128)S(1)} %own_terms.2.refs_3_.refs_0_, f32[320,1024]{1,0:T(8,128)} %collective-permute-done.36.refs_4_.refs_1_, ...), custom_call_target="tpu_custom_call" | custom-call | flops 31457280 | bytes 65536 | tf_op jit(solution)/shard_map/own_terms/pallas_call | solution.py:705
  306.8 2.8 collective-permute-done.45.come_ref
  314.5 4.2 %collective-permute-done.47.refs_3_ = f32[2,2,64,1024]{3,2,1,0:T(8,128)} collective-permute-done((f32[2,2,64,1024]{3,2,1,0:T(8,128)}, f32[2,2,64,1024]{3,2,1,0:T(8,128)}, u32[]{:S(2)}, u32[]{:S(2)}) %collective-permute-start.47) | collective-permute-done | bytes 1048608 | tf_op jit(solution)/shard_map/ppermute | solution.py:882
  322.5 6.2 %collective-permute-done.51 = f32[320,256]{1,0:T(8,128)S(1)} collective-permute-done((f32[320,256]{1,0:T(8,128)}, f32[320,256]{1,0:T(8,128)S(1)}, u32[]{:S(2)}, u32[]{:S(2)}) %collective-permute-start.51) | collective-permute-done | bytes 327712 | tf_op jit(solution)/shard_map/ppermute | solution.py:1110
  336.4 8.8 %collective-permute-done.58.refs_2_ = f32[64,2048]{1,0:T(8,128)S(1)} collective-permute-done((f32[64,2048]{1,0:T(8,128)S(1)}, f32[64,2048]{1,0:T(8,128)S(1)}, u32[]{:S(2)}, u32[]{:S(2)}) %collective-permute-start.58) | collective-permute-done | bytes 524320 | tf_op jit(solution)/shard_map/ppermute | solution.py:882
  346.6 3.4 collective-permute-done.48.refs_1_
  350.0 2.8 unpack.2
  352.9 7.0 %collective-permute-done.49.come_ref = f32[320,512]{1,0:T(8,128)S(1)} collective-permute-done((f32[320,512]{1,0:T(8,128)S(1)}, f32[320,512]{1,0:T(8,128)S(1)}, u32[]{:S(2)}, u32[]{:S(2)}) %collective-permute-start.49) | collective-permute-done | bytes 655392 | tf_op jit(solution)/shard_map/ppermute | solution.py:29
  363.2 3.0 assemble.2.refs_4_
  366.2 6.4 %collective-permute-done.61.refs_2_ = f32[64,2048]{1,0:T(8,128)S(1)} collective-permute-done((f32[64,2048]{1,0:T(8,128)S(1)}, f32[64,2048]{1,0:T(8,128)S(1)}, u32[]{:S(2)}, u32[]{:S(2)}) %collective-permute-start.61) | collective-permute-done | bytes 524320 | tf_op jit(solution)/shard_map/ppermute | solution.py:882
  374.4 3.3 collective-permute-done.55
  (205 shorter events, 78.2 us)
Async XLA Ops:
  0.6 30.4 %collective-permute-start.2 = (f32[2,256,2048]{2,1,0:T(8,128)}, f32[2,256,2048]{2,1,0:T(8,128)}, u32[]{:S(2)}, u32[]{:S(2)}) collective-permute-start(f32[2,256,2048]{2,1,0:T(8,128)} %refs_2_.1), channel_id=1, source_target_pairs={{0,1},{1,0},{2,3},{3,2},{4,5},{5,4},{6,7},{7,6},{8,9},{9,8},{10,11... | collective-permute-start | bytes 12582920 | tf_op jit(solution)/shard_map/ppermute | solution.py:963
  3.2 27.8 %collective-permute-start.1 = (f32[64,2048]{1,0:T(8,128)S(1)}, f32[64,2048]{1,0:T(8,128)}, u32[]{:S(2)}, u32[]{:S(2)}) collective-permute-start(f32[64,2048]{1,0:T(8,128)S(1)} %get-tuple-element.258), channel_id=1, source_target_pairs={{0,4},{4,0},{1,5},{5,1},{2,6},{6,2},{3,7},{7,3},{8,12},{12,8},{9,1... | collective-permute-start | bytes 1572872 | tf_op jit(solution)/shard_map/ppermute | solution.py:960
  8.8 30.9 %collective-permute-start.6 = (f32[640,256]{1,0:T(8,128)S(1)}, f32[640,256]{1,0:T(8,128)S(1)}, u32[]{:S(2)}, u32[]{:S(2)}) collective-permute-start(f32[640,256]{1,0:T(8,128)S(1)} %get-tuple-element.139.refs_0_.refs_6_), channel_id=1, source_target_pairs={{0,2},{2,0},{1,3},{3,1},{4,6},{6,4},{5,7},{7,5},{8,10},{10,8},{9,1... | collective-permute-start | bytes 1966088 | tf_op jit(solution)/shard_map/ppermute | solution.py:29
  10.4 48.4 %collective-permute-start = (f32[640,256]{1,0:T(8,128)S(1)}, f32[640,256]{1,0:T(8,128)S(1)}, u32[]{:S(2)}, u32[]{:S(2)}) collective-permute-start(f32[640,256]{1,0:T(8,128)S(1)} %get-tuple-element.133), channel_id=1, source_target_pairs={{0,4},{4,0},{1,5},{5,1},{2,6},{6,2},{3,7},{7,3},{8,12},{12,8},{9,1... | collective-permute-start | bytes 1966088 | tf_op jit(solution)/shard_map/ppermute | solution.py:960
  31.2 27.6 %collective-permute-start.5 = (f32[64,2048]{1,0:T(8,128)}, f32[64,2048]{1,0:T(8,128)}, u32[]{:S(2)}, u32[]{:S(2)}) collective-permute-start(f32[64,2048]{1,0:T(8,128)} %collective-permute-done.1.refs_12_.refs_8_.refs_7_.refs_4_), channel_id=1, source_target_pairs={{0,24},{8,16},{16,8},{24,0},{1,25},{9,17},{17,9},{25,1},{2,26},{10... | collective-permute-start | bytes 1572872 | tf_op jit(solution)/shard_map/ppermute | solution.py:977
  33.9 24.8 %collective-permute-start.4 = (f32[64,2048]{1,0:T(8,128)}, f32[64,2048]{1,0:T(8,128)}, u32[]{:S(2)}, u32[]{:S(2)}) collective-permute-start(f32[64,2048]{1,0:T(8,128)} %collective-permute-done.1.refs_12_.refs_8_.refs_7_.refs_4_), channel_id=1, source_target_pairs={{0,16},{16,0},{1,17},{17,1},{2,18},{18,2},{3,19},{19,3},{4,20},{20... | collective-permute-start | bytes 1572872 | tf_op jit(solution)/shard_map/ppermute | solution.py:978
  34.5 24.3 %collective-permute-start.3 = (f32[64,2048]{1,0:T(8,128)}, f32[64,2048]{1,0:T(8,128)S(1)}, u32[]{:S(2)}, u32[]{:S(2)}) collective-permute-start(f32[64,2048]{1,0:T(8,128)} %collective-permute-done.1.refs_12_.refs_8_.refs_7_.refs_4_), channel_id=1, source_target_pairs={{0,8},{8,0},{1,9},{9,1},{2,10},{10,2},{3,11},{11,3},{4,12},{12,4},... | collective-permute-start | bytes 1572872 | tf_op jit(solution)/shard_map/ppermute | solution.py:978
  39.7 20.2 %collective-permute-start.10 = (f32[640,256]{1,0:T(8,128)S(1)}, f32[640,256]{1,0:T(8,128)S(1)}, u32[]{:S(2)}, u32[]{:S(2)}) collective-permute-start(f32[640,256]{1,0:T(8,128)S(1)} %collective-permute-done.6.refs_4_.refs_2_), channel_id=1, source_target_pairs={{0,1},{1,0},{2,3},{3,2},{4,5},{5,4},{6,7},{7,6},{8,9},{9,8},{10,11... | collective-permute-start | bytes 1966088 | tf_op jit(solution)/shard_map/ppermute | solution.py:963
  59.9 16.7 %collective-permute-start.7 = (f32[640,256]{1,0:T(8,128)S(1)}, f32[640,256]{1,0:T(8,128)S(1)}, u32[]{:S(2)}, u32[]{:S(2)}) collective-permute-start(f32[640,256]{1,0:T(8,128)S(1)} %collective-permute-done.refs_2_.refs_8_), channel_id=1, source_target_pairs={{0,2},{2,0},{1,3},{3,1},{4,6},{6,4},{5,7},{7,5},{8,10},{10,8},{9,1... | collective-permute-start | bytes 1966088 | tf_op jit(solution)/shard_map/ppermute | solution.py:29
  84.4 34.8 %collective-permute-start.18 = (f32[320,1024]{1,0:T(8,128)S(1)}, f32[320,1024]{1,0:T(8,128)S(1)}, u32[]{:S(2)}, u32[]{:S(2)}) collective-permute-start(f32[320,1024]{1,0:T(8,128)S(1)} %copy-done.8), channel_id=1, source_target_pairs={{0,1},{1,0},{2,3},{3,2},{4,5},{5,4},{6,7},{7,6},{8,9},{9,8},{10,11... | collective-permute-start | bytes 3932168 | tf_op jit(solution)/shard_map/ppermute | solution.py:963
  84.6 35.7 %collective-permute-start.19 = (f32[320,1024]{1,0:T(8,128)}, f32[320,1024]{1,0:T(8,128)}, u32[]{:S(2)}, u32[]{:S(2)}) collective-permute-start(f32[320,1024]{1,0:T(8,128)} %get-tuple-element.155.own_ref), channel_id=1, source_target_pairs={{0,1},{1,0},{2,3},{3,2},{4,5},{5,4},{6,7},{7,6},{8,9},{9,8},{10,11... | collective-permute-start | bytes 3932168 | tf_op jit(solution)/shard_map/ppermute | solution.py:963
  91.1 26.0 %collective-permute-start.20 = (f32[64,2048]{1,0:T(8,128)S(1)}, f32[64,2048]{1,0:T(8,128)S(1)}, u32[]{:S(2)}, u32[]{:S(2)}) collective-permute-start(f32[64,2048]{1,0:T(8,128)S(1)} %copy-done.11), channel_id=1, source_target_pairs={{0,5},{1,4},{4,1},{5,0},{2,7},{3,6},{6,3},{7,2},{8,13},{9,12},{12,... | collective-permute-start | bytes 1572872 | tf_op jit(solution)/shard_map/ppermute | solution.py:1019
  110.0 14.0 %collective-permute-start.17 = (f32[320,1024]{1,0:T(8,128)S(1)}, f32[320,1024]{1,0:T(8,128)}, u32[]{:S(2)}, u32[]{:S(2)}) collective-permute-start(f32[320,1024]{1,0:T(8,128)S(1)} %get-tuple-element.162.refs_0_.own_ref.refs_5_), channel_id=1, source_target_pairs={{0,1},{1,0},{2,3},{3,2},{4,5},{5,4},{6,7},{7,6},{8,9},{9,8},{10,11... | collective-permute-start | bytes 3932168 | tf_op jit(solution)/shard_map/ppermute | solution.py:963
  110.0 37.6 %collective-permute-start.16 = (f32[320,1024]{1,0:T(8,128)S(1)}, f32[320,1024]{1,0:T(8,128)S(1)}, u32[]{:S(2)}, u32[]{:S(2)}) collective-permute-start(f32[320,1024]{1,0:T(8,128)S(1)} %get-tuple-element.162.refs_0_.own_ref.refs_5_), channel_id=1, source_target_pairs={{0,2},{2,0},{1,3},{3,1},{4,6},{6,4},{5,7},{7,5},{8,10},{10,8},{9,1... | collective-permute-start | bytes 3932168 | tf_op jit(solution)/shard_map/ppermute | solution.py:29
  120.3 20.2 %collective-permute-start.24 = (f32[64,2048]{1,0:T(8,128)}, f32[64,2048]{1,0:T(8,128)}, u32[]{:S(2)}, u32[]{:S(2)}) collective-permute-start(f32[64,2048]{1,0:T(8,128)} %collective-permute-done.21.refs_2_.refs_8_.refs_6_), channel_id=1, source_target_pairs={{0,24},{8,16},{16,8},{24,0},{1,25},{9,17},{17,9},{25,1},{2,26},{10... | collective-permute-start | bytes 1572872 | tf_op jit(solution)/shard_map/ppermute | solution.py:977
  122.8 24.1 %collective-permute-start.23 = (f32[64,2048]{1,0:T(8,128)}, f32[64,2048]{1,0:T(8,128)}, u32[]{:S(2)}, u32[]{:S(2)}) collective-permute-start(f32[64,2048]{1,0:T(8,128)} %collective-permute-done.21.refs_2_.refs_8_.refs_6_), channel_id=1, source_target_pairs={{0,16},{16,0},{1,17},{17,1},{2,18},{18,2},{3,19},{19,3},{4,20},{20... | collective-permute-start | bytes 1572872 | tf_op jit(solution)/shard_map/ppermute | solution.py:978
  123.3 23.7 %collective-permute-start.22 = (f32[64,2048]{1,0:T(8,128)}, f32[64,2048]{1,0:T(8,128)}, u32[]{:S(2)}, u32[]{:S(2)}) collective-permute-start(f32[64,2048]{1,0:T(8,128)} %collective-permute-done.21.refs_2_.refs_8_.refs_6_), channel_id=1, source_target_pairs={{0,8},{8,0},{1,9},{9,1},{2,10},{10,2},{3,11},{11,3},{4,12},{12,4},... | collective-permute-start | bytes 1572872 | tf_op jit(solution)/shard_map/ppermute | solution.py:978
  140.5 38.9 %collective-permute-start.30 = (f32[640,256]{1,0:T(8,128)}, f32[640,256]{1,0:T(8,128)}, u32[]{:S(2)}, u32[]{:S(2)}) collective-permute-start(f32[640,256]{1,0:T(8,128)} %get-tuple-element.174), channel_id=1, source_target_pairs={{0,4},{4,0},{1,5},{5,1},{2,6},{6,2},{3,7},{7,3},{8,12},{12,8},{9,1... | collective-permute-start | bytes 1966088 | tf_op jit(solution)/shard_map/ppermute | solution.py:960
  147.0 6.8 %collective-permute-start.25 = (f32[64,2048]{1,0:T(8,128)}, f32[64,2048]{1,0:T(8,128)}, u32[]{:S(2)}, u32[]{:S(2)}) collective-permute-start(f32[64,2048]{1,0:T(8,128)} %collective-permute-done.21.refs_2_.refs_8_.refs_6_), channel_id=1, source_target_pairs={{0,1},{1,0},{2,3},{3,2},{4,5},{5,4},{6,7},{7,6},{8,9},{9,8},{10,11... | collective-permute-start | bytes 1572872 | tf_op jit(solution)/shard_map/ppermute | solution.py:963
  147.0 7.2 %collective-permute-start.26 = (f32[64,2048]{1,0:T(8,128)}, f32[64,2048]{1,0:T(8,128)}, u32[]{:S(2)}, u32[]{:S(2)}) collective-permute-start(f32[64,2048]{1,0:T(8,128)} %collective-permute-done.22.refs_3_.refs_9_.refs_7_), channel_id=1, source_target_pairs={{0,1},{1,0},{2,3},{3,2},{4,5},{5,4},{6,7},{7,6},{8,9},{9,8},{10,11... | collective-permute-start | bytes 1572872 | tf_op jit(solution)/shard_map/ppermute | solution.py:963
  147.6 6.7 %collective-permute-start.27 = (f32[64,2048]{1,0:T(8,128)}, f32[64,2048]{1,0:T(8,128)}, u32[]{:S(2)}, u32[]{:S(2)}) collective-permute-start(f32[64,2048]{1,0:T(8,128)} %collective-permute-done.23.refs_4_.refs_10_.refs_8_), channel_id=1, source_target_pairs={{0,1},{1,0},{2,3},{3,2},{4,5},{5,4},{6,7},{7,6},{8,9},{9,8},{10,11... | collective-permute-start | bytes 1572872 | tf_op jit(solution)/shard_map/ppermute | solution.py:963
  147.6 6.7 %collective-permute-start.28 = (f32[64,2048]{1,0:T(8,128)}, f32[64,2048]{1,0:T(8,128)}, u32[]{:S(2)}, u32[]{:S(2)}) collective-permute-start(f32[64,2048]{1,0:T(8,128)} %collective-permute-done.24.refs_5_.refs_11_.refs_9_), channel_id=1, source_target_pairs={{0,1},{1,0},{2,3},{3,2},{4,5},{5,4},{6,7},{7,6},{8,9},{9,8},{10,11... | collective-permute-start | bytes 1572872 | tf_op jit(solution)/shard_map/ppermute | solution.py:963
  153.9 33.5 %collective-permute-start.29 = (f32[640,256]{1,0:T(8,128)S(1)}, f32[640,256]{1,0:T(8,128)}, u32[]{:S(2)}, u32[]{:S(2)}) collective-permute-start(f32[640,256]{1,0:T(8,128)S(1)} %copy-done.3), channel_id=1, source_target_pairs={{0,1},{1,0},{2,3},{3,2},{4,5},{5,4},{6,7},{7,6},{8,9},{9,8},{10,11... | collective-permute-start | bytes 1966088 | tf_op jit(solution)/shard_map/ppermute | solution.py:963
  179.3 8.1 %collective-permute-start.31 = (f32[640,256]{1,0:T(8,128)}, f32[640,256]{1,0:T(8,128)}, u32[]{:S(2)}, u32[]{:S(2)}) collective-permute-start(f32[640,256]{1,0:T(8,128)} %collective-permute-done.30.refs_6_.refs_2_), channel_id=1, source_target_pairs={{0,1},{1,0},{2,3},{3,2},{4,5},{5,4},{6,7},{7,6},{8,9},{9,8},{10,11... | collective-permute-start | bytes 1966088 | tf_op jit(solution)/shard_map/ppermute | solution.py:963
  187.1 31.1 %collective-permute-start.35 = (f32[320,1024]{1,0:T(8,128)S(1)}, f32[320,1024]{1,0:T(8,128)}, u32[]{:S(2)}, u32[]{:S(2)}) collective-permute-start(f32[320,1024]{1,0:T(8,128)S(1)} %collective-permute-done.16.refs_0_.refs_1_.own_ref), channel_id=1, source_target_pairs={{0,1},{1,0},{2,3},{3,2},{4,5},{5,4},{6,7},{7,6},{8,9},{9,8},{10,11... | collective-permute-start | bytes 3932168 | tf_op jit(solution)/shard_map/ppermute | solution.py:963
  187.4 28.5 %collective-permute-start.33 = (f32[320,256]{1,0:T(8,128)}, f32[320,256]{1,0:T(8,128)S(1)}, u32[]{:S(2)}, u32[]{:S(2)}) collective-permute-start(f32[320,256]{1,0:T(8,128)} %get-tuple-element.182), channel_id=1, source_target_pairs={{0,4},{4,0},{1,5},{5,1},{2,6},{6,2},{3,7},{7,3},{8,12},{12,8},{9,1... | collective-permute-start | bytes 983048 | tf_op jit(solution)/shard_map/ppermute | solution.py:960
  216.1 31.7 %collective-permute-start.36 = (f32[320,1024]{1,0:T(8,128)}, f32[320,1024]{1,0:T(8,128)}, u32[]{:S(2)}, u32[]{:S(2)}) collective-permute-start(f32[320,1024]{1,0:T(8,128)} %get-tuple-element.194), channel_id=1, source_target_pairs={{0,2},{2,0},{1,3},{3,1},{4,6},{6,4},{5,7},{7,5},{8,10},{10,8},{9,1... | collective-permute-start | bytes 3932168 | tf_op jit(solution)/shard_map/ppermute | solution.py:29
  229.3 32.4 %collective-permute-start.37 = (f32[2,2,64,1024]{3,2,1,0:T(8,128)}, f32[2,2,64,1024]{3,2,1,0:T(8,128)}, u32[]{:S(2)}, u32[]{:S(2)}) collective-permute-start(f32[2,2,64,1024]{3,2,1,0:T(8,128)} %get-tuple-element.199), channel_id=1, source_target_pairs={{0,8},{1,17},{8,0},{9,25},{16,24},{17,1},{24,16},{25,9},{2,10},{3,... | collective-permute-start | bytes 3145736 | tf_op jit(solution)/shard_map/ppermute | solution.py:882
  236.7 25.0 %collective-permute-start.40 = (f32[2,2,64,1024]{3,2,1,0:T(8,128)}, f32[2,2,64,1024]{3,2,1,0:T(8,128)}, u32[]{:S(2)}, u32[]{:S(2)}) collective-permute-start(f32[2,2,64,1024]{3,2,1,0:T(8,128)} %get-tuple-element.204), channel_id=1, source_target_pairs={{0,8},{1,17},{8,0},{9,25},{16,24},{17,1},{24,16},{25,9},{2,10},{3,... | collective-permute-start | bytes 3145736 | tf_op jit(solution)/shard_map/ppermute | solution.py:882
  237.5 24.0 %collective-permute-start.39 = (f32[320,256]{1,0:T(8,128)}, f32[320,256]{1,0:T(8,128)S(1)}, u32[]{:S(2)}, u32[]{:S(2)}) collective-permute-start(f32[320,256]{1,0:T(8,128)} %get-tuple-element.202), channel_id=1, source_target_pairs={{0,1},{1,0},{2,3},{3,2},{4,5},{5,4},{6,7},{7,6},{8,9},{9,8},{10,11... | collective-permute-start | bytes 983048 | tf_op jit(solution)/shard_map/ppermute | solution.py:963
  243.6 18.1 %collective-permute-start.38 = (f32[320,256]{1,0:T(8,128)S(1)}, f32[320,256]{1,0:T(8,128)S(1)}, u32[]{:S(2)}, u32[]{:S(2)}) collective-permute-start(f32[320,256]{1,0:T(8,128)S(1)} %copy-done.24), channel_id=1, source_target_pairs={{0,4},{4,0},{1,5},{5,1},{2,6},{6,2},{3,7},{7,3},{8,12},{12,8},{9,1... | collective-permute-start | bytes 983048 | tf_op jit(solution)/shard_map/ppermute | solution.py:960
  264.8 17.8 %collective-permute-start.42 = (f32[2,64,2048]{2,1,0:T(8,128)S(1)}, f32[2,64,2048]{2,1,0:T(8,128)S(1)}, u32[]{:S(2)}, u32[]{:S(2)}) collective-permute-start(f32[2,64,2048]{2,1,0:T(8,128)S(1)} %get-tuple-element.209), channel_id=1, source_target_pairs={{0,16},{1,9},{8,24},{9,1},{16,0},{17,25},{24,8},{25,17},{2,18},{3,... | collective-permute-start | bytes 3145736 | tf_op jit(solution)/shard_map/ppermute | solution.py:882
  281.3 28.2 %collective-permute-start.45 = (f32[320,512]{1,0:T(8,128)}, f32[320,512]{1,0:T(8,128)S(1)}, u32[]{:S(2)}, u32[]{:S(2)}) collective-permute-start(f32[320,512]{1,0:T(8,128)} %get-tuple-element.226), channel_id=1, source_target_pairs={{0,2},{2,0},{1,3},{3,1},{4,6},{6,4},{5,7},{7,5},{8,10},{10,8},{9,1... | collective-permute-start | bytes 1966088 | tf_op jit(solution)/shard_map/ppermute | solution.py:29
  283.7 26.8 %collective-permute-start.44 = (f32[64,2048]{1,0:T(8,128)}, f32[64,2048]{1,0:T(8,128)}, u32[]{:S(2)}, u32[]{:S(2)}) collective-permute-start(f32[64,2048]{1,0:T(8,128)} %get-tuple-element.225), channel_id=1, source_target_pairs={{0,5},{1,4},{4,1},{5,0},{2,7},{3,6},{6,3},{7,2},{8,13},{9,12},{12,... | collective-permute-start | bytes 1572872 | tf_op jit(solution)/shard_map/ppermute | solution.py:1084
  292.3 22.2 %collective-permute-start.43 = (f32[2,2,64,1024]{3,2,1,0:T(8,128)}, f32[2,2,64,1024]{3,2,1,0:T(8,128)}, u32[]{:S(2)}, u32[]{:S(2)}) collective-permute-start(f32[2,2,64,1024]{3,2,1,0:T(8,128)} %get-tuple-element.215), channel_id=1, source_target_pairs={{0,8},{1,17},{8,0},{9,25},{16,24},{17,1},{24,16},{25,9},{2,10},{3,... | collective-permute-start | bytes 3145736 | tf_op jit(solution)/shard_map/ppermute | solution.py:882
  299.8 18.9 %collective-permute-start.47 = (f32[2,2,64,1024]{3,2,1,0:T(8,128)}, f32[2,2,64,1024]{3,2,1,0:T(8,128)}, u32[]{:S(2)}, u32[]{:S(2)}) collective-permute-start(f32[2,2,64,1024]{3,2,1,0:T(8,128)} %get-tuple-element.230), channel_id=1, source_target_pairs={{0,8},{1,17},{8,0},{9,25},{16,24},{17,1},{24,16},{25,9},{2,10},{3,... | collective-permute-start | bytes 3145736 | tf_op jit(solution)/shard_map/ppermute | solution.py:882
  310.6 18.0 %collective-permute-start.51 = (f32[320,256]{1,0:T(8,128)}, f32[320,256]{1,0:T(8,128)S(1)}, u32[]{:S(2)}, u32[]{:S(2)}) collective-permute-start(f32[320,256]{1,0:T(8,128)} %get-tuple-element.227), channel_id=1, source_target_pairs={{0,5},{1,4},{4,1},{5,0},{2,7},{3,6},{6,3},{7,2},{8,13},{9,12},{12,... | collective-permute-start | bytes 983048 | tf_op jit(solution)/shard_map/ppermute | solution.py:1110
  321.1 9.2 %collective-permute-start.53 = (f32[64,2048]{1,0:T(8,128)S(1)}, f32[64,2048]{1,0:T(8,128)S(1)}, u32[]{:S(2)}, u32[]{:S(2)}) collective-permute-start(f32[64,2048]{1,0:T(8,128)S(1)} %get-tuple-element.242), channel_id=1, source_target_pairs={{0,16},{1,9},{8,24},{9,1},{16,0},{17,25},{24,8},{25,17},{2,18},{3,... | collective-permute-start | bytes 1572872 | tf_op jit(solution)/shard_map/ppermute | solution.py:882
  330.4 14.8 %collective-permute-start.58 = (f32[64,2048]{1,0:T(8,128)S(1)}, f32[64,2048]{1,0:T(8,128)S(1)}, u32[]{:S(2)}, u32[]{:S(2)}) collective-permute-start(f32[64,2048]{1,0:T(8,128)S(1)} %copy-done.9), channel_id=1, source_target_pairs={{0,8},{1,17},{8,0},{9,25},{16,24},{17,1},{24,16},{25,9},{2,10},{3,... | collective-permute-start | bytes 1572872 | tf_op jit(solution)/shard_map/ppermute | solution.py:882
  331.8 13.4 %collective-permute-start.57 = (f32[64,2048]{1,0:T(8,128)S(1)}, f32[64,2048]{1,0:T(8,128)S(1)}, u32[]{:S(2)}, u32[]{:S(2)}) collective-permute-start(f32[64,2048]{1,0:T(8,128)S(1)} %copy-done.9), channel_id=1, source_target_pairs={{0,16},{1,9},{8,24},{9,1},{16,0},{17,25},{24,8},{25,17},{2,18},{3,... | collective-permute-start | bytes 1572872 | tf_op jit(solution)/shard_map/ppermute | solution.py:882
  332.5 27.4 %collective-permute-start.49 = (f32[320,512]{1,0:T(8,128)S(1)}, f32[320,512]{1,0:T(8,128)S(1)}, u32[]{:S(2)}, u32[]{:S(2)}) collective-permute-start(f32[320,512]{1,0:T(8,128)S(1)} %copy-done.22), channel_id=1, source_target_pairs={{0,2},{2,0},{1,3},{3,1},{4,6},{6,4},{5,7},{7,5},{8,10},{10,8},{9,1... | collective-permute-start | bytes 1966088 | tf_op jit(solution)/shard_map/ppermute | solution.py:29
  332.8 17.2 %collective-permute-start.48 = (f32[64,2048]{1,0:T(8,128)S(1)}, f32[64,2048]{1,0:T(8,128)S(1)}, u32[]{:S(2)}, u32[]{:S(2)}) collective-permute-start(f32[64,2048]{1,0:T(8,128)S(1)} %get-tuple-element.232), channel_id=1, source_target_pairs={{0,16},{1,9},{8,24},{9,1},{16,0},{17,25},{24,8},{25,17},{2,18},{3,... | collective-permute-start | bytes 1572872 | tf_op jit(solution)/shard_map/ppermute | solution.py:882
  334.1 25.9 %collective-permute-start.54 = (f32[64,2048]{1,0:T(8,128)S(1)}, f32[64,2048]{1,0:T(8,128)S(1)}, u32[]{:S(2)}, u32[]{:S(2)}) collective-permute-start(f32[64,2048]{1,0:T(8,128)S(1)} %reduction_step.12), channel_id=1, source_target_pairs={{0,4},{4,0},{1,5},{5,1},{2,6},{6,2},{3,7},{7,3},{8,12},{12,8},{9,1... | collective-permute-start | bytes 1572872 | tf_op jit(solution)/shard_map/ppermute | solution.py:960
  345.2 14.8 %collective-permute-start.59 = (f32[64,2048]{1,0:T(8,128)S(1)}, f32[64,2048]{1,0:T(8,128)S(1)}, u32[]{:S(2)}, u32[]{:S(2)}) collective-permute-start(f32[64,2048]{1,0:T(8,128)S(1)} %collective-permute-done.58.refs_2_), channel_id=1, source_target_pairs={{0,16},{1,9},{8,24},{9,1},{16,0},{17,25},{24,8},{25,17},{2,18},{3,... | collective-permute-start | bytes 1572872 | tf_op jit(solution)/shard_map/ppermute | solution.py:882
  360.1 12.6 %collective-permute-start.61 = (f32[64,2048]{1,0:T(8,128)S(1)}, f32[64,2048]{1,0:T(8,128)S(1)}, u32[]{:S(2)}, u32[]{:S(2)}) collective-permute-start(f32[64,2048]{1,0:T(8,128)S(1)} %reduction_step.13.refs_0_), channel_id=1, source_target_pairs={{0,8},{1,17},{8,0},{9,25},{16,24},{17,1},{24,16},{25,9},{2,10},{3,... | collective-permute-start | bytes 1572872 | tf_op jit(solution)/shard_map/ppermute | solution.py:882
  360.9 11.7 %collective-permute-start.60 = (f32[64,2048]{1,0:T(8,128)S(1)}, f32[64,2048]{1,0:T(8,128)S(1)}, u32[]{:S(2)}, u32[]{:S(2)}) collective-permute-start(f32[64,2048]{1,0:T(8,128)S(1)} %reduction_step.13.refs_0_), channel_id=1, source_target_pairs={{0,16},{1,9},{8,24},{9,1},{16,0},{17,25},{24,8},{25,17},{2,18},{3,... | collective-permute-start | bytes 1572872 | tf_op jit(solution)/shard_map/ppermute | solution.py:882
  362.2 15.6 %collective-permute-start.55 = (f32[320,256]{1,0:T(8,128)S(1)}, f32[320,256]{1,0:T(8,128)S(1)}, u32[]{:S(2)}, u32[]{:S(2)}) collective-permute-start(f32[320,256]{1,0:T(8,128)S(1)} %copy-done.23), channel_id=1, source_target_pairs={{0,4},{4,0},{1,5},{5,1},{2,6},{6,2},{3,7},{7,3},{8,12},{12,8},{9,1... | collective-permute-start | bytes 983048 | tf_op jit(solution)/shard_map/ppermute | solution.py:960
  372.6 9.2 %collective-permute-start.62 = (f32[64,2048]{1,0:T(8,128)S(1)}, f32[64,2048]{1,0:T(8,128)S(1)}, u32[]{:S(2)}, u32[]{:S(2)}) collective-permute-start(f32[64,2048]{1,0:T(8,128)S(1)} %collective-permute-done.61.refs_2_), channel_id=1, source_target_pairs={{0,16},{1,9},{8,24},{9,1},{16,0},{17,25},{24,8},{25,17},{2,18},{3,... | collective-permute-start | bytes 1572872 | tf_op jit(solution)/shard_map/ppermute | solution.py:882
  (41 other events, 274.7 us)
